TPU v7x, 32 devices: a whole 2x2x4 slice. The times are simulated.
32 devices in a mesh: gx: 4 (over z), gy: 2 (over x), gz: 4 (over y, core).
Axes of the slice: x: 2, y: 2, z: 4, core: 2. Of those that a mesh axis runs over, the one named last changes fastest.
Arguments:
- populations: float32 [19, 16, 16, 512], P(None, 'gx', 'gy', 'gz'), may hold values from 0.02 to 0.09
- solid_cells: int32 [16, 16, 512], P('gx', 'gy', 'gz'), may hold values 0 or 1
- slot_cells: int32 [4, 2, 4, 64, 8, 128], P('gx', 'gy', 'gz'), may hold values from 0 to 4095
- slot_weights: float32 [4, 2, 4, 64, 8, 128], P('gx', 'gy', 'gz'), may hold values from 0 to 0.0625
- slot_owner: int32 [4, 2, 4, 64, 1], P('gx', 'gy', 'gz'), may hold values from 0 to 7; in each aligned block of 64 rows (0 to 63, 64 to 127, ..., all dimensions but the last counted through in order) at most 16 rows name the same one
- slot_block: int32 [4, 2, 4, 64], P('gx', 'gy', 'gz'), may hold values from 0 to 31
- train_of_block: int32 [4, 2, 4, 32], P('gx', 'gy', 'gz'), may hold values from 0 to 3
- marker_area: float32 [4, 2, 4, 32, 128], P('gx', 'gy', 'gz'), may hold values from 0.5 to 2
- train_velocity: float32 [4, 3], replicated, may hold values from -0.1 to 0.1
Outputs:
- populations_next: float32 [19, 16, 16, 512], P(None, 'gx', 'gy', 'gz')
- marker_force: float32 [4, 2, 4, 32, 3, 128], P('gx', 'gy', 'gz')
Inputs may be any that keep to these rules, and one draw needn't show every extreme that they name: `slot_owner`: among the 64 slots of one device no owner is named more than 16 times, a bound that some block reaches.
All inputs are finite; a program needn't handle non-finite values. No bound on the sum of `solid_cells` on one device may be relied on, other than what follows from the above.
Results may differ from a plain program's by a relative error of at most 0.000065.
Values sent between devices are 32-bit elements; how exact they have to be, the bound alone decides.
No kernel may reach another device: no remote copies, remote signals or barrier semaphores. Data moves between devices by JAX's collectives and lax.ppermute only.
A program may use at most 128 MiB of HBM per device.

v0:
```python
import functools
import jax
import jax.numpy as jnp
import numpy as np
from jax import lax
from jax.experimental import pallas as pl
from jax.experimental.pallas import tpu as pltpu
from jax.sharding import PartitionSpec as P

velocity_table = np.array(
    [
        [0, 0, 0],
        [1, 0, 0],
        [-1, 0, 0],
        [0, 1, 0],
        [0, -1, 0],
        [0, 0, 1],
        [0, 0, -1],
        [1, 1, 0],
        [-1, -1, 0],
        [1, -1, 0],
        [-1, 1, 0],
        [1, 0, 1],
        [-1, 0, -1],
        [1, 0, -1],
        [-1, 0, 1],
        [0, 1, 1],
        [0, -1, -1],
        [0, 1, -1],
        [0, -1, 1],
    ]
)
weight_table = [1.0 / 3.0] + [1.0 / 18.0] * 6 + [1.0 / 36.0] * 12
opposite_table = [0, 2, 1, 4, 3, 6, 5, 8, 7, 10, 9, 12, 11, 14, 13, 16, 15, 18, 17]
stress_pairs = [(0, 0), (1, 1), (2, 2), (0, 1), (0, 2), (1, 2)]
tau_base = 0.55
smag_term = 18.0 * 1.4142135623730951 * 0.17 * 0.17
regular_eps = 0.0001
stiffness = 2.0
far_velocity = (0.02, 0.06, 0.0)
vmem_bytes = 40 << 20
group = 8


def going(axis, step):
    return [q for q in range(19) if int(velocity_table[q][axis]) == step]


def project(direction, vector):
    projection = 0.0 * vector[0]
    for component in range(3):
        lattice_step = int(velocity_table[direction][component])
        if lattice_step != 0:
            projection = projection + lattice_step * vector[component]
    return projection


def moments(populations):
    density = populations[0]
    momentum = [jnp.zeros_like(density) for component in range(3)]
    for direction in range(1, 19):
        density = density + populations[direction]
        for component in range(3):
            lattice_step = int(velocity_table[direction][component])
            if lattice_step == 1:
                momentum[component] = momentum[component] + populations[direction]
            elif lattice_step == -1:
                momentum[component] = momentum[component] - populations[direction]
    return (density, momentum)


def equilibrium(density, velocity):
    speed_sq = velocity[0] * velocity[0] + velocity[1] * velocity[1] + velocity[2] * velocity[2]
    result = []
    for direction in range(19):
        projected = project(direction, velocity)
        result.append(
            weight_table[direction]
            * density
            * (1.0 + 3.0 * projected + 4.5 * projected * projected - 1.5 * speed_sq)
        )
    return result


far_field = [float(np.float32(value)) for value in equilibrium(1.0, list(far_velocity))]


def collide(populations, cell_force, solid_cells):
    density, momentum = moments(populations)
    velocity = [
        (momentum[component] + 0.5 * cell_force[component]) / density for component in range(3)
    ]
    balance = equilibrium(density, velocity)
    stress = [jnp.zeros_like(density) for pair_pos in range(6)]
    for direction in range(19):
        non_eq = populations[direction] - balance[direction]
        for pair_pos in range(6):
            row_axis, col_axis = stress_pairs[pair_pos]
            factor = int(velocity_table[direction][row_axis] * velocity_table[direction][col_axis])
            if factor != 0:
                stress[pair_pos] = stress[pair_pos] + factor * non_eq
    shear_sq = stress[0] * stress[0] + stress[1] * stress[1] + stress[2] * stress[2]
    shear_sq = shear_sq + 2.0 * (
        stress[3] * stress[3] + stress[4] * stress[4] + stress[5] * stress[5]
    )
    magnitude = jnp.sqrt(shear_sq + regular_eps)
    relax_time = 0.5 * (tau_base + jnp.sqrt(tau_base * tau_base + smag_term * magnitude / density))
    relax_rate = 1.0 / relax_time
    guo_factor = 1.0 - 0.5 * relax_rate
    speed_force = (
        velocity[0] * cell_force[0] + velocity[1] * cell_force[1] + velocity[2] * cell_force[2]
    )
    result = []
    for direction in range(19):
        along_force = project(direction, cell_force)
        along_speed = project(direction, velocity)
        source = (
            guo_factor
            * weight_table[direction]
            * (3.0 * (along_force - speed_force) + 9.0 * along_speed * along_force)
        )
        relaxed = (
            populations[direction]
            - (populations[direction] - balance[direction]) * relax_rate
            + source
        )
        result.append(jnp.where(solid_cells == 1, populations[opposite_table[direction]], relaxed))
    return result


def with_halo(cells, sides, width):
    for axis, dim in sides:
        count = lax.axis_size(axis)
        head = lax.slice_in_dim(cells, 0, width, axis=dim)
        tail = lax.slice_in_dim(cells, cells.shape[dim] - width, cells.shape[dim], axis=dim)
        cells = jnp.concatenate(
            [
                lax.ppermute(tail, axis, [(i, (i + 1) % count) for i in range(count)]),
                cells,
                lax.ppermute(head, axis, [((i + 1) % count, i) for i in range(count)]),
            ],
            axis=dim,
        )
    return cells


def settle(received, labels, owned, train_of_block, marker_area, train_velocity, mark):
    rows_in = received.reshape(-1, 3 * mark)
    label_rows = labels.reshape(-1)
    owner_match = (label_rows[None, :] == jnp.arange(owned, dtype=jnp.int32)[:, None]).astype(
        jnp.float32
    )
    marker_velocity = jnp.dot(owner_match, rows_in, precision=lax.Precision.HIGHEST).reshape(
        owned, 3, mark
    )
    trains = train_velocity.shape[0]
    train_rows = train_of_block.reshape(owned)
    train_match = (train_rows[:, None] == jnp.arange(trains, dtype=jnp.int32)[None, :]).astype(
        jnp.float32
    )
    target = jnp.dot(train_match, train_velocity, precision=lax.Precision.HIGHEST)
    areas = marker_area.reshape(owned, mark)
    marker_force = stiffness * areas[:, None, :] * (target[:, :, None] - marker_velocity)
    back_rows = jnp.dot(
        owner_match.T, marker_force.reshape(owned, 3 * mark), precision=lax.Precision.HIGHEST
    )
    return (marker_force, back_rows)


def per_device_general(
    populations,
    solid_cells,
    slot_cells,
    slot_weights,
    slot_owner,
    slot_block,
    train_of_block,
    marker_area,
    train_velocity,
):
    size_x, size_y, size_z = (populations.shape[1], populations.shape[2], populations.shape[3])
    cell_count = size_x * size_y * size_z
    slots, kernel, mark = (slot_cells.shape[3], slot_cells.shape[4], slot_cells.shape[5])
    owned = train_of_block.shape[3]
    peers_x = lax.axis_size("gx")
    peers_y = lax.axis_size("gy")
    peers = peers_x * peers_y
    capacity = max(2, 2 * slots // peers)
    density, momentum = moments(populations)
    rest_velocity = jnp.stack([momentum[component] / density for component in range(3)]).reshape(
        3, cell_count
    )
    cells = slot_cells.reshape(slots, kernel, mark)
    weights = slot_weights.reshape(slots, kernel, mark)
    partial_value = jnp.sum(rest_velocity[:, cells] * weights[None], axis=2)
    slot_rows = partial_value.transpose(1, 0, 2).reshape(slots, 3 * mark)
    slot_dest = slot_owner.reshape(slots)
    blocks = slot_block.reshape(slots)
    order = jnp.arange(slots, dtype=jnp.int32)
    earlier = (slot_dest[None, :] == slot_dest[:, None]) & (order[None, :] < order[:, None])
    slot_rank = jnp.sum(earlier.astype(jnp.int32), axis=1)
    target_row = slot_dest * capacity + slot_rank
    buffer_rows = jnp.arange(peers * capacity, dtype=jnp.int32)
    matches = buffer_rows[:, None] == target_row[None, :]
    placement = matches.astype(jnp.float32)
    outgoing = jnp.dot(placement, slot_rows, precision=lax.Precision.HIGHEST)
    labels = jnp.sum(jnp.where(matches, blocks[None, :] + 1, 0), axis=1) - 1
    received, got_labels = (
        lax.all_to_all(
            outgoing.reshape(peers, capacity, 3 * mark),
            ("gx", "gy"),
            split_axis=0,
            concat_axis=0,
            tiled=True,
        ),
        lax.all_to_all(
            labels.reshape(peers, capacity), ("gx", "gy"), split_axis=0, concat_axis=0, tiled=True
        ),
    )
    marker_force, back_rows = settle(
        received, got_labels, owned, train_of_block, marker_area, train_velocity, mark
    )
    returned = lax.all_to_all(
        back_rows.reshape(peers, capacity, 3 * mark),
        ("gx", "gy"),
        split_axis=0,
        concat_axis=0,
        tiled=True,
    )
    slot_force = jnp.dot(
        placement.T, returned.reshape(peers * capacity, 3 * mark), precision=lax.Precision.HIGHEST
    )
    slot_force = slot_force.reshape(slots, 3, mark).transpose(1, 0, 2)
    contrib = weights[None] * slot_force[:, :, None, :]
    cell_force = (
        jnp.zeros((3, cell_count), jnp.float32).at[:, cells.reshape(-1)].add(contrib.reshape(3, -1))
    )
    cell_force = cell_force.reshape(3, size_x, size_y, size_z)
    relaxed = collide(populations, cell_force, solid_cells)
    padded = with_halo(jnp.stack(relaxed), (("gx", 1), ("gy", 2), ("gz", 3)), 1)
    parts = []
    for direction in range(19):
        shift_x = 1 - int(velocity_table[direction][0])
        shift_y = 1 - int(velocity_table[direction][1])
        shift_z = 1 - int(velocity_table[direction][2])
        parts.append(
            padded[
                direction,
                shift_x : shift_x + size_x,
                shift_y : shift_y + size_y,
                shift_z : shift_z + size_z,
            ]
        )
    read = jnp.stack(parts)
    total_y = size_y * lax.axis_size("gy")
    total_z = size_z * lax.axis_size("gz")
    global_y = lax.axis_index("gy") * size_y + jnp.arange(size_y, dtype=jnp.int32)
    global_z = lax.axis_index("gz") * size_z + jnp.arange(size_z, dtype=jnp.int32)
    on_side = ((global_y == 0) | (global_y == total_y - 1))[:, None] | (
        (global_z == 0) | (global_z == total_z - 1)
    )[None, :]
    far_field = jnp.array(equilibrium(1.0, list(far_velocity)), dtype=jnp.float32)
    populations_next = jnp.where(on_side[None, None], far_field[:, None, None, None], read)
    return (populations_next, marker_force.reshape(1, 1, 1, owned, 3, mark))


def full(shape):
    return jax.ShapeDtypeStruct(shape, jnp.float32)


def kernel_params():
    return pltpu.CompilerParams(vmem_limit_bytes=vmem_bytes)


def low_half(shape):
    return lax.broadcasted_iota(jnp.int32, shape, 1) < shape[1] // 2


def fetch(pairs, sems):
    copies = [
        pltpu.make_async_copy(source, target, sems.at[i])
        for i, (source, target) in enumerate(pairs)
    ]
    for copy in copies:
        copy.start()
    return copies


def shard_rows(slots, owned):
    return 3 * slots + owned + 8


def sample_kernel(
    place_ref, pop_any, cells_any, weights_any, areas_ref, owner_ref, block_ref, trains_ref,
    out_ref, pop_ref, cells_ref, weights_ref, table, sems,
):
    rows, lanes = (pop_ref.shape[1], pop_ref.shape[2])
    mark = cells_ref.shape[1]
    owned = areas_ref.shape[0]
    slots = owner_ref.shape[1]
    kernel = cells_ref.shape[0] // slots
    copies = fetch(
        ((pop_any, pop_ref), (cells_any, cells_ref), (weights_any, weights_ref)), sems
    )
    meta = 3 * slots + owned
    out_ref[3 * slots : meta, :] = areas_ref[...]
    out_ref[meta : meta + 8, :] = jnp.zeros((8, mark), jnp.float32)
    ids = (owner_ref[...] * owned + block_ref[...]).astype(jnp.float32)
    out_ref[meta : meta + 1, :] = jnp.concatenate([ids] * (mark // slots), axis=1)
    out_ref[meta + 1 : meta + 2, 0:owned] = trains_ref[...].astype(jnp.float32)
    mine = lax.broadcasted_iota(jnp.int32, (1, mark), 1) % owned + place_ref[2] * owned
    out_ref[meta + 2 : meta + 3, :] = mine.astype(jnp.float32)
    copies[0].wait()
    density, momentum = moments([pop_ref[q] for q in range(19)])
    fixed = [
        ((momentum[c] / density) * float(2**bits) + (2.0 ** (bits - 1) + 0.5)).astype(jnp.int32)
        for c, bits in enumerate((21, 21, 22))
    ]
    table[0] = (fixed[0] << 11) | (fixed[2] >> 11)
    table[1] = (fixed[1] << 11) | (fixed[2] & 2047)
    copies[1].wait()
    copies[2].wait()

    def body(step, carry):
        first = pl.multiple_of(step * group, group)
        total = [jnp.zeros((group, mark), jnp.float32) for c in range(3)]
        for k in range(kernel):
            at = pl.ds(first * kernel + k, group, stride=kernel)
            cells = cells_ref[at, :]
            lane = cells & (lanes - 1)
            row = cells >> (lanes.bit_length() - 1)
            words = [jnp.zeros((group, mark), jnp.int32) for c in range(2)]
            for r in range(rows):
                here = row == r
                for c in range(2):
                    line = jnp.broadcast_to(table[c, r : r + 1, :], (group, lanes))
                    got = jnp.take_along_axis(line, lane, axis=1, mode="promise_in_bounds")
                    words[c] = jnp.where(here, got, words[c])
            last = ((words[0] & 2047) << 11) | (words[1] & 2047)
            picked = [
                lax.shift_right_logical(words[0], 11),
                lax.shift_right_logical(words[1], 11),
                last,
            ]
            weight = weights_ref[at, :]
            for c, bits in enumerate((21, 21, 22)):
                value = (picked[c].astype(jnp.float32) - 2.0 ** (bits - 1)) * 2.0**-bits
                total[c] = total[c] + weight * value
        for c in range(3):
            out_ref[pl.ds(pl.multiple_of(c * slots + first, group), group), :] = total[c]
        return carry

    lax.fori_loop(0, slots // group, body, 0)


def sample(place, populations, cells, weights, areas, owner, block, trains):
    smem = pl.BlockSpec(memory_space=pltpu.SMEM)
    hbm = pl.BlockSpec(memory_space=pltpu.HBM)
    vmem = pl.BlockSpec(memory_space=pltpu.VMEM)
    return pl.pallas_call(
        sample_kernel,
        out_shape=full((shard_rows(owner.shape[1], areas.shape[0]), cells.shape[1])),
        in_specs=[smem] + [hbm] * 3 + [vmem] * 4,
        scratch_shapes=[
            pltpu.VMEM(populations.shape, jnp.float32),
            pltpu.VMEM(cells.shape, jnp.int32),
            pltpu.VMEM(weights.shape, jnp.float32),
            pltpu.VMEM((2,) + populations.shape[1:], jnp.int32),
            pltpu.SemaphoreType.DMA((3,)),
        ],
        compiler_params=kernel_params(),
        name="sample",
    )(place, populations, cells, weights, areas, owner, block, trains)


def three_parts(values):
    parts = []
    for _ in range(3):
        parts.append(values.astype(jnp.bfloat16))
        values = values - parts[-1].astype(jnp.float32)
    return parts


def one_hot(mask):
    return jnp.where(mask, 1.0, 0.0).astype(jnp.bfloat16)


def settle_rows(speeds_ref, shards, slots, owned):
    mark = shards[0].shape[1]
    meta = 3 * slots + owned
    own = shards[0][meta : meta + 8, :]
    ids = jnp.broadcast_to(own[0:1], (mark, mark)).T[0:slots]
    mine = jnp.broadcast_to(own[2:3], (mark, mark)).T[0:owned]
    wanted = jnp.concatenate([ids, mine], axis=0)
    sums = area = trains = None
    for shard in shards:
        labels = shard[meta : meta + 1, :]
        match = one_hot(wanted == labels)
        match = jnp.concatenate([match, match[:, 0:slots]], axis=1)
        values = jnp.concatenate([shard[c * slots : (c + 1) * slots, :] for c in range(3)], axis=1)
        got = jnp.dot(
            match, jnp.concatenate(three_parts(values), axis=0), preferred_element_type=jnp.float32
        )
        sums = got if sums is None else sums + got
        held = ids == shard[meta + 2 : meta + 3, :]
        parts = three_parts(shard[3 * slots : meta, :])
        parts.append(jnp.zeros_like(parts[0]))
        got = jnp.dot(
            one_hot(held), jnp.concatenate(parts, axis=0), preferred_element_type=jnp.float32
        )
        area = got if area is None else area + got
        got = jnp.where(held, shard[meta + 1 : meta + 2, :], 0.0)
        trains = got if trains is None else trains + got
    trains = jnp.sum(trains, axis=1, keepdims=True)
    own_trains = jnp.broadcast_to(own[1:2], (mark, mark)).T[0:owned]
    forces = []
    own_forces = []
    for c in range(3):
        target = jnp.zeros(trains.shape, jnp.float32)
        own_target = jnp.zeros(own_trains.shape, jnp.float32)
        for train in range(speeds_ref.shape[0]):
            speed = speeds_ref[train, c]
            target = jnp.where(trains == float(train), speed, target)
            own_target = jnp.where(own_trains == float(train), speed, own_target)
        got = sums[:, c * mark : (c + 1) * mark]
        forces.append(stiffness * area * (target - got[0:slots]))
        own_area = shards[0][3 * slots : meta, :]
        own_forces.append(stiffness * own_area * (own_target - got[slots:]))
    return (forces, own_forces)


def spread_kernel(shard_count, slots, owned, place_ref, speeds_ref, *refs):
    shards, refs = (refs[:shard_count], refs[shard_count:])
    cells_any, weights_any, pop_any, solid_ref, relaxed_ref, send_ref, marker_ref = refs[:7]
    cells_ref, weights_ref, pop_ref, force_ref, acc, sems = refs[7:]
    rows, lanes = (pop_ref.shape[1], pop_ref.shape[2])
    size_y = 8
    mark = cells_ref.shape[1]
    kernel = cells_ref.shape[0] // slots
    bf = jnp.bfloat16
    copies = fetch(
        ((cells_any, cells_ref), (weights_any, weights_ref), (pop_any, pop_ref)), sems
    )
    forces, own_forces = settle_rows(speeds_ref, shards, slots, owned)
    for c in range(3):
        force_ref[c] = forces[c]
        marker_ref[:, c, :] = own_forces[c]

    acc[...] = jnp.zeros_like(acc)
    iota = lax.broadcasted_iota(jnp.int32, (16, mark), 0).astype(jnp.float32)
    steps = [(iota + 16.0 * j).astype(bf) for j in range(max(rows, lanes) // 16)]
    one, zero = (jnp.ones((16, mark), bf), jnp.zeros((16, mark), bf))
    copies[0].wait()
    copies[1].wait()

    def wide(entries, i):
        return jnp.broadcast_to(entries[i : i + 1, :], (16, mark)).astype(bf)

    def body(step, carry):
        first = pl.multiple_of(step * group, group)
        force = [force_ref[c, pl.ds(first, group), :] for c in range(3)]
        for k in range(kernel):
            at = pl.ds(first * kernel + k, group, stride=kernel)
            cells = cells_ref[at, :]
            weight = weights_ref[at, :]
            lane = (cells & (lanes - 1)).astype(jnp.float32)
            row = (cells >> (lanes.bit_length() - 1)).astype(jnp.float32)
            parts = []
            for c in range(3):
                value = weight * force[c]
                high = value.astype(bf).astype(jnp.float32)
                parts += [high, value - high]
            left, right = ([], [])
            for i in range(group):
                lane_i, row_i = (wide(lane, i), wide(row, i))
                left.append(
                    jnp.concatenate(
                        [jnp.where(steps[j] == lane_i, one, zero) for j in range(lanes // 16)],
                        axis=0,
                    )
                )
                masks = [steps[j] == row_i for j in range(rows // 16)]
                pieces = []
                for part in parts:
                    part_i = wide(part, i)
                    pieces += [jnp.where(mask, part_i, zero) for mask in masks]
                right.append(jnp.concatenate(pieces, axis=0))
            acc[...] += lax.dot_general(
                jnp.concatenate(left, axis=1),
                jnp.concatenate(right, axis=1),
                (((1,), (1,)), ((), ())),
                preferred_element_type=jnp.float32,
            )
        return carry

    lax.fori_loop(0, slots // group, body, 0)
    copies[2].wait()
    spare = jnp.zeros((lanes, -acc.shape[1] % 128), jnp.float32)
    turned = jnp.concatenate([acc[...], spare], axis=1)
    turned = jnp.concatenate([turned[:, 0:128].T, turned[:, 128:256].T], axis=0)
    cell_force = [
        turned[2 * c * rows : (2 * c + 1) * rows] + turned[(2 * c + 1) * rows : (2 * c + 2) * rows]
        for c in range(3)
    ]
    relaxed = collide([pop_ref[q] for q in range(19)], cell_force, solid_ref[...])
    for q in range(19):
        relaxed_ref[q] = relaxed[q]
    lane_at = lax.broadcasted_iota(jnp.int32, (size_y, lanes), 1)
    packs = []
    for step in (1, -1):
        packed = jnp.zeros((size_y, lanes), jnp.float32)
        for i, q in enumerate(going(2, step)):
            edge = lanes - 1 if step == 1 else 0
            for x in range(rows // size_y):
                moved = pltpu.roll(
                    relaxed[q][x * size_y : (x + 1) * size_y], (8 * x + i - edge) % lanes, 1
                )
                packed = jnp.where(lane_at == 8 * x + i, moved, packed)
        packs.append(packed)
    y_index, z_index = (place_ref[0], place_ref[1])
    count_z = peers_z(send_ref)
    side = 1 - y_index
    for peer in range(send_ref.shape[0]):
        peer_y, peer_z = divmod(peer, count_z)
        send_ref[peer, 0:8, :] = jnp.where(z_index < peer_z, packs[0], packs[1])
    face = side * count_z + z_index
    for i in range(5):
        for x in range(rows // size_y):
            up = relaxed[going(1, 1)[i]][size_y * x + size_y - 1 : size_y * x + size_y, :]
            down = relaxed[going(1, -1)[i]][size_y * x : size_y * x + 1, :]
            send_ref[face, 4 * i + x : 4 * i + x + 1, :] = jnp.where(y_index == 0, up, down)


def peers_z(ref):
    return ref.shape[0] // 2


def spread(count_z, slots, owned, place, speeds, shards, cells, weights, populations, solid):
    mark = cells.shape[1]
    line_count, lanes = solid.shape
    smem = pl.BlockSpec(memory_space=pltpu.SMEM)
    hbm = pl.BlockSpec(memory_space=pltpu.HBM)
    vmem = pl.BlockSpec(memory_space=pltpu.VMEM)
    return pl.pallas_call(
        functools.partial(spread_kernel, len(shards), slots, owned),
        out_shape=(
            full(populations.shape),
            full((2 * count_z, 24, lanes)),
            full((owned, 3, mark)),
        ),
        in_specs=[smem] * 2 + [vmem] * len(shards) + [hbm] * 3 + [vmem],
        scratch_shapes=[
            pltpu.VMEM(cells.shape, jnp.int32),
            pltpu.VMEM(weights.shape, jnp.float32),
            pltpu.VMEM(populations.shape, jnp.float32),
            pltpu.VMEM((3, slots, mark), jnp.float32),
            pltpu.VMEM((lanes, 6 * line_count), jnp.float32),
            pltpu.SemaphoreType.DMA((3,)),
        ],
        compiler_params=kernel_params(),
        name="spread",
    )(place, speeds, *shards, cells, weights, populations, solid)


def stream_kernel(place_ref, relaxed_ref, got_ref, out_any, far_ref, near_ref, out_ref, sem):
    size_x, size_y, lanes = out_ref.shape[1:]
    shape = (size_y, lanes)
    y_at = lax.broadcasted_iota(jnp.int32, shape, 0)
    z_at = lax.broadcasted_iota(jnp.int32, shape, 1)
    y_index, z_index = (place_ref[0], place_ref[1])
    count_z = peers_z(got_ref)
    side = (1 - y_index) * count_z
    here = y_index * count_z
    z_from = {1: jnp.maximum(z_index - 1, 0), -1: jnp.minimum(z_index + 1, count_z - 1)}
    near = {step: got_ref[here + z_from[step], 0:8, :] for step in (1, -1)}
    far = {step: got_ref[side + z_from[step], 0:8, :] for step in (1, -1)}
    near[0] = None
    on_side = y_at == jnp.where(y_index == 0, 0, size_y - 1)
    on_side = on_side | ((z_at == 0) & (z_index == 0))
    on_side = on_side | ((z_at == lanes - 1) & (z_index == count_z - 1))
    leaving = {}
    for q in range(19):
        step_x, step_y, step_z = (int(step) for step in velocity_table[q])
        y_edge = 0 if step_y == 1 else size_y - 1
        z_edge = 0 if step_z == 1 else lanes - 1
        column = near[step_z]
        if step_z != 0 and step_y != 0:
            column = jnp.where(
                y_at == y_edge,
                pltpu.roll(far[step_z], step_y % size_y, 0),
                pltpu.roll(column, step_y % size_y, 0),
            )
        for x in range(size_x):
            cells = relaxed_ref[q, x * size_y : (x + 1) * size_y, :]
            if step_y != 0:
                at = 4 * going(1, step_y).index(q) + x
                halo = got_ref[side + z_index, at : at + 1, :]
                cells = jnp.where(y_at == y_edge, halo, pltpu.roll(cells, step_y % size_y, 0))
            if step_z != 0:
                at = 8 * x + going(2, step_z).index(q)
                cells = jnp.where(
                    z_at == z_edge,
                    pltpu.roll(column, (z_edge - at) % lanes, 1),
                    pltpu.roll(cells, step_z % lanes, 1),
                )
            cells = jnp.where(on_side, far_field[q], cells)
            target = x + step_x
            if 0 <= target < size_x:
                out_ref[q, target] = cells
            else:
                leaving[q] = cells
    for q in going(0, 1):
        out_ref[q, 0] = jnp.zeros(shape, jnp.float32)
    for q in going(0, -1):
        out_ref[q, size_x - 1] = jnp.zeros(shape, jnp.float32)
    copy = pltpu.make_async_copy(out_ref, out_any, sem)
    copy.start()
    even = place_ref[3] == 0
    for i in range(5):
        ahead, behind = (leaving[going(0, 1)[i]], leaving[going(0, -1)[i]])
        far_ref[i] = jnp.where(even, behind, ahead)
        near_ref[i] = jnp.where(even, ahead, behind)
    copy.wait()


def stream(size_y, place, relaxed, got):
    rows, lanes = relaxed.shape[1:]
    smem = pl.BlockSpec(memory_space=pltpu.SMEM)
    hbm = pl.BlockSpec(memory_space=pltpu.HBM)
    vmem = pl.BlockSpec(memory_space=pltpu.VMEM)
    face = full((5, size_y, lanes))
    shape = (19, rows // size_y, size_y, lanes)
    return pl.pallas_call(
        stream_kernel,
        out_shape=(full(shape), face, face),
        in_specs=[smem, vmem, vmem],
        out_specs=[hbm, vmem, vmem],
        scratch_shapes=[pltpu.VMEM(shape, jnp.float32), pltpu.SemaphoreType.DMA],
        compiler_params=kernel_params(),
        name="stream",
    )(place, relaxed, got)


def place_kernel(place_ref, next_any, far_any, near_any, out_any, sems):
    size_x = out_any.shape[1]
    odd = place_ref[3]
    copies = []
    for i in range(5):
        ahead, behind = (going(0, 1)[i], going(0, -1)[i])
        for which, source in enumerate((far_any, near_any)):
            from_behind = odd == which
            q = jnp.where(from_behind, ahead, behind)
            x = jnp.where(from_behind, 0, size_x - 1)
            copies.append((source.at[i], out_any.at[q, x]))
    for copy in fetch(copies, sems):
        copy.wait()


def place_faces(place, inner, far, near):
    smem = pl.BlockSpec(memory_space=pltpu.SMEM)
    anywhere = pl.BlockSpec(memory_space=pl.ANY)
    hbm = pl.BlockSpec(memory_space=pltpu.HBM)
    return pl.pallas_call(
        place_kernel,
        out_shape=full(inner.shape),
        in_specs=[smem, hbm, anywhere, anywhere],
        out_specs=hbm,
        scratch_shapes=[pltpu.SemaphoreType.DMA((10,))],
        input_output_aliases={1: 0},
        name="place_faces",
    )(place, inner, far, near)


def per_device(
    populations,
    solid_cells,
    slot_cells,
    slot_weights,
    slot_owner,
    slot_block,
    train_of_block,
    marker_area,
    train_velocity,
):
    size_x, size_y, size_z = (populations.shape[1], populations.shape[2], populations.shape[3])
    lines = size_x * size_y
    slots, kernel, mark = (slot_cells.shape[3], slot_cells.shape[4], slot_cells.shape[5])
    owned = train_of_block.shape[3]
    count_x, count_y, count_z = (lax.axis_size(axis) for axis in ("gx", "gy", "gz"))
    x_index, y_index, z_index = (lax.axis_index(axis) for axis in ("gx", "gy", "gz"))
    place = jnp.stack([y_index, z_index, x_index * count_y + y_index, x_index % 2])
    place = place.astype(jnp.int32)
    pops = populations.reshape(19, lines, size_z)
    cells = slot_cells.reshape(slots * kernel, mark)
    weights = slot_weights.reshape(slots * kernel, mark)
    own = sample(
        place,
        pops,
        cells,
        weights,
        marker_area.reshape(owned, mark),
        slot_owner.reshape(1, slots),
        slot_block.reshape(1, slots),
        train_of_block.reshape(1, owned),
    )
    swap = [(0, 1), (1, 0)]
    column = [own]
    for distance in reversed(range(1, count_x)):
        column.append(lax.ppermute(own, "gx", [(i, i ^ distance) for i in range(count_x)]))
    shards = column + [lax.ppermute(shard, "gy", swap) for shard in column]
    relaxed, sides, marker_force = spread(
        count_z,
        slots,
        owned,
        place,
        train_velocity,
        shards,
        cells,
        weights,
        pops,
        solid_cells.reshape(lines, size_z),
    )
    sides = lax.all_to_all(sides, ("gy", "gz"), split_axis=0, concat_axis=0, tiled=True)
    inner, far, near = stream(size_y, place, relaxed, sides)
    evens = range(0, count_x, 2)
    far = lax.ppermute(
        far,
        "gx",
        [(i, (i - 1) % count_x) for i in evens] + [((i - 1) % count_x, i) for i in evens],
    )
    near = lax.ppermute(near, "gx", [(i, i + 1) for i in evens] + [(i + 1, i) for i in evens])
    return (place_faces(place, inner, far, near), marker_force.reshape(1, 1, 1, owned, 3, mark))


def solution(mesh):
    placed = (
        P(None, "gx", "gy", "gz"),
        P("gx", "gy", "gz"),
        P("gx", "gy", "gz", None, None, None),
        P("gx", "gy", "gz", None, None, None),
        P("gx", "gy", "gz", None, None),
        P("gx", "gy", "gz", None),
        P("gx", "gy", "gz", None),
        P("gx", "gy", "gz", None, None),
        P(),
    )
    small = mesh.shape["gy"] == 2 and mesh.shape["gx"] == 4 and mesh.shape["gz"] > 1
    return jax.shard_map(
        per_device if small else per_device_general,
        mesh=mesh,
        in_specs=placed,
        out_specs=(P(None, "gx", "gy", "gz"), P("gx", "gy", "gz", None, None, None)),
        check_vma=False,
    )
```

profile of v0, /device:TPU:0, one launch (start us, length us, event | category | flops | bytes accessed | tf_op | source)
XLA Modules:
  0.0 63.1 jit_solution(9607885658429938984)
XLA Ops:
  0.6 0.0 copy-start.3
  0.7 0.1 pad_add_fusion.place_ref
  0.7 0.0 copy-start.5
  0.7 0.0 copy-start.7
  0.7 0.0 copy-start.8
  0.7 0.0 copy-start.9
  0.7 0.6 copy-done.3
  1.4 0.0 copy-done.7
  1.4 0.0 copy-done.8
  1.4 0.0 copy-done.9
  1.4 0.0 copy-start
  1.4 1.0 %copy-done = f32[19,4,8,128]{3,2,1,0:T(8,128)S(1)} copy-done((f32[19,4,8,128]{3,2,1,0:T(8,128)S(1)}, f32[19,4,8,128]{3,2,1,0:T(8,128)}, u32[]{:S(2)}) %copy-start) | copy-done | bytes 311320
  2.4 0.0 copy-start.1
  2.4 0.9 %copy-done.1 = s32[1,1,1,64,8,128]{5,4,3,2,1,0:T(8,128)S(1)} copy-done((s32[1,1,1,64,8,128]{5,4,3,2,1,0:T(8,128)S(1)}, s32[1,1,1,64,8,128]{5,4,3,2,1,0:T(8,128)}, u32[]{:S(2)}) %copy-start.1) | copy-done | bytes 262168
  3.3 0.0 copy-start.2
  3.3 0.9 %copy-done.2 = f32[1,1,1,64,8,128]{5,4,3,2,1,0:T(8,128)S(1)} copy-done((f32[1,1,1,64,8,128]{5,4,3,2,1,0:T(8,128)S(1)}, f32[1,1,1,64,8,128]{5,4,3,2,1,0:T(8,128)}, u32[]{:S(2)}) %copy-start.2) | copy-done | bytes 262168
  4.3 0.0 copy-start.4
  4.3 0.0 copy-start.6
  4.3 5.9 %sample.1.refs_0_ = f32[232,128]{1,0:T(8,128)S(1)} custom-call(s32[4]{0:T(128)S(1)} %pad_add_fusion.place_ref, f32[19,32,128]{2,1,0:T(8,128)S(1)} %bitcast.13, s32[512,128]{1,0:T(8,128)S(1)} %bitcast.15, f32[512,128]{1,0:T(8,128)S(1)} %bitcast.17, f32[32,128]{1,0:T(8,128)S(1)} %bitcast.20, s32[1,64]{1,0:T(1,128)S(1)} %bitcast.22, s32[1,64]{1,0:T(1,128)S(1)} %bitcast.23, ...), custom_call_target="tpu_custom_call" | custom-call | tf_op jit(solution)/shard_map/sample/pallas_call | solution.py:360
  10.2 3.1 %collective-permute-start.2 = (f32[232,128]{1,0:T(8,128)S(1)}, f32[232,128]{1,0:T(8,128)S(1)}, u32[]{:S(2)}, u32[]{:S(2)}) collective-permute-start(f32[232,128]{1,0:T(8,128)S(1)} %sample.1.refs_0_), channel_id=1, source_target_pairs={{0,8},{8,0},{16,24},{24,16},{1,9},{9,1},{17,25},{25,17},{2,10},{10... | collective-permute-start | bytes 356360 | tf_op jit(solution)/shard_map/ppermute | solution.py:709
  13.3 2.6 %collective-permute-start.1 = (f32[232,128]{1,0:T(8,128)S(1)}, f32[232,128]{1,0:T(8,128)S(1)}, u32[]{:S(2)}, u32[]{:S(2)}) collective-permute-start(f32[232,128]{1,0:T(8,128)S(1)} %sample.1.refs_0_), channel_id=1, source_target_pairs={{0,16},{8,24},{16,0},{24,8},{1,17},{9,25},{17,1},{25,9},{2,18},{10... | collective-permute-start | bytes 356360 | tf_op jit(solution)/shard_map/ppermute | solution.py:709
  15.9 0.0 collective-permute-start
  15.9 1.7 %collective-permute-start.3 = (f32[232,128]{1,0:T(8,128)S(1)}, f32[232,128]{1,0:T(8,128)S(1)}, u32[]{:S(2)}, u32[]{:S(2)}) collective-permute-start(f32[232,128]{1,0:T(8,128)S(1)} %sample.1.refs_0_), channel_id=1, source_target_pairs={{0,4},{4,0},{1,5},{5,1},{2,6},{6,2},{3,7},{7,3},{8,12},{12,8},{9,1... | collective-permute-start | bytes 356360 | tf_op jit(solution)/shard_map/ppermute | solution.py:710
  17.6 0.2 collective-permute-done.2.refs_3_
  17.8 1.7 %collective-permute-start.6 = (f32[232,128]{1,0:T(8,128)S(1)}, f32[232,128]{1,0:T(8,128)S(1)}, u32[]{:S(2)}, u32[]{:S(2)}) collective-permute-start(f32[232,128]{1,0:T(8,128)S(1)} %collective-permute-done.2.refs_3_), channel_id=1, source_target_pairs={{0,4},{4,0},{1,5},{5,1},{2,6},{6,2},{3,7},{7,3},{8,12},{12,8},{9,1... | collective-permute-start | bytes 356360 | tf_op jit(solution)/shard_map/ppermute | solution.py:710
  19.5 5.8 %collective-permute-done.1.refs_2_ = f32[232,128]{1,0:T(8,128)S(1)} collective-permute-done((f32[232,128]{1,0:T(8,128)S(1)}, f32[232,128]{1,0:T(8,128)S(1)}, u32[]{:S(2)}, u32[]{:S(2)}) %collective-permute-start.1) | collective-permute-done | bytes 118816 | tf_op jit(solution)/shard_map/ppermute | solution.py:709
  25.3 1.5 %collective-permute-start.5 = (f32[232,128]{1,0:T(8,128)S(1)}, f32[232,128]{1,0:T(8,128)S(1)}, u32[]{:S(2)}, u32[]{:S(2)}) collective-permute-start(f32[232,128]{1,0:T(8,128)S(1)} %collective-permute-done.1.refs_2_), channel_id=1, source_target_pairs={{0,4},{4,0},{1,5},{5,1},{2,6},{6,2},{3,7},{7,3},{8,12},{12,8},{9,1... | collective-permute-start | bytes 356360 | tf_op jit(solution)/shard_map/ppermute | solution.py:710
  26.8 0.0 collective-permute-done.refs_1_
  26.8 0.5 collective-permute-start.4
  27.4 0.0 collective-permute-done.3.refs_4_
  27.4 0.0 collective-permute-done.6.refs_7_
  27.4 2.8 %collective-permute-done.5.refs_6_ = f32[232,128]{1,0:T(8,128)S(1)} collective-permute-done((f32[232,128]{1,0:T(8,128)S(1)}, f32[232,128]{1,0:T(8,128)S(1)}, u32[]{:S(2)}, u32[]{:S(2)}) %collective-permute-start.5) | collective-permute-done | bytes 118816 | tf_op jit(solution)/shard_map/ppermute | solution.py:710
  30.2 1.5 %collective-permute-done.4.refs_5_ = f32[232,128]{1,0:T(8,128)S(1)} collective-permute-done((f32[232,128]{1,0:T(8,128)S(1)}, f32[232,128]{1,0:T(8,128)S(1)}, u32[]{:S(2)}, u32[]{:S(2)}) %collective-permute-start.4) | collective-permute-done | bytes 118816 | tf_op jit(solution)/shard_map/ppermute | solution.py:710
  31.7 0.0 copy-done.4
  31.7 0.0 copy-done.6
  31.7 11.8 %spread.1 = (f32[19,32,128]{2,1,0:T(8,128)S(1)}, f32[8,24,128]{2,1,0:T(8,128)S(1)}, f32[32,3,128]{2,1,0:T(4,128)S(1)}) custom-call(s32[4]{0:T(128)S(1)} %pad_add_fusion.place_ref, f32[4,3]{1,0:T(4,128)S(1)} %copy-done.6, f32[232,128]{1,0:T(8,128)S(1)} %sample.1.refs_0_, f32[232,128]{1,0:T(8,128)S(1)} %collective-permute-done.refs_1_, ...), custom_call_target="tpu_custom_call" | custom-call | tf_op jit(solution)/shard_map/spread/pallas_call | solution.py:544
  43.5 8.2 %all_to_all.5.got_ref = f32[8,24,128]{2,1,0:T(8,128)S(1)} all-to-all(f32[8,24,128]{2,1,0:T(8,128)S(1)} %get-tuple-element.9), channel_id=1, replica_groups=mesh['gx'=4,'gy'=2,'gz'=4] {'gy','gz'}, dimensions={0} | all-to-all | bytes 196608 | tf_op jit(solution)/shard_map/all_to_all | solution.py:723
  51.7 0.0 copy-done.5
  51.7 1.4 %stream.1 = (f32[19,4,8,128]{3,2,1,0:T(8,128)}, f32[5,8,128]{2,1,0:T(8,128)S(1)}, f32[5,8,128]{2,1,0:T(8,128)S(1)}) custom-call(s32[4]{0:T(128)S(1)} %pad_add_fusion.place_ref, f32[19,32,128]{2,1,0:T(8,128)S(1)} %get-tuple-element.8.relaxed_ref, f32[8,24,128]{2,1,0:T(8,128)S(1)} %all_to_all.5.got_ref), custom_call_target="tpu_custom_call" | custom-call | tf_op jit(solution)/shard_map/stream/pallas_call | solution.py:633
  53.1 2.5 %collective-permute-start.7 = (f32[5,8,128]{2,1,0:T(8,128)S(1)}, f32[5,8,128]{2,1,0:T(8,128)S(1)}, u32[]{:S(2)}, u32[]{:S(2)}) collective-permute-start(f32[5,8,128]{2,1,0:T(8,128)S(1)} %get-tuple-element.11), channel_id=1, source_target_pairs={{0,24},{16,8},{24,0},{8,16},{1,25},{17,9},{25,1},{9,17},{2,26},{18... | collective-permute-start | bytes 61448 | tf_op jit(solution)/shard_map/ppermute | solution.py:726
  55.6 0.0 collective-permute-start.8
  55.6 0.6 copy.12
  56.2 2.5 %collective-permute-done.7.far_any = f32[5,8,128]{2,1,0:T(8,128)S(1)} collective-permute-done((f32[5,8,128]{2,1,0:T(8,128)S(1)}, f32[5,8,128]{2,1,0:T(8,128)S(1)}, u32[]{:S(2)}, u32[]{:S(2)}) %collective-permute-start.7) | collective-permute-done | bytes 20512 | tf_op jit(solution)/shard_map/ppermute | solution.py:726
  58.8 0.0 copy-start.10
  58.8 0.6 %collective-permute-done.8.near_any = f32[5,8,128]{2,1,0:T(8,128)S(1)} collective-permute-done((f32[5,8,128]{2,1,0:T(8,128)S(1)}, f32[5,8,128]{2,1,0:T(8,128)S(1)}, u32[]{:S(2)}, u32[]{:S(2)}) %collective-permute-start.8) | collective-permute-done | bytes 20512 | tf_op jit(solution)/shard_map/ppermute | solution.py:731
  59.4 0.0 copy-done.10
  59.4 0.6 copy-done.11
  60.0 3.1 %place_faces.1 = f32[19,4,8,128]{3,2,1,0:T(8,128)} custom-call(s32[4]{0:T(128)} %copy-done.5, f32[19,4,8,128]{3,2,1,0:T(8,128)} %get-tuple-element.10.next_any, f32[5,8,128]{2,1,0:T(8,128)} %copy-done.10, f32[5,8,128]{2,1,0:T(8,128)} %copy-done.11), custom_call_target="tpu_custom_call", output_to_operand_aliasing={{}: (1, {})} | custom-call | tf_op jit(solution)/shard_map/place_faces/pallas_call | solution.py:663
  (1 shorter events, 0.0 us)
Async XLA Ops:
  0.6 0.7 %copy-start.3 = (f32[1,1,1,32,128]{4,3,2,1,0:T(8,128)S(1)}, f32[1,1,1,32,128]{4,3,2,1,0:T(8,128)}, u32[]{:S(2)}) copy-start(f32[1,1,1,32,128]{4,3,2,1,0:T(8,128)} %param.16) | copy-start | bytes 49156
  0.7 51.0 %copy-start.5 = (s32[4]{0:T(128)}, s32[4]{0:T(128)S(1)}, u32[]{:S(2)}) copy-start(s32[4]{0:T(128)S(1)} %pad_add_fusion.place_ref) | copy-start | bytes 52
  0.7 0.7 %copy-start.7 = (s32[1,1,1,64,1]{3,4,2,1,0:T(1,128)S(1)}, s32[1,1,1,64,1]{3,4,2,1,0:T(1,128)}, u32[]{:S(2)}) copy-start(s32[1,1,1,64,1]{3,4,2,1,0:T(1,128)} %param.13) | copy-start | bytes 772
  0.7 0.7 %copy-start.8 = (s32[1,1,1,64]{3,2,1,0:T(1,128)S(1)}, s32[1,1,1,64]{3,2,1,0:T(1,128)}, u32[]{:S(2)}) copy-start(s32[1,1,1,64]{3,2,1,0:T(1,128)} %param.14) | copy-start | bytes 772
  0.7 0.7 %copy-start.9 = (s32[1,1,1,32]{3,2,1,0:T(1,128)S(1)}, s32[1,1,1,32]{3,2,1,0:T(1,128)}, u32[]{:S(2)}) copy-start(s32[1,1,1,32]{3,2,1,0:T(1,128)} %param.15) | copy-start | bytes 388
  1.4 1.0 %copy-start = (f32[19,4,8,128]{3,2,1,0:T(8,128)S(1)}, f32[19,4,8,128]{3,2,1,0:T(8,128)}, u32[]{:S(2)}) copy-start(f32[19,4,8,128]{3,2,1,0:T(8,128)} %param.9) | copy-start | bytes 933892
  2.4 0.9 %copy-start.1 = (s32[1,1,1,64,8,128]{5,4,3,2,1,0:T(8,128)S(1)}, s32[1,1,1,64,8,128]{5,4,3,2,1,0:T(8,128)}, u32[]{:S(2)}) copy-start(s32[1,1,1,64,8,128]{5,4,3,2,1,0:T(8,128)} %param.11) | copy-start | bytes 786436
  3.3 0.9 %copy-start.2 = (f32[1,1,1,64,8,128]{5,4,3,2,1,0:T(8,128)S(1)}, f32[1,1,1,64,8,128]{5,4,3,2,1,0:T(8,128)}, u32[]{:S(2)}) copy-start(f32[1,1,1,64,8,128]{5,4,3,2,1,0:T(8,128)} %param.12) | copy-start | bytes 786436
  4.3 27.4 %copy-start.4 = (s32[4,8,128]{2,1,0:T(8,128)S(1)}, s32[4,8,128]{2,1,0:T(8,128)}, u32[]{:S(2)}) copy-start(s32[4,8,128]{2,1,0:T(8,128)} %param.10) | copy-start | bytes 49156
  4.3 27.4 %copy-start.6 = (f32[4,3]{1,0:T(4,128)S(1)}, f32[4,3]{1,0:T(4,128)}, u32[]{:S(2)}) copy-start(f32[4,3]{1,0:T(4,128)} %speeds_ref.1) | copy-start | bytes 148
  10.2 7.6 %collective-permute-start.2 = (f32[232,128]{1,0:T(8,128)S(1)}, f32[232,128]{1,0:T(8,128)S(1)}, u32[]{:S(2)}, u32[]{:S(2)}) collective-permute-start(f32[232,128]{1,0:T(8,128)S(1)} %sample.1.refs_0_), channel_id=1, source_target_pairs={{0,8},{8,0},{16,24},{24,16},{1,9},{9,1},{17,25},{25,17},{2,10},{10... | collective-permute-start | bytes 356360 | tf_op jit(solution)/shard_map/ppermute | solution.py:709
  13.3 12.0 %collective-permute-start.1 = (f32[232,128]{1,0:T(8,128)S(1)}, f32[232,128]{1,0:T(8,128)S(1)}, u32[]{:S(2)}, u32[]{:S(2)}) collective-permute-start(f32[232,128]{1,0:T(8,128)S(1)} %sample.1.refs_0_), channel_id=1, source_target_pairs={{0,16},{8,24},{16,0},{24,8},{1,17},{9,25},{17,1},{25,9},{2,18},{10... | collective-permute-start | bytes 356360 | tf_op jit(solution)/shard_map/ppermute | solution.py:709
  15.9 10.9 %collective-permute-start = (f32[232,128]{1,0:T(8,128)S(1)}, f32[232,128]{1,0:T(8,128)S(1)}, u32[]{:S(2)}, u32[]{:S(2)}) collective-permute-start(f32[232,128]{1,0:T(8,128)S(1)} %sample.1.refs_0_), channel_id=1, source_target_pairs={{0,24},{8,16},{16,8},{24,0},{1,25},{9,17},{17,9},{25,1},{2,26},{10... | collective-permute-start | bytes 356360 | tf_op jit(solution)/shard_map/ppermute | solution.py:709
  15.9 11.4 %collective-permute-start.3 = (f32[232,128]{1,0:T(8,128)S(1)}, f32[232,128]{1,0:T(8,128)S(1)}, u32[]{:S(2)}, u32[]{:S(2)}) collective-permute-start(f32[232,128]{1,0:T(8,128)S(1)} %sample.1.refs_0_), channel_id=1, source_target_pairs={{0,4},{4,0},{1,5},{5,1},{2,6},{6,2},{3,7},{7,3},{8,12},{12,8},{9,1... | collective-permute-start | bytes 356360 | tf_op jit(solution)/shard_map/ppermute | solution.py:710
  17.8 9.5 %collective-permute-start.6 = (f32[232,128]{1,0:T(8,128)S(1)}, f32[232,128]{1,0:T(8,128)S(1)}, u32[]{:S(2)}, u32[]{:S(2)}) collective-permute-start(f32[232,128]{1,0:T(8,128)S(1)} %collective-permute-done.2.refs_3_), channel_id=1, source_target_pairs={{0,4},{4,0},{1,5},{5,1},{2,6},{6,2},{3,7},{7,3},{8,12},{12,8},{9,1... | collective-permute-start | bytes 356360 | tf_op jit(solution)/shard_map/ppermute | solution.py:710
  25.3 4.8 %collective-permute-start.5 = (f32[232,128]{1,0:T(8,128)S(1)}, f32[232,128]{1,0:T(8,128)S(1)}, u32[]{:S(2)}, u32[]{:S(2)}) collective-permute-start(f32[232,128]{1,0:T(8,128)S(1)} %collective-permute-done.1.refs_2_), channel_id=1, source_target_pairs={{0,4},{4,0},{1,5},{5,1},{2,6},{6,2},{3,7},{7,3},{8,12},{12,8},{9,1... | collective-permute-start | bytes 356360 | tf_op jit(solution)/shard_map/ppermute | solution.py:710
  26.8 4.8 %collective-permute-start.4 = (f32[232,128]{1,0:T(8,128)S(1)}, f32[232,128]{1,0:T(8,128)S(1)}, u32[]{:S(2)}, u32[]{:S(2)}) collective-permute-start(f32[232,128]{1,0:T(8,128)S(1)} %collective-permute-done.refs_1_), channel_id=1, source_target_pairs={{0,4},{4,0},{1,5},{5,1},{2,6},{6,2},{3,7},{7,3},{8,12},{12,8},{9,1... | collective-permute-start | bytes 356360 | tf_op jit(solution)/shard_map/ppermute | solution.py:710
  53.1 5.6 %collective-permute-start.7 = (f32[5,8,128]{2,1,0:T(8,128)S(1)}, f32[5,8,128]{2,1,0:T(8,128)S(1)}, u32[]{:S(2)}, u32[]{:S(2)}) collective-permute-start(f32[5,8,128]{2,1,0:T(8,128)S(1)} %get-tuple-element.11), channel_id=1, source_target_pairs={{0,24},{16,8},{24,0},{8,16},{1,25},{17,9},{25,1},{9,17},{2,26},{18... | collective-permute-start | bytes 61448 | tf_op jit(solution)/shard_map/ppermute | solution.py:726
  55.6 3.8 %collective-permute-start.8 = (f32[5,8,128]{2,1,0:T(8,128)S(1)}, f32[5,8,128]{2,1,0:T(8,128)S(1)}, u32[]{:S(2)}, u32[]{:S(2)}) collective-permute-start(f32[5,8,128]{2,1,0:T(8,128)S(1)} %get-tuple-element.12), channel_id=1, source_target_pairs={{0,8},{16,24},{8,0},{24,16},{1,9},{17,25},{9,1},{25,17},{2,10},{18... | collective-permute-start | bytes 61448 | tf_op jit(solution)/shard_map/ppermute | solution.py:731
  58.8 0.6 %copy-start.10 = (f32[5,8,128]{2,1,0:T(8,128)}, f32[5,8,128]{2,1,0:T(8,128)S(1)}, u32[]{:S(2)}) copy-start(f32[5,8,128]{2,1,0:T(8,128)S(1)} %collective-permute-done.7.far_any) | copy-start | bytes 61444
  59.4 0.6 copy-start.11
where the time goes:
time: 63.4 us; the launch traced here: 63.1 us
  Pallas kernels  22.2 us (35%)
  starting transfers between devices  13.6 us (21%)
  waiting for transfers between devices  13.5 us (21%)
  blocking collectives  8.23 us (13%)
  local copies, waits for them, and re-layouts  4.79 us (8%)
  between operations  0.7 us (1%)
    pallas_call x1, Pallas kernels, spread(): pl.pallas_call(functools.partial(spread_kernel, len(shards), slots, owned...  11.8 us
    all_to_all x1, blocking collectives, per_device(): lax.all_to_all(sides, ('gy', 'gz'), split_axis=0, concat_axis=0, tiled=True)  8.23 us
    ppermute x3, waiting for transfers between devices, per_device(): lax.ppermute(own, 'gx', [(i, i ^ distance) for i in range(count_x)])  6.02 us
    pallas_call x1, Pallas kernels, sample(): pl.pallas_call(sample_kernel, out_shape=full((shard_rows(owner.shape[1],...  5.94 us
    ppermute x3, starting transfers between devices, per_device(): lax.ppermute(own, 'gx', [(i, i ^ distance) for i in range(count_x)])  5.68 us
    ppermute x4, starting transfers between devices, per_device(): shards = column + [lax.ppermute(shard, 'gy', swap) for shard in column]  5.42 us
    unnamed x25, local copies, waits for them, and re-layouts  4.79 us
    ppermute x4, waiting for transfers between devices, per_device(): shards = column + [lax.ppermute(shard, 'gy', swap) for shard in column]  4.3 us
  transfers between devices with their start and end apart: 9, of which 6 were waited for; matrix products, arithmetic and copies ran while one was open for 1% of the time, Pallas kernels for 0%

commit v1 on v0

--- a/solution.py
+++ b/solution.py
@@ -291,8 +291,9 @@
 
 
 def sample_kernel(
-    place_ref, pop_any, cells_any, weights_any, areas_ref, owner_ref, block_ref, trains_ref,
-    out_ref, pop_ref, cells_ref, weights_ref, table, sems,
+    place_ref, pop_any, cells_any, weights_any, areas_any, owner_any, block_any, trains_any,
+    out_ref, pop_ref, cells_ref, weights_ref, areas_ref, owner_ref, block_ref, trains_ref,
+    table, sems,
 ):
     rows, lanes = (pop_ref.shape[1], pop_ref.shape[2])
     mark = cells_ref.shape[1]
@@ -300,8 +301,27 @@
     slots = owner_ref.shape[1]
     kernel = cells_ref.shape[0] // slots
     copies = fetch(
-        ((pop_any, pop_ref), (cells_any, cells_ref), (weights_any, weights_ref)), sems
-    )
+        (
+            (pop_any, pop_ref),
+            (cells_any, cells_ref),
+            (weights_any, weights_ref),
+            (areas_any, areas_ref),
+            (owner_any, owner_ref),
+            (block_any, block_ref),
+            (trains_any, trains_ref),
+        ),
+        sems,
+    )
+    copies[0].wait()
+    density, momentum = moments([pop_ref[q] for q in range(19)])
+    fixed = [
+        ((momentum[c] / density) * float(2**bits) + (2.0 ** (bits - 1) + 0.5)).astype(jnp.int32)
+        for c, bits in enumerate((21, 21, 22))
+    ]
+    table[0] = (fixed[0] << 11) | (fixed[2] >> 11)
+    table[1] = (fixed[1] << 11) | (fixed[2] & 2047)
+    for copy in copies[1:]:
+        copy.wait()
     meta = 3 * slots + owned
     out_ref[3 * slots : meta, :] = areas_ref[...]
     out_ref[meta : meta + 8, :] = jnp.zeros((8, mark), jnp.float32)
@@ -310,16 +330,6 @@
     out_ref[meta + 1 : meta + 2, 0:owned] = trains_ref[...].astype(jnp.float32)
     mine = lax.broadcasted_iota(jnp.int32, (1, mark), 1) % owned + place_ref[2] * owned
     out_ref[meta + 2 : meta + 3, :] = mine.astype(jnp.float32)
-    copies[0].wait()
-    density, momentum = moments([pop_ref[q] for q in range(19)])
-    fixed = [
-        ((momentum[c] / density) * float(2**bits) + (2.0 ** (bits - 1) + 0.5)).astype(jnp.int32)
-        for c, bits in enumerate((21, 21, 22))
-    ]
-    table[0] = (fixed[0] << 11) | (fixed[2] >> 11)
-    table[1] = (fixed[1] << 11) | (fixed[2] & 2047)
-    copies[1].wait()
-    copies[2].wait()
 
     def body(step, carry):
         first = pl.multiple_of(step * group, group)
@@ -360,13 +370,14 @@
     return pl.pallas_call(
         sample_kernel,
         out_shape=full((shard_rows(owner.shape[1], areas.shape[0]), cells.shape[1])),
-        in_specs=[smem] + [hbm] * 3 + [vmem] * 4,
+        in_specs=[smem] + [hbm] * 7,
         scratch_shapes=[
-            pltpu.VMEM(populations.shape, jnp.float32),
-            pltpu.VMEM(cells.shape, jnp.int32),
-            pltpu.VMEM(weights.shape, jnp.float32),
+            pltpu.VMEM(entries.shape, entries.dtype)
+            for entries in (populations, cells, weights, areas, owner, block, trains)
+        ]
+        + [
             pltpu.VMEM((2,) + populations.shape[1:], jnp.int32),
-            pltpu.SemaphoreType.DMA((3,)),
+            pltpu.SemaphoreType.DMA((7,)),
         ],
         compiler_params=kernel_params(),
         name="sample",
@@ -431,8 +442,9 @@
 
 def spread_kernel(shard_count, slots, owned, place_ref, speeds_ref, *refs):
     shards, refs = (refs[:shard_count], refs[shard_count:])
-    cells_any, weights_any, pop_any, solid_ref, relaxed_ref, send_ref, marker_ref = refs[:7]
-    cells_ref, weights_ref, pop_ref, force_ref, acc, sems = refs[7:]
+    cells_any, weights_any, pop_any, solid_ref = refs[:4]
+    relaxed_ref, far_ref, near_ref, marker_ref = refs[4:8]
+    cells_ref, weights_ref, pop_ref, force_ref, lines_ref, acc, sems = refs[8:]
     rows, lanes = (pop_ref.shape[1], pop_ref.shape[2])
     size_y = 8
     mark = cells_ref.shape[1]
@@ -444,7 +456,7 @@
     forces, own_forces = settle_rows(speeds_ref, shards, slots, owned)
     for c in range(3):
         force_ref[c] = forces[c]
-        marker_ref[:, c, :] = own_forces[c]
+        marker_ref[c] = own_forces[c]
 
     acc[...] = jnp.zeros_like(acc)
     iota = lax.broadcasted_iota(jnp.int32, (16, mark), 0).astype(jnp.float32)
@@ -452,9 +464,6 @@
     one, zero = (jnp.ones((16, mark), bf), jnp.zeros((16, mark), bf))
     copies[0].wait()
     copies[1].wait()
-
-    def wide(entries, i):
-        return jnp.broadcast_to(entries[i : i + 1, :], (16, mark)).astype(bf)
 
     def body(step, carry):
         first = pl.multiple_of(step * group, group)
@@ -470,9 +479,16 @@
                 value = weight * force[c]
                 high = value.astype(bf).astype(jnp.float32)
                 parts += [high, value - high]
+            for which, entries in enumerate([lane, row] + parts):
+                lines_ref[k, which] = entries
+
+            def wide(which, i):
+                entries = lines_ref[k, which, i : i + 1, :]
+                return jnp.broadcast_to(entries, (16, mark)).astype(bf)
+
             left, right = ([], [])
             for i in range(group):
-                lane_i, row_i = (wide(lane, i), wide(row, i))
+                lane_i, row_i = (wide(0, i), wide(1, i))
                 left.append(
                     jnp.concatenate(
                         [jnp.where(steps[j] == lane_i, one, zero) for j in range(lanes // 16)],
@@ -481,8 +497,8 @@
                 )
                 masks = [steps[j] == row_i for j in range(rows // 16)]
                 pieces = []
-                for part in parts:
-                    part_i = wide(part, i)
+                for which in range(len(parts)):
+                    part_i = wide(2 + which, i)
                     pieces += [jnp.where(mask, part_i, zero) for mask in masks]
                 right.append(jnp.concatenate(pieces, axis=0))
             acc[...] += lax.dot_general(
@@ -505,37 +521,19 @@
     relaxed = collide([pop_ref[q] for q in range(19)], cell_force, solid_ref[...])
     for q in range(19):
         relaxed_ref[q] = relaxed[q]
-    lane_at = lax.broadcasted_iota(jnp.int32, (size_y, lanes), 1)
-    packs = []
-    for step in (1, -1):
-        packed = jnp.zeros((size_y, lanes), jnp.float32)
-        for i, q in enumerate(going(2, step)):
-            edge = lanes - 1 if step == 1 else 0
-            for x in range(rows // size_y):
-                moved = pltpu.roll(
-                    relaxed[q][x * size_y : (x + 1) * size_y], (8 * x + i - edge) % lanes, 1
-                )
-                packed = jnp.where(lane_at == 8 * x + i, moved, packed)
-        packs.append(packed)
-    y_index, z_index = (place_ref[0], place_ref[1])
-    count_z = peers_z(send_ref)
-    side = 1 - y_index
-    for peer in range(send_ref.shape[0]):
-        peer_y, peer_z = divmod(peer, count_z)
-        send_ref[peer, 0:8, :] = jnp.where(z_index < peer_z, packs[0], packs[1])
-    face = side * count_z + z_index
+    even = place_ref[3] == 0
     for i in range(5):
-        for x in range(rows // size_y):
-            up = relaxed[going(1, 1)[i]][size_y * x + size_y - 1 : size_y * x + size_y, :]
-            down = relaxed[going(1, -1)[i]][size_y * x : size_y * x + 1, :]
-            send_ref[face, 4 * i + x : 4 * i + x + 1, :] = jnp.where(y_index == 0, up, down)
+        ahead = relaxed[going(0, 1)[i]][rows - size_y :]
+        behind = relaxed[going(0, -1)[i]][:size_y]
+        far_ref[i] = jnp.where(even, behind, ahead)
+        near_ref[i] = jnp.where(even, ahead, behind)
 
 
 def peers_z(ref):
     return ref.shape[0] // 2
 
 
-def spread(count_z, slots, owned, place, speeds, shards, cells, weights, populations, solid):
+def spread(slots, owned, place, speeds, shards, cells, weights, populations, solid):
     mark = cells.shape[1]
     line_count, lanes = solid.shape
     smem = pl.BlockSpec(memory_space=pltpu.SMEM)
@@ -545,8 +543,9 @@
         functools.partial(spread_kernel, len(shards), slots, owned),
         out_shape=(
             full(populations.shape),
-            full((2 * count_z, 24, lanes)),
-            full((owned, 3, mark)),
+            full((5, 8, lanes)),
+            full((5, 8, lanes)),
+            full((3, owned, mark)),
         ),
         in_specs=[smem] * 2 + [vmem] * len(shards) + [hbm] * 3 + [vmem],
         scratch_shapes=[
@@ -554,6 +553,7 @@
             pltpu.VMEM(weights.shape, jnp.float32),
             pltpu.VMEM(populations.shape, jnp.float32),
             pltpu.VMEM((3, slots, mark), jnp.float32),
+            pltpu.VMEM((cells.shape[0] // slots, 8, group, mark), jnp.float32),
             pltpu.VMEM((lanes, 6 * line_count), jnp.float32),
             pltpu.SemaphoreType.DMA((3,)),
         ],
@@ -562,9 +562,71 @@
     )(place, speeds, *shards, cells, weights, populations, solid)
 
 
-def stream_kernel(place_ref, relaxed_ref, got_ref, out_any, far_ref, near_ref, out_ref, sem):
+def downwind(place_ref, relaxed_ref, far_ref, near_ref):
+    size_y = far_ref.shape[1]
+    size_x = relaxed_ref.shape[1] // size_y
+    even = place_ref[3] == 0
+
+    def cells(q, x):
+        step = int(velocity_table[q][0])
+        source = x - step
+        if 0 <= source < size_x:
+            return relaxed_ref[q, source * size_y : (source + 1) * size_y, :]
+        i = going(0, step).index(q)
+        if step == 1:
+            return jnp.where(even, far_ref[i], near_ref[i])
+        return jnp.where(even, near_ref[i], far_ref[i])
+
+    return cells
+
+
+def pack_kernel(place_ref, relaxed_ref, far_ref, near_ref, send_ref):
+    size_y, lanes = far_ref.shape[1:]
+    size_x = relaxed_ref.shape[1] // size_y
+    cells = downwind(place_ref, relaxed_ref, far_ref, near_ref)
+    lane_at = lax.broadcasted_iota(jnp.int32, (size_y, lanes), 1)
+    packs = []
+    for step in (1, -1):
+        packed = jnp.zeros((size_y, lanes), jnp.float32)
+        for i, q in enumerate(going(2, step)):
+            edge = lanes - 1 if step == 1 else 0
+            for x in range(size_x):
+                at = 8 * x + i
+                moved = pltpu.roll(cells(q, x), (at - edge) % lanes, 1)
+                packed = jnp.where(lane_at == at, moved, packed)
+        packs.append(packed)
+    y_index, z_index = (place_ref[0], place_ref[1])
+    count_z = peers_z(send_ref)
+    for peer in range(send_ref.shape[0]):
+        send_ref[peer, 0:8, :] = jnp.where(z_index < peer % count_z, packs[0], packs[1])
+    face = (1 - y_index) * count_z + z_index
+    for i in range(5):
+        for x in range(size_x):
+            up = cells(going(1, 1)[i], x)[size_y - 1 : size_y, :]
+            down = cells(going(1, -1)[i], x)[0:1, :]
+            at = size_x * i + x
+            send_ref[face, at : at + 1, :] = jnp.where(y_index == 0, up, down)
+
+
+def pack(count_z, place, relaxed, far, near):
+    lanes = relaxed.shape[2]
+    smem = pl.BlockSpec(memory_space=pltpu.SMEM)
+    vmem = pl.BlockSpec(memory_space=pltpu.VMEM)
+    return pl.pallas_call(
+        pack_kernel,
+        out_shape=full((2 * count_z, 24, lanes)),
+        in_specs=[smem] + [vmem] * 3,
+        compiler_params=kernel_params(),
+        name="pack",
+    )(place, relaxed, far, near)
+
+
+def stream_kernel(
+    place_ref, relaxed_ref, far_ref, near_ref, got_ref, out_any, out_ref, sems
+):
     size_x, size_y, lanes = out_ref.shape[1:]
     shape = (size_y, lanes)
+    streamed = downwind(place_ref, relaxed_ref, far_ref, near_ref)
     y_at = lax.broadcasted_iota(jnp.int32, shape, 0)
     z_at = lax.broadcasted_iota(jnp.int32, shape, 1)
     y_index, z_index = (place_ref[0], place_ref[1])
@@ -572,28 +634,27 @@
     side = (1 - y_index) * count_z
     here = y_index * count_z
     z_from = {1: jnp.maximum(z_index - 1, 0), -1: jnp.minimum(z_index + 1, count_z - 1)}
-    near = {step: got_ref[here + z_from[step], 0:8, :] for step in (1, -1)}
-    far = {step: got_ref[side + z_from[step], 0:8, :] for step in (1, -1)}
-    near[0] = None
+    level = {step: got_ref[here + z_from[step], 0:8, :] for step in (1, -1)}
+    across = {step: got_ref[side + z_from[step], 0:8, :] for step in (1, -1)}
     on_side = y_at == jnp.where(y_index == 0, 0, size_y - 1)
     on_side = on_side | ((z_at == 0) & (z_index == 0))
     on_side = on_side | ((z_at == lanes - 1) & (z_index == count_z - 1))
-    leaving = {}
+    copies = []
     for q in range(19):
-        step_x, step_y, step_z = (int(step) for step in velocity_table[q])
+        _, step_y, step_z = (int(step) for step in velocity_table[q])
         y_edge = 0 if step_y == 1 else size_y - 1
         z_edge = 0 if step_z == 1 else lanes - 1
-        column = near[step_z]
+        column = level.get(step_z)
         if step_z != 0 and step_y != 0:
             column = jnp.where(
                 y_at == y_edge,
-                pltpu.roll(far[step_z], step_y % size_y, 0),
+                pltpu.roll(across[step_z], step_y % size_y, 0),
                 pltpu.roll(column, step_y % size_y, 0),
             )
         for x in range(size_x):
-            cells = relaxed_ref[q, x * size_y : (x + 1) * size_y, :]
+            cells = streamed(q, x)
             if step_y != 0:
-                at = 4 * going(1, step_y).index(q) + x
+                at = size_x * going(1, step_y).index(q) + x
                 halo = got_ref[side + z_index, at : at + 1, :]
                 cells = jnp.where(y_at == y_edge, halo, pltpu.roll(cells, step_y % size_y, 0))
             if step_z != 0:
@@ -603,72 +664,28 @@
                     pltpu.roll(column, (z_edge - at) % lanes, 1),
                     pltpu.roll(cells, step_z % lanes, 1),
                 )
-            cells = jnp.where(on_side, far_field[q], cells)
-            target = x + step_x
-            if 0 <= target < size_x:
-                out_ref[q, target] = cells
-            else:
-                leaving[q] = cells
-    for q in going(0, 1):
-        out_ref[q, 0] = jnp.zeros(shape, jnp.float32)
-    for q in going(0, -1):
-        out_ref[q, size_x - 1] = jnp.zeros(shape, jnp.float32)
-    copy = pltpu.make_async_copy(out_ref, out_any, sem)
-    copy.start()
-    even = place_ref[3] == 0
-    for i in range(5):
-        ahead, behind = (leaving[going(0, 1)[i]], leaving[going(0, -1)[i]])
-        far_ref[i] = jnp.where(even, behind, ahead)
-        near_ref[i] = jnp.where(even, ahead, behind)
-    copy.wait()
-
-
-def stream(size_y, place, relaxed, got):
+            out_ref[q, x] = jnp.where(on_side, far_field[q], cells)
+        copies.append(pltpu.make_async_copy(out_ref.at[q], out_any.at[q], sems.at[q]))
+        copies[-1].start()
+    for copy in copies:
+        copy.wait()
+
+
+def stream(place, relaxed, far, near, got):
     rows, lanes = relaxed.shape[1:]
+    size_y = far.shape[1]
     smem = pl.BlockSpec(memory_space=pltpu.SMEM)
-    hbm = pl.BlockSpec(memory_space=pltpu.HBM)
     vmem = pl.BlockSpec(memory_space=pltpu.VMEM)
-    face = full((5, size_y, lanes))
     shape = (19, rows // size_y, size_y, lanes)
     return pl.pallas_call(
         stream_kernel,
-        out_shape=(full(shape), face, face),
-        in_specs=[smem, vmem, vmem],
-        out_specs=[hbm, vmem, vmem],
-        scratch_shapes=[pltpu.VMEM(shape, jnp.float32), pltpu.SemaphoreType.DMA],
+        out_shape=full(shape),
+        in_specs=[smem] + [vmem] * 4,
+        out_specs=pl.BlockSpec(memory_space=pltpu.HBM),
+        scratch_shapes=[pltpu.VMEM(shape, jnp.float32), pltpu.SemaphoreType.DMA((19,))],
         compiler_params=kernel_params(),
         name="stream",
-    )(place, relaxed, got)
-
-
-def place_kernel(place_ref, next_any, far_any, near_any, out_any, sems):
-    size_x = out_any.shape[1]
-    odd = place_ref[3]
-    copies = []
-    for i in range(5):
-        ahead, behind = (going(0, 1)[i], going(0, -1)[i])
-        for which, source in enumerate((far_any, near_any)):
-            from_behind = odd == which
-            q = jnp.where(from_behind, ahead, behind)
-            x = jnp.where(from_behind, 0, size_x - 1)
-            copies.append((source.at[i], out_any.at[q, x]))
-    for copy in fetch(copies, sems):
-        copy.wait()
-
-
-def place_faces(place, inner, far, near):
-    smem = pl.BlockSpec(memory_space=pltpu.SMEM)
-    anywhere = pl.BlockSpec(memory_space=pl.ANY)
-    hbm = pl.BlockSpec(memory_space=pltpu.HBM)
-    return pl.pallas_call(
-        place_kernel,
-        out_shape=full(inner.shape),
-        in_specs=[smem, hbm, anywhere, anywhere],
-        out_specs=hbm,
-        scratch_shapes=[pltpu.SemaphoreType.DMA((10,))],
-        input_output_aliases={1: 0},
-        name="place_faces",
-    )(place, inner, far, near)
+    )(place, relaxed, far, near, got)
 
 
 def per_device(
@@ -690,26 +707,26 @@
     x_index, y_index, z_index = (lax.axis_index(axis) for axis in ("gx", "gy", "gz"))
     place = jnp.stack([y_index, z_index, x_index * count_y + y_index, x_index % 2])
     place = place.astype(jnp.int32)
-    pops = populations.reshape(19, lines, size_z)
-    cells = slot_cells.reshape(slots * kernel, mark)
-    weights = slot_weights.reshape(slots * kernel, mark)
-    own = sample(
-        place,
-        pops,
-        cells,
-        weights,
-        marker_area.reshape(owned, mark),
-        slot_owner.reshape(1, slots),
-        slot_block.reshape(1, slots),
-        train_of_block.reshape(1, owned),
-    )
+    inputs = [
+        pltpu.with_memory_space_constraint(entries, pltpu.HBM)
+        for entries in (
+            populations.reshape(19, lines, size_z),
+            slot_cells.reshape(slots * kernel, mark),
+            slot_weights.reshape(slots * kernel, mark),
+            marker_area.reshape(owned, mark),
+            slot_owner.reshape(1, slots),
+            slot_block.reshape(1, slots),
+            train_of_block.reshape(1, owned),
+        )
+    ]
+    pops, cells, weights = inputs[:3]
+    own = sample(place, *inputs)
     swap = [(0, 1), (1, 0)]
     column = [own]
     for distance in reversed(range(1, count_x)):
         column.append(lax.ppermute(own, "gx", [(i, i ^ distance) for i in range(count_x)]))
     shards = column + [lax.ppermute(shard, "gy", swap) for shard in column]
-    relaxed, sides, marker_force = spread(
-        count_z,
+    relaxed, far, near, marker_force = spread(
         slots,
         owned,
         place,
@@ -720,8 +737,6 @@
         pops,
         solid_cells.reshape(lines, size_z),
     )
-    sides = lax.all_to_all(sides, ("gy", "gz"), split_axis=0, concat_axis=0, tiled=True)
-    inner, far, near = stream(size_y, place, relaxed, sides)
     evens = range(0, count_x, 2)
     far = lax.ppermute(
         far,
@@ -729,7 +744,11 @@
         [(i, (i - 1) % count_x) for i in evens] + [((i - 1) % count_x, i) for i in evens],
     )
     near = lax.ppermute(near, "gx", [(i, i + 1) for i in evens] + [(i + 1, i) for i in evens])
-    return (place_faces(place, inner, far, near), marker_force.reshape(1, 1, 1, owned, 3, mark))
+    sides = pack(count_z, place, relaxed, far, near)
+    sides = lax.all_to_all(sides, ("gy", "gz"), split_axis=0, concat_axis=0, tiled=True)
+    populations_next = stream(place, relaxed, far, near, sides)
+    marker_force = marker_force.transpose(1, 0, 2).reshape(1, 1, 1, owned, 3, mark)
+    return (populations_next, marker_force)
 
 
 def solution(mesh):

time: 63.4 us -> 58.6 us (0.924)
  the two profiles are of different devices: /device:TPU:0 before, /device:TPU:1 now
where the time goes in v1:
time: 58.6 us; the launch traced here: 57.6 us
  Pallas kernels  21.7 us (37%)
  blocking collectives  13.1 us (22%)
  starting transfers between devices  13 us (22%)
  waiting for transfers between devices  9.11 us (16%)
  between operations  0.68 us (1%)
    all_to_all x1, blocking collectives, per_device(): lax.all_to_all(sides, ('gy', 'gz'), split_axis=0, concat_axis=0, tiled=True)  13.1 us
    pallas_call x1, Pallas kernels, spread(): pl.pallas_call(functools.partial(spread_kernel, len(shards), slots, owned...  12.6 us
    pallas_call x1, Pallas kernels, sample(): pl.pallas_call(sample_kernel, out_shape=full((shard_rows(owner.shape[1],...  6.94 us
    ppermute x3, waiting for transfers between devices, per_device(): lax.ppermute(own, 'gx', [(i, i ^ distance) for i in range(count_x)])  4.74 us
    ppermute x3, starting transfers between devices, per_device(): lax.ppermute(own, 'gx', [(i, i ^ distance) for i in range(count_x)])  4.5 us
    ppermute x4, starting transfers between devices, per_device(): shards = column + [lax.ppermute(shard, 'gy', swap) for shard in column]  4.12 us
    ppermute x1, starting transfers between devices, per_device(): lax.ppermute(far, 'gx', [(i, (i - 1) % count_x) for i in evens] + [((i -...  3.63 us
    ppermute x4, waiting for transfers between devices, per_device(): shards = column + [lax.ppermute(shard, 'gy', swap) for shard in column]  2.47 us
  transfers between devices with their start and end apart: 9, of which 5 were waited for; matrix products, arithmetic and copies ran while one was open for 0% of the time, Pallas kernels for 0%

profile of v1, /device:TPU:1, one launch (start us, length us, event | category | flops | bytes accessed | tf_op | source)
XLA Modules:
  0.0 57.6 jit_solution(6651425987530528090)
XLA Ops:
  0.6 0.1 pad_add_fusion.place_ref
  0.7 0.0 copy-start
  0.7 0.0 copy-start.1
  0.7 6.9 %sample.1.refs_0_ = f32[232,128]{1,0:T(8,128)S(1)} custom-call(s32[4]{0:T(128)S(1)} %pad_add_fusion.place_ref, f32[19,32,128]{2,1,0:T(8,128)} %bitcast.16, s32[512,128]{1,0:T(8,128)} %bitcast.18, f32[512,128]{1,0:T(8,128)} %bitcast.20, f32[32,128]{1,0:T(8,128)} %bitcast.22, s32[1,64]{1,0:T(1,128)} %bitcast.23, s32[1,64]{1,0:T(1,128)} %bitcast.24, ...), custom_call_target="tpu_custom_call" | custom-call | tf_op jit(solution)/shard_map/sample/pallas_call | solution.py:370
  7.7 2.2 %collective-permute-start.2 = (f32[232,128]{1,0:T(8,128)S(1)}, f32[232,128]{1,0:T(8,128)S(1)}, u32[]{:S(2)}, u32[]{:S(2)}) collective-permute-start(f32[232,128]{1,0:T(8,128)S(1)} %sample.1.refs_0_), channel_id=1, source_target_pairs={{0,8},{8,0},{16,24},{24,16},{1,9},{9,1},{17,25},{25,17},{2,10},{10... | collective-permute-start | bytes 356360 | tf_op jit(solution)/shard_map/ppermute | solution.py:727
  9.9 2.3 %collective-permute-start.1 = (f32[232,128]{1,0:T(8,128)S(1)}, f32[232,128]{1,0:T(8,128)S(1)}, u32[]{:S(2)}, u32[]{:S(2)}) collective-permute-start(f32[232,128]{1,0:T(8,128)S(1)} %sample.1.refs_0_), channel_id=1, source_target_pairs={{0,16},{8,24},{16,0},{24,8},{1,17},{9,25},{17,1},{25,9},{2,18},{10... | collective-permute-start | bytes 356360 | tf_op jit(solution)/shard_map/ppermute | solution.py:727
  12.2 0.0 collective-permute-start
  12.2 1.2 %collective-permute-start.3 = (f32[232,128]{1,0:T(8,128)S(1)}, f32[232,128]{1,0:T(8,128)S(1)}, u32[]{:S(2)}, u32[]{:S(2)}) collective-permute-start(f32[232,128]{1,0:T(8,128)S(1)} %sample.1.refs_0_), channel_id=1, source_target_pairs={{0,4},{4,0},{1,5},{5,1},{2,6},{6,2},{3,7},{7,3},{8,12},{12,8},{9,1... | collective-permute-start | bytes 356360 | tf_op jit(solution)/shard_map/ppermute | solution.py:728
  13.4 0.0 collective-permute-done.2.refs_3_
  13.4 0.5 collective-permute-start.6
  13.9 0.7 %collective-permute-done.1.refs_2_ = f32[232,128]{1,0:T(8,128)S(1)} collective-permute-done((f32[232,128]{1,0:T(8,128)S(1)}, f32[232,128]{1,0:T(8,128)S(1)}, u32[]{:S(2)}, u32[]{:S(2)}) %collective-permute-start.1) | collective-permute-done | bytes 118816 | tf_op jit(solution)/shard_map/ppermute | solution.py:727
  14.6 1.2 %collective-permute-start.5 = (f32[232,128]{1,0:T(8,128)S(1)}, f32[232,128]{1,0:T(8,128)S(1)}, u32[]{:S(2)}, u32[]{:S(2)}) collective-permute-start(f32[232,128]{1,0:T(8,128)S(1)} %collective-permute-done.1.refs_2_), channel_id=1, source_target_pairs={{0,4},{4,0},{1,5},{5,1},{2,6},{6,2},{3,7},{7,3},{8,12},{12,8},{9,1... | collective-permute-start | bytes 356360 | tf_op jit(solution)/shard_map/ppermute | solution.py:728
  15.8 4.0 %collective-permute-done.refs_1_ = f32[232,128]{1,0:T(8,128)S(1)} collective-permute-done((f32[232,128]{1,0:T(8,128)S(1)}, f32[232,128]{1,0:T(8,128)S(1)}, u32[]{:S(2)}, u32[]{:S(2)}) %collective-permute-start) | collective-permute-done | bytes 118816 | tf_op jit(solution)/shard_map/ppermute | solution.py:727
  19.8 1.2 %collective-permute-start.4 = (f32[232,128]{1,0:T(8,128)S(1)}, f32[232,128]{1,0:T(8,128)S(1)}, u32[]{:S(2)}, u32[]{:S(2)}) collective-permute-start(f32[232,128]{1,0:T(8,128)S(1)} %collective-permute-done.refs_1_), channel_id=1, source_target_pairs={{0,4},{4,0},{1,5},{5,1},{2,6},{6,2},{3,7},{7,3},{8,12},{12,8},{9,1... | collective-permute-start | bytes 356360 | tf_op jit(solution)/shard_map/ppermute | solution.py:728
  21.0 0.0 collective-permute-done.3.refs_4_
  21.0 0.0 collective-permute-done.6.refs_7_
  21.1 0.0 collective-permute-done.5.refs_6_
  21.1 2.5 %collective-permute-done.4.refs_5_ = f32[232,128]{1,0:T(8,128)S(1)} collective-permute-done((f32[232,128]{1,0:T(8,128)S(1)}, f32[232,128]{1,0:T(8,128)S(1)}, u32[]{:S(2)}, u32[]{:S(2)}) %collective-permute-start.4) | collective-permute-done | bytes 118816 | tf_op jit(solution)/shard_map/ppermute | solution.py:728
  23.5 0.0 copy-done
  23.5 0.0 copy-done.1
  23.5 12.6 %spread.1 = (f32[19,32,128]{2,1,0:T(8,128)S(1)}, f32[5,8,128]{2,1,0:T(8,128)S(1)}, f32[5,8,128]{2,1,0:T(8,128)S(1)}, f32[3,32,128]{2,1,0:T(8,128)}) custom-call(s32[4]{0:T(128)S(1)} %pad_add_fusion.place_ref, f32[4,3]{1,0:T(4,128)S(1)} %copy-done.1, f32[232,128]{1,0:T(8,128)S(1)} %sample.1.refs_0_, f32[232,128]{1,0:T(8,128)S(1)} %collective-permute-done.refs_1_, ...), custom_call_target="tpu_custom_call" | custom-call | tf_op jit(solution)/shard_map/spread/pallas_call | solution.py:542
  36.2 3.6 %collective-permute-start.7 = (f32[5,8,128]{2,1,0:T(8,128)S(1)}, f32[5,8,128]{2,1,0:T(8,128)S(1)}, u32[]{:S(2)}, u32[]{:S(2)}) collective-permute-start(f32[5,8,128]{2,1,0:T(8,128)S(1)} %get-tuple-element.7), channel_id=1, source_target_pairs={{0,24},{16,8},{24,0},{8,16},{1,25},{17,9},{25,1},{9,17},{2,26},{18... | collective-permute-start | bytes 61448 | tf_op jit(solution)/shard_map/ppermute | solution.py:741
  39.8 0.7 %collective-permute-start.8 = (f32[5,8,128]{2,1,0:T(8,128)S(1)}, f32[5,8,128]{2,1,0:T(8,128)S(1)}, u32[]{:S(2)}, u32[]{:S(2)}) collective-permute-start(f32[5,8,128]{2,1,0:T(8,128)S(1)} %get-tuple-element.8), channel_id=1, source_target_pairs={{0,8},{16,24},{8,0},{24,16},{1,9},{17,25},{9,1},{25,17},{2,10},{18... | collective-permute-start | bytes 61448 | tf_op jit(solution)/shard_map/ppermute | solution.py:746
  40.5 0.4 collective-permute-done.7.far_ref
  41.0 1.5 %collective-permute-done.8.near_ref = f32[5,8,128]{2,1,0:T(8,128)S(1)} collective-permute-done((f32[5,8,128]{2,1,0:T(8,128)S(1)}, f32[5,8,128]{2,1,0:T(8,128)S(1)}, u32[]{:S(2)}, u32[]{:S(2)}) %collective-permute-start.8) | collective-permute-done | bytes 20512 | tf_op jit(solution)/shard_map/ppermute | solution.py:746
  42.4 0.7 %pack.1 = f32[8,24,128]{2,1,0:T(8,128)S(1)} custom-call(s32[4]{0:T(128)S(1)} %pad_add_fusion.place_ref, f32[19,32,128]{2,1,0:T(8,128)S(1)} %get-tuple-element.6.relaxed_ref, f32[5,8,128]{2,1,0:T(8,128)S(1)} %collective-permute-done.7.far_ref, f32[5,8,128]{2,1,0:T(8,128)S(1)} %collective-permute-done.8.near_ref), custom_call_target="tpu_custom_call" | custom-call | tf_op jit(solution)/shard_map/pack/pallas_call | solution.py:615
  43.1 13.1 %all_to_all.5.got_ref = f32[8,24,128]{2,1,0:T(8,128)S(1)} all-to-all(f32[8,24,128]{2,1,0:T(8,128)S(1)} %pack.1), channel_id=1, replica_groups=mesh['gx'=4,'gy'=2,'gz'=4] {'gy','gz'}, dimensions={0} | all-to-all | bytes 196608 | tf_op jit(solution)/shard_map/all_to_all | solution.py:748
  56.2 1.5 %stream.1 = f32[19,4,8,128]{3,2,1,0:T(8,128)} custom-call(s32[4]{0:T(128)S(1)} %pad_add_fusion.place_ref, f32[19,32,128]{2,1,0:T(8,128)S(1)} %get-tuple-element.6.relaxed_ref, f32[5,8,128]{2,1,0:T(8,128)S(1)} %collective-permute-done.7.far_ref, f32[5,8,128]{2,1,0:T(8,128)S(1)} %collective-permute-done.8.near_ref, f32[8,24,128]{2,1,0:T(8,128)S(1)} %all_to_all.5.got_ref), custom_call_target="tpu_custom_call" | custom-call | tf_op jit(solution)/shard_map/stream/pallas_call | solution.py:680
Async XLA Ops:
  0.7 22.8 %copy-start = (s32[4,8,128]{2,1,0:T(8,128)S(1)}, s32[4,8,128]{2,1,0:T(8,128)}, u32[]{:S(2)}) copy-start(s32[4,8,128]{2,1,0:T(8,128)} %param.10) | copy-start | bytes 49156
  0.7 22.8 %copy-start.1 = (f32[4,3]{1,0:T(4,128)S(1)}, f32[4,3]{1,0:T(4,128)}, u32[]{:S(2)}) copy-start(f32[4,3]{1,0:T(4,128)} %speeds_ref.1) | copy-start | bytes 148
  7.7 5.7 %collective-permute-start.2 = (f32[232,128]{1,0:T(8,128)S(1)}, f32[232,128]{1,0:T(8,128)S(1)}, u32[]{:S(2)}, u32[]{:S(2)}) collective-permute-start(f32[232,128]{1,0:T(8,128)S(1)} %sample.1.refs_0_), channel_id=1, source_target_pairs={{0,8},{8,0},{16,24},{24,16},{1,9},{9,1},{17,25},{25,17},{2,10},{10... | collective-permute-start | bytes 356360 | tf_op jit(solution)/shard_map/ppermute | solution.py:727
  9.9 4.7 %collective-permute-start.1 = (f32[232,128]{1,0:T(8,128)S(1)}, f32[232,128]{1,0:T(8,128)S(1)}, u32[]{:S(2)}, u32[]{:S(2)}) collective-permute-start(f32[232,128]{1,0:T(8,128)S(1)} %sample.1.refs_0_), channel_id=1, source_target_pairs={{0,16},{8,24},{16,0},{24,8},{1,17},{9,25},{17,1},{25,9},{2,18},{10... | collective-permute-start | bytes 356360 | tf_op jit(solution)/shard_map/ppermute | solution.py:727
  12.2 7.7 %collective-permute-start = (f32[232,128]{1,0:T(8,128)S(1)}, f32[232,128]{1,0:T(8,128)S(1)}, u32[]{:S(2)}, u32[]{:S(2)}) collective-permute-start(f32[232,128]{1,0:T(8,128)S(1)} %sample.1.refs_0_), channel_id=1, source_target_pairs={{0,24},{8,16},{16,8},{24,0},{1,25},{9,17},{17,9},{25,1},{2,26},{10... | collective-permute-start | bytes 356360 | tf_op jit(solution)/shard_map/ppermute | solution.py:727
  12.2 8.9 %collective-permute-start.3 = (f32[232,128]{1,0:T(8,128)S(1)}, f32[232,128]{1,0:T(8,128)S(1)}, u32[]{:S(2)}, u32[]{:S(2)}) collective-permute-start(f32[232,128]{1,0:T(8,128)S(1)} %sample.1.refs_0_), channel_id=1, source_target_pairs={{0,4},{4,0},{1,5},{5,1},{2,6},{6,2},{3,7},{7,3},{8,12},{12,8},{9,1... | collective-permute-start | bytes 356360 | tf_op jit(solution)/shard_map/ppermute | solution.py:728
  13.4 7.7 %collective-permute-start.6 = (f32[232,128]{1,0:T(8,128)S(1)}, f32[232,128]{1,0:T(8,128)S(1)}, u32[]{:S(2)}, u32[]{:S(2)}) collective-permute-start(f32[232,128]{1,0:T(8,128)S(1)} %collective-permute-done.2.refs_3_), channel_id=1, source_target_pairs={{0,4},{4,0},{1,5},{5,1},{2,6},{6,2},{3,7},{7,3},{8,12},{12,8},{9,1... | collective-permute-start | bytes 356360 | tf_op jit(solution)/shard_map/ppermute | solution.py:728
  14.6 6.5 %collective-permute-start.5 = (f32[232,128]{1,0:T(8,128)S(1)}, f32[232,128]{1,0:T(8,128)S(1)}, u32[]{:S(2)}, u32[]{:S(2)}) collective-permute-start(f32[232,128]{1,0:T(8,128)S(1)} %collective-permute-done.1.refs_2_), channel_id=1, source_target_pairs={{0,4},{4,0},{1,5},{5,1},{2,6},{6,2},{3,7},{7,3},{8,12},{12,8},{9,1... | collective-permute-start | bytes 356360 | tf_op jit(solution)/shard_map/ppermute | solution.py:728
  19.8 3.7 %collective-permute-start.4 = (f32[232,128]{1,0:T(8,128)S(1)}, f32[232,128]{1,0:T(8,128)S(1)}, u32[]{:S(2)}, u32[]{:S(2)}) collective-permute-start(f32[232,128]{1,0:T(8,128)S(1)} %collective-permute-done.refs_1_), channel_id=1, source_target_pairs={{0,4},{4,0},{1,5},{5,1},{2,6},{6,2},{3,7},{7,3},{8,12},{12,8},{9,1... | collective-permute-start | bytes 356360 | tf_op jit(solution)/shard_map/ppermute | solution.py:728
  36.2 4.8 %collective-permute-start.7 = (f32[5,8,128]{2,1,0:T(8,128)S(1)}, f32[5,8,128]{2,1,0:T(8,128)S(1)}, u32[]{:S(2)}, u32[]{:S(2)}) collective-permute-start(f32[5,8,128]{2,1,0:T(8,128)S(1)} %get-tuple-element.7), channel_id=1, source_target_pairs={{0,24},{16,8},{24,0},{8,16},{1,25},{17,9},{25,1},{9,17},{2,26},{18... | collective-permute-start | bytes 61448 | tf_op jit(solution)/shard_map/ppermute | solution.py:741
  39.8 2.6 %collective-permute-start.8 = (f32[5,8,128]{2,1,0:T(8,128)S(1)}, f32[5,8,128]{2,1,0:T(8,128)S(1)}, u32[]{:S(2)}, u32[]{:S(2)}) collective-permute-start(f32[5,8,128]{2,1,0:T(8,128)S(1)} %get-tuple-element.8), channel_id=1, source_target_pairs={{0,8},{16,24},{8,0},{24,16},{1,9},{17,25},{9,1},{25,17},{2,10},{18... | collective-permute-start | bytes 61448 | tf_op jit(solution)/shard_map/ppermute | solution.py:746

commit v2 on v1

--- a/solution.py
+++ b/solution.py
@@ -339,13 +339,16 @@
             cells = cells_ref[at, :]
             lane = cells & (lanes - 1)
             row = cells >> (lanes.bit_length() - 1)
-            words = [jnp.zeros((group, mark), jnp.int32) for c in range(2)]
-            for r in range(rows):
-                here = row == r
-                for c in range(2):
-                    line = jnp.broadcast_to(table[c, r : r + 1, :], (group, lanes))
-                    got = jnp.take_along_axis(line, lane, axis=1, mode="promise_in_bounds")
-                    words[c] = jnp.where(here, got, words[c])
+            bits = [(row >> bit) & 1 == 1 for bit in range(rows.bit_length() - 1)]
+
+            def choose(c, low, level):
+                if level < 0:
+                    line = jnp.broadcast_to(table[c, low : low + 1, :], (group, lanes))
+                    return jnp.take_along_axis(line, lane, axis=1, mode="promise_in_bounds")
+                lower = choose(c, low, level - 1)
+                return jnp.where(bits[level], choose(c, low + (1 << level), level - 1), lower)
+
+            words = [choose(c, 0, len(bits) - 1) for c in range(2)]
             last = ((words[0] & 2047) << 11) | (words[1] & 2047)
             picked = [
                 lax.shift_right_logical(words[0], 11),
@@ -353,8 +356,8 @@
                 last,
             ]
             weight = weights_ref[at, :]
-            for c, bits in enumerate((21, 21, 22)):
-                value = (picked[c].astype(jnp.float32) - 2.0 ** (bits - 1)) * 2.0**-bits
+            for c, width in enumerate((21, 21, 22)):
+                value = (picked[c].astype(jnp.float32) - 2.0 ** (width - 1)) * 2.0**-width
                 total[c] = total[c] + weight * value
         for c in range(3):
             out_ref[pl.ds(pl.multiple_of(c * slots + first, group), group), :] = total[c]
@@ -489,7 +492,7 @@
             left, right = ([], [])
             for i in range(group):
                 lane_i, row_i = (wide(0, i), wide(1, i))
-                left.append(
+                right.append(
                     jnp.concatenate(
                         [jnp.where(steps[j] == lane_i, one, zero) for j in range(lanes // 16)],
                         axis=0,
@@ -500,7 +503,7 @@
                 for which in range(len(parts)):
                     part_i = wide(2 + which, i)
                     pieces += [jnp.where(mask, part_i, zero) for mask in masks]
-                right.append(jnp.concatenate(pieces, axis=0))
+                left.append(jnp.concatenate(pieces, axis=0))
             acc[...] += lax.dot_general(
                 jnp.concatenate(left, axis=1),
                 jnp.concatenate(right, axis=1),
@@ -511,11 +514,8 @@
 
     lax.fori_loop(0, slots // group, body, 0)
     copies[2].wait()
-    spare = jnp.zeros((lanes, -acc.shape[1] % 128), jnp.float32)
-    turned = jnp.concatenate([acc[...], spare], axis=1)
-    turned = jnp.concatenate([turned[:, 0:128].T, turned[:, 128:256].T], axis=0)
     cell_force = [
-        turned[2 * c * rows : (2 * c + 1) * rows] + turned[(2 * c + 1) * rows : (2 * c + 2) * rows]
+        acc[2 * c * rows : (2 * c + 1) * rows, :] + acc[(2 * c + 1) * rows : (2 * c + 2) * rows, :]
         for c in range(3)
     ]
     relaxed = collide([pop_ref[q] for q in range(19)], cell_force, solid_ref[...])
@@ -554,7 +554,7 @@
             pltpu.VMEM(populations.shape, jnp.float32),
             pltpu.VMEM((3, slots, mark), jnp.float32),
             pltpu.VMEM((cells.shape[0] // slots, 8, group, mark), jnp.float32),
-            pltpu.VMEM((lanes, 6 * line_count), jnp.float32),
+            pltpu.VMEM((6 * line_count, lanes), jnp.float32),
             pltpu.SemaphoreType.DMA((3,)),
         ],
         compiler_params=kernel_params(),
@@ -722,10 +722,12 @@
     pops, cells, weights = inputs[:3]
     own = sample(place, *inputs)
     swap = [(0, 1), (1, 0)]
-    column = [own]
+    column = {0: own}
     for distance in reversed(range(1, count_x)):
-        column.append(lax.ppermute(own, "gx", [(i, i ^ distance) for i in range(count_x)]))
-    shards = column + [lax.ppermute(shard, "gy", swap) for shard in column]
+        column[distance] = lax.ppermute(own, "gx", [(i, i ^ distance) for i in range(count_x)])
+    shards = []
+    for distance in (0, 2, 3, 1):
+        shards += [column[distance], lax.ppermute(column[distance], "gy", swap)]
     relaxed, far, near, marker_force = spread(
         slots,
         owned,

time: 58.6 us -> 56.6 us (0.966)
  waiting for transfers between devices: 9.11 us -> 12.9 us
  starting transfers between devices: 13 us -> 10.7 us
  Pallas kernels: 21.7 us -> 19.6 us
  blocking collectives: 13.1 us -> 11.7 us
    ppermute x3, waiting for transfers between devices: 4.74 us -> 7.74 us  [per_device(): lax.ppermute(own, 'gx', [(i, i ^ distance) for i in range(count_x)])]
    pallas_call x1, Pallas kernels: 12.6 us -> 10.5 us  [spread(): pl.pallas_call(functools.partial(spread_kernel, len(shards), slots, owned...]
    ppermute x1, waiting for transfers between devices: 0.44 us -> 2.45 us  [per_device(): lax.ppermute(far, 'gx', [(i, (i - 1) % count_x) for i in evens] + [((i -...]
    ppermute x1, starting transfers between devices: 3.63 us -> 2.04 us  [per_device(): lax.ppermute(far, 'gx', [(i, (i - 1) % count_x) for i in evens] + [((i -...]
    all_to_all x1, blocking collectives: 13.1 us -> 11.7 us  [per_device(): lax.all_to_all(sides, ('gy', 'gz'), split_axis=0, concat_axis=0, tiled=True)]
    ppermute x1, waiting for transfers between devices: 1.46 us -> 0.22 us  [per_device(): lax.ppermute(near, 'gx', [(i, i + 1) for i in evens] + [(i + 1, i) for i...]
    ppermute x1, starting transfers between devices: 0.74 us -> 0.01 us  [per_device(): lax.ppermute(near, 'gx', [(i, i + 1) for i in evens] + [(i + 1, i) for i...]
where the time goes in v2:
time: 56.6 us; the launch traced here: 55.7 us
  Pallas kernels  19.6 us (35%)
  waiting for transfers between devices  12.9 us (23%)
  blocking collectives  11.7 us (21%)
  starting transfers between devices  10.7 us (19%)
  between operations  0.68 us (1%)
    all_to_all x1, blocking collectives, per_device(): lax.all_to_all(sides, ('gy', 'gz'), split_axis=0, concat_axis=0, tiled=True)  11.7 us
    pallas_call x1, Pallas kernels, spread(): pl.pallas_call(functools.partial(spread_kernel, len(shards), slots, owned...  10.5 us
    ppermute x3, waiting for transfers between devices, per_device(): lax.ppermute(own, 'gx', [(i, i ^ distance) for i in range(count_x)])  7.74 us
    pallas_call x1, Pallas kernels, sample(): pl.pallas_call(sample_kernel, out_shape=full((shard_rows(owner.shape[1],...  6.95 us
    ppermute x3, starting transfers between devices, per_device(): lax.ppermute(own, 'gx', [(i, i ^ distance) for i in range(count_x)])  4.5 us
    ppermute x4, starting transfers between devices, per_device(): shards += [column[distance], lax.ppermute(column[distance], 'gy', swap)]  4.12 us
    ppermute x4, waiting for transfers between devices, per_device(): shards += [column[distance], lax.ppermute(column[distance], 'gy', swap)]  2.47 us
    ppermute x1, waiting for transfers between devices, per_device(): lax.ppermute(far, 'gx', [(i, (i - 1) % count_x) for i in evens] + [((i -...  2.45 us
  transfers between devices with their start and end apart: 9, of which 5 were waited for; matrix products, arithmetic and copies ran while one was open for 0% of the time, Pallas kernels for 0%

profile of v2, /device:TPU:1, one launch (start us, length us, event | category | flops | bytes accessed | tf_op | source)
XLA Modules:
  0.0 55.7 jit_solution(2340579183766450778)
XLA Ops:
  0.6 0.1 pad_add_fusion.place_ref
  0.7 0.0 copy-start
  0.7 0.0 copy-start.1
  0.7 7.0 %sample.1.refs_0_ = f32[232,128]{1,0:T(8,128)S(1)} custom-call(s32[4]{0:T(128)S(1)} %pad_add_fusion.place_ref, f32[19,32,128]{2,1,0:T(8,128)} %bitcast.16, s32[512,128]{1,0:T(8,128)} %bitcast.18, f32[512,128]{1,0:T(8,128)} %bitcast.20, f32[32,128]{1,0:T(8,128)} %bitcast.22, s32[1,64]{1,0:T(1,128)} %bitcast.23, s32[1,64]{1,0:T(1,128)} %bitcast.24, ...), custom_call_target="tpu_custom_call" | custom-call | tf_op jit(solution)/shard_map/sample/pallas_call | solution.py:373
  7.7 2.2 %collective-permute-start.5 = (f32[232,128]{1,0:T(8,128)S(1)}, f32[232,128]{1,0:T(8,128)S(1)}, u32[]{:S(2)}, u32[]{:S(2)}) collective-permute-start(f32[232,128]{1,0:T(8,128)S(1)} %sample.1.refs_0_), channel_id=1, source_target_pairs={{0,8},{8,0},{16,24},{24,16},{1,9},{9,1},{17,25},{25,17},{2,10},{10... | collective-permute-start | bytes 356360 | tf_op jit(solution)/shard_map/ppermute | solution.py:727
  9.9 2.2 %collective-permute-start.3 = (f32[232,128]{1,0:T(8,128)S(1)}, f32[232,128]{1,0:T(8,128)S(1)}, u32[]{:S(2)}, u32[]{:S(2)}) collective-permute-start(f32[232,128]{1,0:T(8,128)S(1)} %sample.1.refs_0_), channel_id=1, source_target_pairs={{0,24},{8,16},{16,8},{24,0},{1,25},{9,17},{17,9},{25,1},{2,26},{10... | collective-permute-start | bytes 356360 | tf_op jit(solution)/shard_map/ppermute | solution.py:727
  12.1 0.1 collective-permute-start.1
  12.2 1.2 %collective-permute-start = (f32[232,128]{1,0:T(8,128)S(1)}, f32[232,128]{1,0:T(8,128)S(1)}, u32[]{:S(2)}, u32[]{:S(2)}) collective-permute-start(f32[232,128]{1,0:T(8,128)S(1)} %sample.1.refs_0_), channel_id=1, source_target_pairs={{0,4},{4,0},{1,5},{5,1},{2,6},{6,2},{3,7},{7,3},{8,12},{12,8},{9,1... | collective-permute-start | bytes 356360 | tf_op jit(solution)/shard_map/ppermute | solution.py:730
  13.4 0.0 collective-permute-done.5.refs_6_
  13.4 0.5 collective-permute-start.6
  13.9 3.4 %collective-permute-done.3.refs_4_ = f32[232,128]{1,0:T(8,128)S(1)} collective-permute-done((f32[232,128]{1,0:T(8,128)S(1)}, f32[232,128]{1,0:T(8,128)S(1)}, u32[]{:S(2)}, u32[]{:S(2)}) %collective-permute-start.3) | collective-permute-done | bytes 118816 | tf_op jit(solution)/shard_map/ppermute | solution.py:727
  17.3 1.2 %collective-permute-start.4 = (f32[232,128]{1,0:T(8,128)S(1)}, f32[232,128]{1,0:T(8,128)S(1)}, u32[]{:S(2)}, u32[]{:S(2)}) collective-permute-start(f32[232,128]{1,0:T(8,128)S(1)} %collective-permute-done.3.refs_4_), channel_id=1, source_target_pairs={{0,4},{4,0},{1,5},{5,1},{2,6},{6,2},{3,7},{7,3},{8,12},{12,8},{9,1... | collective-permute-start | bytes 356360 | tf_op jit(solution)/shard_map/ppermute | solution.py:730
  18.5 4.4 %collective-permute-done.1.refs_2_ = f32[232,128]{1,0:T(8,128)S(1)} collective-permute-done((f32[232,128]{1,0:T(8,128)S(1)}, f32[232,128]{1,0:T(8,128)S(1)}, u32[]{:S(2)}, u32[]{:S(2)}) %collective-permute-start.1) | collective-permute-done | bytes 118816 | tf_op jit(solution)/shard_map/ppermute | solution.py:727
  22.8 1.2 %collective-permute-start.2 = (f32[232,128]{1,0:T(8,128)S(1)}, f32[232,128]{1,0:T(8,128)S(1)}, u32[]{:S(2)}, u32[]{:S(2)}) collective-permute-start(f32[232,128]{1,0:T(8,128)S(1)} %collective-permute-done.1.refs_2_), channel_id=1, source_target_pairs={{0,4},{4,0},{1,5},{5,1},{2,6},{6,2},{3,7},{7,3},{8,12},{12,8},{9,1... | collective-permute-start | bytes 356360 | tf_op jit(solution)/shard_map/ppermute | solution.py:730
  24.1 0.0 collective-permute-done.refs_1_
  24.1 0.0 collective-permute-done.6.refs_7_
  24.1 0.0 collective-permute-done.4.refs_5_
  24.1 2.5 %collective-permute-done.2.refs_3_ = f32[232,128]{1,0:T(8,128)S(1)} collective-permute-done((f32[232,128]{1,0:T(8,128)S(1)}, f32[232,128]{1,0:T(8,128)S(1)}, u32[]{:S(2)}, u32[]{:S(2)}) %collective-permute-start.2) | collective-permute-done | bytes 118816 | tf_op jit(solution)/shard_map/ppermute | solution.py:730
  26.5 0.0 copy-done
  26.5 0.0 copy-done.1
  26.5 10.5 %spread.1 = (f32[19,32,128]{2,1,0:T(8,128)S(1)}, f32[5,8,128]{2,1,0:T(8,128)S(1)}, f32[5,8,128]{2,1,0:T(8,128)S(1)}, f32[3,32,128]{2,1,0:T(8,128)}) custom-call(s32[4]{0:T(128)S(1)} %pad_add_fusion.place_ref, f32[4,3]{1,0:T(4,128)S(1)} %copy-done.1, f32[232,128]{1,0:T(8,128)S(1)} %sample.1.refs_0_, f32[232,128]{1,0:T(8,128)S(1)} %collective-permute-done.refs_1_, ...), custom_call_target="tpu_custom_call" | custom-call | tf_op jit(solution)/shard_map/spread/pallas_call | solution.py:542
  37.1 2.0 %collective-permute-start.7 = (f32[5,8,128]{2,1,0:T(8,128)S(1)}, f32[5,8,128]{2,1,0:T(8,128)S(1)}, u32[]{:S(2)}, u32[]{:S(2)}) collective-permute-start(f32[5,8,128]{2,1,0:T(8,128)S(1)} %get-tuple-element.7), channel_id=1, source_target_pairs={{0,24},{16,8},{24,0},{8,16},{1,25},{17,9},{25,1},{9,17},{2,26},{18... | collective-permute-start | bytes 61448 | tf_op jit(solution)/shard_map/ppermute | solution.py:743
  39.1 0.0 collective-permute-start.8
  39.1 2.4 %collective-permute-done.7.far_ref = f32[5,8,128]{2,1,0:T(8,128)S(1)} collective-permute-done((f32[5,8,128]{2,1,0:T(8,128)S(1)}, f32[5,8,128]{2,1,0:T(8,128)S(1)}, u32[]{:S(2)}, u32[]{:S(2)}) %collective-permute-start.7) | collective-permute-done | bytes 20512 | tf_op jit(solution)/shard_map/ppermute | solution.py:743
  41.6 0.2 collective-permute-done.8.near_ref
  41.8 0.7 %pack.1 = f32[8,24,128]{2,1,0:T(8,128)S(1)} custom-call(s32[4]{0:T(128)S(1)} %pad_add_fusion.place_ref, f32[19,32,128]{2,1,0:T(8,128)S(1)} %get-tuple-element.6.relaxed_ref, f32[5,8,128]{2,1,0:T(8,128)S(1)} %collective-permute-done.7.far_ref, f32[5,8,128]{2,1,0:T(8,128)S(1)} %collective-permute-done.8.near_ref), custom_call_target="tpu_custom_call" | custom-call | tf_op jit(solution)/shard_map/pack/pallas_call | solution.py:615
  42.5 11.7 %all_to_all.5.got_ref = f32[8,24,128]{2,1,0:T(8,128)S(1)} all-to-all(f32[8,24,128]{2,1,0:T(8,128)S(1)} %pack.1), channel_id=1, replica_groups=mesh['gx'=4,'gy'=2,'gz'=4] {'gy','gz'}, dimensions={0} | all-to-all | bytes 196608 | tf_op jit(solution)/shard_map/all_to_all | solution.py:750
  54.2 1.5 %stream.1 = f32[19,4,8,128]{3,2,1,0:T(8,128)} custom-call(s32[4]{0:T(128)S(1)} %pad_add_fusion.place_ref, f32[19,32,128]{2,1,0:T(8,128)S(1)} %get-tuple-element.6.relaxed_ref, f32[5,8,128]{2,1,0:T(8,128)S(1)} %collective-permute-done.7.far_ref, f32[5,8,128]{2,1,0:T(8,128)S(1)} %collective-permute-done.8.near_ref, f32[8,24,128]{2,1,0:T(8,128)S(1)} %all_to_all.5.got_ref), custom_call_target="tpu_custom_call" | custom-call | tf_op jit(solution)/shard_map/stream/pallas_call | solution.py:680
Async XLA Ops:
  0.7 25.8 %copy-start = (s32[4,8,128]{2,1,0:T(8,128)S(1)}, s32[4,8,128]{2,1,0:T(8,128)}, u32[]{:S(2)}) copy-start(s32[4,8,128]{2,1,0:T(8,128)} %param.10) | copy-start | bytes 49156
  0.7 25.8 %copy-start.1 = (f32[4,3]{1,0:T(4,128)S(1)}, f32[4,3]{1,0:T(4,128)}, u32[]{:S(2)}) copy-start(f32[4,3]{1,0:T(4,128)} %speeds_ref.1) | copy-start | bytes 148
  7.7 5.7 %collective-permute-start.5 = (f32[232,128]{1,0:T(8,128)S(1)}, f32[232,128]{1,0:T(8,128)S(1)}, u32[]{:S(2)}, u32[]{:S(2)}) collective-permute-start(f32[232,128]{1,0:T(8,128)S(1)} %sample.1.refs_0_), channel_id=1, source_target_pairs={{0,8},{8,0},{16,24},{24,16},{1,9},{9,1},{17,25},{25,17},{2,10},{10... | collective-permute-start | bytes 356360 | tf_op jit(solution)/shard_map/ppermute | solution.py:727
  9.9 7.4 %collective-permute-start.3 = (f32[232,128]{1,0:T(8,128)S(1)}, f32[232,128]{1,0:T(8,128)S(1)}, u32[]{:S(2)}, u32[]{:S(2)}) collective-permute-start(f32[232,128]{1,0:T(8,128)S(1)} %sample.1.refs_0_), channel_id=1, source_target_pairs={{0,24},{8,16},{16,8},{24,0},{1,25},{9,17},{17,9},{25,1},{2,26},{10... | collective-permute-start | bytes 356360 | tf_op jit(solution)/shard_map/ppermute | solution.py:727
  12.1 10.8 %collective-permute-start.1 = (f32[232,128]{1,0:T(8,128)S(1)}, f32[232,128]{1,0:T(8,128)S(1)}, u32[]{:S(2)}, u32[]{:S(2)}) collective-permute-start(f32[232,128]{1,0:T(8,128)S(1)} %sample.1.refs_0_), channel_id=1, source_target_pairs={{0,16},{8,24},{16,0},{24,8},{1,17},{9,25},{17,1},{25,9},{2,18},{10... | collective-permute-start | bytes 356360 | tf_op jit(solution)/shard_map/ppermute | solution.py:727
  12.2 11.9 %collective-permute-start = (f32[232,128]{1,0:T(8,128)S(1)}, f32[232,128]{1,0:T(8,128)S(1)}, u32[]{:S(2)}, u32[]{:S(2)}) collective-permute-start(f32[232,128]{1,0:T(8,128)S(1)} %sample.1.refs_0_), channel_id=1, source_target_pairs={{0,4},{4,0},{1,5},{5,1},{2,6},{6,2},{3,7},{7,3},{8,12},{12,8},{9,1... | collective-permute-start | bytes 356360 | tf_op jit(solution)/shard_map/ppermute | solution.py:730
  13.4 10.7 %collective-permute-start.6 = (f32[232,128]{1,0:T(8,128)S(1)}, f32[232,128]{1,0:T(8,128)S(1)}, u32[]{:S(2)}, u32[]{:S(2)}) collective-permute-start(f32[232,128]{1,0:T(8,128)S(1)} %collective-permute-done.5.refs_6_), channel_id=1, source_target_pairs={{0,4},{4,0},{1,5},{5,1},{2,6},{6,2},{3,7},{7,3},{8,12},{12,8},{9,1... | collective-permute-start | bytes 356360 | tf_op jit(solution)/shard_map/ppermute | solution.py:730
  17.3 6.8 %collective-permute-start.4 = (f32[232,128]{1,0:T(8,128)S(1)}, f32[232,128]{1,0:T(8,128)S(1)}, u32[]{:S(2)}, u32[]{:S(2)}) collective-permute-start(f32[232,128]{1,0:T(8,128)S(1)} %collective-permute-done.3.refs_4_), channel_id=1, source_target_pairs={{0,4},{4,0},{1,5},{5,1},{2,6},{6,2},{3,7},{7,3},{8,12},{12,8},{9,1... | collective-permute-start | bytes 356360 | tf_op jit(solution)/shard_map/ppermute | solution.py:730
  22.8 3.7 %collective-permute-start.2 = (f32[232,128]{1,0:T(8,128)S(1)}, f32[232,128]{1,0:T(8,128)S(1)}, u32[]{:S(2)}, u32[]{:S(2)}) collective-permute-start(f32[232,128]{1,0:T(8,128)S(1)} %collective-permute-done.1.refs_2_), channel_id=1, source_target_pairs={{0,4},{4,0},{1,5},{5,1},{2,6},{6,2},{3,7},{7,3},{8,12},{12,8},{9,1... | collective-permute-start | bytes 356360 | tf_op jit(solution)/shard_map/ppermute | solution.py:730
  37.1 4.5 %collective-permute-start.7 = (f32[5,8,128]{2,1,0:T(8,128)S(1)}, f32[5,8,128]{2,1,0:T(8,128)S(1)}, u32[]{:S(2)}, u32[]{:S(2)}) collective-permute-start(f32[5,8,128]{2,1,0:T(8,128)S(1)} %get-tuple-element.7), channel_id=1, source_target_pairs={{0,24},{16,8},{24,0},{8,16},{1,25},{17,9},{25,1},{9,17},{2,26},{18... | collective-permute-start | bytes 61448 | tf_op jit(solution)/shard_map/ppermute | solution.py:743
  39.1 2.7 %collective-permute-start.8 = (f32[5,8,128]{2,1,0:T(8,128)S(1)}, f32[5,8,128]{2,1,0:T(8,128)S(1)}, u32[]{:S(2)}, u32[]{:S(2)}) collective-permute-start(f32[5,8,128]{2,1,0:T(8,128)S(1)} %get-tuple-element.8), channel_id=1, source_target_pairs={{0,8},{16,24},{8,0},{24,16},{1,9},{17,25},{9,1},{25,17},{2,10},{18... | collective-permute-start | bytes 61448 | tf_op jit(solution)/shard_map/ppermute | solution.py:748

commit v3 on v2

--- a/solution.py
+++ b/solution.py
@@ -293,7 +293,7 @@
 def sample_kernel(
     place_ref, pop_any, cells_any, weights_any, areas_any, owner_any, block_any, trains_any,
     out_ref, pop_ref, cells_ref, weights_ref, areas_ref, owner_ref, block_ref, trains_ref,
-    table, sems,
+    table, sems, group_sems,
 ):
     rows, lanes = (pop_ref.shape[1], pop_ref.shape[2])
     mark = cells_ref.shape[1]
@@ -303,8 +303,6 @@
     copies = fetch(
         (
             (pop_any, pop_ref),
-            (cells_any, cells_ref),
-            (weights_any, weights_ref),
             (areas_any, areas_ref),
             (owner_any, owner_ref),
             (block_any, block_ref),
@@ -312,6 +310,19 @@
         ),
         sems,
     )
+
+    def group_copies(step):
+        here = pl.ds(pl.multiple_of(step * group * kernel, group * kernel), group * kernel)
+        return (
+            pltpu.make_async_copy(cells_any.at[here], cells_ref.at[here], group_sems.at[0, step]),
+            pltpu.make_async_copy(
+                weights_any.at[here], weights_ref.at[here], group_sems.at[1, step]
+            ),
+        )
+
+    for step in range(slots // group):
+        for copy in group_copies(step):
+            copy.start()
     copies[0].wait()
     density, momentum = moments([pop_ref[q] for q in range(19)])
     fixed = [
@@ -332,6 +343,8 @@
     out_ref[meta + 2 : meta + 3, :] = mine.astype(jnp.float32)
 
     def body(step, carry):
+        for copy in group_copies(step):
+            copy.wait()
         first = pl.multiple_of(step * group, group)
         total = [jnp.zeros((group, mark), jnp.float32) for c in range(3)]
         for k in range(kernel):
@@ -363,7 +376,7 @@
             out_ref[pl.ds(pl.multiple_of(c * slots + first, group), group), :] = total[c]
         return carry
 
-    lax.fori_loop(0, slots // group, body, 0)
+    lax.fori_loop(0, slots // group, body, 0, unroll=2)
 
 
 def sample(place, populations, cells, weights, areas, owner, block, trains):
@@ -380,7 +393,8 @@
         ]
         + [
             pltpu.VMEM((2,) + populations.shape[1:], jnp.int32),
-            pltpu.SemaphoreType.DMA((7,)),
+            pltpu.SemaphoreType.DMA((5,)),
+            pltpu.SemaphoreType.DMA((2, owner.shape[1] // group)),
         ],
         compiler_params=kernel_params(),
         name="sample",
@@ -399,36 +413,64 @@
     return jnp.where(mask, 1.0, 0.0).astype(jnp.bfloat16)
 
 
-def settle_rows(speeds_ref, shards, slots, owned):
-    mark = shards[0].shape[1]
+def wanted_labels(own_ref, slots, owned):
+    mark = own_ref.shape[1]
+    own = own_ref[3 * slots + owned : 3 * slots + owned + 8, :]
+    ids, trains, mine = (jnp.broadcast_to(own[i : i + 1], (mark, mark)).T for i in range(3))
+    return (ids[0:slots], mine[0:owned], trains[0:owned])
+
+
+def add_shards(totals, shards, ids, mine):
+    slots, owned = (ids.shape[0], mine.shape[0])
     meta = 3 * slots + owned
-    own = shards[0][meta : meta + 8, :]
-    ids = jnp.broadcast_to(own[0:1], (mark, mark)).T[0:slots]
-    mine = jnp.broadcast_to(own[2:3], (mark, mark)).T[0:owned]
     wanted = jnp.concatenate([ids, mine], axis=0)
-    sums = area = trains = None
     for shard in shards:
-        labels = shard[meta : meta + 1, :]
-        match = one_hot(wanted == labels)
+        match = one_hot(wanted == shard[meta : meta + 1, :])
         match = jnp.concatenate([match, match[:, 0:slots]], axis=1)
         values = jnp.concatenate([shard[c * slots : (c + 1) * slots, :] for c in range(3)], axis=1)
-        got = jnp.dot(
+        sums = jnp.dot(
             match, jnp.concatenate(three_parts(values), axis=0), preferred_element_type=jnp.float32
         )
-        sums = got if sums is None else sums + got
         held = ids == shard[meta + 2 : meta + 3, :]
         parts = three_parts(shard[3 * slots : meta, :])
         parts.append(jnp.zeros_like(parts[0]))
-        got = jnp.dot(
+        area = jnp.dot(
             one_hot(held), jnp.concatenate(parts, axis=0), preferred_element_type=jnp.float32
         )
-        area = got if area is None else area + got
-        got = jnp.where(held, shard[meta + 1 : meta + 2, :], 0.0)
-        trains = got if trains is None else trains + got
+        trains = jnp.where(held, shard[meta + 1 : meta + 2, :], 0.0)
+        got = (sums, area, trains)
+        totals = got if totals is None else [total + new for total, new in zip(totals, got)]
+    return totals
+
+
+def settle_kernel(slots, owned, *refs):
+    shards, (sums_ref, area_ref, trains_ref) = (refs[:-3], refs[-3:])
+    ids, mine, _ = wanted_labels(shards[0], slots, owned)
+    sums_ref[...], area_ref[...], trains_ref[...] = add_shards(None, shards, ids, mine)
+
+
+def settle_early(slots, owned, shards):
+    mark = shards[0].shape[1]
+    vmem = pl.BlockSpec(memory_space=pltpu.VMEM)
+    return pl.pallas_call(
+        functools.partial(settle_kernel, slots, owned),
+        out_shape=(full((slots + owned, 3 * mark)), full((slots, mark)), full((slots, mark))),
+        in_specs=[vmem] * len(shards),
+        compiler_params=kernel_params(),
+        cost_estimate=pl.CostEstimate(
+            flops=10**9, bytes_accessed=len(shards) * shards[0].size * 4, transcendentals=0
+        ),
+        name="settle",
+    )(*shards)
+
+
+def block_forces(speeds_ref, totals, own_ref, slots, owned):
+    mark = own_ref.shape[1]
+    ids, mine, own_trains = wanted_labels(own_ref, slots, owned)
+    sums, area, trains = totals
     trains = jnp.sum(trains, axis=1, keepdims=True)
-    own_trains = jnp.broadcast_to(own[1:2], (mark, mark)).T[0:owned]
-    forces = []
-    own_forces = []
+    own_area = own_ref[3 * slots : 3 * slots + owned, :]
+    forces, own_forces = ([], [])
     for c in range(3):
         target = jnp.zeros(trains.shape, jnp.float32)
         own_target = jnp.zeros(own_trains.shape, jnp.float32)
@@ -438,16 +480,15 @@
             own_target = jnp.where(own_trains == float(train), speed, own_target)
         got = sums[:, c * mark : (c + 1) * mark]
         forces.append(stiffness * area * (target - got[0:slots]))
-        own_area = shards[0][3 * slots : meta, :]
         own_forces.append(stiffness * own_area * (own_target - got[slots:]))
     return (forces, own_forces)
 
 
 def spread_kernel(shard_count, slots, owned, place_ref, speeds_ref, *refs):
     shards, refs = (refs[:shard_count], refs[shard_count:])
-    cells_any, weights_any, pop_any, solid_ref = refs[:4]
-    relaxed_ref, far_ref, near_ref, marker_ref = refs[4:8]
-    cells_ref, weights_ref, pop_ref, force_ref, lines_ref, acc, sems = refs[8:]
+    sums_ref, area_ref, trains_ref, cells_any, weights_any, pop_any, solid_ref = refs[:7]
+    relaxed_ref, far_ref, near_ref, side_ref, marker_ref = refs[7:12]
+    cells_ref, weights_ref, pop_ref, force_ref, lines_ref, acc, sems = refs[12:]
     rows, lanes = (pop_ref.shape[1], pop_ref.shape[2])
     size_y = 8
     mark = cells_ref.shape[1]
@@ -456,7 +497,11 @@
     copies = fetch(
         ((cells_any, cells_ref), (weights_any, weights_ref), (pop_any, pop_ref)), sems
     )
-    forces, own_forces = settle_rows(speeds_ref, shards, slots, owned)
+    own_ref = shards[0]
+    ids, mine, _ = wanted_labels(own_ref, slots, owned)
+    totals = (sums_ref[...], area_ref[...], trains_ref[...])
+    totals = add_shards(totals, shards[1:], ids, mine)
+    forces, own_forces = block_forces(speeds_ref, totals, own_ref, slots, owned)
     for c in range(3):
         force_ref[c] = forces[c]
         marker_ref[c] = own_forces[c]
@@ -527,13 +572,14 @@
         behind = relaxed[going(0, -1)[i]][:size_y]
         far_ref[i] = jnp.where(even, behind, ahead)
         near_ref[i] = jnp.where(even, ahead, behind)
-
-
-def peers_z(ref):
-    return ref.shape[0] // 2
-
-
-def spread(slots, owned, place, speeds, shards, cells, weights, populations, solid):
+        for x in range(rows // size_y):
+            up = relaxed[going(1, 1)[i]][size_y * x + size_y - 1 : size_y * x + size_y, :]
+            down = relaxed[going(1, -1)[i]][size_y * x : size_y * x + 1, :]
+            at = rows // size_y * i + x
+            side_ref[at : at + 1, :] = jnp.where(place_ref[0] == 0, up, down)
+
+
+def spread(slots, owned, place, speeds, shards, early, cells, weights, populations, solid):
     mark = cells.shape[1]
     line_count, lanes = solid.shape
     smem = pl.BlockSpec(memory_space=pltpu.SMEM)
@@ -545,9 +591,10 @@
             full(populations.shape),
             full((5, 8, lanes)),
             full((5, 8, lanes)),
+            full((24, lanes)),
             full((3, owned, mark)),
         ),
-        in_specs=[smem] * 2 + [vmem] * len(shards) + [hbm] * 3 + [vmem],
+        in_specs=[smem] * 2 + [vmem] * (len(shards) + 3) + [hbm] * 3 + [vmem],
         scratch_shapes=[
             pltpu.VMEM(cells.shape, jnp.int32),
             pltpu.VMEM(weights.shape, jnp.float32),
@@ -559,7 +606,7 @@
         ],
         compiler_params=kernel_params(),
         name="spread",
-    )(place, speeds, *shards, cells, weights, populations, solid)
+    )(place, speeds, *shards, *early, cells, weights, populations, solid)
 
 
 def downwind(place_ref, relaxed_ref, far_ref, near_ref):
@@ -580,11 +627,56 @@
     return cells
 
 
-def pack_kernel(place_ref, relaxed_ref, far_ref, near_ref, send_ref):
+def sideways(cells, side_ref, edge):
+    def result(q, x, y_at):
+        step_x, step_y = (int(step) for step in velocity_table[q][:2])
+        size_y = y_at.shape[0]
+        size_x = side_ref.shape[0] // 6
+        if step_y == 0:
+            return cells(q, x)
+        source = x - step_x
+        at = size_x * going(1, step_y).index(q) + source
+        halo = side_ref[at : at + 1, :] if 0 <= source < size_x else edge(q)
+        turned = pltpu.roll(cells(q, x), step_y % size_y, 0)
+        return jnp.where(y_at == (0 if step_y == 1 else size_y - 1), halo, turned)
+
+    return result
+
+
+def corner_index(q):
+    step_y = int(velocity_table[q][1])
+    return [p for p in going(1, step_y) if int(velocity_table[p][0]) != 0].index(q)
+
+
+def pack_kernel(
+    place_ref, relaxed_ref, far_ref, near_ref, side_ref, corner_ref, first_ref, second_ref
+):
     size_y, lanes = far_ref.shape[1:]
     size_x = relaxed_ref.shape[1] // size_y
     cells = downwind(place_ref, relaxed_ref, far_ref, near_ref)
+    corner_ref[...] = jnp.zeros(corner_ref.shape, jnp.float32)
+    for ahead in going(1, 1):
+        step_x = int(velocity_table[ahead][0])
+        if step_x == 0:
+            continue
+        behind = opposite_table[ahead]
+        up = cells(ahead, 0 if step_x == 1 else size_x - 1)[size_y - 1 : size_y, :]
+        down = cells(behind, size_x - 1 if step_x == 1 else 0)[0:1, :]
+        at = corner_index(ahead)
+        from_behind = corner_index(behind)
+        lower = place_ref[0] == 0
+
+        @pl.when(lower)
+        def _(at=at, up=up):
+            corner_ref[at : at + 1, :] = up
+
+        @pl.when(jnp.logical_not(lower))
+        def _(at=from_behind, down=down):
+            corner_ref[at : at + 1, :] = down
+
+    y_at = lax.broadcasted_iota(jnp.int32, (size_y, lanes), 0)
     lane_at = lax.broadcasted_iota(jnp.int32, (size_y, lanes), 1)
+    level = sideways(cells, side_ref, None)
     packs = []
     for step in (1, -1):
         packed = jnp.zeros((size_y, lanes), jnp.float32)
@@ -592,76 +684,60 @@
             edge = lanes - 1 if step == 1 else 0
             for x in range(size_x):
                 at = 8 * x + i
-                moved = pltpu.roll(cells(q, x), (at - edge) % lanes, 1)
+                moved = pltpu.roll(level(q, x, y_at), (at - edge) % lanes, 1)
                 packed = jnp.where(lane_at == at, moved, packed)
         packs.append(packed)
-    y_index, z_index = (place_ref[0], place_ref[1])
-    count_z = peers_z(send_ref)
-    for peer in range(send_ref.shape[0]):
-        send_ref[peer, 0:8, :] = jnp.where(z_index < peer % count_z, packs[0], packs[1])
-    face = (1 - y_index) * count_z + z_index
-    for i in range(5):
-        for x in range(size_x):
-            up = cells(going(1, 1)[i], x)[size_y - 1 : size_y, :]
-            down = cells(going(1, -1)[i], x)[0:1, :]
-            at = size_x * i + x
-            send_ref[face, at : at + 1, :] = jnp.where(y_index == 0, up, down)
-
-
-def pack(count_z, place, relaxed, far, near):
-    lanes = relaxed.shape[2]
+    even = place_ref[1] % 2 == 0
+    first_ref[...] = jnp.where(even, packs[0], packs[1])
+    second_ref[...] = jnp.where(even, packs[1], packs[0])
+
+
+def pack(place, relaxed, far, near, side):
     smem = pl.BlockSpec(memory_space=pltpu.SMEM)
     vmem = pl.BlockSpec(memory_space=pltpu.VMEM)
+    edge = full(far.shape[1:])
     return pl.pallas_call(
         pack_kernel,
-        out_shape=full((2 * count_z, 24, lanes)),
-        in_specs=[smem] + [vmem] * 3,
+        out_shape=(edge, edge, edge),
+        in_specs=[smem] + [vmem] * 4,
         compiler_params=kernel_params(),
         name="pack",
-    )(place, relaxed, far, near)
+    )(place, relaxed, far, near, side)
 
 
 def stream_kernel(
-    place_ref, relaxed_ref, far_ref, near_ref, got_ref, out_any, out_ref, sems
+    count_z, place_ref, relaxed_ref, far_ref, near_ref, side_ref, corner_ref, first_ref,
+    second_ref, out_any, out_ref, sems,
 ):
     size_x, size_y, lanes = out_ref.shape[1:]
     shape = (size_y, lanes)
-    streamed = downwind(place_ref, relaxed_ref, far_ref, near_ref)
     y_at = lax.broadcasted_iota(jnp.int32, shape, 0)
     z_at = lax.broadcasted_iota(jnp.int32, shape, 1)
     y_index, z_index = (place_ref[0], place_ref[1])
-    count_z = peers_z(got_ref)
-    side = (1 - y_index) * count_z
-    here = y_index * count_z
-    z_from = {1: jnp.maximum(z_index - 1, 0), -1: jnp.minimum(z_index + 1, count_z - 1)}
-    level = {step: got_ref[here + z_from[step], 0:8, :] for step in (1, -1)}
-    across = {step: got_ref[side + z_from[step], 0:8, :] for step in (1, -1)}
+    streamed = sideways(
+        downwind(place_ref, relaxed_ref, far_ref, near_ref),
+        side_ref,
+        lambda q: corner_ref[corner_index(q) : corner_index(q) + 1, :],
+    )
+    even = z_index % 2 == 0
+    columns = {
+        -1: jnp.where(even, first_ref[...], second_ref[...]),
+        1: jnp.where(even, second_ref[...], first_ref[...]),
+    }
     on_side = y_at == jnp.where(y_index == 0, 0, size_y - 1)
     on_side = on_side | ((z_at == 0) & (z_index == 0))
     on_side = on_side | ((z_at == lanes - 1) & (z_index == count_z - 1))
     copies = []
     for q in range(19):
-        _, step_y, step_z = (int(step) for step in velocity_table[q])
-        y_edge = 0 if step_y == 1 else size_y - 1
+        step_z = int(velocity_table[q][2])
         z_edge = 0 if step_z == 1 else lanes - 1
-        column = level.get(step_z)
-        if step_z != 0 and step_y != 0:
-            column = jnp.where(
-                y_at == y_edge,
-                pltpu.roll(across[step_z], step_y % size_y, 0),
-                pltpu.roll(column, step_y % size_y, 0),
-            )
         for x in range(size_x):
-            cells = streamed(q, x)
-            if step_y != 0:
-                at = size_x * going(1, step_y).index(q) + x
-                halo = got_ref[side + z_index, at : at + 1, :]
-                cells = jnp.where(y_at == y_edge, halo, pltpu.roll(cells, step_y % size_y, 0))
+            cells = streamed(q, x, y_at)
             if step_z != 0:
                 at = 8 * x + going(2, step_z).index(q)
                 cells = jnp.where(
                     z_at == z_edge,
-                    pltpu.roll(column, (z_edge - at) % lanes, 1),
+                    pltpu.roll(columns[step_z], (z_edge - at) % lanes, 1),
                     pltpu.roll(cells, step_z % lanes, 1),
                 )
             out_ref[q, x] = jnp.where(on_side, far_field[q], cells)
@@ -671,21 +747,21 @@
         copy.wait()
 
 
-def stream(place, relaxed, far, near, got):
+def stream(count_z, place, relaxed, *halos):
     rows, lanes = relaxed.shape[1:]
-    size_y = far.shape[1]
+    size_y = halos[0].shape[1]
     smem = pl.BlockSpec(memory_space=pltpu.SMEM)
     vmem = pl.BlockSpec(memory_space=pltpu.VMEM)
     shape = (19, rows // size_y, size_y, lanes)
     return pl.pallas_call(
-        stream_kernel,
+        functools.partial(stream_kernel, count_z),
         out_shape=full(shape),
-        in_specs=[smem] + [vmem] * 4,
+        in_specs=[smem] + [vmem] * (1 + len(halos)),
         out_specs=pl.BlockSpec(memory_space=pltpu.HBM),
         scratch_shapes=[pltpu.VMEM(shape, jnp.float32), pltpu.SemaphoreType.DMA((19,))],
         compiler_params=kernel_params(),
         name="stream",
-    )(place, relaxed, far, near, got)
+    )(place, relaxed, *halos)
 
 
 def per_device(
@@ -722,18 +798,26 @@
     pops, cells, weights = inputs[:3]
     own = sample(place, *inputs)
     swap = [(0, 1), (1, 0)]
-    column = {0: own}
+
+    def across_x(entries, distance):
+        return lax.ppermute(entries, "gx", [(i, i ^ distance) for i in range(count_x)])
+
+    def across_y(entries):
+        return lax.ppermute(entries, "gy", swap)
+
+    shards = {0: own}
     for distance in reversed(range(1, count_x)):
-        column[distance] = lax.ppermute(own, "gx", [(i, i ^ distance) for i in range(count_x)])
-    shards = []
-    for distance in (0, 2, 3, 1):
-        shards += [column[distance], lax.ppermute(column[distance], "gy", swap)]
-    relaxed, far, near, marker_force = spread(
+        shards[distance] = across_x(own, distance)
+    beside = {distance: across_y(shards[distance]) for distance in (0, 1, 3, 2)}
+    last = beside.pop(2)
+    early = settle_early(slots, owned, [*shards.values(), *beside.values()])
+    relaxed, far, near, side, marker_force = spread(
         slots,
         owned,
         place,
         train_velocity,
-        shards,
+        [own, last],
+        early,
         cells,
         weights,
         pops,
@@ -746,9 +830,16 @@
         [(i, (i - 1) % count_x) for i in evens] + [((i - 1) % count_x, i) for i in evens],
     )
     near = lax.ppermute(near, "gx", [(i, i + 1) for i in evens] + [(i + 1, i) for i in evens])
-    sides = pack(count_z, place, relaxed, far, near)
-    sides = lax.all_to_all(sides, ("gy", "gz"), split_axis=0, concat_axis=0, tiled=True)
-    populations_next = stream(place, relaxed, far, near, sides)
+    side = across_y(side)
+    corner, up_first, down_first = pack(place, relaxed, far, near, side)
+    corner = across_y(corner)
+    inner = [(i, i + 1) for i in range(0, count_z - 1, 2)]
+    outer = [(i, i + 1) for i in range(1, count_z - 1, 2)]
+    up_first = lax.ppermute(up_first, "gz", inner + [(j, i) for i, j in inner])
+    down_first = lax.ppermute(down_first, "gz", outer + [(j, i) for i, j in outer])
+    populations_next = stream(
+        count_z, place, relaxed, far, near, side, corner, up_first, down_first
+    )
     marker_force = marker_force.transpose(1, 0, 2).reshape(1, 1, 1, owned, 3, mark)
     return (populations_next, marker_force)
 
@@ -765,7 +856,7 @@
         P("gx", "gy", "gz", None, None),
         P(),
     )
-    small = mesh.shape["gy"] == 2 and mesh.shape["gx"] == 4 and mesh.shape["gz"] > 1
+    small = mesh.shape["gy"] == 2 and mesh.shape["gx"] == 4 and mesh.shape["gz"] % 2 == 0
     return jax.shard_map(
         per_device if small else per_device_general,
         mesh=mesh,

time: 56.6 us -> 55.5 us (0.981); the launches traced: 55.7 us -> 55.3 us
  blocking collectives: 11.7 us -> 0 us
  starting transfers between devices: 10.7 us -> 20.5 us
  Pallas kernels: 19.6 us -> 20.3 us
  local copies, waits for them, and re-layouts: 0.01 us -> 0.69 us
    all_to_all x1 -> x0, blocking collectives: 11.7 us -> none  [per_device(): lax.all_to_all(sides, ('gy', 'gz'), split_axis=0, concat_axis=0, tiled=True)]
    ppermute x7 -> x11, starting transfers between devices: 8.63 us -> 18.5 us  [the longest x6 6.6 us: across_y(): return lax.ppermute(entries, 'gy', swap)]
    ppermute x7 -> x11, waiting for transfers between devices: 10.2 us -> 12.9 us  [the longest x3 7.74 us: across_x(): lax.ppermute(entries, 'gx', [(i, i ^ distance) for i in range(count_x)])]
    ppermute x1, waiting for transfers between devices: 2.45 us -> 0.01 us  [per_device(): lax.ppermute(far, 'gx', [(i, (i - 1) % count_x) for i in evens] + [((i -...]
    unnamed x4, local copies, waits for them, and re-layouts: 0.01 us -> 0.69 us
    pallas_call x2 -> x3, Pallas kernels: 2.12 us -> 2.65 us  [the longest x1 1.47 us: stream(): pl.pallas_call(functools.partial(stream_kernel, count_z), out_shape=full(...]
  transfers between devices with their start and end apart: 9 -> 13, of which waited for: 5 -> 6; matrix products, arithmetic and copies ran while one was open for 0% -> 0% of each run, Pallas kernels for 0% -> 1%
where the time goes in v3:
time: 55.5 us; the launch traced here: 55.3 us
  starting transfers between devices  20.5 us (37%)
  Pallas kernels  20.3 us (37%)
  waiting for transfers between devices  13 us (23%)
  between operations  0.72 us (1%)
  local copies, waits for them, and re-layouts  0.69 us (1%)
    pallas_call x1, Pallas kernels, spread(): pl.pallas_call(functools.partial(spread_kernel, len(shards), slots, owned...  10.4 us
    ppermute x3, waiting for transfers between devices, across_x(): lax.ppermute(entries, 'gx', [(i, i ^ distance) for i in range(count_x)])  7.74 us
    pallas_call x1, Pallas kernels, sample(): pl.pallas_call(sample_kernel, out_shape=full((shard_rows(owner.shape[1],...  7.19 us
    ppermute x6, starting transfers between devices, across_y(): return lax.ppermute(entries, 'gy', swap)  6.6 us
    ppermute x3, starting transfers between devices, across_x(): lax.ppermute(entries, 'gx', [(i, i ^ distance) for i in range(count_x)])  4.5 us
    ppermute x1, starting transfers between devices, per_device(): up_first = lax.ppermute(up_first, 'gz', inner + [(j, i) for i, j in inner])  4.37 us
    ppermute x6, waiting for transfers between devices, across_y(): return lax.ppermute(entries, 'gy', swap)  3.28 us
    ppermute x1, starting transfers between devices, per_device(): lax.ppermute(down_first, 'gz', outer + [(j, i) for i, j in outer])  3.02 us
  transfers between devices with their start and end apart: 13, of which 6 were waited for; matrix products, arithmetic and copies ran while one was open for 0% of the time, Pallas kernels for 1%

profile of v3, /device:TPU:1, one launch (start us, length us, event | category | flops | bytes accessed | tf_op | source)
XLA Modules:
  0.0 55.3 jit_solution(1739071326971989602)
XLA Ops:
  0.6 0.1 pad_add_fusion.place_ref
  0.7 7.2 %sample.1.refs_0_ = f32[232,128]{1,0:T(8,128)S(1)} custom-call(s32[4]{0:T(128)S(1)} %pad_add_fusion.place_ref, f32[19,32,128]{2,1,0:T(8,128)} %bitcast.16, s32[512,128]{1,0:T(8,128)} %bitcast.18, f32[512,128]{1,0:T(8,128)} %bitcast.20, f32[32,128]{1,0:T(8,128)} %bitcast.22, s32[1,64]{1,0:T(1,128)} %bitcast.23, s32[1,64]{1,0:T(1,128)} %bitcast.24, ...), custom_call_target="tpu_custom_call" | custom-call | tf_op jit(solution)/shard_map/sample/pallas_call | solution.py:386
  7.9 2.2 %collective-permute-start.3 = (f32[232,128]{1,0:T(8,128)S(1)}, f32[232,128]{1,0:T(8,128)S(1)}, u32[]{:S(2)}, u32[]{:S(2)}) collective-permute-start(f32[232,128]{1,0:T(8,128)S(1)} %sample.1.refs_0_), channel_id=1, source_target_pairs={{0,8},{8,0},{16,24},{24,16},{1,9},{9,1},{17,25},{25,17},{2,10},{10... | collective-permute-start | bytes 356360 | tf_op jit(solution)/shard_map/ppermute | solution.py:803
  10.1 2.2 %collective-permute-start.2 = (f32[232,128]{1,0:T(8,128)S(1)}, f32[232,128]{1,0:T(8,128)S(1)}, u32[]{:S(2)}, u32[]{:S(2)}) collective-permute-start(f32[232,128]{1,0:T(8,128)S(1)} %sample.1.refs_0_), channel_id=1, source_target_pairs={{0,24},{8,16},{16,8},{24,0},{1,25},{9,17},{17,9},{25,1},{2,26},{10... | collective-permute-start | bytes 356360 | tf_op jit(solution)/shard_map/ppermute | solution.py:803
  12.3 0.1 collective-permute-start
  12.4 1.2 %collective-permute-start.4 = (f32[232,128]{1,0:T(8,128)S(1)}, f32[232,128]{1,0:T(8,128)S(1)}, u32[]{:S(2)}, u32[]{:S(2)}) collective-permute-start(f32[232,128]{1,0:T(8,128)S(1)} %sample.1.refs_0_), channel_id=1, source_target_pairs={{0,4},{4,0},{1,5},{5,1},{2,6},{6,2},{3,7},{7,3},{8,12},{12,8},{9,1... | collective-permute-start | bytes 356360 | tf_op jit(solution)/shard_map/ppermute | solution.py:806
  13.6 0.0 collective-permute-done.3.refs_3_
  13.6 0.5 collective-permute-start.5
  14.1 3.4 %collective-permute-done.2.refs_1_ = f32[232,128]{1,0:T(8,128)S(1)} collective-permute-done((f32[232,128]{1,0:T(8,128)S(1)}, f32[232,128]{1,0:T(8,128)S(1)}, u32[]{:S(2)}, u32[]{:S(2)}) %collective-permute-start.2) | collective-permute-done | bytes 118816 | tf_op jit(solution)/shard_map/ppermute | solution.py:803
  17.5 1.2 %collective-permute-start.6 = (f32[232,128]{1,0:T(8,128)S(1)}, f32[232,128]{1,0:T(8,128)S(1)}, u32[]{:S(2)}, u32[]{:S(2)}) collective-permute-start(f32[232,128]{1,0:T(8,128)S(1)} %collective-permute-done.2.refs_1_), channel_id=1, source_target_pairs={{0,4},{4,0},{1,5},{5,1},{2,6},{6,2},{3,7},{7,3},{8,12},{12,8},{9,1... | collective-permute-start | bytes 356360 | tf_op jit(solution)/shard_map/ppermute | solution.py:806
  18.7 4.4 %collective-permute-done.refs_2_ = f32[232,128]{1,0:T(8,128)S(1)} collective-permute-done((f32[232,128]{1,0:T(8,128)S(1)}, f32[232,128]{1,0:T(8,128)S(1)}, u32[]{:S(2)}, u32[]{:S(2)}) %collective-permute-start) | collective-permute-done | bytes 118816 | tf_op jit(solution)/shard_map/ppermute | solution.py:803
  23.1 1.2 %collective-permute-start.1 = (f32[232,128]{1,0:T(8,128)S(1)}, f32[232,128]{1,0:T(8,128)S(1)}, u32[]{:S(2)}, u32[]{:S(2)}) collective-permute-start(f32[232,128]{1,0:T(8,128)S(1)} %collective-permute-done.refs_2_), channel_id=1, source_target_pairs={{0,4},{4,0},{1,5},{5,1},{2,6},{6,2},{3,7},{7,3},{8,12},{12,8},{9,1... | collective-permute-start | bytes 356360 | tf_op jit(solution)/shard_map/ppermute | solution.py:806
  24.3 0.0 collective-permute-done.4.refs_4_
  24.3 0.0 collective-permute-done.5.refs_5_
  24.3 0.0 collective-permute-done.6.refs_6_
  24.3 0.0 copy-start
  24.3 0.5 settle.1
  24.8 1.9 %collective-permute-done.1.refs_1_ = f32[232,128]{1,0:T(8,128)S(1)} collective-permute-done((f32[232,128]{1,0:T(8,128)S(1)}, f32[232,128]{1,0:T(8,128)S(1)}, u32[]{:S(2)}, u32[]{:S(2)}) %collective-permute-start.1) | collective-permute-done | bytes 118816 | tf_op jit(solution)/shard_map/ppermute | solution.py:806
  26.8 0.0 copy-start.1
  26.8 0.0 copy-done
  26.8 0.7 %copy-done.1 = f32[4,3]{1,0:T(4,128)S(1)} copy-done((f32[4,3]{1,0:T(4,128)S(1)}, f32[4,3]{1,0:T(4,128)}, u32[]{:S(2)}) %copy-start.1) | copy-done | bytes 72
  27.4 10.4 %spread.1 = (f32[19,32,128]{2,1,0:T(8,128)S(1)}, f32[5,8,128]{2,1,0:T(8,128)S(1)}, f32[5,8,128]{2,1,0:T(8,128)S(1)}, f32[24,128]{1,0:T(8,128)S(1)}, f32[3,32,128]{2,1,0:T(8,128)}) custom-call(s32[4]{0:T(128)S(1)} %pad_add_fusion.place_ref, f32[4,3]{1,0:T(4,128)S(1)} %copy-done.1, f32[232,128]{1,0:T(8,128)S(1)} %sample.1.refs_0_, ...), custom_call_target="tpu_custom_call" | custom-call | tf_op jit(solution)/shard_map/spread/pallas_call | solution.py:588
  37.9 2.0 %collective-permute-start.7 = (f32[5,8,128]{2,1,0:T(8,128)S(1)}, f32[5,8,128]{2,1,0:T(8,128)S(1)}, u32[]{:S(2)}, u32[]{:S(2)}) collective-permute-start(f32[5,8,128]{2,1,0:T(8,128)S(1)} %get-tuple-element.17), channel_id=1, source_target_pairs={{0,24},{16,8},{24,0},{8,16},{1,25},{17,9},{25,1},{9,17},{2,26},{18... | collective-permute-start | bytes 61448 | tf_op jit(solution)/shard_map/ppermute | solution.py:827
  39.9 0.0 collective-permute-start.8
  39.9 1.2 %collective-permute-start.9 = (f32[24,128]{1,0:T(8,128)S(1)}, f32[24,128]{1,0:T(8,128)S(1)}, u32[]{:S(2)}, u32[]{:S(2)}) collective-permute-start(f32[24,128]{1,0:T(8,128)S(1)} %get-tuple-element.19), channel_id=1, source_target_pairs={{0,4},{4,0},{1,5},{5,1},{2,6},{6,2},{3,7},{7,3},{8,12},{12,8},{9,1... | collective-permute-start | bytes 36872 | tf_op jit(solution)/shard_map/ppermute | solution.py:806
  41.1 1.3 %collective-permute-done.9.side_ref = f32[24,128]{1,0:T(8,128)S(1)} collective-permute-done((f32[24,128]{1,0:T(8,128)S(1)}, f32[24,128]{1,0:T(8,128)S(1)}, u32[]{:S(2)}, u32[]{:S(2)}) %collective-permute-start.9) | collective-permute-done | bytes 12320 | tf_op jit(solution)/shard_map/ppermute | solution.py:806
  42.5 0.0 collective-permute-done.7.far_ref
  42.5 0.1 collective-permute-done.8.near_ref
  42.6 0.7 %pack.1 = (f32[8,128]{1,0:T(8,128)S(1)}, f32[8,128]{1,0:T(8,128)S(1)}, f32[8,128]{1,0:T(8,128)S(1)}) custom-call(s32[4]{0:T(128)S(1)} %pad_add_fusion.place_ref, f32[19,32,128]{2,1,0:T(8,128)S(1)} %get-tuple-element.16.relaxed_ref, f32[5,8,128]{2,1,0:T(8,128)S(1)} %collective-permute-done.7.far_ref, f32[5,8,128]{2,1,0:T(8,128)S(1)} %collective-permute-done.8.near_ref, ...), custom_call_target="tpu_custom_call" | custom-call | tf_op jit(solution)/shard_map/pack/pallas_call | solution.py:699
  43.3 1.3 %collective-permute-start.10 = (f32[8,128]{1,0:T(8,128)S(1)}, f32[8,128]{1,0:T(8,128)S(1)}, u32[]{:S(2)}, u32[]{:S(2)}) collective-permute-start(f32[8,128]{1,0:T(8,128)S(1)} %get-tuple-element.20), channel_id=1, source_target_pairs={{0,4},{4,0},{1,5},{5,1},{2,6},{6,2},{3,7},{7,3},{8,12},{12,8},{9,1... | collective-permute-start | bytes 12296 | tf_op jit(solution)/shard_map/ppermute | solution.py:806
  44.6 4.4 %collective-permute-start.11 = (f32[8,128]{1,0:T(8,128)S(1)}, f32[8,128]{1,0:T(8,128)S(1)}, u32[]{:S(2)}, u32[]{:S(2)}) collective-permute-start(f32[8,128]{1,0:T(8,128)S(1)} %get-tuple-element.21), channel_id=1, source_target_pairs={{0,1},{2,3},{1,0},{3,2},{4,5},{6,7},{5,4},{7,6},{8,9},{10,11},{9,8... | collective-permute-start | bytes 12296 | tf_op jit(solution)/shard_map/ppermute | solution.py:838
  48.9 3.0 %collective-permute-start.12 = (f32[8,128]{1,0:T(8,128)S(1)}, f32[8,128]{1,0:T(8,128)S(1)}, u32[]{:S(2)}, u32[]{:S(2)}) collective-permute-start(f32[8,128]{1,0:T(8,128)S(1)} %get-tuple-element.22), channel_id=1, source_target_pairs={{1,2},{2,1},{5,6},{6,5},{9,10},{10,9},{13,14},{14,13},{17,18},{18,... | collective-permute-start | bytes 12296 | tf_op jit(solution)/shard_map/ppermute | solution.py:839
  52.0 0.0 collective-permute-done.10.corner_ref
  52.0 0.0 collective-permute-done.11.first_ref
  52.0 1.9 %collective-permute-done.12.second_ref = f32[8,128]{1,0:T(8,128)S(1)} collective-permute-done((f32[8,128]{1,0:T(8,128)S(1)}, f32[8,128]{1,0:T(8,128)S(1)}, u32[]{:S(2)}, u32[]{:S(2)}) %collective-permute-start.12) | collective-permute-done | bytes 4128 | tf_op jit(solution)/shard_map/ppermute | solution.py:839
  53.8 1.5 %stream.1 = f32[19,4,8,128]{3,2,1,0:T(8,128)} custom-call(s32[4]{0:T(128)S(1)} %pad_add_fusion.place_ref, f32[19,32,128]{2,1,0:T(8,128)S(1)} %get-tuple-element.16.relaxed_ref, f32[5,8,128]{2,1,0:T(8,128)S(1)} %collective-permute-done.7.far_ref, f32[5,8,128]{2,1,0:T(8,128)S(1)} %collective-permute-done.8.near_ref, ...), custom_call_target="tpu_custom_call" | custom-call | tf_op jit(solution)/shard_map/stream/pallas_call | solution.py:756
Async XLA Ops:
  7.9 5.7 %collective-permute-start.3 = (f32[232,128]{1,0:T(8,128)S(1)}, f32[232,128]{1,0:T(8,128)S(1)}, u32[]{:S(2)}, u32[]{:S(2)}) collective-permute-start(f32[232,128]{1,0:T(8,128)S(1)} %sample.1.refs_0_), channel_id=1, source_target_pairs={{0,8},{8,0},{16,24},{24,16},{1,9},{9,1},{17,25},{25,17},{2,10},{10... | collective-permute-start | bytes 356360 | tf_op jit(solution)/shard_map/ppermute | solution.py:803
  10.1 7.4 %collective-permute-start.2 = (f32[232,128]{1,0:T(8,128)S(1)}, f32[232,128]{1,0:T(8,128)S(1)}, u32[]{:S(2)}, u32[]{:S(2)}) collective-permute-start(f32[232,128]{1,0:T(8,128)S(1)} %sample.1.refs_0_), channel_id=1, source_target_pairs={{0,24},{8,16},{16,8},{24,0},{1,25},{9,17},{17,9},{25,1},{2,26},{10... | collective-permute-start | bytes 356360 | tf_op jit(solution)/shard_map/ppermute | solution.py:803
  12.3 10.8 %collective-permute-start = (f32[232,128]{1,0:T(8,128)S(1)}, f32[232,128]{1,0:T(8,128)S(1)}, u32[]{:S(2)}, u32[]{:S(2)}) collective-permute-start(f32[232,128]{1,0:T(8,128)S(1)} %sample.1.refs_0_), channel_id=1, source_target_pairs={{0,16},{8,24},{16,0},{24,8},{1,17},{9,25},{17,1},{25,9},{2,18},{10... | collective-permute-start | bytes 356360 | tf_op jit(solution)/shard_map/ppermute | solution.py:803
  12.4 11.9 %collective-permute-start.4 = (f32[232,128]{1,0:T(8,128)S(1)}, f32[232,128]{1,0:T(8,128)S(1)}, u32[]{:S(2)}, u32[]{:S(2)}) collective-permute-start(f32[232,128]{1,0:T(8,128)S(1)} %sample.1.refs_0_), channel_id=1, source_target_pairs={{0,4},{4,0},{1,5},{5,1},{2,6},{6,2},{3,7},{7,3},{8,12},{12,8},{9,1... | collective-permute-start | bytes 356360 | tf_op jit(solution)/shard_map/ppermute | solution.py:806
  13.6 10.7 %collective-permute-start.5 = (f32[232,128]{1,0:T(8,128)S(1)}, f32[232,128]{1,0:T(8,128)S(1)}, u32[]{:S(2)}, u32[]{:S(2)}) collective-permute-start(f32[232,128]{1,0:T(8,128)S(1)} %collective-permute-done.3.refs_3_), channel_id=1, source_target_pairs={{0,4},{4,0},{1,5},{5,1},{2,6},{6,2},{3,7},{7,3},{8,12},{12,8},{9,1... | collective-permute-start | bytes 356360 | tf_op jit(solution)/shard_map/ppermute | solution.py:806
  17.5 6.8 %collective-permute-start.6 = (f32[232,128]{1,0:T(8,128)S(1)}, f32[232,128]{1,0:T(8,128)S(1)}, u32[]{:S(2)}, u32[]{:S(2)}) collective-permute-start(f32[232,128]{1,0:T(8,128)S(1)} %collective-permute-done.2.refs_1_), channel_id=1, source_target_pairs={{0,4},{4,0},{1,5},{5,1},{2,6},{6,2},{3,7},{7,3},{8,12},{12,8},{9,1... | collective-permute-start | bytes 356360 | tf_op jit(solution)/shard_map/ppermute | solution.py:806
  23.1 3.7 %collective-permute-start.1 = (f32[232,128]{1,0:T(8,128)S(1)}, f32[232,128]{1,0:T(8,128)S(1)}, u32[]{:S(2)}, u32[]{:S(2)}) collective-permute-start(f32[232,128]{1,0:T(8,128)S(1)} %collective-permute-done.refs_2_), channel_id=1, source_target_pairs={{0,4},{4,0},{1,5},{5,1},{2,6},{6,2},{3,7},{7,3},{8,12},{12,8},{9,1... | collective-permute-start | bytes 356360 | tf_op jit(solution)/shard_map/ppermute | solution.py:806
  24.3 2.5 %copy-start = (s32[4,8,128]{2,1,0:T(8,128)S(1)}, s32[4,8,128]{2,1,0:T(8,128)}, u32[]{:S(2)}) copy-start(s32[4,8,128]{2,1,0:T(8,128)} %param.10) | copy-start | bytes 49156
  26.8 0.7 %copy-start.1 = (f32[4,3]{1,0:T(4,128)S(1)}, f32[4,3]{1,0:T(4,128)}, u32[]{:S(2)}) copy-start(f32[4,3]{1,0:T(4,128)} %speeds_ref.1) | copy-start | bytes 148
  37.9 4.6 %collective-permute-start.7 = (f32[5,8,128]{2,1,0:T(8,128)S(1)}, f32[5,8,128]{2,1,0:T(8,128)S(1)}, u32[]{:S(2)}, u32[]{:S(2)}) collective-permute-start(f32[5,8,128]{2,1,0:T(8,128)S(1)} %get-tuple-element.17), channel_id=1, source_target_pairs={{0,24},{16,8},{24,0},{8,16},{1,25},{17,9},{25,1},{9,17},{2,26},{18... | collective-permute-start | bytes 61448 | tf_op jit(solution)/shard_map/ppermute | solution.py:827
  39.9 2.7 %collective-permute-start.8 = (f32[5,8,128]{2,1,0:T(8,128)S(1)}, f32[5,8,128]{2,1,0:T(8,128)S(1)}, u32[]{:S(2)}, u32[]{:S(2)}) collective-permute-start(f32[5,8,128]{2,1,0:T(8,128)S(1)} %get-tuple-element.18), channel_id=1, source_target_pairs={{0,8},{16,24},{8,0},{24,16},{1,9},{17,25},{9,1},{25,17},{2,10},{18... | collective-permute-start | bytes 61448 | tf_op jit(solution)/shard_map/ppermute | solution.py:832
  39.9 2.5 %collective-permute-start.9 = (f32[24,128]{1,0:T(8,128)S(1)}, f32[24,128]{1,0:T(8,128)S(1)}, u32[]{:S(2)}, u32[]{:S(2)}) collective-permute-start(f32[24,128]{1,0:T(8,128)S(1)} %get-tuple-element.19), channel_id=1, source_target_pairs={{0,4},{4,0},{1,5},{5,1},{2,6},{6,2},{3,7},{7,3},{8,12},{12,8},{9,1... | collective-permute-start | bytes 36872 | tf_op jit(solution)/shard_map/ppermute | solution.py:806
  43.3 8.7 %collective-permute-start.10 = (f32[8,128]{1,0:T(8,128)S(1)}, f32[8,128]{1,0:T(8,128)S(1)}, u32[]{:S(2)}, u32[]{:S(2)}) collective-permute-start(f32[8,128]{1,0:T(8,128)S(1)} %get-tuple-element.20), channel_id=1, source_target_pairs={{0,4},{4,0},{1,5},{5,1},{2,6},{6,2},{3,7},{7,3},{8,12},{12,8},{9,1... | collective-permute-start | bytes 12296 | tf_op jit(solution)/shard_map/ppermute | solution.py:806
  44.6 7.4 %collective-permute-start.11 = (f32[8,128]{1,0:T(8,128)S(1)}, f32[8,128]{1,0:T(8,128)S(1)}, u32[]{:S(2)}, u32[]{:S(2)}) collective-permute-start(f32[8,128]{1,0:T(8,128)S(1)} %get-tuple-element.21), channel_id=1, source_target_pairs={{0,1},{2,3},{1,0},{3,2},{4,5},{6,7},{5,4},{7,6},{8,9},{10,11},{9,8... | collective-permute-start | bytes 12296 | tf_op jit(solution)/shard_map/ppermute | solution.py:838
  48.9 4.9 %collective-permute-start.12 = (f32[8,128]{1,0:T(8,128)S(1)}, f32[8,128]{1,0:T(8,128)S(1)}, u32[]{:S(2)}, u32[]{:S(2)}) collective-permute-start(f32[8,128]{1,0:T(8,128)S(1)} %get-tuple-element.22), channel_id=1, source_target_pairs={{1,2},{2,1},{5,6},{6,5},{9,10},{10,9},{13,14},{14,13},{17,18},{18,... | collective-permute-start | bytes 12296 | tf_op jit(solution)/shard_map/ppermute | solution.py:839

commit v4 on v3

--- a/solution.py
+++ b/solution.py
@@ -38,7 +38,7 @@
 regular_eps = 0.0001
 stiffness = 2.0
 far_velocity = (0.02, 0.06, 0.0)
-vmem_bytes = 40 << 20
+vmem_bytes = 16 << 20
 group = 8
 
 
@@ -293,7 +293,7 @@
 def sample_kernel(
     place_ref, pop_any, cells_any, weights_any, areas_any, owner_any, block_any, trains_any,
     out_ref, pop_ref, cells_ref, weights_ref, areas_ref, owner_ref, block_ref, trains_ref,
-    table, sems, group_sems,
+    table, sems,
 ):
     rows, lanes = (pop_ref.shape[1], pop_ref.shape[2])
     mark = cells_ref.shape[1]
@@ -303,6 +303,8 @@
     copies = fetch(
         (
             (pop_any, pop_ref),
+            (cells_any, cells_ref),
+            (weights_any, weights_ref),
             (areas_any, areas_ref),
             (owner_any, owner_ref),
             (block_any, block_ref),
@@ -311,26 +313,15 @@
         sems,
     )
 
-    def group_copies(step):
-        here = pl.ds(pl.multiple_of(step * group * kernel, group * kernel), group * kernel)
-        return (
-            pltpu.make_async_copy(cells_any.at[here], cells_ref.at[here], group_sems.at[0, step]),
-            pltpu.make_async_copy(
-                weights_any.at[here], weights_ref.at[here], group_sems.at[1, step]
-            ),
-        )
-
-    for step in range(slots // group):
-        for copy in group_copies(step):
-            copy.start()
     copies[0].wait()
     density, momentum = moments([pop_ref[q] for q in range(19)])
-    fixed = [
-        ((momentum[c] / density) * float(2**bits) + (2.0 ** (bits - 1) + 0.5)).astype(jnp.int32)
-        for c, bits in enumerate((21, 21, 22))
-    ]
-    table[0] = (fixed[0] << 11) | (fixed[2] >> 11)
-    table[1] = (fixed[1] << 11) | (fixed[2] & 2047)
+    speed = [momentum[c] / density for c in range(3)]
+    largest = jnp.maximum(jnp.maximum(jnp.abs(speed[0]), jnp.abs(speed[1])), jnp.abs(speed[2]))
+    largest = jnp.max(largest, axis=(0, 1), keepdims=True) + 1e-20
+    scale = largest * (1.0 / 32767.0)
+    fixed = [(speed[c] * (1.0 / scale) + 32768.5).astype(jnp.int32) for c in range(3)]
+    table[0:rows] = (fixed[0] << 16) | fixed[1]
+    table[rows:] = (fixed[2][: rows // 2] << 16) | fixed[2][rows // 2 :]
     for copy in copies[1:]:
         copy.wait()
     meta = 3 * slots + owned
@@ -343,8 +334,6 @@
     out_ref[meta + 2 : meta + 3, :] = mine.astype(jnp.float32)
 
     def body(step, carry):
-        for copy in group_copies(step):
-            copy.wait()
         first = pl.multiple_of(step * group, group)
         total = [jnp.zeros((group, mark), jnp.float32) for c in range(3)]
         for k in range(kernel):
@@ -354,51 +343,83 @@
             row = cells >> (lanes.bit_length() - 1)
             bits = [(row >> bit) & 1 == 1 for bit in range(rows.bit_length() - 1)]
 
-            def choose(c, low, level):
+            def choose(low, level):
                 if level < 0:
-                    line = jnp.broadcast_to(table[c, low : low + 1, :], (group, lanes))
+                    line = jnp.broadcast_to(table[low : low + 1, :], (group, lanes))
                     return jnp.take_along_axis(line, lane, axis=1, mode="promise_in_bounds")
-                lower = choose(c, low, level - 1)
-                return jnp.where(bits[level], choose(c, low + (1 << level), level - 1), lower)
-
-            words = [choose(c, 0, len(bits) - 1) for c in range(2)]
-            last = ((words[0] & 2047) << 11) | (words[1] & 2047)
+                lower = choose(low, level - 1)
+                return jnp.where(bits[level], choose(low + (1 << level), level - 1), lower)
+
+            pair = choose(0, len(bits) - 1)
+            third = choose(rows, len(bits) - 2)
             picked = [
-                lax.shift_right_logical(words[0], 11),
-                lax.shift_right_logical(words[1], 11),
-                last,
+                lax.shift_right_logical(pair, 16),
+                pair & 65535,
+                jnp.where(bits[-1], third & 65535, lax.shift_right_logical(third, 16)),
             ]
             weight = weights_ref[at, :]
-            for c, width in enumerate((21, 21, 22)):
-                value = (picked[c].astype(jnp.float32) - 2.0 ** (width - 1)) * 2.0**-width
-                total[c] = total[c] + weight * value
+            for c in range(3):
+                total[c] = total[c] + weight * (picked[c].astype(jnp.float32) - 32768.0)
         for c in range(3):
-            out_ref[pl.ds(pl.multiple_of(c * slots + first, group), group), :] = total[c]
+            here = pl.ds(pl.multiple_of(c * slots + first, group), group)
+            out_ref[here, :] = total[c] * scale
         return carry
 
-    lax.fori_loop(0, slots // group, body, 0, unroll=2)
+    lax.fori_loop(0, slots // group, body, 0)
 
 
 def sample(place, populations, cells, weights, areas, owner, block, trains):
     smem = pl.BlockSpec(memory_space=pltpu.SMEM)
     hbm = pl.BlockSpec(memory_space=pltpu.HBM)
     vmem = pl.BlockSpec(memory_space=pltpu.VMEM)
+    kept = (populations, cells, weights)
     return pl.pallas_call(
         sample_kernel,
-        out_shape=full((shard_rows(owner.shape[1], areas.shape[0]), cells.shape[1])),
+        out_shape=[full((shard_rows(owner.shape[1], areas.shape[0]), cells.shape[1]))]
+        + [jax.ShapeDtypeStruct(entries.shape, entries.dtype) for entries in kept],
         in_specs=[smem] + [hbm] * 7,
+        out_specs=[vmem] * 4,
         scratch_shapes=[
-            pltpu.VMEM(entries.shape, entries.dtype)
-            for entries in (populations, cells, weights, areas, owner, block, trains)
+            pltpu.VMEM(entries.shape, entries.dtype) for entries in (areas, owner, block, trains)
         ]
         + [
-            pltpu.VMEM((2,) + populations.shape[1:], jnp.int32),
-            pltpu.SemaphoreType.DMA((5,)),
-            pltpu.SemaphoreType.DMA((2, owner.shape[1] // group)),
+            pltpu.VMEM((populations.shape[1] * 3 // 2, cells.shape[1]), jnp.int32),
+            pltpu.SemaphoreType.DMA((7,)),
         ],
         compiler_params=kernel_params(),
         name="sample",
     )(place, populations, cells, weights, areas, owner, block, trains)
+
+
+def prepare_kernel(cells_ref, out_ref):
+    chunk, mark = (128, cells_ref.shape[1])
+    z_at = lax.broadcasted_iota(jnp.int32, (mark, mark), 1).astype(jnp.float32)
+
+    def body(step, carry):
+        here = pl.ds(pl.multiple_of(step * chunk, chunk), chunk)
+        lane = (cells_ref[here, :] & (mark - 1)).astype(jnp.float32).T
+        for j in range(chunk):
+            there = pl.ds(pl.multiple_of((step * chunk + j) * mark, mark), mark)
+            out_ref[there, :] = one_hot(lane[:, j : j + 1] == z_at)
+        return carry
+
+    lax.fori_loop(0, cells_ref.shape[0] // chunk, body, 0)
+
+
+def prepare(cells):
+    count, mark = cells.shape
+    vmem = pl.BlockSpec(memory_space=pltpu.VMEM)
+    return pl.pallas_call(
+        prepare_kernel,
+        out_shape=jax.ShapeDtypeStruct((count * mark, mark), jnp.bfloat16),
+        in_specs=[vmem],
+        out_specs=vmem,
+        compiler_params=kernel_params(),
+        cost_estimate=pl.CostEstimate(
+            flops=4 * 10**9, bytes_accessed=count * mark * 4, transcendentals=0
+        ),
+        name="prepare",
+    )(cells)
 
 
 def three_parts(values):
@@ -443,39 +464,50 @@
     return totals
 
 
-def settle_kernel(slots, owned, *refs):
-    shards, (sums_ref, area_ref, trains_ref) = (refs[:-3], refs[-3:])
+def settle_kernel(slots, owned, speeds_ref, *refs):
+    shards, (sums_ref, area_ref, trains_ref, rows_ref) = (refs[:-4], refs[-4:])
+    mark = rows_ref.shape[1]
+    for train in range(speeds_ref.shape[0]):
+        for c in range(3):
+            at = 3 * train + c
+            rows_ref[at : at + 1, :] = jnp.full((1, mark), speeds_ref[train, c], jnp.float32)
     ids, mine, _ = wanted_labels(shards[0], slots, owned)
     sums_ref[...], area_ref[...], trains_ref[...] = add_shards(None, shards, ids, mine)
 
 
-def settle_early(slots, owned, shards):
+def settle_early(slots, owned, speeds, shards):
     mark = shards[0].shape[1]
+    smem = pl.BlockSpec(memory_space=pltpu.SMEM)
     vmem = pl.BlockSpec(memory_space=pltpu.VMEM)
     return pl.pallas_call(
         functools.partial(settle_kernel, slots, owned),
-        out_shape=(full((slots + owned, 3 * mark)), full((slots, mark)), full((slots, mark))),
-        in_specs=[vmem] * len(shards),
+        out_shape=(
+            full((slots + owned, 3 * mark)),
+            full((slots, mark)),
+            full((slots, mark)),
+            full((3 * speeds.shape[0], mark)),
+        ),
+        in_specs=[smem] + [vmem] * len(shards),
         compiler_params=kernel_params(),
         cost_estimate=pl.CostEstimate(
             flops=10**9, bytes_accessed=len(shards) * shards[0].size * 4, transcendentals=0
         ),
         name="settle",
-    )(*shards)
-
-
-def block_forces(speeds_ref, totals, own_ref, slots, owned):
+    )(speeds, *shards)
+
+
+def block_forces(rows_ref, totals, own_ref, slots, owned):
     mark = own_ref.shape[1]
     ids, mine, own_trains = wanted_labels(own_ref, slots, owned)
     sums, area, trains = totals
-    trains = jnp.sum(trains, axis=1, keepdims=True)
+    trains = jnp.broadcast_to(jnp.sum(trains, axis=1, keepdims=True), area.shape)
     own_area = own_ref[3 * slots : 3 * slots + owned, :]
     forces, own_forces = ([], [])
     for c in range(3):
-        target = jnp.zeros(trains.shape, jnp.float32)
-        own_target = jnp.zeros(own_trains.shape, jnp.float32)
-        for train in range(speeds_ref.shape[0]):
-            speed = speeds_ref[train, c]
+        target, own_target = (jnp.zeros_like(area), jnp.zeros_like(own_area))
+        for train in range(rows_ref.shape[0] // 3):
+            at = 3 * train + c
+            speed = rows_ref[at : at + 1, :]
             target = jnp.where(trains == float(train), speed, target)
             own_target = jnp.where(own_trains == float(train), speed, own_target)
         got = sums[:, c * mark : (c + 1) * mark]
@@ -484,23 +516,20 @@
     return (forces, own_forces)
 
 
-def spread_kernel(shard_count, slots, owned, place_ref, speeds_ref, *refs):
-    shards, refs = (refs[:shard_count], refs[shard_count:])
-    sums_ref, area_ref, trains_ref, cells_any, weights_any, pop_any, solid_ref = refs[:7]
-    relaxed_ref, far_ref, near_ref, side_ref, marker_ref = refs[7:12]
-    cells_ref, weights_ref, pop_ref, force_ref, lines_ref, acc, sems = refs[12:]
+def spread_kernel(
+    slots, owned, place_ref, own_ref, last_ref, sums_ref, area_ref, trains_ref, speeds_ref,
+    cells_ref, weights_ref, pop_ref, lanes_ref, solid_ref,
+    relaxed_ref, far_ref, near_ref, side_ref, marker_ref, force_ref, lines_ref, acc,
+):
     rows, lanes = (pop_ref.shape[1], pop_ref.shape[2])
     size_y = 8
     mark = cells_ref.shape[1]
     kernel = cells_ref.shape[0] // slots
+    points = kernel * mark
     bf = jnp.bfloat16
-    copies = fetch(
-        ((cells_any, cells_ref), (weights_any, weights_ref), (pop_any, pop_ref)), sems
-    )
-    own_ref = shards[0]
     ids, mine, _ = wanted_labels(own_ref, slots, owned)
     totals = (sums_ref[...], area_ref[...], trains_ref[...])
-    totals = add_shards(totals, shards[1:], ids, mine)
+    totals = add_shards(totals, [last_ref], ids, mine)
     forces, own_forces = block_forces(speeds_ref, totals, own_ref, slots, owned)
     for c in range(3):
         force_ref[c] = forces[c]
@@ -508,57 +537,45 @@
 
     acc[...] = jnp.zeros_like(acc)
     iota = lax.broadcasted_iota(jnp.int32, (16, mark), 0).astype(jnp.float32)
-    steps = [(iota + 16.0 * j).astype(bf) for j in range(max(rows, lanes) // 16)]
-    one, zero = (jnp.ones((16, mark), bf), jnp.zeros((16, mark), bf))
-    copies[0].wait()
-    copies[1].wait()
+    steps = [(iota + 16.0 * j).astype(bf) for j in range(rows // 16)]
+    zero = jnp.zeros((16, mark), bf)
 
     def body(step, carry):
         first = pl.multiple_of(step * group, group)
-        force = [force_ref[c, pl.ds(first, group), :] for c in range(3)]
-        for k in range(kernel):
-            at = pl.ds(first * kernel + k, group, stride=kernel)
-            cells = cells_ref[at, :]
+        for c in range(3):
+            lines_ref[group, c] = force_ref[c, pl.ds(first, group), :]
+        for i in range(group):
+            at = pl.ds(pl.multiple_of((first + i) * kernel, kernel), kernel)
             weight = weights_ref[at, :]
-            lane = (cells & (lanes - 1)).astype(jnp.float32)
-            row = (cells >> (lanes.bit_length() - 1)).astype(jnp.float32)
-            parts = []
+            lines_ref[i, 6] = (cells_ref[at, :] >> (lanes.bit_length() - 1)).astype(jnp.float32)
             for c in range(3):
-                value = weight * force[c]
+                value = weight * lines_ref[group, c, i : i + 1, :]
                 high = value.astype(bf).astype(jnp.float32)
-                parts += [high, value - high]
-            for which, entries in enumerate([lane, row] + parts):
-                lines_ref[k, which] = entries
-
-            def wide(which, i):
-                entries = lines_ref[k, which, i : i + 1, :]
+                lines_ref[i, 2 * c] = high
+                lines_ref[i, 2 * c + 1] = value - high
+
+            def wide(which, k, i=i):
+                entries = lines_ref[i, which, k : k + 1, :]
                 return jnp.broadcast_to(entries, (16, mark)).astype(bf)
 
-            left, right = ([], [])
-            for i in range(group):
-                lane_i, row_i = (wide(0, i), wide(1, i))
-                right.append(
-                    jnp.concatenate(
-                        [jnp.where(steps[j] == lane_i, one, zero) for j in range(lanes // 16)],
-                        axis=0,
-                    )
-                )
-                masks = [steps[j] == row_i for j in range(rows // 16)]
+            left = []
+            for k in range(kernel):
+                row = wide(6, k)
+                masks = [steps[j] == row for j in range(rows // 16)]
                 pieces = []
-                for which in range(len(parts)):
-                    part_i = wide(2 + which, i)
-                    pieces += [jnp.where(mask, part_i, zero) for mask in masks]
+                for which in range(6):
+                    part = wide(which, k)
+                    pieces += [jnp.where(mask, part, zero) for mask in masks]
                 left.append(jnp.concatenate(pieces, axis=0))
-            acc[...] += lax.dot_general(
+            here = pl.ds(pl.multiple_of((first + i) * points, points), points)
+            acc[...] += jnp.dot(
                 jnp.concatenate(left, axis=1),
-                jnp.concatenate(right, axis=1),
-                (((1,), (1,)), ((), ())),
+                lanes_ref[here, :],
                 preferred_element_type=jnp.float32,
             )
         return carry
 
     lax.fori_loop(0, slots // group, body, 0)
-    copies[2].wait()
     cell_force = [
         acc[2 * c * rows : (2 * c + 1) * rows, :] + acc[(2 * c + 1) * rows : (2 * c + 2) * rows, :]
         for c in range(3)
@@ -579,14 +596,14 @@
             side_ref[at : at + 1, :] = jnp.where(place_ref[0] == 0, up, down)
 
 
-def spread(slots, owned, place, speeds, shards, early, cells, weights, populations, solid):
+def spread(owned, place, own, last, early, cells, weights, populations, lane_match, solid):
     mark = cells.shape[1]
+    slots = early[1].shape[0]
     line_count, lanes = solid.shape
     smem = pl.BlockSpec(memory_space=pltpu.SMEM)
-    hbm = pl.BlockSpec(memory_space=pltpu.HBM)
     vmem = pl.BlockSpec(memory_space=pltpu.VMEM)
     return pl.pallas_call(
-        functools.partial(spread_kernel, len(shards), slots, owned),
+        functools.partial(spread_kernel, slots, owned),
         out_shape=(
             full(populations.shape),
             full((5, 8, lanes)),
@@ -594,19 +611,15 @@
             full((24, lanes)),
             full((3, owned, mark)),
         ),
-        in_specs=[smem] * 2 + [vmem] * (len(shards) + 3) + [hbm] * 3 + [vmem],
+        in_specs=[smem] + [vmem] * 11,
         scratch_shapes=[
-            pltpu.VMEM(cells.shape, jnp.int32),
-            pltpu.VMEM(weights.shape, jnp.float32),
-            pltpu.VMEM(populations.shape, jnp.float32),
             pltpu.VMEM((3, slots, mark), jnp.float32),
-            pltpu.VMEM((cells.shape[0] // slots, 8, group, mark), jnp.float32),
+            pltpu.VMEM((group + 1, 7, cells.shape[0] // slots, mark), jnp.float32),
             pltpu.VMEM((6 * line_count, lanes), jnp.float32),
-            pltpu.SemaphoreType.DMA((3,)),
         ],
         compiler_params=kernel_params(),
         name="spread",
-    )(place, speeds, *shards, *early, cells, weights, populations, solid)
+    )(place, own, last, *early, cells, weights, populations, lane_match, solid)
 
 
 def downwind(place_ref, relaxed_ref, far_ref, near_ref):
@@ -795,8 +808,7 @@
             train_of_block.reshape(1, owned),
         )
     ]
-    pops, cells, weights = inputs[:3]
-    own = sample(place, *inputs)
+    own, pops, cells, weights = sample(place, *inputs)
     swap = [(0, 1), (1, 0)]
 
     def across_x(entries, distance):
@@ -808,20 +820,13 @@
     shards = {0: own}
     for distance in reversed(range(1, count_x)):
         shards[distance] = across_x(own, distance)
-    beside = {distance: across_y(shards[distance]) for distance in (0, 1, 3, 2)}
-    last = beside.pop(2)
-    early = settle_early(slots, owned, [*shards.values(), *beside.values()])
+    beside = {distance: across_y(shards[distance]) for distance in (0, 1, 3)}
+    lane_match, waiting = lax.optimization_barrier((prepare(cells), shards[2]))
+    last = across_y(waiting)
+    early = settle_early(slots, owned, train_velocity, [*shards.values(), *beside.values()])
+    solid = solid_cells.reshape(lines, size_z)
     relaxed, far, near, side, marker_force = spread(
-        slots,
-        owned,
-        place,
-        train_velocity,
-        [own, last],
-        early,
-        cells,
-        weights,
-        pops,
-        solid_cells.reshape(lines, size_z),
+        owned, place, own, last, early, cells, weights, pops, lane_match, solid
     )
     evens = range(0, count_x, 2)
     far = lax.ppermute(

time: 55.5 us -> 61.1 us (1.10)
  Pallas kernels: 20.3 us -> 28.3 us
  waiting for transfers between devices: 13 us -> 9.84 us
  starting transfers between devices: 20.5 us -> 21.9 us
  local copies, waits for them, and re-layouts: 0.69 us -> 0.01 us
    pallas_call x2 -> x3, Pallas kernels: 17.6 us -> 25.1 us  [the longest x1 10.2 us: prepare(): pl.pallas_call(prepare_kernel, out_shape=jax.ShapeDtypeStruct((count * ma...]
    ppermute x3, waiting for transfers between devices: 7.74 us -> 3.36 us  [across_x(): lax.ppermute(entries, 'gx', [(i, i ^ distance) for i in range(count_x)])]
    ppermute x1, starting transfers between devices: 0.01 us -> 3.26 us  [per_device(): lax.ppermute(near, 'gx', [(i, i + 1) for i in evens] + [(i + 1, i) for i...]
    ppermute x6, starting transfers between devices: 6.6 us -> 3.82 us  [across_y(): return lax.ppermute(entries, 'gy', swap)]
    ppermute x1, starting transfers between devices: 4.37 us -> 6.12 us  [per_device(): up_first = lax.ppermute(up_first, 'gz', inner + [(j, i) for i, j in inner])]
    ppermute x6, waiting for transfers between devices: 3.28 us -> 4.62 us  [across_y(): return lax.ppermute(entries, 'gy', swap)]
    ppermute x1, starting transfers between devices: 2.04 us -> 1.21 us  [per_device(): lax.ppermute(far, 'gx', [(i, (i - 1) % count_x) for i in evens] + [((i -...]
    unnamed x4, local copies, waits for them, and re-layouts: 0.69 us -> 0.01 us
  transfers between devices with their start and end apart: 13 -> 13, of which waited for: 6 -> 4; matrix products, arithmetic and copies ran while one was open for 0% -> 0% of each run, Pallas kernels for 1% -> 18%
where the time goes in v4:
time: 61.1 us; the launch traced here: 60.9 us
  Pallas kernels  28.3 us (46%)
  starting transfers between devices  21.9 us (36%)
  waiting for transfers between devices  9.84 us (16%)
  between operations  0.75 us (1%)
    pallas_call x1, Pallas kernels, prepare(): pl.pallas_call(prepare_kernel, out_shape=jax.ShapeDtypeStruct((count * ma...  10.2 us
    pallas_call x1, Pallas kernels, spread(): pl.pallas_call(functools.partial(spread_kernel, slots, owned), out_shape=...  8.99 us
    ppermute x1, starting transfers between devices, per_device(): up_first = lax.ppermute(up_first, 'gz', inner + [(j, i) for i, j in inner])  6.12 us
    pallas_call x1, Pallas kernels, sample(): pl.pallas_call(sample_kernel, out_shape=[full((shard_rows(owner.shape[1],...  5.89 us
    ppermute x6, waiting for transfers between devices, across_y(): return lax.ppermute(entries, 'gy', swap)  4.62 us
    ppermute x3, starting transfers between devices, across_x(): lax.ppermute(entries, 'gx', [(i, i ^ distance) for i in range(count_x)])  4.5 us
    ppermute x6, starting transfers between devices, across_y(): return lax.ppermute(entries, 'gy', swap)  3.82 us
    ppermute x3, waiting for transfers between devices, across_x(): lax.ppermute(entries, 'gx', [(i, i ^ distance) for i in range(count_x)])  3.36 us
  transfers between devices with their start and end apart: 13, of which 4 were waited for; matrix products, arithmetic and copies ran while one was open for 0% of the time, Pallas kernels for 18%

profile of v4, /device:TPU:1, one launch (start us, length us, event | category | flops | bytes accessed | tf_op | source)
XLA Modules:
  0.0 60.9 jit_solution(2631510894750279535)
XLA Ops:
  0.6 0.0 copy-start.1
  0.6 0.0 copy-start
  0.7 0.1 pad_add_fusion.place_ref
  0.7 5.9 %sample.1 = (f32[232,128]{1,0:T(8,128)S(1)}, f32[19,32,128]{2,1,0:T(8,128)S(1)}, s32[512,128]{1,0:T(8,128)S(1)}, f32[512,128]{1,0:T(8,128)S(1)}) custom-call(s32[4]{0:T(128)S(1)} %pad_add_fusion.place_ref, f32[19,32,128]{2,1,0:T(8,128)} %bitcast.16, s32[512,128]{1,0:T(8,128)} %bitcast.17, f32[512,128]{1,0:T(8,128)} %bitcast.18, f32[32,128]{1,0:T(8,128)} %bitcast.19, ...), custom_call_target="tpu_custom_call" | custom-call | tf_op jit(solution)/shard_map/sample/pallas_call | solution.py:376
  6.6 2.2 %collective-permute-start.3 = (f32[232,128]{1,0:T(8,128)S(1)}, f32[232,128]{1,0:T(8,128)S(1)}, u32[]{:S(2)}, u32[]{:S(2)}) collective-permute-start(f32[232,128]{1,0:T(8,128)S(1)} %get-tuple-element.20.refs_0_.own_ref), channel_id=1, source_target_pairs={{0,8},{8,0},{16,24},{24,16},{1,9},{9,1},{17,25},{25,17},{2,10},{10... | collective-permute-start | bytes 356360 | tf_op jit(solution)/shard_map/ppermute | solution.py:815
  8.8 2.2 %collective-permute-start.2 = (f32[232,128]{1,0:T(8,128)S(1)}, f32[232,128]{1,0:T(8,128)S(1)}, u32[]{:S(2)}, u32[]{:S(2)}) collective-permute-start(f32[232,128]{1,0:T(8,128)S(1)} %get-tuple-element.20.refs_0_.own_ref), channel_id=1, source_target_pairs={{0,24},{8,16},{16,8},{24,0},{1,25},{9,17},{17,9},{25,1},{2,26},{10... | collective-permute-start | bytes 356360 | tf_op jit(solution)/shard_map/ppermute | solution.py:815
  11.0 1.2 %collective-permute-start.4 = (f32[232,128]{1,0:T(8,128)S(1)}, f32[232,128]{1,0:T(8,128)S(1)}, u32[]{:S(2)}, u32[]{:S(2)}) collective-permute-start(f32[232,128]{1,0:T(8,128)S(1)} %get-tuple-element.20.refs_0_.own_ref), channel_id=1, source_target_pairs={{0,4},{4,0},{1,5},{5,1},{2,6},{6,2},{3,7},{7,3},{8,12},{12,8},{9,1... | collective-permute-start | bytes 356360 | tf_op jit(solution)/shard_map/ppermute | solution.py:818
  12.2 0.1 collective-permute-start
  12.4 0.0 collective-permute-done.3.refs_3_
  12.4 0.5 collective-permute-start.5
  12.8 3.4 %collective-permute-done.2.refs_1_ = f32[232,128]{1,0:T(8,128)S(1)} collective-permute-done((f32[232,128]{1,0:T(8,128)S(1)}, f32[232,128]{1,0:T(8,128)S(1)}, u32[]{:S(2)}, u32[]{:S(2)}) %collective-permute-start.2) | collective-permute-done | bytes 118816 | tf_op jit(solution)/shard_map/ppermute | solution.py:815
  16.2 1.2 %collective-permute-start.6 = (f32[232,128]{1,0:T(8,128)S(1)}, f32[232,128]{1,0:T(8,128)S(1)}, u32[]{:S(2)}, u32[]{:S(2)}) collective-permute-start(f32[232,128]{1,0:T(8,128)S(1)} %collective-permute-done.2.refs_1_), channel_id=1, source_target_pairs={{0,4},{4,0},{1,5},{5,1},{2,6},{6,2},{3,7},{7,3},{8,12},{12,8},{9,1... | collective-permute-start | bytes 356360 | tf_op jit(solution)/shard_map/ppermute | solution.py:818
  17.4 10.2 %prepare.1.lanes_ref = bf16[65536,128]{1,0:T(8,128)(2,1)S(1)} custom-call(s32[512,128]{1,0:T(8,128)S(1)} %get-tuple-element.21.cells_ref), custom_call_target="tpu_custom_call" | custom-call | flops 4000000000 | bytes 262144 | tf_op jit(solution)/shard_map/prepare/pallas_call | solution.py:412
  27.6 0.0 collective-permute-done.refs_2_
  27.6 0.3 collective-permute-start.1
  27.9 0.0 collective-permute-done.4.refs_4_
  27.9 0.0 collective-permute-done.5.refs_5_
  27.9 0.0 collective-permute-done.6.refs_6_
  27.9 0.0 copy-done.1
  28.0 1.1 %settle.1 = (f32[96,384]{1,0:T(8,128)S(1)}, f32[64,128]{1,0:T(8,128)S(1)}, f32[64,128]{1,0:T(8,128)S(1)}, f32[12,128]{1,0:T(8,128)S(1)}) custom-call(f32[4,3]{1,0:T(4,128)S(1)} %copy-done.1, f32[232,128]{1,0:T(8,128)S(1)} %get-tuple-element.20.refs_0_.own_ref, f32[232,128]{1,0:T(8,128)S(1)} %collective-permute-done.2.refs_1_, ...), custom_call_target="tpu_custom_call" | custom-call | flops 1000000000 | bytes 831488 | tf_op jit(solution)/shard_map/settle/pallas_call | solution.py:482
  29.0 2.3 %collective-permute-done.1.last_ref = f32[232,128]{1,0:T(8,128)S(1)} collective-permute-done((f32[232,128]{1,0:T(8,128)S(1)}, f32[232,128]{1,0:T(8,128)S(1)}, u32[]{:S(2)}, u32[]{:S(2)}) %collective-permute-start.1) | collective-permute-done | bytes 118816 | tf_op jit(solution)/shard_map/ppermute | solution.py:818
  31.4 0.0 copy-done
  31.4 9.0 %spread.1 = (f32[19,32,128]{2,1,0:T(8,128)S(1)}, f32[5,8,128]{2,1,0:T(8,128)S(1)}, f32[5,8,128]{2,1,0:T(8,128)S(1)}, f32[24,128]{1,0:T(8,128)S(1)}, f32[3,32,128]{2,1,0:T(8,128)}) custom-call(s32[4]{0:T(128)S(1)} %pad_add_fusion.place_ref, f32[232,128]{1,0:T(8,128)S(1)} %get-tuple-element.20.refs_0_.own_ref, f32[232,128]{1,0:T(8,128)S(1)} %collective-permute-done.1.last_ref, ...), custom_call_target="tpu_custom_call" | custom-call | tf_op jit(solution)/shard_map/spread/pallas_call | solution.py:605
  40.4 1.2 %collective-permute-start.7 = (f32[5,8,128]{2,1,0:T(8,128)S(1)}, f32[5,8,128]{2,1,0:T(8,128)S(1)}, u32[]{:S(2)}, u32[]{:S(2)}) collective-permute-start(f32[5,8,128]{2,1,0:T(8,128)S(1)} %get-tuple-element.31), channel_id=1, source_target_pairs={{0,24},{16,8},{24,0},{8,16},{1,25},{17,9},{25,1},{9,17},{2,26},{18... | collective-permute-start | bytes 61448 | tf_op jit(solution)/shard_map/ppermute | solution.py:832
  41.6 3.3 %collective-permute-start.8 = (f32[5,8,128]{2,1,0:T(8,128)S(1)}, f32[5,8,128]{2,1,0:T(8,128)S(1)}, u32[]{:S(2)}, u32[]{:S(2)}) collective-permute-start(f32[5,8,128]{2,1,0:T(8,128)S(1)} %get-tuple-element.32), channel_id=1, source_target_pairs={{0,8},{16,24},{8,0},{24,16},{1,9},{17,25},{9,1},{25,17},{2,10},{18... | collective-permute-start | bytes 61448 | tf_op jit(solution)/shard_map/ppermute | solution.py:837
  44.8 0.3 collective-permute-start.9
  45.1 2.3 %collective-permute-done.9.side_ref = f32[24,128]{1,0:T(8,128)S(1)} collective-permute-done((f32[24,128]{1,0:T(8,128)S(1)}, f32[24,128]{1,0:T(8,128)S(1)}, u32[]{:S(2)}, u32[]{:S(2)}) %collective-permute-start.9) | collective-permute-done | bytes 12320 | tf_op jit(solution)/shard_map/ppermute | solution.py:818
  47.4 0.0 collective-permute-done.7.far_ref
  47.4 0.0 collective-permute-done.8.near_ref
  47.4 0.7 %pack.1 = (f32[8,128]{1,0:T(8,128)S(1)}, f32[8,128]{1,0:T(8,128)S(1)}, f32[8,128]{1,0:T(8,128)S(1)}) custom-call(s32[4]{0:T(128)S(1)} %pad_add_fusion.place_ref, f32[19,32,128]{2,1,0:T(8,128)S(1)} %get-tuple-element.30.relaxed_ref, f32[5,8,128]{2,1,0:T(8,128)S(1)} %collective-permute-done.7.far_ref, f32[5,8,128]{2,1,0:T(8,128)S(1)} %collective-permute-done.8.near_ref, ...), custom_call_target="tpu_custom_call" | custom-call | tf_op jit(solution)/shard_map/pack/pallas_call | solution.py:712
  48.1 0.3 collective-permute-start.10
  48.4 6.1 %collective-permute-start.11 = (f32[8,128]{1,0:T(8,128)S(1)}, f32[8,128]{1,0:T(8,128)S(1)}, u32[]{:S(2)}, u32[]{:S(2)}) collective-permute-start(f32[8,128]{1,0:T(8,128)S(1)} %get-tuple-element.35), channel_id=1, source_target_pairs={{0,1},{2,3},{1,0},{3,2},{4,5},{6,7},{5,4},{7,6},{8,9},{10,11},{9,8... | collective-permute-start | bytes 12296 | tf_op jit(solution)/shard_map/ppermute | solution.py:843
  54.5 3.0 %collective-permute-start.12 = (f32[8,128]{1,0:T(8,128)S(1)}, f32[8,128]{1,0:T(8,128)S(1)}, u32[]{:S(2)}, u32[]{:S(2)}) collective-permute-start(f32[8,128]{1,0:T(8,128)S(1)} %get-tuple-element.36), channel_id=1, source_target_pairs={{1,2},{2,1},{5,6},{6,5},{9,10},{10,9},{13,14},{14,13},{17,18},{18,... | collective-permute-start | bytes 12296 | tf_op jit(solution)/shard_map/ppermute | solution.py:844
  57.6 0.0 collective-permute-done.10.corner_ref
  57.6 0.0 collective-permute-done.11.first_ref
  57.6 1.9 %collective-permute-done.12.second_ref = f32[8,128]{1,0:T(8,128)S(1)} collective-permute-done((f32[8,128]{1,0:T(8,128)S(1)}, f32[8,128]{1,0:T(8,128)S(1)}, u32[]{:S(2)}, u32[]{:S(2)}) %collective-permute-start.12) | collective-permute-done | bytes 4128 | tf_op jit(solution)/shard_map/ppermute | solution.py:844
  59.4 1.5 %stream.1 = f32[19,4,8,128]{3,2,1,0:T(8,128)} custom-call(s32[4]{0:T(128)S(1)} %pad_add_fusion.place_ref, f32[19,32,128]{2,1,0:T(8,128)S(1)} %get-tuple-element.30.relaxed_ref, f32[5,8,128]{2,1,0:T(8,128)S(1)} %collective-permute-done.7.far_ref, f32[5,8,128]{2,1,0:T(8,128)S(1)} %collective-permute-done.8.near_ref, ...), custom_call_target="tpu_custom_call" | custom-call | tf_op jit(solution)/shard_map/stream/pallas_call | solution.py:769
Async XLA Ops:
  0.6 27.3 %copy-start.1 = (f32[4,3]{1,0:T(4,128)S(1)}, f32[4,3]{1,0:T(4,128)}, u32[]{:S(2)}) copy-start(f32[4,3]{1,0:T(4,128)} %speeds_ref.1) | copy-start | bytes 148
  0.6 30.7 %copy-start = (s32[4,8,128]{2,1,0:T(8,128)S(1)}, s32[4,8,128]{2,1,0:T(8,128)}, u32[]{:S(2)}) copy-start(s32[4,8,128]{2,1,0:T(8,128)} %param.10) | copy-start | bytes 49156
  6.6 5.7 %collective-permute-start.3 = (f32[232,128]{1,0:T(8,128)S(1)}, f32[232,128]{1,0:T(8,128)S(1)}, u32[]{:S(2)}, u32[]{:S(2)}) collective-permute-start(f32[232,128]{1,0:T(8,128)S(1)} %get-tuple-element.20.refs_0_.own_ref), channel_id=1, source_target_pairs={{0,8},{8,0},{16,24},{24,16},{1,9},{9,1},{17,25},{25,17},{2,10},{10... | collective-permute-start | bytes 356360 | tf_op jit(solution)/shard_map/ppermute | solution.py:815
  8.8 7.4 %collective-permute-start.2 = (f32[232,128]{1,0:T(8,128)S(1)}, f32[232,128]{1,0:T(8,128)S(1)}, u32[]{:S(2)}, u32[]{:S(2)}) collective-permute-start(f32[232,128]{1,0:T(8,128)S(1)} %get-tuple-element.20.refs_0_.own_ref), channel_id=1, source_target_pairs={{0,24},{8,16},{16,8},{24,0},{1,25},{9,17},{17,9},{25,1},{2,26},{10... | collective-permute-start | bytes 356360 | tf_op jit(solution)/shard_map/ppermute | solution.py:815
  11.0 16.9 %collective-permute-start.4 = (f32[232,128]{1,0:T(8,128)S(1)}, f32[232,128]{1,0:T(8,128)S(1)}, u32[]{:S(2)}, u32[]{:S(2)}) collective-permute-start(f32[232,128]{1,0:T(8,128)S(1)} %get-tuple-element.20.refs_0_.own_ref), channel_id=1, source_target_pairs={{0,4},{4,0},{1,5},{5,1},{2,6},{6,2},{3,7},{7,3},{8,12},{12,8},{9,1... | collective-permute-start | bytes 356360 | tf_op jit(solution)/shard_map/ppermute | solution.py:818
  12.2 15.4 %collective-permute-start = (f32[232,128]{1,0:T(8,128)S(1)}, f32[232,128]{1,0:T(8,128)S(1)}, u32[]{:S(2)}, u32[]{:S(2)}) collective-permute-start(f32[232,128]{1,0:T(8,128)S(1)} %get-tuple-element.20.refs_0_.own_ref), channel_id=1, source_target_pairs={{0,16},{8,24},{16,0},{24,8},{1,17},{9,25},{17,1},{25,9},{2,18},{10... | collective-permute-start | bytes 356360 | tf_op jit(solution)/shard_map/ppermute | solution.py:815
  12.4 15.6 %collective-permute-start.5 = (f32[232,128]{1,0:T(8,128)S(1)}, f32[232,128]{1,0:T(8,128)S(1)}, u32[]{:S(2)}, u32[]{:S(2)}) collective-permute-start(f32[232,128]{1,0:T(8,128)S(1)} %collective-permute-done.3.refs_3_), channel_id=1, source_target_pairs={{0,4},{4,0},{1,5},{5,1},{2,6},{6,2},{3,7},{7,3},{8,12},{12,8},{9,1... | collective-permute-start | bytes 356360 | tf_op jit(solution)/shard_map/ppermute | solution.py:818
  16.2 11.7 %collective-permute-start.6 = (f32[232,128]{1,0:T(8,128)S(1)}, f32[232,128]{1,0:T(8,128)S(1)}, u32[]{:S(2)}, u32[]{:S(2)}) collective-permute-start(f32[232,128]{1,0:T(8,128)S(1)} %collective-permute-done.2.refs_1_), channel_id=1, source_target_pairs={{0,4},{4,0},{1,5},{5,1},{2,6},{6,2},{3,7},{7,3},{8,12},{12,8},{9,1... | collective-permute-start | bytes 356360 | tf_op jit(solution)/shard_map/ppermute | solution.py:818
  27.6 3.8 %collective-permute-start.1 = (f32[232,128]{1,0:T(8,128)S(1)}, f32[232,128]{1,0:T(8,128)S(1)}, u32[]{:S(2)}, u32[]{:S(2)}) collective-permute-start(f32[232,128]{1,0:T(8,128)S(1)} %collective-permute-done.refs_2_), channel_id=1, source_target_pairs={{0,4},{4,0},{1,5},{5,1},{2,6},{6,2},{3,7},{7,3},{8,12},{12,8},{9,1... | collective-permute-start | bytes 356360 | tf_op jit(solution)/shard_map/ppermute | solution.py:818
  40.4 7.0 %collective-permute-start.7 = (f32[5,8,128]{2,1,0:T(8,128)S(1)}, f32[5,8,128]{2,1,0:T(8,128)S(1)}, u32[]{:S(2)}, u32[]{:S(2)}) collective-permute-start(f32[5,8,128]{2,1,0:T(8,128)S(1)} %get-tuple-element.31), channel_id=1, source_target_pairs={{0,24},{16,8},{24,0},{8,16},{1,25},{17,9},{25,1},{9,17},{2,26},{18... | collective-permute-start | bytes 61448 | tf_op jit(solution)/shard_map/ppermute | solution.py:832
  41.6 5.8 %collective-permute-start.8 = (f32[5,8,128]{2,1,0:T(8,128)S(1)}, f32[5,8,128]{2,1,0:T(8,128)S(1)}, u32[]{:S(2)}, u32[]{:S(2)}) collective-permute-start(f32[5,8,128]{2,1,0:T(8,128)S(1)} %get-tuple-element.32), channel_id=1, source_target_pairs={{0,8},{16,24},{8,0},{24,16},{1,9},{17,25},{9,1},{25,17},{2,10},{18... | collective-permute-start | bytes 61448 | tf_op jit(solution)/shard_map/ppermute | solution.py:837
  44.8 2.5 %collective-permute-start.9 = (f32[24,128]{1,0:T(8,128)S(1)}, f32[24,128]{1,0:T(8,128)S(1)}, u32[]{:S(2)}, u32[]{:S(2)}) collective-permute-start(f32[24,128]{1,0:T(8,128)S(1)} %get-tuple-element.33), channel_id=1, source_target_pairs={{0,4},{4,0},{1,5},{5,1},{2,6},{6,2},{3,7},{7,3},{8,12},{12,8},{9,1... | collective-permute-start | bytes 36872 | tf_op jit(solution)/shard_map/ppermute | solution.py:818
  48.1 9.5 %collective-permute-start.10 = (f32[8,128]{1,0:T(8,128)S(1)}, f32[8,128]{1,0:T(8,128)S(1)}, u32[]{:S(2)}, u32[]{:S(2)}) collective-permute-start(f32[8,128]{1,0:T(8,128)S(1)} %get-tuple-element.34), channel_id=1, source_target_pairs={{0,4},{4,0},{1,5},{5,1},{2,6},{6,2},{3,7},{7,3},{8,12},{12,8},{9,1... | collective-permute-start | bytes 12296 | tf_op jit(solution)/shard_map/ppermute | solution.py:818
  48.4 9.2 %collective-permute-start.11 = (f32[8,128]{1,0:T(8,128)S(1)}, f32[8,128]{1,0:T(8,128)S(1)}, u32[]{:S(2)}, u32[]{:S(2)}) collective-permute-start(f32[8,128]{1,0:T(8,128)S(1)} %get-tuple-element.35), channel_id=1, source_target_pairs={{0,1},{2,3},{1,0},{3,2},{4,5},{6,7},{5,4},{7,6},{8,9},{10,11},{9,8... | collective-permute-start | bytes 12296 | tf_op jit(solution)/shard_map/ppermute | solution.py:843
  54.5 4.9 %collective-permute-start.12 = (f32[8,128]{1,0:T(8,128)S(1)}, f32[8,128]{1,0:T(8,128)S(1)}, u32[]{:S(2)}, u32[]{:S(2)}) collective-permute-start(f32[8,128]{1,0:T(8,128)S(1)} %get-tuple-element.36), channel_id=1, source_target_pairs={{1,2},{2,1},{5,6},{6,5},{9,10},{10,9},{13,14},{14,13},{17,18},{18,... | collective-permute-start | bytes 12296 | tf_op jit(solution)/shard_map/ppermute | solution.py:844

commit v5 on v4

--- a/solution.py
+++ b/solution.py
@@ -320,8 +320,15 @@
     largest = jnp.max(largest, axis=(0, 1), keepdims=True) + 1e-20
     scale = largest * (1.0 / 32767.0)
     fixed = [(speed[c] * (1.0 / scale) + 32768.5).astype(jnp.int32) for c in range(3)]
-    table[0:rows] = (fixed[0] << 16) | fixed[1]
-    table[rows:] = (fixed[2][: rows // 2] << 16) | fixed[2][rows // 2 :]
+    words = jnp.concatenate(
+        [
+            (fixed[0] << 16) | fixed[1],
+            (fixed[2][: rows // 2] << 16) | fixed[2][rows // 2 :],
+        ],
+        axis=0,
+    )
+    for r in range(table.shape[0]):
+        table[r] = jnp.broadcast_to(words[r : r + 1], (group, lanes))
     for copy in copies[1:]:
         copy.wait()
     meta = 3 * slots + owned
@@ -345,8 +352,7 @@
 
             def choose(low, level):
                 if level < 0:
-                    line = jnp.broadcast_to(table[low : low + 1, :], (group, lanes))
-                    return jnp.take_along_axis(line, lane, axis=1, mode="promise_in_bounds")
+                    return jnp.take_along_axis(table[low], lane, axis=1, mode="promise_in_bounds")
                 lower = choose(low, level - 1)
                 return jnp.where(bits[level], choose(low + (1 << level), level - 1), lower)
 
@@ -383,43 +389,12 @@
             pltpu.VMEM(entries.shape, entries.dtype) for entries in (areas, owner, block, trains)
         ]
         + [
-            pltpu.VMEM((populations.shape[1] * 3 // 2, cells.shape[1]), jnp.int32),
+            pltpu.VMEM((populations.shape[1] * 3 // 2, group, populations.shape[2]), jnp.int32),
             pltpu.SemaphoreType.DMA((7,)),
         ],
         compiler_params=kernel_params(),
         name="sample",
     )(place, populations, cells, weights, areas, owner, block, trains)
-
-
-def prepare_kernel(cells_ref, out_ref):
-    chunk, mark = (128, cells_ref.shape[1])
-    z_at = lax.broadcasted_iota(jnp.int32, (mark, mark), 1).astype(jnp.float32)
-
-    def body(step, carry):
-        here = pl.ds(pl.multiple_of(step * chunk, chunk), chunk)
-        lane = (cells_ref[here, :] & (mark - 1)).astype(jnp.float32).T
-        for j in range(chunk):
-            there = pl.ds(pl.multiple_of((step * chunk + j) * mark, mark), mark)
-            out_ref[there, :] = one_hot(lane[:, j : j + 1] == z_at)
-        return carry
-
-    lax.fori_loop(0, cells_ref.shape[0] // chunk, body, 0)
-
-
-def prepare(cells):
-    count, mark = cells.shape
-    vmem = pl.BlockSpec(memory_space=pltpu.VMEM)
-    return pl.pallas_call(
-        prepare_kernel,
-        out_shape=jax.ShapeDtypeStruct((count * mark, mark), jnp.bfloat16),
-        in_specs=[vmem],
-        out_specs=vmem,
-        compiler_params=kernel_params(),
-        cost_estimate=pl.CostEstimate(
-            flops=4 * 10**9, bytes_accessed=count * mark * 4, transcendentals=0
-        ),
-        name="prepare",
-    )(cells)
 
 
 def three_parts(values):
@@ -518,14 +493,13 @@
 
 def spread_kernel(
     slots, owned, place_ref, own_ref, last_ref, sums_ref, area_ref, trains_ref, speeds_ref,
-    cells_ref, weights_ref, pop_ref, lanes_ref, solid_ref,
+    cells_ref, weights_ref, pop_ref, solid_ref,
     relaxed_ref, far_ref, near_ref, side_ref, marker_ref, force_ref, lines_ref, acc,
 ):
     rows, lanes = (pop_ref.shape[1], pop_ref.shape[2])
     size_y = 8
     mark = cells_ref.shape[1]
     kernel = cells_ref.shape[0] // slots
-    points = kernel * mark
     bf = jnp.bfloat16
     ids, mine, _ = wanted_labels(own_ref, slots, owned)
     totals = (sums_ref[...], area_ref[...], trains_ref[...])
@@ -537,40 +511,49 @@
 
     acc[...] = jnp.zeros_like(acc)
     iota = lax.broadcasted_iota(jnp.int32, (16, mark), 0).astype(jnp.float32)
-    steps = [(iota + 16.0 * j).astype(bf) for j in range(rows // 16)]
-    zero = jnp.zeros((16, mark), bf)
+    steps = [(iota + 16.0 * j).astype(bf) for j in range(max(rows, lanes) // 16)]
+    one, zero = (jnp.ones((16, mark), bf), jnp.zeros((16, mark), bf))
 
     def body(step, carry):
         first = pl.multiple_of(step * group, group)
-        for c in range(3):
-            lines_ref[group, c] = force_ref[c, pl.ds(first, group), :]
-        for i in range(group):
-            at = pl.ds(pl.multiple_of((first + i) * kernel, kernel), kernel)
+        force = [force_ref[c, pl.ds(first, group), :] for c in range(3)]
+        for k in range(kernel):
+            at = pl.ds(first * kernel + k, group, stride=kernel)
+            cells = cells_ref[at, :]
             weight = weights_ref[at, :]
-            lines_ref[i, 6] = (cells_ref[at, :] >> (lanes.bit_length() - 1)).astype(jnp.float32)
+            lane = (cells & (lanes - 1)).astype(jnp.float32)
+            row = (cells >> (lanes.bit_length() - 1)).astype(jnp.float32)
+            parts = []
             for c in range(3):
-                value = weight * lines_ref[group, c, i : i + 1, :]
+                value = weight * force[c]
                 high = value.astype(bf).astype(jnp.float32)
-                lines_ref[i, 2 * c] = high
-                lines_ref[i, 2 * c + 1] = value - high
-
-            def wide(which, k, i=i):
-                entries = lines_ref[i, which, k : k + 1, :]
-                return jnp.broadcast_to(entries, (16, mark)).astype(bf)
-
-            left = []
-            for k in range(kernel):
-                row = wide(6, k)
-                masks = [steps[j] == row for j in range(rows // 16)]
+                parts += [high, value - high]
+            for which, entries in enumerate([lane, row] + parts):
+                lines_ref[k, which] = entries
+
+            def wide(which, i):
+                entries = lines_ref[k, which, pl.ds(i, 8, stride=0), :]
+                return jnp.concatenate([entries, entries], axis=0).astype(bf)
+
+            left, right = ([], [])
+            for i in range(group):
+                lane_i, row_i = (wide(0, i), wide(1, i))
+                right.append(
+                    jnp.concatenate(
+                        [jnp.where(steps[j] == lane_i, one, zero) for j in range(lanes // 16)],
+                        axis=0,
+                    )
+                )
+                masks = [steps[j] == row_i for j in range(rows // 16)]
                 pieces = []
-                for which in range(6):
-                    part = wide(which, k)
-                    pieces += [jnp.where(mask, part, zero) for mask in masks]
+                for which in range(len(parts)):
+                    part_i = wide(2 + which, i)
+                    pieces += [jnp.where(mask, part_i, zero) for mask in masks]
                 left.append(jnp.concatenate(pieces, axis=0))
-            here = pl.ds(pl.multiple_of((first + i) * points, points), points)
-            acc[...] += jnp.dot(
+            acc[...] += lax.dot_general(
                 jnp.concatenate(left, axis=1),
-                lanes_ref[here, :],
+                jnp.concatenate(right, axis=1),
+                (((1,), (1,)), ((), ())),
                 preferred_element_type=jnp.float32,
             )
         return carry
@@ -596,7 +579,7 @@
             side_ref[at : at + 1, :] = jnp.where(place_ref[0] == 0, up, down)
 
 
-def spread(owned, place, own, last, early, cells, weights, populations, lane_match, solid):
+def spread(owned, place, own, last, early, cells, weights, populations, solid):
     mark = cells.shape[1]
     slots = early[1].shape[0]
     line_count, lanes = solid.shape
@@ -611,15 +594,15 @@
             full((24, lanes)),
             full((3, owned, mark)),
         ),
-        in_specs=[smem] + [vmem] * 11,
+        in_specs=[smem] + [vmem] * 10,
         scratch_shapes=[
             pltpu.VMEM((3, slots, mark), jnp.float32),
-            pltpu.VMEM((group + 1, 7, cells.shape[0] // slots, mark), jnp.float32),
+            pltpu.VMEM((cells.shape[0] // slots, 8, group, mark), jnp.float32),
             pltpu.VMEM((6 * line_count, lanes), jnp.float32),
         ],
         compiler_params=kernel_params(),
         name="spread",
-    )(place, own, last, *early, cells, weights, populations, lane_match, solid)
+    )(place, own, last, *early, cells, weights, populations, solid)
 
 
 def downwind(place_ref, relaxed_ref, far_ref, near_ref):
@@ -719,8 +702,8 @@
 
 
 def stream_kernel(
-    count_z, place_ref, relaxed_ref, far_ref, near_ref, side_ref, corner_ref, first_ref,
-    second_ref, out_any, out_ref, sems,
+    count_z, place_ref, relaxed_ref, far_ref, near_ref, side_ref, second_ref, corner_ref,
+    first_ref, out_any, out_ref, sems,
 ):
     size_x, size_y, lanes = out_ref.shape[1:]
     shape = (size_y, lanes)
@@ -820,13 +803,12 @@
     shards = {0: own}
     for distance in reversed(range(1, count_x)):
         shards[distance] = across_x(own, distance)
-    beside = {distance: across_y(shards[distance]) for distance in (0, 1, 3)}
-    lane_match, waiting = lax.optimization_barrier((prepare(cells), shards[2]))
-    last = across_y(waiting)
+    beside = {distance: across_y(shards[distance]) for distance in (0, 1, 3, 2)}
+    last = beside.pop(2)
     early = settle_early(slots, owned, train_velocity, [*shards.values(), *beside.values()])
     solid = solid_cells.reshape(lines, size_z)
     relaxed, far, near, side, marker_force = spread(
-        owned, place, own, last, early, cells, weights, pops, lane_match, solid
+        owned, place, own, last, early, cells, weights, pops, solid
     )
     evens = range(0, count_x, 2)
     far = lax.ppermute(
@@ -837,13 +819,13 @@
     near = lax.ppermute(near, "gx", [(i, i + 1) for i in evens] + [(i + 1, i) for i in evens])
     side = across_y(side)
     corner, up_first, down_first = pack(place, relaxed, far, near, side)
-    corner = across_y(corner)
     inner = [(i, i + 1) for i in range(0, count_z - 1, 2)]
     outer = [(i, i + 1) for i in range(1, count_z - 1, 2)]
+    down_first = lax.ppermute(down_first, "gz", outer + [(j, i) for i, j in outer])
+    corner = across_y(corner)
     up_first = lax.ppermute(up_first, "gz", inner + [(j, i) for i, j in inner])
-    down_first = lax.ppermute(down_first, "gz", outer + [(j, i) for i, j in outer])
     populations_next = stream(
-        count_z, place, relaxed, far, near, side, corner, up_first, down_first
+        count_z, place, relaxed, far, near, side, down_first, corner, up_first
     )
     marker_force = marker_force.transpose(1, 0, 2).reshape(1, 1, 1, owned, 3, mark)
     return (populations_next, marker_force)

time: 61.1 us -> 51.2 us (0.84)
  Pallas kernels: 28.3 us -> 18.2 us
  waiting for transfers between devices: 9.84 us -> 11.8 us
  starting transfers between devices: 21.9 us -> 20.3 us
    pallas_call x1 -> x0, Pallas kernels: 10.2 us -> none  [prepare(): pl.pallas_call(prepare_kernel, out_shape=jax.ShapeDtypeStruct((count * ma...]
    ppermute x1, starting transfers between devices: 6.12 us -> 0.01 us  [per_device(): up_first = lax.ppermute(up_first, 'gz', inner + [(j, i) for i, j in inner])]
    ppermute x3, waiting for transfers between devices: 3.36 us -> 7.74 us  [across_x(): lax.ppermute(entries, 'gx', [(i, i ^ distance) for i in range(count_x)])]
    ppermute x1, starting transfers between devices: 3.03 us -> 7.13 us  [per_device(): lax.ppermute(down_first, 'gz', outer + [(j, i) for i, j in outer])]
    ppermute x1, starting transfers between devices: 3.26 us -> 0.01 us  [per_device(): lax.ppermute(near, 'gx', [(i, i + 1) for i in evens] + [(i + 1, i) for i...]
    ppermute x6, starting transfers between devices: 3.82 us -> 6.6 us  [across_y(): return lax.ppermute(entries, 'gy', swap)]
    ppermute x1, waiting for transfers between devices: 1.86 us -> 0.01 us  [per_device(): lax.ppermute(down_first, 'gz', outer + [(j, i) for i, j in outer])]
    ppermute x1, starting transfers between devices: 1.21 us -> 2.04 us  [per_device(): lax.ppermute(far, 'gx', [(i, (i - 1) % count_x) for i in evens] + [((i -...]
  transfers between devices with their start and end apart: 13 -> 13, of which waited for: 4 -> 6; matrix products, arithmetic and copies ran while one was open for 0% -> 0% of each run, Pallas kernels for 18% -> 2%
where the time goes in v5:
time: 51.2 us; the launch traced here: 51 us
  starting transfers between devices  20.3 us (40%)
  Pallas kernels  18.2 us (36%)
  waiting for transfers between devices  11.8 us (23%)
  between operations  0.72 us (1%)
    pallas_call x1, Pallas kernels, spread(): pl.pallas_call(functools.partial(spread_kernel, slots, owned), out_shape=...  9.04 us
    ppermute x3, waiting for transfers between devices, across_x(): lax.ppermute(entries, 'gx', [(i, i ^ distance) for i in range(count_x)])  7.74 us
    ppermute x1, starting transfers between devices, per_device(): lax.ppermute(down_first, 'gz', outer + [(j, i) for i, j in outer])  7.13 us
    ppermute x6, starting transfers between devices, across_y(): return lax.ppermute(entries, 'gy', swap)  6.6 us
    pallas_call x1, Pallas kernels, sample(): pl.pallas_call(sample_kernel, out_shape=[full((shard_rows(owner.shape[1],...  5.9 us
    ppermute x3, starting transfers between devices, across_x(): lax.ppermute(entries, 'gx', [(i, i ^ distance) for i in range(count_x)])  4.5 us
    ppermute x6, waiting for transfers between devices, across_y(): return lax.ppermute(entries, 'gy', swap)  3.94 us
    ppermute x1, starting transfers between devices, per_device(): lax.ppermute(far, 'gx', [(i, (i - 1) % count_x) for i in evens] + [((i -...  2.04 us
  transfers between devices with their start and end apart: 13, of which 6 were waited for; matrix products, arithmetic and copies ran while one was open for 0% of the time, Pallas kernels for 2%

profile of v5, /device:TPU:1, one launch (start us, length us, event | category | flops | bytes accessed | tf_op | source)
XLA Modules:
  0.0 51.0 jit_solution(13252184518406508560)
XLA Ops:
  0.6 0.1 pad_add_fusion.place_ref
  0.7 0.0 copy-start.1
  0.7 5.9 %sample.1 = (f32[232,128]{1,0:T(8,128)S(1)}, f32[19,32,128]{2,1,0:T(8,128)S(1)}, s32[512,128]{1,0:T(8,128)S(1)}, f32[512,128]{1,0:T(8,128)S(1)}) custom-call(s32[4]{0:T(128)S(1)} %pad_add_fusion.place_ref, f32[19,32,128]{2,1,0:T(8,128)} %bitcast.16, s32[512,128]{1,0:T(8,128)} %bitcast.17, f32[512,128]{1,0:T(8,128)} %bitcast.18, f32[32,128]{1,0:T(8,128)} %bitcast.19, ...), custom_call_target="tpu_custom_call" | custom-call | tf_op jit(solution)/shard_map/sample/pallas_call | solution.py:382
  6.6 2.2 %collective-permute-start.3 = (f32[232,128]{1,0:T(8,128)S(1)}, f32[232,128]{1,0:T(8,128)S(1)}, u32[]{:S(2)}, u32[]{:S(2)}) collective-permute-start(f32[232,128]{1,0:T(8,128)S(1)} %get-tuple-element.18.refs_0_.own_ref), channel_id=1, source_target_pairs={{0,8},{8,0},{16,24},{24,16},{1,9},{9,1},{17,25},{25,17},{2,10},{10... | collective-permute-start | bytes 356360 | tf_op jit(solution)/shard_map/ppermute | solution.py:798
  8.8 2.2 %collective-permute-start.2 = (f32[232,128]{1,0:T(8,128)S(1)}, f32[232,128]{1,0:T(8,128)S(1)}, u32[]{:S(2)}, u32[]{:S(2)}) collective-permute-start(f32[232,128]{1,0:T(8,128)S(1)} %get-tuple-element.18.refs_0_.own_ref), channel_id=1, source_target_pairs={{0,24},{8,16},{16,8},{24,0},{1,25},{9,17},{17,9},{25,1},{2,26},{10... | collective-permute-start | bytes 356360 | tf_op jit(solution)/shard_map/ppermute | solution.py:798
  11.0 0.1 collective-permute-start
  11.1 1.2 %collective-permute-start.4 = (f32[232,128]{1,0:T(8,128)S(1)}, f32[232,128]{1,0:T(8,128)S(1)}, u32[]{:S(2)}, u32[]{:S(2)}) collective-permute-start(f32[232,128]{1,0:T(8,128)S(1)} %get-tuple-element.18.refs_0_.own_ref), channel_id=1, source_target_pairs={{0,4},{4,0},{1,5},{5,1},{2,6},{6,2},{3,7},{7,3},{8,12},{12,8},{9,1... | collective-permute-start | bytes 356360 | tf_op jit(solution)/shard_map/ppermute | solution.py:801
  12.3 0.0 collective-permute-done.3.refs_3_
  12.3 0.5 collective-permute-start.5
  12.8 3.4 %collective-permute-done.2.refs_1_ = f32[232,128]{1,0:T(8,128)S(1)} collective-permute-done((f32[232,128]{1,0:T(8,128)S(1)}, f32[232,128]{1,0:T(8,128)S(1)}, u32[]{:S(2)}, u32[]{:S(2)}) %collective-permute-start.2) | collective-permute-done | bytes 118816 | tf_op jit(solution)/shard_map/ppermute | solution.py:798
  16.2 1.2 %collective-permute-start.6 = (f32[232,128]{1,0:T(8,128)S(1)}, f32[232,128]{1,0:T(8,128)S(1)}, u32[]{:S(2)}, u32[]{:S(2)}) collective-permute-start(f32[232,128]{1,0:T(8,128)S(1)} %collective-permute-done.2.refs_1_), channel_id=1, source_target_pairs={{0,4},{4,0},{1,5},{5,1},{2,6},{6,2},{3,7},{7,3},{8,12},{12,8},{9,1... | collective-permute-start | bytes 356360 | tf_op jit(solution)/shard_map/ppermute | solution.py:801
  17.4 4.4 %collective-permute-done.refs_2_ = f32[232,128]{1,0:T(8,128)S(1)} collective-permute-done((f32[232,128]{1,0:T(8,128)S(1)}, f32[232,128]{1,0:T(8,128)S(1)}, u32[]{:S(2)}, u32[]{:S(2)}) %collective-permute-start) | collective-permute-done | bytes 118816 | tf_op jit(solution)/shard_map/ppermute | solution.py:798
  21.8 1.2 %collective-permute-start.1 = (f32[232,128]{1,0:T(8,128)S(1)}, f32[232,128]{1,0:T(8,128)S(1)}, u32[]{:S(2)}, u32[]{:S(2)}) collective-permute-start(f32[232,128]{1,0:T(8,128)S(1)} %collective-permute-done.refs_2_), channel_id=1, source_target_pairs={{0,4},{4,0},{1,5},{5,1},{2,6},{6,2},{3,7},{7,3},{8,12},{12,8},{9,1... | collective-permute-start | bytes 356360 | tf_op jit(solution)/shard_map/ppermute | solution.py:801
  23.0 0.0 collective-permute-done.4.refs_4_
  23.0 0.0 collective-permute-done.5.refs_5_
  23.0 0.0 collective-permute-done.6.refs_6_
  23.0 0.0 copy-done.1
  23.0 0.0 copy-start
  23.0 1.1 %settle.1 = (f32[96,384]{1,0:T(8,128)S(1)}, f32[64,128]{1,0:T(8,128)S(1)}, f32[64,128]{1,0:T(8,128)S(1)}, f32[12,128]{1,0:T(8,128)S(1)}) custom-call(f32[4,3]{1,0:T(4,128)S(1)} %copy-done.1, f32[232,128]{1,0:T(8,128)S(1)} %get-tuple-element.18.refs_0_.own_ref, f32[232,128]{1,0:T(8,128)S(1)} %collective-permute-done.2.refs_1_, ...), custom_call_target="tpu_custom_call" | custom-call | flops 1000000000 | bytes 831488 | tf_op jit(solution)/shard_map/settle/pallas_call | solution.py:457
  24.1 1.4 %collective-permute-done.1.last_ref = f32[232,128]{1,0:T(8,128)S(1)} collective-permute-done((f32[232,128]{1,0:T(8,128)S(1)}, f32[232,128]{1,0:T(8,128)S(1)}, u32[]{:S(2)}, u32[]{:S(2)}) %collective-permute-start.1) | collective-permute-done | bytes 118816 | tf_op jit(solution)/shard_map/ppermute | solution.py:801
  25.5 0.0 copy-done
  25.5 9.0 %spread.1 = (f32[19,32,128]{2,1,0:T(8,128)S(1)}, f32[5,8,128]{2,1,0:T(8,128)S(1)}, f32[5,8,128]{2,1,0:T(8,128)S(1)}, f32[24,128]{1,0:T(8,128)S(1)}, f32[3,32,128]{2,1,0:T(8,128)}) custom-call(s32[4]{0:T(128)S(1)} %pad_add_fusion.place_ref, f32[232,128]{1,0:T(8,128)S(1)} %get-tuple-element.18.refs_0_.own_ref, f32[232,128]{1,0:T(8,128)S(1)} %collective-permute-done.1.last_ref, ...), custom_call_target="tpu_custom_call" | custom-call | tf_op jit(solution)/shard_map/spread/pallas_call | solution.py:588
  34.5 2.0 %collective-permute-start.7 = (f32[5,8,128]{2,1,0:T(8,128)S(1)}, f32[5,8,128]{2,1,0:T(8,128)S(1)}, u32[]{:S(2)}, u32[]{:S(2)}) collective-permute-start(f32[5,8,128]{2,1,0:T(8,128)S(1)} %get-tuple-element.27), channel_id=1, source_target_pairs={{0,24},{16,8},{24,0},{8,16},{1,25},{17,9},{25,1},{9,17},{2,26},{18... | collective-permute-start | bytes 61448 | tf_op jit(solution)/shard_map/ppermute | solution.py:814
  36.6 0.0 collective-permute-start.8
  36.6 1.2 %collective-permute-start.9 = (f32[24,128]{1,0:T(8,128)S(1)}, f32[24,128]{1,0:T(8,128)S(1)}, u32[]{:S(2)}, u32[]{:S(2)}) collective-permute-start(f32[24,128]{1,0:T(8,128)S(1)} %get-tuple-element.29), channel_id=1, source_target_pairs={{0,4},{4,0},{1,5},{5,1},{2,6},{6,2},{3,7},{7,3},{8,12},{12,8},{9,1... | collective-permute-start | bytes 36872 | tf_op jit(solution)/shard_map/ppermute | solution.py:801
  37.8 1.3 %collective-permute-done.9.side_ref = f32[24,128]{1,0:T(8,128)S(1)} collective-permute-done((f32[24,128]{1,0:T(8,128)S(1)}, f32[24,128]{1,0:T(8,128)S(1)}, u32[]{:S(2)}, u32[]{:S(2)}) %collective-permute-start.9) | collective-permute-done | bytes 12320 | tf_op jit(solution)/shard_map/ppermute | solution.py:801
  39.1 0.0 collective-permute-done.7.far_ref
  39.1 0.1 collective-permute-done.8.near_ref
  39.2 0.7 %pack.1 = (f32[8,128]{1,0:T(8,128)S(1)}, f32[8,128]{1,0:T(8,128)S(1)}, f32[8,128]{1,0:T(8,128)S(1)}) custom-call(s32[4]{0:T(128)S(1)} %pad_add_fusion.place_ref, f32[19,32,128]{2,1,0:T(8,128)S(1)} %get-tuple-element.26.relaxed_ref, f32[5,8,128]{2,1,0:T(8,128)S(1)} %collective-permute-done.7.far_ref, f32[5,8,128]{2,1,0:T(8,128)S(1)} %collective-permute-done.8.near_ref, ...), custom_call_target="tpu_custom_call" | custom-call | tf_op jit(solution)/shard_map/pack/pallas_call | solution.py:695
  39.9 7.1 %collective-permute-start.10 = (f32[8,128]{1,0:T(8,128)S(1)}, f32[8,128]{1,0:T(8,128)S(1)}, u32[]{:S(2)}, u32[]{:S(2)}) collective-permute-start(f32[8,128]{1,0:T(8,128)S(1)} %get-tuple-element.30), channel_id=1, source_target_pairs={{1,2},{2,1},{5,6},{6,5},{9,10},{10,9},{13,14},{14,13},{17,18},{18,... | collective-permute-start | bytes 12296 | tf_op jit(solution)/shard_map/ppermute | solution.py:824
  47.0 1.3 %collective-permute-start.11 = (f32[8,128]{1,0:T(8,128)S(1)}, f32[8,128]{1,0:T(8,128)S(1)}, u32[]{:S(2)}, u32[]{:S(2)}) collective-permute-start(f32[8,128]{1,0:T(8,128)S(1)} %get-tuple-element.31), channel_id=1, source_target_pairs={{0,4},{4,0},{1,5},{5,1},{2,6},{6,2},{3,7},{7,3},{8,12},{12,8},{9,1... | collective-permute-start | bytes 12296 | tf_op jit(solution)/shard_map/ppermute | solution.py:801
  48.3 0.0 collective-permute-start.12
  48.3 0.0 collective-permute-done.10.second_ref
  48.3 1.2 %collective-permute-done.11.corner_ref = f32[8,128]{1,0:T(8,128)S(1)} collective-permute-done((f32[8,128]{1,0:T(8,128)S(1)}, f32[8,128]{1,0:T(8,128)S(1)}, u32[]{:S(2)}, u32[]{:S(2)}) %collective-permute-start.11) | collective-permute-done | bytes 4128 | tf_op jit(solution)/shard_map/ppermute | solution.py:801
  49.6 0.0 collective-permute-done.12.first_ref
  49.6 1.5 %stream.1 = f32[19,4,8,128]{3,2,1,0:T(8,128)} custom-call(s32[4]{0:T(128)S(1)} %pad_add_fusion.place_ref, f32[19,32,128]{2,1,0:T(8,128)S(1)} %get-tuple-element.26.relaxed_ref, f32[5,8,128]{2,1,0:T(8,128)S(1)} %collective-permute-done.7.far_ref, f32[5,8,128]{2,1,0:T(8,128)S(1)} %collective-permute-done.8.near_ref, ...), custom_call_target="tpu_custom_call" | custom-call | tf_op jit(solution)/shard_map/stream/pallas_call | solution.py:752
Async XLA Ops:
  0.7 22.3 %copy-start.1 = (f32[4,3]{1,0:T(4,128)S(1)}, f32[4,3]{1,0:T(4,128)}, u32[]{:S(2)}) copy-start(f32[4,3]{1,0:T(4,128)} %speeds_ref.1) | copy-start | bytes 148
  6.6 5.7 %collective-permute-start.3 = (f32[232,128]{1,0:T(8,128)S(1)}, f32[232,128]{1,0:T(8,128)S(1)}, u32[]{:S(2)}, u32[]{:S(2)}) collective-permute-start(f32[232,128]{1,0:T(8,128)S(1)} %get-tuple-element.18.refs_0_.own_ref), channel_id=1, source_target_pairs={{0,8},{8,0},{16,24},{24,16},{1,9},{9,1},{17,25},{25,17},{2,10},{10... | collective-permute-start | bytes 356360 | tf_op jit(solution)/shard_map/ppermute | solution.py:798
  8.8 7.4 %collective-permute-start.2 = (f32[232,128]{1,0:T(8,128)S(1)}, f32[232,128]{1,0:T(8,128)S(1)}, u32[]{:S(2)}, u32[]{:S(2)}) collective-permute-start(f32[232,128]{1,0:T(8,128)S(1)} %get-tuple-element.18.refs_0_.own_ref), channel_id=1, source_target_pairs={{0,24},{8,16},{16,8},{24,0},{1,25},{9,17},{17,9},{25,1},{2,26},{10... | collective-permute-start | bytes 356360 | tf_op jit(solution)/shard_map/ppermute | solution.py:798
  11.0 10.8 %collective-permute-start = (f32[232,128]{1,0:T(8,128)S(1)}, f32[232,128]{1,0:T(8,128)S(1)}, u32[]{:S(2)}, u32[]{:S(2)}) collective-permute-start(f32[232,128]{1,0:T(8,128)S(1)} %get-tuple-element.18.refs_0_.own_ref), channel_id=1, source_target_pairs={{0,16},{8,24},{16,0},{24,8},{1,17},{9,25},{17,1},{25,9},{2,18},{10... | collective-permute-start | bytes 356360 | tf_op jit(solution)/shard_map/ppermute | solution.py:798
  11.1 11.9 %collective-permute-start.4 = (f32[232,128]{1,0:T(8,128)S(1)}, f32[232,128]{1,0:T(8,128)S(1)}, u32[]{:S(2)}, u32[]{:S(2)}) collective-permute-start(f32[232,128]{1,0:T(8,128)S(1)} %get-tuple-element.18.refs_0_.own_ref), channel_id=1, source_target_pairs={{0,4},{4,0},{1,5},{5,1},{2,6},{6,2},{3,7},{7,3},{8,12},{12,8},{9,1... | collective-permute-start | bytes 356360 | tf_op jit(solution)/shard_map/ppermute | solution.py:801
  12.3 10.7 %collective-permute-start.5 = (f32[232,128]{1,0:T(8,128)S(1)}, f32[232,128]{1,0:T(8,128)S(1)}, u32[]{:S(2)}, u32[]{:S(2)}) collective-permute-start(f32[232,128]{1,0:T(8,128)S(1)} %collective-permute-done.3.refs_3_), channel_id=1, source_target_pairs={{0,4},{4,0},{1,5},{5,1},{2,6},{6,2},{3,7},{7,3},{8,12},{12,8},{9,1... | collective-permute-start | bytes 356360 | tf_op jit(solution)/shard_map/ppermute | solution.py:801
  16.2 6.8 %collective-permute-start.6 = (f32[232,128]{1,0:T(8,128)S(1)}, f32[232,128]{1,0:T(8,128)S(1)}, u32[]{:S(2)}, u32[]{:S(2)}) collective-permute-start(f32[232,128]{1,0:T(8,128)S(1)} %collective-permute-done.2.refs_1_), channel_id=1, source_target_pairs={{0,4},{4,0},{1,5},{5,1},{2,6},{6,2},{3,7},{7,3},{8,12},{12,8},{9,1... | collective-permute-start | bytes 356360 | tf_op jit(solution)/shard_map/ppermute | solution.py:801
  21.8 3.7 %collective-permute-start.1 = (f32[232,128]{1,0:T(8,128)S(1)}, f32[232,128]{1,0:T(8,128)S(1)}, u32[]{:S(2)}, u32[]{:S(2)}) collective-permute-start(f32[232,128]{1,0:T(8,128)S(1)} %collective-permute-done.refs_2_), channel_id=1, source_target_pairs={{0,4},{4,0},{1,5},{5,1},{2,6},{6,2},{3,7},{7,3},{8,12},{12,8},{9,1... | collective-permute-start | bytes 356360 | tf_op jit(solution)/shard_map/ppermute | solution.py:801
  23.0 2.5 %copy-start = (s32[4,8,128]{2,1,0:T(8,128)S(1)}, s32[4,8,128]{2,1,0:T(8,128)}, u32[]{:S(2)}) copy-start(s32[4,8,128]{2,1,0:T(8,128)} %param.10) | copy-start | bytes 49156
  34.5 4.6 %collective-permute-start.7 = (f32[5,8,128]{2,1,0:T(8,128)S(1)}, f32[5,8,128]{2,1,0:T(8,128)S(1)}, u32[]{:S(2)}, u32[]{:S(2)}) collective-permute-start(f32[5,8,128]{2,1,0:T(8,128)S(1)} %get-tuple-element.27), channel_id=1, source_target_pairs={{0,24},{16,8},{24,0},{8,16},{1,25},{17,9},{25,1},{9,17},{2,26},{18... | collective-permute-start | bytes 61448 | tf_op jit(solution)/shard_map/ppermute | solution.py:814
  36.6 2.7 %collective-permute-start.8 = (f32[5,8,128]{2,1,0:T(8,128)S(1)}, f32[5,8,128]{2,1,0:T(8,128)S(1)}, u32[]{:S(2)}, u32[]{:S(2)}) collective-permute-start(f32[5,8,128]{2,1,0:T(8,128)S(1)} %get-tuple-element.28), channel_id=1, source_target_pairs={{0,8},{16,24},{8,0},{24,16},{1,9},{17,25},{9,1},{25,17},{2,10},{18... | collective-permute-start | bytes 61448 | tf_op jit(solution)/shard_map/ppermute | solution.py:819
  36.6 2.5 %collective-permute-start.9 = (f32[24,128]{1,0:T(8,128)S(1)}, f32[24,128]{1,0:T(8,128)S(1)}, u32[]{:S(2)}, u32[]{:S(2)}) collective-permute-start(f32[24,128]{1,0:T(8,128)S(1)} %get-tuple-element.29), channel_id=1, source_target_pairs={{0,4},{4,0},{1,5},{5,1},{2,6},{6,2},{3,7},{7,3},{8,12},{12,8},{9,1... | collective-permute-start | bytes 36872 | tf_op jit(solution)/shard_map/ppermute | solution.py:801
  39.9 8.4 %collective-permute-start.10 = (f32[8,128]{1,0:T(8,128)S(1)}, f32[8,128]{1,0:T(8,128)S(1)}, u32[]{:S(2)}, u32[]{:S(2)}) collective-permute-start(f32[8,128]{1,0:T(8,128)S(1)} %get-tuple-element.30), channel_id=1, source_target_pairs={{1,2},{2,1},{5,6},{6,5},{9,10},{10,9},{13,14},{14,13},{17,18},{18,... | collective-permute-start | bytes 12296 | tf_op jit(solution)/shard_map/ppermute | solution.py:824
  47.0 2.5 %collective-permute-start.11 = (f32[8,128]{1,0:T(8,128)S(1)}, f32[8,128]{1,0:T(8,128)S(1)}, u32[]{:S(2)}, u32[]{:S(2)}) collective-permute-start(f32[8,128]{1,0:T(8,128)S(1)} %get-tuple-element.31), channel_id=1, source_target_pairs={{0,4},{4,0},{1,5},{5,1},{2,6},{6,2},{3,7},{7,3},{8,12},{12,8},{9,1... | collective-permute-start | bytes 12296 | tf_op jit(solution)/shard_map/ppermute | solution.py:801
  48.3 1.3 %collective-permute-start.12 = (f32[8,128]{1,0:T(8,128)S(1)}, f32[8,128]{1,0:T(8,128)S(1)}, u32[]{:S(2)}, u32[]{:S(2)}) collective-permute-start(f32[8,128]{1,0:T(8,128)S(1)} %get-tuple-element.32), channel_id=1, source_target_pairs={{0,1},{2,3},{1,0},{3,2},{4,5},{6,7},{5,4},{7,6},{8,9},{10,11},{9,8... | collective-permute-start | bytes 12296 | tf_op jit(solution)/shard_map/ppermute | solution.py:826

commit v6 on v5

--- a/solution.py
+++ b/solution.py
@@ -287,7 +287,7 @@
 
 
 def shard_rows(slots, owned):
-    return 3 * slots + owned + 8
+    return 8 + owned + 3 * slots
 
 
 def sample_kernel(
@@ -331,14 +331,13 @@
         table[r] = jnp.broadcast_to(words[r : r + 1], (group, lanes))
     for copy in copies[1:]:
         copy.wait()
-    meta = 3 * slots + owned
-    out_ref[3 * slots : meta, :] = areas_ref[...]
-    out_ref[meta : meta + 8, :] = jnp.zeros((8, mark), jnp.float32)
+    out_ref[8 : 8 + owned, :] = areas_ref[...]
+    out_ref[0:8, :] = jnp.zeros((8, mark), jnp.float32)
     ids = (owner_ref[...] * owned + block_ref[...]).astype(jnp.float32)
-    out_ref[meta : meta + 1, :] = jnp.concatenate([ids] * (mark // slots), axis=1)
-    out_ref[meta + 1 : meta + 2, 0:owned] = trains_ref[...].astype(jnp.float32)
+    out_ref[0:1, :] = jnp.concatenate([ids] * (mark // slots), axis=1)
+    out_ref[1:2, 0:owned] = trains_ref[...].astype(jnp.float32)
     mine = lax.broadcasted_iota(jnp.int32, (1, mark), 1) % owned + place_ref[2] * owned
-    out_ref[meta + 2 : meta + 3, :] = mine.astype(jnp.float32)
+    out_ref[2:3, :] = mine.astype(jnp.float32)
 
     def body(step, carry):
         first = pl.multiple_of(step * group, group)
@@ -367,7 +366,7 @@
             for c in range(3):
                 total[c] = total[c] + weight * (picked[c].astype(jnp.float32) - 32768.0)
         for c in range(3):
-            here = pl.ds(pl.multiple_of(c * slots + first, group), group)
+            here = pl.ds(pl.multiple_of(8 + owned + c * slots + first, group), group)
             out_ref[here, :] = total[c] * scale
         return carry
 
@@ -379,9 +378,10 @@
     hbm = pl.BlockSpec(memory_space=pltpu.HBM)
     vmem = pl.BlockSpec(memory_space=pltpu.VMEM)
     kept = (populations, cells, weights)
+    count = shard_rows(owner.shape[1], areas.shape[0])
     return pl.pallas_call(
         sample_kernel,
-        out_shape=[full((shard_rows(owner.shape[1], areas.shape[0]), cells.shape[1]))]
+        out_shape=[full((count, cells.shape[1]))]
         + [jax.ShapeDtypeStruct(entries.shape, entries.dtype) for entries in kept],
         in_specs=[smem] + [hbm] * 7,
         out_specs=[vmem] * 4,
@@ -411,36 +411,35 @@
 
 def wanted_labels(own_ref, slots, owned):
     mark = own_ref.shape[1]
-    own = own_ref[3 * slots + owned : 3 * slots + owned + 8, :]
+    own = own_ref[0:8, :]
     ids, trains, mine = (jnp.broadcast_to(own[i : i + 1], (mark, mark)).T for i in range(3))
     return (ids[0:slots], mine[0:owned], trains[0:owned])
 
 
 def add_shards(totals, shards, ids, mine):
     slots, owned = (ids.shape[0], mine.shape[0])
-    meta = 3 * slots + owned
     wanted = jnp.concatenate([ids, mine], axis=0)
     for shard in shards:
-        match = one_hot(wanted == shard[meta : meta + 1, :])
+        match = one_hot(wanted == shard[0:1, :])
         match = jnp.concatenate([match, match[:, 0:slots]], axis=1)
-        values = jnp.concatenate([shard[c * slots : (c + 1) * slots, :] for c in range(3)], axis=1)
+        starts = [8 + owned + c * slots for c in range(3)]
+        values = jnp.concatenate([shard[at : at + slots, :] for at in starts], axis=1)
         sums = jnp.dot(
             match, jnp.concatenate(three_parts(values), axis=0), preferred_element_type=jnp.float32
         )
-        held = ids == shard[meta + 2 : meta + 3, :]
-        parts = three_parts(shard[3 * slots : meta, :])
+        held = ids == shard[2:3, :]
+        parts = three_parts(shard[8 : 8 + owned, :])
         parts.append(jnp.zeros_like(parts[0]))
         area = jnp.dot(
             one_hot(held), jnp.concatenate(parts, axis=0), preferred_element_type=jnp.float32
         )
-        trains = jnp.where(held, shard[meta + 1 : meta + 2, :], 0.0)
-        got = (sums, area, trains)
+        got = (sums, area, jnp.where(held, shard[1:2, :], 0.0))
         totals = got if totals is None else [total + new for total, new in zip(totals, got)]
     return totals
 
 
 def settle_kernel(slots, owned, speeds_ref, *refs):
-    shards, (sums_ref, area_ref, trains_ref, rows_ref) = (refs[:-4], refs[-4:])
+    *shards, sums_ref, area_ref, trains_ref, rows_ref = refs
     mark = rows_ref.shape[1]
     for train in range(speeds_ref.shape[0]):
         for c in range(3):
@@ -476,7 +475,7 @@
     ids, mine, own_trains = wanted_labels(own_ref, slots, owned)
     sums, area, trains = totals
     trains = jnp.broadcast_to(jnp.sum(trains, axis=1, keepdims=True), area.shape)
-    own_area = own_ref[3 * slots : 3 * slots + owned, :]
+    own_area = own_ref[8 : 8 + owned, :]
     forces, own_forces = ([], [])
     for c in range(3):
         target, own_target = (jnp.zeros_like(area), jnp.zeros_like(own_area))
@@ -494,7 +493,8 @@
 def spread_kernel(
     slots, owned, place_ref, own_ref, last_ref, sums_ref, area_ref, trains_ref, speeds_ref,
     cells_ref, weights_ref, pop_ref, solid_ref,
-    relaxed_ref, far_ref, near_ref, side_ref, marker_ref, force_ref, lines_ref, acc,
+    relaxed_ref, far_ref, near_ref, side_ref, marker_any, marker_ref, force_ref, lines_ref, acc,
+    sem,
 ):
     rows, lanes = (pop_ref.shape[1], pop_ref.shape[2])
     size_y = 8
@@ -502,12 +502,13 @@
     kernel = cells_ref.shape[0] // slots
     bf = jnp.bfloat16
     ids, mine, _ = wanted_labels(own_ref, slots, owned)
-    totals = (sums_ref[...], area_ref[...], trains_ref[...])
-    totals = add_shards(totals, [last_ref], ids, mine)
+    totals = add_shards((sums_ref[...], area_ref[...], trains_ref[...]), [last_ref], ids, mine)
     forces, own_forces = block_forces(speeds_ref, totals, own_ref, slots, owned)
     for c in range(3):
         force_ref[c] = forces[c]
         marker_ref[c] = own_forces[c]
+    marker_copy = pltpu.make_async_copy(marker_ref, marker_any, sem)
+    marker_copy.start()
 
     acc[...] = jnp.zeros_like(acc)
     iota = lax.broadcasted_iota(jnp.int32, (16, mark), 0).astype(jnp.float32)
@@ -577,6 +578,7 @@
             down = relaxed[going(1, -1)[i]][size_y * x : size_y * x + 1, :]
             at = rows // size_y * i + x
             side_ref[at : at + 1, :] = jnp.where(place_ref[0] == 0, up, down)
+    marker_copy.wait()
 
 
 def spread(owned, place, own, last, early, cells, weights, populations, solid):
@@ -595,10 +597,13 @@
             full((3, owned, mark)),
         ),
         in_specs=[smem] + [vmem] * 10,
+        out_specs=[vmem] * 4 + [pl.BlockSpec(memory_space=pltpu.HBM)],
         scratch_shapes=[
+            pltpu.VMEM((3, owned, mark), jnp.float32),
             pltpu.VMEM((3, slots, mark), jnp.float32),
             pltpu.VMEM((cells.shape[0] // slots, 8, group, mark), jnp.float32),
             pltpu.VMEM((6 * line_count, lanes), jnp.float32),
+            pltpu.SemaphoreType.DMA,
         ],
         compiler_params=kernel_params(),
         name="spread",
@@ -800,12 +805,14 @@
     def across_y(entries):
         return lax.ppermute(entries, "gy", swap)
 
-    shards = {0: own}
-    for distance in reversed(range(1, count_x)):
-        shards[distance] = across_x(own, distance)
-    beside = {distance: across_y(shards[distance]) for distance in (0, 1, 3, 2)}
-    last = beside.pop(2)
-    early = settle_early(slots, owned, train_velocity, [*shards.values(), *beside.values()])
+    third, first = (across_x(own, distance) for distance in (3, 1))
+    beside = across_y(own)
+    third_beside = across_y(lax.optimization_barrier((third, beside))[0])
+    second = across_x(third, 1)
+    first_beside = across_y(first)
+    last = across_x(third_beside, 1)
+    whole = [own, first, third, second, beside, first_beside, third_beside]
+    early = settle_early(slots, owned, train_velocity, whole)
     solid = solid_cells.reshape(lines, size_z)
     relaxed, far, near, side, marker_force = spread(
         owned, place, own, last, early, cells, weights, pops, solid

time: 51.2 us -> 50.8 us (level)
  waiting for transfers between devices: 11.8 us -> 10.2 us
  starting transfers between devices: 20.3 us -> 21.4 us
    ppermute x3 -> x4, waiting for transfers between devices: 7.74 us -> 3.89 us  [across_x(): lax.ppermute(entries, 'gx', [(i, i ^ distance) for i in range(count_x)])]
    ppermute x6 -> x5, waiting for transfers between devices: 3.94 us -> 5.53 us  [across_y(): return lax.ppermute(entries, 'gy', swap)]
    ppermute x1, starting transfers between devices: 7.13 us -> 8.66 us  [per_device(): lax.ppermute(down_first, 'gz', outer + [(j, i) for i, j in outer])]
    ppermute x3 -> x4, starting transfers between devices: 4.5 us -> 5.38 us  [across_x(): lax.ppermute(entries, 'gx', [(i, i ^ distance) for i in range(count_x)])]
    ppermute x1, starting transfers between devices: 2.04 us -> 1.29 us  [per_device(): lax.ppermute(far, 'gx', [(i, (i - 1) % count_x) for i in evens] + [((i -...]
    ppermute x1, waiting for transfers between devices: 0.01 us -> 0.56 us  [per_device(): lax.ppermute(down_first, 'gz', outer + [(j, i) for i, j in outer])]
    ppermute x6 -> x5, starting transfers between devices: 6.6 us -> 6.1 us  [across_y(): return lax.ppermute(entries, 'gy', swap)]
  transfers between devices with their start and end apart: 13 -> 13, of which waited for: 6 -> 10; matrix products, arithmetic and copies ran while one was open for 0% -> 0% of each run, Pallas kernels for 2% -> 2%
where the time goes in v6:
time: 50.8 us; the launch traced here: 50.6 us
  starting transfers between devices  21.4 us (42%)
  Pallas kernels  18.2 us (36%)
  waiting for transfers between devices  10.2 us (20%)
  between operations  0.7 us (1%)
    pallas_call x1, Pallas kernels, spread(): pl.pallas_call(functools.partial(spread_kernel, slots, owned), out_shape=...  9.05 us
    ppermute x1, starting transfers between devices, per_device(): lax.ppermute(down_first, 'gz', outer + [(j, i) for i, j in outer])  8.66 us
    ppermute x5, starting transfers between devices, across_y(): return lax.ppermute(entries, 'gy', swap)  6.1 us
    pallas_call x1, Pallas kernels, sample(): pl.pallas_call(sample_kernel, out_shape=[full((count, cells.shape[1]))] +...  5.9 us
    ppermute x5, waiting for transfers between devices, across_y(): return lax.ppermute(entries, 'gy', swap)  5.53 us
    ppermute x4, starting transfers between devices, across_x(): lax.ppermute(entries, 'gx', [(i, i ^ distance) for i in range(count_x)])  5.38 us
    ppermute x4, waiting for transfers between devices, across_x(): lax.ppermute(entries, 'gx', [(i, i ^ distance) for i in range(count_x)])  3.89 us
    pallas_call x1, Pallas kernels, stream(): pl.pallas_call(functools.partial(stream_kernel, count_z), out_shape=full(...  1.47 us
  transfers between devices with their start and end apart: 13, of which 10 were waited for; matrix products, arithmetic and copies ran while one was open for 0% of the time, Pallas kernels for 2%

profile of v6, /device:TPU:1, one launch (start us, length us, event | category | flops | bytes accessed | tf_op | source)
XLA Modules:
  0.0 50.6 jit_solution(14553069973127610489)
XLA Ops:
  0.6 0.1 pad_add_fusion.place_ref
  0.7 0.0 copy-start.1
  0.7 5.9 %sample.1 = (f32[232,128]{1,0:T(8,128)S(1)}, f32[19,32,128]{2,1,0:T(8,128)S(1)}, s32[512,128]{1,0:T(8,128)S(1)}, f32[512,128]{1,0:T(8,128)S(1)}) custom-call(s32[4]{0:T(128)S(1)} %pad_add_fusion.place_ref, f32[19,32,128]{2,1,0:T(8,128)} %bitcast.16, s32[512,128]{1,0:T(8,128)} %bitcast.17, f32[512,128]{1,0:T(8,128)} %bitcast.18, f32[32,128]{1,0:T(8,128)} %bitcast.19, ...), custom_call_target="tpu_custom_call" | custom-call | tf_op jit(solution)/shard_map/sample/pallas_call | solution.py:382
  6.6 4.2 %collective-permute-start = (f32[232,128]{1,0:T(8,128)S(1)}, f32[232,128]{1,0:T(8,128)S(1)}, u32[]{:S(2)}, u32[]{:S(2)}) collective-permute-start(f32[232,128]{1,0:T(8,128)S(1)} %get-tuple-element.19.refs_0_.own_ref), channel_id=1, source_target_pairs={{0,24},{8,16},{16,8},{24,0},{1,25},{9,17},{17,9},{25,1},{2,26},{10... | collective-permute-start | bytes 356360 | tf_op jit(solution)/shard_map/ppermute | solution.py:803
  10.8 1.2 %collective-permute-start.1 = (f32[232,128]{1,0:T(8,128)S(1)}, f32[232,128]{1,0:T(8,128)S(1)}, u32[]{:S(2)}, u32[]{:S(2)}) collective-permute-start(f32[232,128]{1,0:T(8,128)S(1)} %get-tuple-element.19.refs_0_.own_ref), channel_id=1, source_target_pairs={{0,4},{4,0},{1,5},{5,1},{2,6},{6,2},{3,7},{7,3},{8,12},{12,8},{9,1... | collective-permute-start | bytes 356360 | tf_op jit(solution)/shard_map/ppermute | solution.py:806
  12.1 0.0 collective-permute-start.4
  12.1 1.8 %collective-permute-done.refs_2_ = f32[232,128]{1,0:T(8,128)S(1)} collective-permute-done((f32[232,128]{1,0:T(8,128)S(1)}, f32[232,128]{1,0:T(8,128)S(1)}, u32[]{:S(2)}, u32[]{:S(2)}) %collective-permute-start) | collective-permute-done | bytes 118816 | tf_op jit(solution)/shard_map/ppermute | solution.py:803
  13.8 1.0 %collective-permute-done.1.refs_4_ = f32[232,128]{1,0:T(8,128)S(1)} collective-permute-done((f32[232,128]{1,0:T(8,128)S(1)}, f32[232,128]{1,0:T(8,128)S(1)}, u32[]{:S(2)}, u32[]{:S(2)}) %collective-permute-start.1) | collective-permute-done | bytes 118816 | tf_op jit(solution)/shard_map/ppermute | solution.py:806
  14.8 1.2 %collective-permute-start.2 = (f32[232,128]{1,0:T(8,128)S(1)}, f32[232,128]{1,0:T(8,128)S(1)}, u32[]{:S(2)}, u32[]{:S(2)}) collective-permute-start(f32[232,128]{1,0:T(8,128)S(1)} %collective-permute-done.refs_2_), channel_id=1, source_target_pairs={{0,4},{4,0},{1,5},{5,1},{2,6},{6,2},{3,7},{7,3},{8,12},{12,8},{9,1... | collective-permute-start | bytes 356360 | tf_op jit(solution)/shard_map/ppermute | solution.py:806
  16.0 0.5 collective-permute-start.5
  16.5 0.0 collective-permute-done.4.refs_1_
  16.5 1.1 %collective-permute-start.6 = (f32[232,128]{1,0:T(8,128)S(1)}, f32[232,128]{1,0:T(8,128)S(1)}, u32[]{:S(2)}, u32[]{:S(2)}) collective-permute-start(f32[232,128]{1,0:T(8,128)S(1)} %collective-permute-done.4.refs_1_), channel_id=1, source_target_pairs={{0,4},{4,0},{1,5},{5,1},{2,6},{6,2},{3,7},{7,3},{8,12},{12,8},{9,1... | collective-permute-start | bytes 356360 | tf_op jit(solution)/shard_map/ppermute | solution.py:806
  17.6 0.9 %collective-permute-done.2.refs_6_ = f32[232,128]{1,0:T(8,128)S(1)} collective-permute-done((f32[232,128]{1,0:T(8,128)S(1)}, f32[232,128]{1,0:T(8,128)S(1)}, u32[]{:S(2)}, u32[]{:S(2)}) %collective-permute-start.2) | collective-permute-done | bytes 118816 | tf_op jit(solution)/shard_map/ppermute | solution.py:806
  18.5 0.7 %collective-permute-start.3 = (f32[232,128]{1,0:T(8,128)S(1)}, f32[232,128]{1,0:T(8,128)S(1)}, u32[]{:S(2)}, u32[]{:S(2)}) collective-permute-start(f32[232,128]{1,0:T(8,128)S(1)} %collective-permute-done.2.refs_6_), channel_id=1, source_target_pairs={{0,8},{8,0},{16,24},{24,16},{1,9},{9,1},{17,25},{25,17},{2,10},{10... | collective-permute-start | bytes 356360 | tf_op jit(solution)/shard_map/ppermute | solution.py:803
  19.2 0.8 %collective-permute-done.5.refs_3_ = f32[232,128]{1,0:T(8,128)S(1)} collective-permute-done((f32[232,128]{1,0:T(8,128)S(1)}, f32[232,128]{1,0:T(8,128)S(1)}, u32[]{:S(2)}, u32[]{:S(2)}) %collective-permute-start.5) | collective-permute-done | bytes 118816 | tf_op jit(solution)/shard_map/ppermute | solution.py:803
  20.0 1.3 %collective-permute-done.6.refs_5_ = f32[232,128]{1,0:T(8,128)S(1)} collective-permute-done((f32[232,128]{1,0:T(8,128)S(1)}, f32[232,128]{1,0:T(8,128)S(1)}, u32[]{:S(2)}, u32[]{:S(2)}) %collective-permute-start.6) | collective-permute-done | bytes 118816 | tf_op jit(solution)/shard_map/ppermute | solution.py:806
  21.3 0.0 copy-done.1
  21.3 0.0 copy-start
  21.3 1.1 %settle.1 = (f32[96,384]{1,0:T(8,128)S(1)}, f32[64,128]{1,0:T(8,128)S(1)}, f32[64,128]{1,0:T(8,128)S(1)}, f32[12,128]{1,0:T(8,128)S(1)}) custom-call(f32[4,3]{1,0:T(4,128)S(1)} %copy-done.1, f32[232,128]{1,0:T(8,128)S(1)} %get-tuple-element.19.refs_0_.own_ref, f32[232,128]{1,0:T(8,128)S(1)} %collective-permute-done.4.refs_1_, ...), custom_call_target="tpu_custom_call" | custom-call | flops 1000000000 | bytes 831488 | tf_op jit(solution)/shard_map/settle/pallas_call | solution.py:456
  22.4 1.3 %collective-permute-done.3.last_ref = f32[232,128]{1,0:T(8,128)S(1)} collective-permute-done((f32[232,128]{1,0:T(8,128)S(1)}, f32[232,128]{1,0:T(8,128)S(1)}, u32[]{:S(2)}, u32[]{:S(2)}) %collective-permute-start.3) | collective-permute-done | bytes 118816 | tf_op jit(solution)/shard_map/ppermute | solution.py:803
  23.7 0.0 copy-done
  23.7 9.1 %spread.1 = (f32[19,32,128]{2,1,0:T(8,128)S(1)}, f32[5,8,128]{2,1,0:T(8,128)S(1)}, f32[5,8,128]{2,1,0:T(8,128)S(1)}, f32[24,128]{1,0:T(8,128)S(1)}, f32[3,32,128]{2,1,0:T(8,128)}) custom-call(s32[4]{0:T(128)S(1)} %pad_add_fusion.place_ref, f32[232,128]{1,0:T(8,128)S(1)} %get-tuple-element.19.refs_0_.own_ref, f32[232,128]{1,0:T(8,128)S(1)} %collective-permute-done.3.last_ref, ...), custom_call_target="tpu_custom_call" | custom-call | tf_op jit(solution)/shard_map/spread/pallas_call | solution.py:590
  32.8 1.3 %collective-permute-start.7 = (f32[5,8,128]{2,1,0:T(8,128)S(1)}, f32[5,8,128]{2,1,0:T(8,128)S(1)}, u32[]{:S(2)}, u32[]{:S(2)}) collective-permute-start(f32[5,8,128]{2,1,0:T(8,128)S(1)} %get-tuple-element.29), channel_id=1, source_target_pairs={{0,24},{16,8},{24,0},{8,16},{1,25},{17,9},{25,1},{9,17},{2,26},{18... | collective-permute-start | bytes 61448 | tf_op jit(solution)/shard_map/ppermute | solution.py:821
  34.1 0.0 collective-permute-start.8
  34.1 1.9 %collective-permute-start.9 = (f32[24,128]{1,0:T(8,128)S(1)}, f32[24,128]{1,0:T(8,128)S(1)}, u32[]{:S(2)}, u32[]{:S(2)}) collective-permute-start(f32[24,128]{1,0:T(8,128)S(1)} %get-tuple-element.31), channel_id=1, source_target_pairs={{0,4},{4,0},{1,5},{5,1},{2,6},{6,2},{3,7},{7,3},{8,12},{12,8},{9,1... | collective-permute-start | bytes 36872 | tf_op jit(solution)/shard_map/ppermute | solution.py:806
  35.9 1.1 %collective-permute-done.9.side_ref = f32[24,128]{1,0:T(8,128)S(1)} collective-permute-done((f32[24,128]{1,0:T(8,128)S(1)}, f32[24,128]{1,0:T(8,128)S(1)}, u32[]{:S(2)}, u32[]{:S(2)}) %collective-permute-start.9) | collective-permute-done | bytes 12320 | tf_op jit(solution)/shard_map/ppermute | solution.py:806
  37.0 0.2 collective-permute-done.7.far_ref
  37.3 0.0 collective-permute-done.8.near_ref
  37.3 0.7 %pack.1 = (f32[8,128]{1,0:T(8,128)S(1)}, f32[8,128]{1,0:T(8,128)S(1)}, f32[8,128]{1,0:T(8,128)S(1)}) custom-call(s32[4]{0:T(128)S(1)} %pad_add_fusion.place_ref, f32[19,32,128]{2,1,0:T(8,128)S(1)} %get-tuple-element.28.relaxed_ref, f32[5,8,128]{2,1,0:T(8,128)S(1)} %collective-permute-done.7.far_ref, f32[5,8,128]{2,1,0:T(8,128)S(1)} %collective-permute-done.8.near_ref, ...), custom_call_target="tpu_custom_call" | custom-call | tf_op jit(solution)/shard_map/pack/pallas_call | solution.py:700
  37.9 8.7 %collective-permute-start.10 = (f32[8,128]{1,0:T(8,128)S(1)}, f32[8,128]{1,0:T(8,128)S(1)}, u32[]{:S(2)}, u32[]{:S(2)}) collective-permute-start(f32[8,128]{1,0:T(8,128)S(1)} %get-tuple-element.32), channel_id=1, source_target_pairs={{1,2},{2,1},{5,6},{6,5},{9,10},{10,9},{13,14},{14,13},{17,18},{18,... | collective-permute-start | bytes 12296 | tf_op jit(solution)/shard_map/ppermute | solution.py:831
  46.6 0.7 %collective-permute-start.11 = (f32[8,128]{1,0:T(8,128)S(1)}, f32[8,128]{1,0:T(8,128)S(1)}, u32[]{:S(2)}, u32[]{:S(2)}) collective-permute-start(f32[8,128]{1,0:T(8,128)S(1)} %get-tuple-element.33), channel_id=1, source_target_pairs={{0,4},{4,0},{1,5},{5,1},{2,6},{6,2},{3,7},{7,3},{8,12},{12,8},{9,1... | collective-permute-start | bytes 12296 | tf_op jit(solution)/shard_map/ppermute | solution.py:806
  47.3 0.0 collective-permute-start.12
  47.3 0.6 %collective-permute-done.10.second_ref = f32[8,128]{1,0:T(8,128)S(1)} collective-permute-done((f32[8,128]{1,0:T(8,128)S(1)}, f32[8,128]{1,0:T(8,128)S(1)}, u32[]{:S(2)}, u32[]{:S(2)}) %collective-permute-start.10) | collective-permute-done | bytes 4128 | tf_op jit(solution)/shard_map/ppermute | solution.py:831
  47.9 1.2 %collective-permute-done.11.corner_ref = f32[8,128]{1,0:T(8,128)S(1)} collective-permute-done((f32[8,128]{1,0:T(8,128)S(1)}, f32[8,128]{1,0:T(8,128)S(1)}, u32[]{:S(2)}, u32[]{:S(2)}) %collective-permute-start.11) | collective-permute-done | bytes 4128 | tf_op jit(solution)/shard_map/ppermute | solution.py:806
  49.1 0.0 collective-permute-done.12.first_ref
  49.1 1.5 %stream.1 = f32[19,4,8,128]{3,2,1,0:T(8,128)} custom-call(s32[4]{0:T(128)S(1)} %pad_add_fusion.place_ref, f32[19,32,128]{2,1,0:T(8,128)S(1)} %get-tuple-element.28.relaxed_ref, f32[5,8,128]{2,1,0:T(8,128)S(1)} %collective-permute-done.7.far_ref, f32[5,8,128]{2,1,0:T(8,128)S(1)} %collective-permute-done.8.near_ref, ...), custom_call_target="tpu_custom_call" | custom-call | tf_op jit(solution)/shard_map/stream/pallas_call | solution.py:757
Async XLA Ops:
  0.7 20.6 %copy-start.1 = (f32[4,3]{1,0:T(4,128)S(1)}, f32[4,3]{1,0:T(4,128)}, u32[]{:S(2)}) copy-start(f32[4,3]{1,0:T(4,128)} %speeds_ref.1) | copy-start | bytes 148
  6.6 7.2 %collective-permute-start = (f32[232,128]{1,0:T(8,128)S(1)}, f32[232,128]{1,0:T(8,128)S(1)}, u32[]{:S(2)}, u32[]{:S(2)}) collective-permute-start(f32[232,128]{1,0:T(8,128)S(1)} %get-tuple-element.19.refs_0_.own_ref), channel_id=1, source_target_pairs={{0,24},{8,16},{16,8},{24,0},{1,25},{9,17},{17,9},{25,1},{2,26},{10... | collective-permute-start | bytes 356360 | tf_op jit(solution)/shard_map/ppermute | solution.py:803
  10.8 4.0 %collective-permute-start.1 = (f32[232,128]{1,0:T(8,128)S(1)}, f32[232,128]{1,0:T(8,128)S(1)}, u32[]{:S(2)}, u32[]{:S(2)}) collective-permute-start(f32[232,128]{1,0:T(8,128)S(1)} %get-tuple-element.19.refs_0_.own_ref), channel_id=1, source_target_pairs={{0,4},{4,0},{1,5},{5,1},{2,6},{6,2},{3,7},{7,3},{8,12},{12,8},{9,1... | collective-permute-start | bytes 356360 | tf_op jit(solution)/shard_map/ppermute | solution.py:806
  12.1 4.5 %collective-permute-start.4 = (f32[232,128]{1,0:T(8,128)S(1)}, f32[232,128]{1,0:T(8,128)S(1)}, u32[]{:S(2)}, u32[]{:S(2)}) collective-permute-start(f32[232,128]{1,0:T(8,128)S(1)} %get-tuple-element.19.refs_0_.own_ref), channel_id=1, source_target_pairs={{0,8},{8,0},{16,24},{24,16},{1,9},{9,1},{17,25},{25,17},{2,10},{10... | collective-permute-start | bytes 356360 | tf_op jit(solution)/shard_map/ppermute | solution.py:803
  14.8 3.7 %collective-permute-start.2 = (f32[232,128]{1,0:T(8,128)S(1)}, f32[232,128]{1,0:T(8,128)S(1)}, u32[]{:S(2)}, u32[]{:S(2)}) collective-permute-start(f32[232,128]{1,0:T(8,128)S(1)} %collective-permute-done.refs_2_), channel_id=1, source_target_pairs={{0,4},{4,0},{1,5},{5,1},{2,6},{6,2},{3,7},{7,3},{8,12},{12,8},{9,1... | collective-permute-start | bytes 356360 | tf_op jit(solution)/shard_map/ppermute | solution.py:806
  16.0 4.0 %collective-permute-start.5 = (f32[232,128]{1,0:T(8,128)S(1)}, f32[232,128]{1,0:T(8,128)S(1)}, u32[]{:S(2)}, u32[]{:S(2)}) collective-permute-start(f32[232,128]{1,0:T(8,128)S(1)} %collective-permute-done.refs_2_), channel_id=1, source_target_pairs={{0,8},{8,0},{16,24},{24,16},{1,9},{9,1},{17,25},{25,17},{2,10},{10... | collective-permute-start | bytes 356360 | tf_op jit(solution)/shard_map/ppermute | solution.py:803
  16.5 4.8 %collective-permute-start.6 = (f32[232,128]{1,0:T(8,128)S(1)}, f32[232,128]{1,0:T(8,128)S(1)}, u32[]{:S(2)}, u32[]{:S(2)}) collective-permute-start(f32[232,128]{1,0:T(8,128)S(1)} %collective-permute-done.4.refs_1_), channel_id=1, source_target_pairs={{0,4},{4,0},{1,5},{5,1},{2,6},{6,2},{3,7},{7,3},{8,12},{12,8},{9,1... | collective-permute-start | bytes 356360 | tf_op jit(solution)/shard_map/ppermute | solution.py:806
  18.5 5.2 %collective-permute-start.3 = (f32[232,128]{1,0:T(8,128)S(1)}, f32[232,128]{1,0:T(8,128)S(1)}, u32[]{:S(2)}, u32[]{:S(2)}) collective-permute-start(f32[232,128]{1,0:T(8,128)S(1)} %collective-permute-done.2.refs_6_), channel_id=1, source_target_pairs={{0,8},{8,0},{16,24},{24,16},{1,9},{9,1},{17,25},{25,17},{2,10},{10... | collective-permute-start | bytes 356360 | tf_op jit(solution)/shard_map/ppermute | solution.py:803
  21.3 2.4 %copy-start = (s32[4,8,128]{2,1,0:T(8,128)S(1)}, s32[4,8,128]{2,1,0:T(8,128)}, u32[]{:S(2)}) copy-start(s32[4,8,128]{2,1,0:T(8,128)} %param.10) | copy-start | bytes 49156
  32.8 4.5 %collective-permute-start.7 = (f32[5,8,128]{2,1,0:T(8,128)S(1)}, f32[5,8,128]{2,1,0:T(8,128)S(1)}, u32[]{:S(2)}, u32[]{:S(2)}) collective-permute-start(f32[5,8,128]{2,1,0:T(8,128)S(1)} %get-tuple-element.29), channel_id=1, source_target_pairs={{0,24},{16,8},{24,0},{8,16},{1,25},{17,9},{25,1},{9,17},{2,26},{18... | collective-permute-start | bytes 61448 | tf_op jit(solution)/shard_map/ppermute | solution.py:821
  34.1 3.2 %collective-permute-start.8 = (f32[5,8,128]{2,1,0:T(8,128)S(1)}, f32[5,8,128]{2,1,0:T(8,128)S(1)}, u32[]{:S(2)}, u32[]{:S(2)}) collective-permute-start(f32[5,8,128]{2,1,0:T(8,128)S(1)} %get-tuple-element.30), channel_id=1, source_target_pairs={{0,8},{16,24},{8,0},{24,16},{1,9},{17,25},{9,1},{25,17},{2,10},{18... | collective-permute-start | bytes 61448 | tf_op jit(solution)/shard_map/ppermute | solution.py:826
  34.1 3.0 %collective-permute-start.9 = (f32[24,128]{1,0:T(8,128)S(1)}, f32[24,128]{1,0:T(8,128)S(1)}, u32[]{:S(2)}, u32[]{:S(2)}) collective-permute-start(f32[24,128]{1,0:T(8,128)S(1)} %get-tuple-element.31), channel_id=1, source_target_pairs={{0,4},{4,0},{1,5},{5,1},{2,6},{6,2},{3,7},{7,3},{8,12},{12,8},{9,1... | collective-permute-start | bytes 36872 | tf_op jit(solution)/shard_map/ppermute | solution.py:806
  37.9 9.9 %collective-permute-start.10 = (f32[8,128]{1,0:T(8,128)S(1)}, f32[8,128]{1,0:T(8,128)S(1)}, u32[]{:S(2)}, u32[]{:S(2)}) collective-permute-start(f32[8,128]{1,0:T(8,128)S(1)} %get-tuple-element.32), channel_id=1, source_target_pairs={{1,2},{2,1},{5,6},{6,5},{9,10},{10,9},{13,14},{14,13},{17,18},{18,... | collective-permute-start | bytes 12296 | tf_op jit(solution)/shard_map/ppermute | solution.py:831
  46.6 2.5 %collective-permute-start.11 = (f32[8,128]{1,0:T(8,128)S(1)}, f32[8,128]{1,0:T(8,128)S(1)}, u32[]{:S(2)}, u32[]{:S(2)}) collective-permute-start(f32[8,128]{1,0:T(8,128)S(1)} %get-tuple-element.33), channel_id=1, source_target_pairs={{0,4},{4,0},{1,5},{5,1},{2,6},{6,2},{3,7},{7,3},{8,12},{12,8},{9,1... | collective-permute-start | bytes 12296 | tf_op jit(solution)/shard_map/ppermute | solution.py:806
  47.3 1.8 %collective-permute-start.12 = (f32[8,128]{1,0:T(8,128)S(1)}, f32[8,128]{1,0:T(8,128)S(1)}, u32[]{:S(2)}, u32[]{:S(2)}) collective-permute-start(f32[8,128]{1,0:T(8,128)S(1)} %get-tuple-element.34), channel_id=1, source_target_pairs={{0,1},{2,3},{1,0},{3,2},{4,5},{6,7},{5,4},{7,6},{8,9},{10,11},{9,8... | collective-permute-start | bytes 12296 | tf_op jit(solution)/shard_map/ppermute | solution.py:833

commit v7 on v6

--- a/solution.py
+++ b/solution.py
@@ -300,11 +300,13 @@
     owned = areas_ref.shape[0]
     slots = owner_ref.shape[1]
     kernel = cells_ref.shape[0] // slots
+    planes = [pl.ds(at, min(5, 19 - at)) for at in range(0, 19, 5)]
+    halves = [pl.ds(at, slots * kernel // 2) for at in (0, slots * kernel // 2)]
     copies = fetch(
         (
-            (pop_any, pop_ref),
-            (cells_any, cells_ref),
-            (weights_any, weights_ref),
+            *((pop_any.at[part], pop_ref.at[part]) for part in planes),
+            *((cells_any.at[part], cells_ref.at[part]) for part in halves),
+            *((weights_any.at[part], weights_ref.at[part]) for part in halves),
             (areas_any, areas_ref),
             (owner_any, owner_ref),
             (block_any, block_ref),
@@ -313,7 +315,8 @@
         sems,
     )
 
-    copies[0].wait()
+    for copy in copies[: len(planes)]:
+        copy.wait()
     density, momentum = moments([pop_ref[q] for q in range(19)])
     speed = [momentum[c] / density for c in range(3)]
     largest = jnp.maximum(jnp.maximum(jnp.abs(speed[0]), jnp.abs(speed[1])), jnp.abs(speed[2]))
@@ -329,7 +332,7 @@
     )
     for r in range(table.shape[0]):
         table[r] = jnp.broadcast_to(words[r : r + 1], (group, lanes))
-    for copy in copies[1:]:
+    for copy in copies[len(planes) :]:
         copy.wait()
     out_ref[8 : 8 + owned, :] = areas_ref[...]
     out_ref[0:8, :] = jnp.zeros((8, mark), jnp.float32)
@@ -390,7 +393,7 @@
         ]
         + [
             pltpu.VMEM((populations.shape[1] * 3 // 2, group, populations.shape[2]), jnp.int32),
-            pltpu.SemaphoreType.DMA((7,)),
+            pltpu.SemaphoreType.DMA((12,)),
         ],
         compiler_params=kernel_params(),
         name="sample",
@@ -518,6 +521,7 @@
     def body(step, carry):
         first = pl.multiple_of(step * group, group)
         force = [force_ref[c, pl.ds(first, group), :] for c in range(3)]
+        left, right = ([], [])
         for k in range(kernel):
             at = pl.ds(first * kernel + k, group, stride=kernel)
             cells = cells_ref[at, :]
@@ -532,11 +536,10 @@
             for which, entries in enumerate([lane, row] + parts):
                 lines_ref[k, which] = entries
 
-            def wide(which, i):
+            def wide(which, i, k=k):
                 entries = lines_ref[k, which, pl.ds(i, 8, stride=0), :]
                 return jnp.concatenate([entries, entries], axis=0).astype(bf)
 
-            left, right = ([], [])
             for i in range(group):
                 lane_i, row_i = (wide(0, i), wide(1, i))
                 right.append(
@@ -551,12 +554,12 @@
                     part_i = wide(2 + which, i)
                     pieces += [jnp.where(mask, part_i, zero) for mask in masks]
                 left.append(jnp.concatenate(pieces, axis=0))
-            acc[...] += lax.dot_general(
-                jnp.concatenate(left, axis=1),
-                jnp.concatenate(right, axis=1),
-                (((1,), (1,)), ((), ())),
-                preferred_element_type=jnp.float32,
-            )
+        acc[...] += lax.dot_general(
+            jnp.concatenate(left, axis=1),
+            jnp.concatenate(right, axis=1),
+            (((1,), (1,)), ((), ())),
+            preferred_element_type=jnp.float32,
+        )
         return carry
 
     lax.fori_loop(0, slots // group, body, 0)

time: 50.8 us -> 51 us (level)
  no operation moved by 1% of the time
where the time goes in v7:
time: 51 us; the launch traced here: 50.9 us
  starting transfers between devices  21.4 us (42%)
  Pallas kernels  18.5 us (36%)
  waiting for transfers between devices  10.2 us (20%)
  between operations  0.7 us (1%)
    pallas_call x1, Pallas kernels, spread(): pl.pallas_call(functools.partial(spread_kernel, slots, owned), out_shape=...  9.23 us
    ppermute x1, starting transfers between devices, per_device(): lax.ppermute(down_first, 'gz', outer + [(j, i) for i, j in outer])  8.66 us
    ppermute x5, starting transfers between devices, across_y(): return lax.ppermute(entries, 'gy', swap)  6.1 us
    pallas_call x1, Pallas kernels, sample(): pl.pallas_call(sample_kernel, out_shape=[full((count, cells.shape[1]))] +...  6.01 us
    ppermute x5, waiting for transfers between devices, across_y(): return lax.ppermute(entries, 'gy', swap)  5.53 us
    ppermute x4, starting transfers between devices, across_x(): lax.ppermute(entries, 'gx', [(i, i ^ distance) for i in range(count_x)])  5.38 us
    ppermute x4, waiting for transfers between devices, across_x(): lax.ppermute(entries, 'gx', [(i, i ^ distance) for i in range(count_x)])  3.89 us
    pallas_call x1, Pallas kernels, stream(): pl.pallas_call(functools.partial(stream_kernel, count_z), out_shape=full(...  1.47 us
  transfers between devices with their start and end apart: 13, of which 10 were waited for; matrix products, arithmetic and copies ran while one was open for 0% of the time, Pallas kernels for 2%

profile of v7, /device:TPU:1, one launch (start us, length us, event | category | flops | bytes accessed | tf_op | source)
XLA Modules:
  0.0 50.9 jit_solution(7264177060059906526)
XLA Ops:
  0.6 0.1 pad_add_fusion.place_ref
  0.7 0.0 copy-start.1
  0.7 6.0 %sample.1 = (f32[232,128]{1,0:T(8,128)S(1)}, f32[19,32,128]{2,1,0:T(8,128)S(1)}, s32[512,128]{1,0:T(8,128)S(1)}, f32[512,128]{1,0:T(8,128)S(1)}) custom-call(s32[4]{0:T(128)S(1)} %pad_add_fusion.place_ref, f32[19,32,128]{2,1,0:T(8,128)} %bitcast.16, s32[512,128]{1,0:T(8,128)} %bitcast.17, f32[512,128]{1,0:T(8,128)} %bitcast.18, f32[32,128]{1,0:T(8,128)} %bitcast.19, ...), custom_call_target="tpu_custom_call" | custom-call | tf_op jit(solution)/shard_map/sample/pallas_call | solution.py:385
  6.7 4.2 %collective-permute-start = (f32[232,128]{1,0:T(8,128)S(1)}, f32[232,128]{1,0:T(8,128)S(1)}, u32[]{:S(2)}, u32[]{:S(2)}) collective-permute-start(f32[232,128]{1,0:T(8,128)S(1)} %get-tuple-element.19.refs_0_.own_ref), channel_id=1, source_target_pairs={{0,24},{8,16},{16,8},{24,0},{1,25},{9,17},{17,9},{25,1},{2,26},{10... | collective-permute-start | bytes 356360 | tf_op jit(solution)/shard_map/ppermute | solution.py:806
  11.0 1.2 %collective-permute-start.1 = (f32[232,128]{1,0:T(8,128)S(1)}, f32[232,128]{1,0:T(8,128)S(1)}, u32[]{:S(2)}, u32[]{:S(2)}) collective-permute-start(f32[232,128]{1,0:T(8,128)S(1)} %get-tuple-element.19.refs_0_.own_ref), channel_id=1, source_target_pairs={{0,4},{4,0},{1,5},{5,1},{2,6},{6,2},{3,7},{7,3},{8,12},{12,8},{9,1... | collective-permute-start | bytes 356360 | tf_op jit(solution)/shard_map/ppermute | solution.py:809
  12.2 0.0 collective-permute-start.4
  12.2 1.8 %collective-permute-done.refs_2_ = f32[232,128]{1,0:T(8,128)S(1)} collective-permute-done((f32[232,128]{1,0:T(8,128)S(1)}, f32[232,128]{1,0:T(8,128)S(1)}, u32[]{:S(2)}, u32[]{:S(2)}) %collective-permute-start) | collective-permute-done | bytes 118816 | tf_op jit(solution)/shard_map/ppermute | solution.py:806
  14.0 1.0 %collective-permute-done.1.refs_4_ = f32[232,128]{1,0:T(8,128)S(1)} collective-permute-done((f32[232,128]{1,0:T(8,128)S(1)}, f32[232,128]{1,0:T(8,128)S(1)}, u32[]{:S(2)}, u32[]{:S(2)}) %collective-permute-start.1) | collective-permute-done | bytes 118816 | tf_op jit(solution)/shard_map/ppermute | solution.py:809
  14.9 1.2 %collective-permute-start.2 = (f32[232,128]{1,0:T(8,128)S(1)}, f32[232,128]{1,0:T(8,128)S(1)}, u32[]{:S(2)}, u32[]{:S(2)}) collective-permute-start(f32[232,128]{1,0:T(8,128)S(1)} %collective-permute-done.refs_2_), channel_id=1, source_target_pairs={{0,4},{4,0},{1,5},{5,1},{2,6},{6,2},{3,7},{7,3},{8,12},{12,8},{9,1... | collective-permute-start | bytes 356360 | tf_op jit(solution)/shard_map/ppermute | solution.py:809
  16.2 0.5 collective-permute-start.5
  16.6 0.0 collective-permute-done.4.refs_1_
  16.6 1.1 %collective-permute-start.6 = (f32[232,128]{1,0:T(8,128)S(1)}, f32[232,128]{1,0:T(8,128)S(1)}, u32[]{:S(2)}, u32[]{:S(2)}) collective-permute-start(f32[232,128]{1,0:T(8,128)S(1)} %collective-permute-done.4.refs_1_), channel_id=1, source_target_pairs={{0,4},{4,0},{1,5},{5,1},{2,6},{6,2},{3,7},{7,3},{8,12},{12,8},{9,1... | collective-permute-start | bytes 356360 | tf_op jit(solution)/shard_map/ppermute | solution.py:809
  17.7 0.9 %collective-permute-done.2.refs_6_ = f32[232,128]{1,0:T(8,128)S(1)} collective-permute-done((f32[232,128]{1,0:T(8,128)S(1)}, f32[232,128]{1,0:T(8,128)S(1)}, u32[]{:S(2)}, u32[]{:S(2)}) %collective-permute-start.2) | collective-permute-done | bytes 118816 | tf_op jit(solution)/shard_map/ppermute | solution.py:809
  18.6 0.7 %collective-permute-start.3 = (f32[232,128]{1,0:T(8,128)S(1)}, f32[232,128]{1,0:T(8,128)S(1)}, u32[]{:S(2)}, u32[]{:S(2)}) collective-permute-start(f32[232,128]{1,0:T(8,128)S(1)} %collective-permute-done.2.refs_6_), channel_id=1, source_target_pairs={{0,8},{8,0},{16,24},{24,16},{1,9},{9,1},{17,25},{25,17},{2,10},{10... | collective-permute-start | bytes 356360 | tf_op jit(solution)/shard_map/ppermute | solution.py:806
  19.3 0.8 %collective-permute-done.5.refs_3_ = f32[232,128]{1,0:T(8,128)S(1)} collective-permute-done((f32[232,128]{1,0:T(8,128)S(1)}, f32[232,128]{1,0:T(8,128)S(1)}, u32[]{:S(2)}, u32[]{:S(2)}) %collective-permute-start.5) | collective-permute-done | bytes 118816 | tf_op jit(solution)/shard_map/ppermute | solution.py:806
  20.1 1.3 %collective-permute-done.6.refs_5_ = f32[232,128]{1,0:T(8,128)S(1)} collective-permute-done((f32[232,128]{1,0:T(8,128)S(1)}, f32[232,128]{1,0:T(8,128)S(1)}, u32[]{:S(2)}, u32[]{:S(2)}) %collective-permute-start.6) | collective-permute-done | bytes 118816 | tf_op jit(solution)/shard_map/ppermute | solution.py:809
  21.4 0.0 copy-done.1
  21.5 0.0 copy-start
  21.5 1.1 %settle.1 = (f32[96,384]{1,0:T(8,128)S(1)}, f32[64,128]{1,0:T(8,128)S(1)}, f32[64,128]{1,0:T(8,128)S(1)}, f32[12,128]{1,0:T(8,128)S(1)}) custom-call(f32[4,3]{1,0:T(4,128)S(1)} %copy-done.1, f32[232,128]{1,0:T(8,128)S(1)} %get-tuple-element.19.refs_0_.own_ref, f32[232,128]{1,0:T(8,128)S(1)} %collective-permute-done.4.refs_1_, ...), custom_call_target="tpu_custom_call" | custom-call | flops 1000000000 | bytes 831488 | tf_op jit(solution)/shard_map/settle/pallas_call | solution.py:459
  22.5 1.3 %collective-permute-done.3.last_ref = f32[232,128]{1,0:T(8,128)S(1)} collective-permute-done((f32[232,128]{1,0:T(8,128)S(1)}, f32[232,128]{1,0:T(8,128)S(1)}, u32[]{:S(2)}, u32[]{:S(2)}) %collective-permute-start.3) | collective-permute-done | bytes 118816 | tf_op jit(solution)/shard_map/ppermute | solution.py:806
  23.8 0.0 copy-done
  23.8 9.2 %spread.1 = (f32[19,32,128]{2,1,0:T(8,128)S(1)}, f32[5,8,128]{2,1,0:T(8,128)S(1)}, f32[5,8,128]{2,1,0:T(8,128)S(1)}, f32[24,128]{1,0:T(8,128)S(1)}, f32[3,32,128]{2,1,0:T(8,128)}) custom-call(s32[4]{0:T(128)S(1)} %pad_add_fusion.place_ref, f32[232,128]{1,0:T(8,128)S(1)} %get-tuple-element.19.refs_0_.own_ref, f32[232,128]{1,0:T(8,128)S(1)} %collective-permute-done.3.last_ref, ...), custom_call_target="tpu_custom_call" | custom-call | tf_op jit(solution)/shard_map/spread/pallas_call | solution.py:593
  33.0 1.3 %collective-permute-start.7 = (f32[5,8,128]{2,1,0:T(8,128)S(1)}, f32[5,8,128]{2,1,0:T(8,128)S(1)}, u32[]{:S(2)}, u32[]{:S(2)}) collective-permute-start(f32[5,8,128]{2,1,0:T(8,128)S(1)} %get-tuple-element.29), channel_id=1, source_target_pairs={{0,24},{16,8},{24,0},{8,16},{1,25},{17,9},{25,1},{9,17},{2,26},{18... | collective-permute-start | bytes 61448 | tf_op jit(solution)/shard_map/ppermute | solution.py:824
  34.3 0.0 collective-permute-start.8
  34.3 1.9 %collective-permute-start.9 = (f32[24,128]{1,0:T(8,128)S(1)}, f32[24,128]{1,0:T(8,128)S(1)}, u32[]{:S(2)}, u32[]{:S(2)}) collective-permute-start(f32[24,128]{1,0:T(8,128)S(1)} %get-tuple-element.31), channel_id=1, source_target_pairs={{0,4},{4,0},{1,5},{5,1},{2,6},{6,2},{3,7},{7,3},{8,12},{12,8},{9,1... | collective-permute-start | bytes 36872 | tf_op jit(solution)/shard_map/ppermute | solution.py:809
  36.2 1.1 %collective-permute-done.9.side_ref = f32[24,128]{1,0:T(8,128)S(1)} collective-permute-done((f32[24,128]{1,0:T(8,128)S(1)}, f32[24,128]{1,0:T(8,128)S(1)}, u32[]{:S(2)}, u32[]{:S(2)}) %collective-permute-start.9) | collective-permute-done | bytes 12320 | tf_op jit(solution)/shard_map/ppermute | solution.py:809
  37.3 0.2 collective-permute-done.7.far_ref
  37.5 0.0 collective-permute-done.8.near_ref
  37.5 0.7 %pack.1 = (f32[8,128]{1,0:T(8,128)S(1)}, f32[8,128]{1,0:T(8,128)S(1)}, f32[8,128]{1,0:T(8,128)S(1)}) custom-call(s32[4]{0:T(128)S(1)} %pad_add_fusion.place_ref, f32[19,32,128]{2,1,0:T(8,128)S(1)} %get-tuple-element.28.relaxed_ref, f32[5,8,128]{2,1,0:T(8,128)S(1)} %collective-permute-done.7.far_ref, f32[5,8,128]{2,1,0:T(8,128)S(1)} %collective-permute-done.8.near_ref, ...), custom_call_target="tpu_custom_call" | custom-call | tf_op jit(solution)/shard_map/pack/pallas_call | solution.py:703
  38.2 8.7 %collective-permute-start.10 = (f32[8,128]{1,0:T(8,128)S(1)}, f32[8,128]{1,0:T(8,128)S(1)}, u32[]{:S(2)}, u32[]{:S(2)}) collective-permute-start(f32[8,128]{1,0:T(8,128)S(1)} %get-tuple-element.32), channel_id=1, source_target_pairs={{1,2},{2,1},{5,6},{6,5},{9,10},{10,9},{13,14},{14,13},{17,18},{18,... | collective-permute-start | bytes 12296 | tf_op jit(solution)/shard_map/ppermute | solution.py:834
  46.9 0.7 %collective-permute-start.11 = (f32[8,128]{1,0:T(8,128)S(1)}, f32[8,128]{1,0:T(8,128)S(1)}, u32[]{:S(2)}, u32[]{:S(2)}) collective-permute-start(f32[8,128]{1,0:T(8,128)S(1)} %get-tuple-element.33), channel_id=1, source_target_pairs={{0,4},{4,0},{1,5},{5,1},{2,6},{6,2},{3,7},{7,3},{8,12},{12,8},{9,1... | collective-permute-start | bytes 12296 | tf_op jit(solution)/shard_map/ppermute | solution.py:809
  47.6 0.0 collective-permute-start.12
  47.6 0.6 %collective-permute-done.10.second_ref = f32[8,128]{1,0:T(8,128)S(1)} collective-permute-done((f32[8,128]{1,0:T(8,128)S(1)}, f32[8,128]{1,0:T(8,128)S(1)}, u32[]{:S(2)}, u32[]{:S(2)}) %collective-permute-start.10) | collective-permute-done | bytes 4128 | tf_op jit(solution)/shard_map/ppermute | solution.py:834
  48.2 1.2 %collective-permute-done.11.corner_ref = f32[8,128]{1,0:T(8,128)S(1)} collective-permute-done((f32[8,128]{1,0:T(8,128)S(1)}, f32[8,128]{1,0:T(8,128)S(1)}, u32[]{:S(2)}, u32[]{:S(2)}) %collective-permute-start.11) | collective-permute-done | bytes 4128 | tf_op jit(solution)/shard_map/ppermute | solution.py:809
  49.4 0.0 collective-permute-done.12.first_ref
  49.4 1.5 %stream.1 = f32[19,4,8,128]{3,2,1,0:T(8,128)} custom-call(s32[4]{0:T(128)S(1)} %pad_add_fusion.place_ref, f32[19,32,128]{2,1,0:T(8,128)S(1)} %get-tuple-element.28.relaxed_ref, f32[5,8,128]{2,1,0:T(8,128)S(1)} %collective-permute-done.7.far_ref, f32[5,8,128]{2,1,0:T(8,128)S(1)} %collective-permute-done.8.near_ref, ...), custom_call_target="tpu_custom_call" | custom-call | tf_op jit(solution)/shard_map/stream/pallas_call | solution.py:760
Async XLA Ops:
  0.7 20.7 %copy-start.1 = (f32[4,3]{1,0:T(4,128)S(1)}, f32[4,3]{1,0:T(4,128)}, u32[]{:S(2)}) copy-start(f32[4,3]{1,0:T(4,128)} %speeds_ref.1) | copy-start | bytes 148
  6.7 7.2 %collective-permute-start = (f32[232,128]{1,0:T(8,128)S(1)}, f32[232,128]{1,0:T(8,128)S(1)}, u32[]{:S(2)}, u32[]{:S(2)}) collective-permute-start(f32[232,128]{1,0:T(8,128)S(1)} %get-tuple-element.19.refs_0_.own_ref), channel_id=1, source_target_pairs={{0,24},{8,16},{16,8},{24,0},{1,25},{9,17},{17,9},{25,1},{2,26},{10... | collective-permute-start | bytes 356360 | tf_op jit(solution)/shard_map/ppermute | solution.py:806
  11.0 4.0 %collective-permute-start.1 = (f32[232,128]{1,0:T(8,128)S(1)}, f32[232,128]{1,0:T(8,128)S(1)}, u32[]{:S(2)}, u32[]{:S(2)}) collective-permute-start(f32[232,128]{1,0:T(8,128)S(1)} %get-tuple-element.19.refs_0_.own_ref), channel_id=1, source_target_pairs={{0,4},{4,0},{1,5},{5,1},{2,6},{6,2},{3,7},{7,3},{8,12},{12,8},{9,1... | collective-permute-start | bytes 356360 | tf_op jit(solution)/shard_map/ppermute | solution.py:809
  12.2 4.5 %collective-permute-start.4 = (f32[232,128]{1,0:T(8,128)S(1)}, f32[232,128]{1,0:T(8,128)S(1)}, u32[]{:S(2)}, u32[]{:S(2)}) collective-permute-start(f32[232,128]{1,0:T(8,128)S(1)} %get-tuple-element.19.refs_0_.own_ref), channel_id=1, source_target_pairs={{0,8},{8,0},{16,24},{24,16},{1,9},{9,1},{17,25},{25,17},{2,10},{10... | collective-permute-start | bytes 356360 | tf_op jit(solution)/shard_map/ppermute | solution.py:806
  14.9 3.7 %collective-permute-start.2 = (f32[232,128]{1,0:T(8,128)S(1)}, f32[232,128]{1,0:T(8,128)S(1)}, u32[]{:S(2)}, u32[]{:S(2)}) collective-permute-start(f32[232,128]{1,0:T(8,128)S(1)} %collective-permute-done.refs_2_), channel_id=1, source_target_pairs={{0,4},{4,0},{1,5},{5,1},{2,6},{6,2},{3,7},{7,3},{8,12},{12,8},{9,1... | collective-permute-start | bytes 356360 | tf_op jit(solution)/shard_map/ppermute | solution.py:809
  16.2 4.0 %collective-permute-start.5 = (f32[232,128]{1,0:T(8,128)S(1)}, f32[232,128]{1,0:T(8,128)S(1)}, u32[]{:S(2)}, u32[]{:S(2)}) collective-permute-start(f32[232,128]{1,0:T(8,128)S(1)} %collective-permute-done.refs_2_), channel_id=1, source_target_pairs={{0,8},{8,0},{16,24},{24,16},{1,9},{9,1},{17,25},{25,17},{2,10},{10... | collective-permute-start | bytes 356360 | tf_op jit(solution)/shard_map/ppermute | solution.py:806
  16.6 4.8 %collective-permute-start.6 = (f32[232,128]{1,0:T(8,128)S(1)}, f32[232,128]{1,0:T(8,128)S(1)}, u32[]{:S(2)}, u32[]{:S(2)}) collective-permute-start(f32[232,128]{1,0:T(8,128)S(1)} %collective-permute-done.4.refs_1_), channel_id=1, source_target_pairs={{0,4},{4,0},{1,5},{5,1},{2,6},{6,2},{3,7},{7,3},{8,12},{12,8},{9,1... | collective-permute-start | bytes 356360 | tf_op jit(solution)/shard_map/ppermute | solution.py:809
  18.6 5.2 %collective-permute-start.3 = (f32[232,128]{1,0:T(8,128)S(1)}, f32[232,128]{1,0:T(8,128)S(1)}, u32[]{:S(2)}, u32[]{:S(2)}) collective-permute-start(f32[232,128]{1,0:T(8,128)S(1)} %collective-permute-done.2.refs_6_), channel_id=1, source_target_pairs={{0,8},{8,0},{16,24},{24,16},{1,9},{9,1},{17,25},{25,17},{2,10},{10... | collective-permute-start | bytes 356360 | tf_op jit(solution)/shard_map/ppermute | solution.py:806
  21.5 2.4 %copy-start = (s32[4,8,128]{2,1,0:T(8,128)S(1)}, s32[4,8,128]{2,1,0:T(8,128)}, u32[]{:S(2)}) copy-start(s32[4,8,128]{2,1,0:T(8,128)} %param.10) | copy-start | bytes 49156
  33.0 4.5 %collective-permute-start.7 = (f32[5,8,128]{2,1,0:T(8,128)S(1)}, f32[5,8,128]{2,1,0:T(8,128)S(1)}, u32[]{:S(2)}, u32[]{:S(2)}) collective-permute-start(f32[5,8,128]{2,1,0:T(8,128)S(1)} %get-tuple-element.29), channel_id=1, source_target_pairs={{0,24},{16,8},{24,0},{8,16},{1,25},{17,9},{25,1},{9,17},{2,26},{18... | collective-permute-start | bytes 61448 | tf_op jit(solution)/shard_map/ppermute | solution.py:824
  34.3 3.2 %collective-permute-start.8 = (f32[5,8,128]{2,1,0:T(8,128)S(1)}, f32[5,8,128]{2,1,0:T(8,128)S(1)}, u32[]{:S(2)}, u32[]{:S(2)}) collective-permute-start(f32[5,8,128]{2,1,0:T(8,128)S(1)} %get-tuple-element.30), channel_id=1, source_target_pairs={{0,8},{16,24},{8,0},{24,16},{1,9},{17,25},{9,1},{25,17},{2,10},{18... | collective-permute-start | bytes 61448 | tf_op jit(solution)/shard_map/ppermute | solution.py:829
  34.3 3.0 %collective-permute-start.9 = (f32[24,128]{1,0:T(8,128)S(1)}, f32[24,128]{1,0:T(8,128)S(1)}, u32[]{:S(2)}, u32[]{:S(2)}) collective-permute-start(f32[24,128]{1,0:T(8,128)S(1)} %get-tuple-element.31), channel_id=1, source_target_pairs={{0,4},{4,0},{1,5},{5,1},{2,6},{6,2},{3,7},{7,3},{8,12},{12,8},{9,1... | collective-permute-start | bytes 36872 | tf_op jit(solution)/shard_map/ppermute | solution.py:809
  38.2 9.9 %collective-permute-start.10 = (f32[8,128]{1,0:T(8,128)S(1)}, f32[8,128]{1,0:T(8,128)S(1)}, u32[]{:S(2)}, u32[]{:S(2)}) collective-permute-start(f32[8,128]{1,0:T(8,128)S(1)} %get-tuple-element.32), channel_id=1, source_target_pairs={{1,2},{2,1},{5,6},{6,5},{9,10},{10,9},{13,14},{14,13},{17,18},{18,... | collective-permute-start | bytes 12296 | tf_op jit(solution)/shard_map/ppermute | solution.py:834
  46.9 2.5 %collective-permute-start.11 = (f32[8,128]{1,0:T(8,128)S(1)}, f32[8,128]{1,0:T(8,128)S(1)}, u32[]{:S(2)}, u32[]{:S(2)}) collective-permute-start(f32[8,128]{1,0:T(8,128)S(1)} %get-tuple-element.33), channel_id=1, source_target_pairs={{0,4},{4,0},{1,5},{5,1},{2,6},{6,2},{3,7},{7,3},{8,12},{12,8},{9,1... | collective-permute-start | bytes 12296 | tf_op jit(solution)/shard_map/ppermute | solution.py:809
  47.6 1.8 %collective-permute-start.12 = (f32[8,128]{1,0:T(8,128)S(1)}, f32[8,128]{1,0:T(8,128)S(1)}, u32[]{:S(2)}, u32[]{:S(2)}) collective-permute-start(f32[8,128]{1,0:T(8,128)S(1)} %get-tuple-element.34), channel_id=1, source_target_pairs={{0,1},{2,3},{1,0},{3,2},{4,5},{6,7},{5,4},{7,6},{8,9},{10,11},{9,8... | collective-permute-start | bytes 12296 | tf_op jit(solution)/shard_map/ppermute | solution.py:836

commit v8 on v6

--- a/solution.py
+++ b/solution.py
@@ -807,9 +807,9 @@
 
     third, first = (across_x(own, distance) for distance in (3, 1))
     beside = across_y(own)
-    third_beside = across_y(lax.optimization_barrier((third, beside))[0])
-    second = across_x(third, 1)
-    first_beside = across_y(first)
+    first_beside = across_x(beside, 1)
+    third_beside = across_y(lax.optimization_barrier((third, beside, first))[0])
+    second = across_x(lax.optimization_barrier((third, first_beside))[0], 1)
     last = across_x(third_beside, 1)
     whole = [own, first, third, second, beside, first_beside, third_beside]
     early = settle_early(slots, owned, train_velocity, whole)

time: 50.8 us -> 52.3 us (1.030)
  waiting for transfers between devices: 10.2 us -> 14.2 us
  starting transfers between devices: 21.4 us -> 19 us
    ppermute x4 -> x5, waiting for transfers between devices: 3.89 us -> 9.29 us  [across_x(): lax.ppermute(entries, 'gx', [(i, i ^ distance) for i in range(count_x)])]
    ppermute x5 -> x4, starting transfers between devices: 6.1 us -> 3.13 us  [across_y(): return lax.ppermute(entries, 'gy', swap)]
    ppermute x5 -> x4, waiting for transfers between devices: 5.53 us -> 3.63 us  [across_y(): return lax.ppermute(entries, 'gy', swap)]
    ppermute x4 -> x5, starting transfers between devices: 5.38 us -> 6.46 us  [across_x(): lax.ppermute(entries, 'gx', [(i, i ^ distance) for i in range(count_x)])]
    ppermute x1, starting transfers between devices: 8.66 us -> 7.79 us  [per_device(): lax.ppermute(down_first, 'gz', outer + [(j, i) for i, j in outer])]
where the time goes in v8:
time: 52.3 us; the launch traced here: 52.2 us
  starting transfers between devices  19 us (36%)
  Pallas kernels  18.2 us (35%)
  waiting for transfers between devices  14.2 us (27%)
  between operations  0.7 us (1%)
    ppermute x5, waiting for transfers between devices, across_x(): lax.ppermute(entries, 'gx', [(i, i ^ distance) for i in range(count_x)])  9.29 us
    pallas_call x1, Pallas kernels, spread(): pl.pallas_call(functools.partial(spread_kernel, slots, owned), out_shape=...  9.05 us
    ppermute x1, starting transfers between devices, per_device(): lax.ppermute(down_first, 'gz', outer + [(j, i) for i, j in outer])  7.79 us
    ppermute x5, starting transfers between devices, across_x(): lax.ppermute(entries, 'gx', [(i, i ^ distance) for i in range(count_x)])  6.46 us
    pallas_call x1, Pallas kernels, sample(): pl.pallas_call(sample_kernel, out_shape=[full((count, cells.shape[1]))] +...  5.9 us
    ppermute x4, waiting for transfers between devices, across_y(): return lax.ppermute(entries, 'gy', swap)  3.63 us
    ppermute x4, starting transfers between devices, across_y(): return lax.ppermute(entries, 'gy', swap)  3.13 us
    ppermute x1, starting transfers between devices, per_device(): lax.ppermute(far, 'gx', [(i, (i - 1) % count_x) for i in evens] + [((i -...  1.63 us
  transfers between devices with their start and end apart: 13, of which 10 were waited for; matrix products, arithmetic and copies ran while one was open for 0% of the time, Pallas kernels for 2%

profile of v8, /device:TPU:1, one launch (start us, length us, event | category | flops | bytes accessed | tf_op | source)
XLA Modules:
  0.0 52.2 jit_solution(12423456327617208774)
XLA Ops:
  0.6 0.1 pad_add_fusion.place_ref
  0.7 0.0 copy-start.1
  0.7 5.9 %sample.1 = (f32[232,128]{1,0:T(8,128)S(1)}, f32[19,32,128]{2,1,0:T(8,128)S(1)}, s32[512,128]{1,0:T(8,128)S(1)}, f32[512,128]{1,0:T(8,128)S(1)}) custom-call(s32[4]{0:T(128)S(1)} %pad_add_fusion.place_ref, f32[19,32,128]{2,1,0:T(8,128)} %bitcast.16, s32[512,128]{1,0:T(8,128)} %bitcast.17, f32[512,128]{1,0:T(8,128)} %bitcast.18, f32[32,128]{1,0:T(8,128)} %bitcast.19, ...), custom_call_target="tpu_custom_call" | custom-call | tf_op jit(solution)/shard_map/sample/pallas_call | solution.py:382
  6.6 2.1 %collective-permute-start.1 = (f32[232,128]{1,0:T(8,128)S(1)}, f32[232,128]{1,0:T(8,128)S(1)}, u32[]{:S(2)}, u32[]{:S(2)}) collective-permute-start(f32[232,128]{1,0:T(8,128)S(1)} %get-tuple-element.20.refs_0_.own_ref), channel_id=1, source_target_pairs={{0,4},{4,0},{1,5},{5,1},{2,6},{6,2},{3,7},{7,3},{8,12},{12,8},{9,1... | collective-permute-start | bytes 356360 | tf_op jit(solution)/shard_map/ppermute | solution.py:806
  8.7 3.3 %collective-permute-start = (f32[232,128]{1,0:T(8,128)S(1)}, f32[232,128]{1,0:T(8,128)S(1)}, u32[]{:S(2)}, u32[]{:S(2)}) collective-permute-start(f32[232,128]{1,0:T(8,128)S(1)} %get-tuple-element.20.refs_0_.own_ref), channel_id=1, source_target_pairs={{0,24},{8,16},{16,8},{24,0},{1,25},{9,17},{17,9},{25,1},{2,26},{10... | collective-permute-start | bytes 356360 | tf_op jit(solution)/shard_map/ppermute | solution.py:803
  12.1 0.0 collective-permute-start.2
  12.1 0.0 collective-permute-done.1.refs_4_
  12.1 1.5 %collective-permute-start.5 = (f32[232,128]{1,0:T(8,128)S(1)}, f32[232,128]{1,0:T(8,128)S(1)}, u32[]{:S(2)}, u32[]{:S(2)}) collective-permute-start(f32[232,128]{1,0:T(8,128)S(1)} %collective-permute-done.1.refs_4_), channel_id=1, source_target_pairs={{0,8},{8,0},{16,24},{24,16},{1,9},{9,1},{17,25},{25,17},{2,10},{10... | collective-permute-start | bytes 356360 | tf_op jit(solution)/shard_map/ppermute | solution.py:803
  13.5 0.9 %collective-permute-done.refs_2_ = f32[232,128]{1,0:T(8,128)S(1)} collective-permute-done((f32[232,128]{1,0:T(8,128)S(1)}, f32[232,128]{1,0:T(8,128)S(1)}, u32[]{:S(2)}, u32[]{:S(2)}) %collective-permute-start) | collective-permute-done | bytes 118816 | tf_op jit(solution)/shard_map/ppermute | solution.py:803
  14.4 3.3 %collective-permute-done.2.refs_1_ = f32[232,128]{1,0:T(8,128)S(1)} collective-permute-done((f32[232,128]{1,0:T(8,128)S(1)}, f32[232,128]{1,0:T(8,128)S(1)}, u32[]{:S(2)}, u32[]{:S(2)}) %collective-permute-start.2) | collective-permute-done | bytes 118816 | tf_op jit(solution)/shard_map/ppermute | solution.py:803
  17.6 0.3 collective-permute-start.3
  17.9 2.3 %collective-permute-done.5.refs_5_ = f32[232,128]{1,0:T(8,128)S(1)} collective-permute-done((f32[232,128]{1,0:T(8,128)S(1)}, f32[232,128]{1,0:T(8,128)S(1)}, u32[]{:S(2)}, u32[]{:S(2)}) %collective-permute-start.5) | collective-permute-done | bytes 118816 | tf_op jit(solution)/shard_map/ppermute | solution.py:803
  20.2 0.8 %collective-permute-start.6 = (f32[232,128]{1,0:T(8,128)S(1)}, f32[232,128]{1,0:T(8,128)S(1)}, u32[]{:S(2)}, u32[]{:S(2)}) collective-permute-start(f32[232,128]{1,0:T(8,128)S(1)} %collective-permute-done.refs_2_), channel_id=1, source_target_pairs={{0,8},{8,0},{16,24},{24,16},{1,9},{9,1},{17,25},{25,17},{2,10},{10... | collective-permute-start | bytes 356360 | tf_op jit(solution)/shard_map/ppermute | solution.py:803
  21.0 0.3 collective-permute-done.3.refs_6_
  21.3 0.8 %collective-permute-start.4 = (f32[232,128]{1,0:T(8,128)S(1)}, f32[232,128]{1,0:T(8,128)S(1)}, u32[]{:S(2)}, u32[]{:S(2)}) collective-permute-start(f32[232,128]{1,0:T(8,128)S(1)} %collective-permute-done.3.refs_6_), channel_id=1, source_target_pairs={{0,8},{8,0},{16,24},{24,16},{1,9},{9,1},{17,25},{25,17},{2,10},{10... | collective-permute-start | bytes 356360 | tf_op jit(solution)/shard_map/ppermute | solution.py:803
  22.2 2.0 %collective-permute-done.6.refs_3_ = f32[232,128]{1,0:T(8,128)S(1)} collective-permute-done((f32[232,128]{1,0:T(8,128)S(1)}, f32[232,128]{1,0:T(8,128)S(1)}, u32[]{:S(2)}, u32[]{:S(2)}) %collective-permute-start.6) | collective-permute-done | bytes 118816 | tf_op jit(solution)/shard_map/ppermute | solution.py:803
  24.2 0.0 copy-done.1
  24.2 0.0 copy-start
  24.2 1.1 %settle.1 = (f32[96,384]{1,0:T(8,128)S(1)}, f32[64,128]{1,0:T(8,128)S(1)}, f32[64,128]{1,0:T(8,128)S(1)}, f32[12,128]{1,0:T(8,128)S(1)}) custom-call(f32[4,3]{1,0:T(4,128)S(1)} %copy-done.1, f32[232,128]{1,0:T(8,128)S(1)} %get-tuple-element.20.refs_0_.own_ref, f32[232,128]{1,0:T(8,128)S(1)} %collective-permute-done.2.refs_1_, ...), custom_call_target="tpu_custom_call" | custom-call | flops 1000000000 | bytes 831488 | tf_op jit(solution)/shard_map/settle/pallas_call | solution.py:456
  25.3 0.9 %collective-permute-done.4.last_ref = f32[232,128]{1,0:T(8,128)S(1)} collective-permute-done((f32[232,128]{1,0:T(8,128)S(1)}, f32[232,128]{1,0:T(8,128)S(1)}, u32[]{:S(2)}, u32[]{:S(2)}) %collective-permute-start.4) | collective-permute-done | bytes 118816 | tf_op jit(solution)/shard_map/ppermute | solution.py:803
  26.1 0.0 copy-done
  26.2 9.0 %spread.1 = (f32[19,32,128]{2,1,0:T(8,128)S(1)}, f32[5,8,128]{2,1,0:T(8,128)S(1)}, f32[5,8,128]{2,1,0:T(8,128)S(1)}, f32[24,128]{1,0:T(8,128)S(1)}, f32[3,32,128]{2,1,0:T(8,128)}) custom-call(s32[4]{0:T(128)S(1)} %pad_add_fusion.place_ref, f32[232,128]{1,0:T(8,128)S(1)} %get-tuple-element.20.refs_0_.own_ref, f32[232,128]{1,0:T(8,128)S(1)} %collective-permute-done.4.last_ref, ...), custom_call_target="tpu_custom_call" | custom-call | tf_op jit(solution)/shard_map/spread/pallas_call | solution.py:590
  35.2 1.6 %collective-permute-start.7 = (f32[5,8,128]{2,1,0:T(8,128)S(1)}, f32[5,8,128]{2,1,0:T(8,128)S(1)}, u32[]{:S(2)}, u32[]{:S(2)}) collective-permute-start(f32[5,8,128]{2,1,0:T(8,128)S(1)} %get-tuple-element.31), channel_id=1, source_target_pairs={{0,24},{16,8},{24,0},{8,16},{1,25},{17,9},{25,1},{9,17},{2,26},{18... | collective-permute-start | bytes 61448 | tf_op jit(solution)/shard_map/ppermute | solution.py:821
  36.8 0.0 collective-permute-start.8
  36.8 0.5 collective-permute-start.9
  37.3 2.1 %collective-permute-done.9.side_ref = f32[24,128]{1,0:T(8,128)S(1)} collective-permute-done((f32[24,128]{1,0:T(8,128)S(1)}, f32[24,128]{1,0:T(8,128)S(1)}, u32[]{:S(2)}, u32[]{:S(2)}) %collective-permute-start.9) | collective-permute-done | bytes 12320 | tf_op jit(solution)/shard_map/ppermute | solution.py:806
  39.4 0.3 collective-permute-done.7.far_ref
  39.7 0.0 collective-permute-done.8.near_ref
  39.7 0.7 %pack.1 = (f32[8,128]{1,0:T(8,128)S(1)}, f32[8,128]{1,0:T(8,128)S(1)}, f32[8,128]{1,0:T(8,128)S(1)}) custom-call(s32[4]{0:T(128)S(1)} %pad_add_fusion.place_ref, f32[19,32,128]{2,1,0:T(8,128)S(1)} %get-tuple-element.30.relaxed_ref, f32[5,8,128]{2,1,0:T(8,128)S(1)} %collective-permute-done.7.far_ref, f32[5,8,128]{2,1,0:T(8,128)S(1)} %collective-permute-done.8.near_ref, ...), custom_call_target="tpu_custom_call" | custom-call | tf_op jit(solution)/shard_map/pack/pallas_call | solution.py:700
  40.4 7.8 %collective-permute-start.10 = (f32[8,128]{1,0:T(8,128)S(1)}, f32[8,128]{1,0:T(8,128)S(1)}, u32[]{:S(2)}, u32[]{:S(2)}) collective-permute-start(f32[8,128]{1,0:T(8,128)S(1)} %get-tuple-element.34), channel_id=1, source_target_pairs={{1,2},{2,1},{5,6},{6,5},{9,10},{10,9},{13,14},{14,13},{17,18},{18,... | collective-permute-start | bytes 12296 | tf_op jit(solution)/shard_map/ppermute | solution.py:831
  48.2 0.3 collective-permute-start.11
  48.5 0.0 collective-permute-start.12
  48.5 1.0 %collective-permute-done.10.second_ref = f32[8,128]{1,0:T(8,128)S(1)} collective-permute-done((f32[8,128]{1,0:T(8,128)S(1)}, f32[8,128]{1,0:T(8,128)S(1)}, u32[]{:S(2)}, u32[]{:S(2)}) %collective-permute-start.10) | collective-permute-done | bytes 4128 | tf_op jit(solution)/shard_map/ppermute | solution.py:831
  49.5 1.2 %collective-permute-done.11.corner_ref = f32[8,128]{1,0:T(8,128)S(1)} collective-permute-done((f32[8,128]{1,0:T(8,128)S(1)}, f32[8,128]{1,0:T(8,128)S(1)}, u32[]{:S(2)}, u32[]{:S(2)}) %collective-permute-start.11) | collective-permute-done | bytes 4128 | tf_op jit(solution)/shard_map/ppermute | solution.py:806
  50.7 0.0 collective-permute-done.12.first_ref
  50.7 1.5 %stream.1 = f32[19,4,8,128]{3,2,1,0:T(8,128)} custom-call(s32[4]{0:T(128)S(1)} %pad_add_fusion.place_ref, f32[19,32,128]{2,1,0:T(8,128)S(1)} %get-tuple-element.30.relaxed_ref, f32[5,8,128]{2,1,0:T(8,128)S(1)} %collective-permute-done.7.far_ref, f32[5,8,128]{2,1,0:T(8,128)S(1)} %collective-permute-done.8.near_ref, ...), custom_call_target="tpu_custom_call" | custom-call | tf_op jit(solution)/shard_map/stream/pallas_call | solution.py:757
Async XLA Ops:
  0.7 23.5 %copy-start.1 = (f32[4,3]{1,0:T(4,128)S(1)}, f32[4,3]{1,0:T(4,128)}, u32[]{:S(2)}) copy-start(f32[4,3]{1,0:T(4,128)} %speeds_ref.1) | copy-start | bytes 148
  6.6 5.4 %collective-permute-start.1 = (f32[232,128]{1,0:T(8,128)S(1)}, f32[232,128]{1,0:T(8,128)S(1)}, u32[]{:S(2)}, u32[]{:S(2)}) collective-permute-start(f32[232,128]{1,0:T(8,128)S(1)} %get-tuple-element.20.refs_0_.own_ref), channel_id=1, source_target_pairs={{0,4},{4,0},{1,5},{5,1},{2,6},{6,2},{3,7},{7,3},{8,12},{12,8},{9,1... | collective-permute-start | bytes 356360 | tf_op jit(solution)/shard_map/ppermute | solution.py:806
  8.7 5.7 %collective-permute-start = (f32[232,128]{1,0:T(8,128)S(1)}, f32[232,128]{1,0:T(8,128)S(1)}, u32[]{:S(2)}, u32[]{:S(2)}) collective-permute-start(f32[232,128]{1,0:T(8,128)S(1)} %get-tuple-element.20.refs_0_.own_ref), channel_id=1, source_target_pairs={{0,24},{8,16},{16,8},{24,0},{1,25},{9,17},{17,9},{25,1},{2,26},{10... | collective-permute-start | bytes 356360 | tf_op jit(solution)/shard_map/ppermute | solution.py:803
  12.1 5.6 %collective-permute-start.2 = (f32[232,128]{1,0:T(8,128)S(1)}, f32[232,128]{1,0:T(8,128)S(1)}, u32[]{:S(2)}, u32[]{:S(2)}) collective-permute-start(f32[232,128]{1,0:T(8,128)S(1)} %get-tuple-element.20.refs_0_.own_ref), channel_id=1, source_target_pairs={{0,8},{8,0},{16,24},{24,16},{1,9},{9,1},{17,25},{25,17},{2,10},{10... | collective-permute-start | bytes 356360 | tf_op jit(solution)/shard_map/ppermute | solution.py:803
  12.1 8.1 %collective-permute-start.5 = (f32[232,128]{1,0:T(8,128)S(1)}, f32[232,128]{1,0:T(8,128)S(1)}, u32[]{:S(2)}, u32[]{:S(2)}) collective-permute-start(f32[232,128]{1,0:T(8,128)S(1)} %collective-permute-done.1.refs_4_), channel_id=1, source_target_pairs={{0,8},{8,0},{16,24},{24,16},{1,9},{9,1},{17,25},{25,17},{2,10},{10... | collective-permute-start | bytes 356360 | tf_op jit(solution)/shard_map/ppermute | solution.py:803
  17.6 3.7 %collective-permute-start.3 = (f32[232,128]{1,0:T(8,128)S(1)}, f32[232,128]{1,0:T(8,128)S(1)}, u32[]{:S(2)}, u32[]{:S(2)}) collective-permute-start(f32[232,128]{1,0:T(8,128)S(1)} %collective-permute-done.refs_2_), channel_id=1, source_target_pairs={{0,4},{4,0},{1,5},{5,1},{2,6},{6,2},{3,7},{7,3},{8,12},{12,8},{9,1... | collective-permute-start | bytes 356360 | tf_op jit(solution)/shard_map/ppermute | solution.py:806
  20.2 4.0 %collective-permute-start.6 = (f32[232,128]{1,0:T(8,128)S(1)}, f32[232,128]{1,0:T(8,128)S(1)}, u32[]{:S(2)}, u32[]{:S(2)}) collective-permute-start(f32[232,128]{1,0:T(8,128)S(1)} %collective-permute-done.refs_2_), channel_id=1, source_target_pairs={{0,8},{8,0},{16,24},{24,16},{1,9},{9,1},{17,25},{25,17},{2,10},{10... | collective-permute-start | bytes 356360 | tf_op jit(solution)/shard_map/ppermute | solution.py:803
  21.3 4.8 %collective-permute-start.4 = (f32[232,128]{1,0:T(8,128)S(1)}, f32[232,128]{1,0:T(8,128)S(1)}, u32[]{:S(2)}, u32[]{:S(2)}) collective-permute-start(f32[232,128]{1,0:T(8,128)S(1)} %collective-permute-done.3.refs_6_), channel_id=1, source_target_pairs={{0,8},{8,0},{16,24},{24,16},{1,9},{9,1},{17,25},{25,17},{2,10},{10... | collective-permute-start | bytes 356360 | tf_op jit(solution)/shard_map/ppermute | solution.py:803
  24.2 2.0 %copy-start = (s32[4,8,128]{2,1,0:T(8,128)S(1)}, s32[4,8,128]{2,1,0:T(8,128)}, u32[]{:S(2)}) copy-start(s32[4,8,128]{2,1,0:T(8,128)} %param.10) | copy-start | bytes 49156
  35.2 4.5 %collective-permute-start.7 = (f32[5,8,128]{2,1,0:T(8,128)S(1)}, f32[5,8,128]{2,1,0:T(8,128)S(1)}, u32[]{:S(2)}, u32[]{:S(2)}) collective-permute-start(f32[5,8,128]{2,1,0:T(8,128)S(1)} %get-tuple-element.31), channel_id=1, source_target_pairs={{0,24},{16,8},{24,0},{8,16},{1,25},{17,9},{25,1},{9,17},{2,26},{18... | collective-permute-start | bytes 61448 | tf_op jit(solution)/shard_map/ppermute | solution.py:821
  36.8 2.9 %collective-permute-start.8 = (f32[5,8,128]{2,1,0:T(8,128)S(1)}, f32[5,8,128]{2,1,0:T(8,128)S(1)}, u32[]{:S(2)}, u32[]{:S(2)}) collective-permute-start(f32[5,8,128]{2,1,0:T(8,128)S(1)} %get-tuple-element.32), channel_id=1, source_target_pairs={{0,8},{16,24},{8,0},{24,16},{1,9},{17,25},{9,1},{25,17},{2,10},{18... | collective-permute-start | bytes 61448 | tf_op jit(solution)/shard_map/ppermute | solution.py:826
  36.8 2.5 %collective-permute-start.9 = (f32[24,128]{1,0:T(8,128)S(1)}, f32[24,128]{1,0:T(8,128)S(1)}, u32[]{:S(2)}, u32[]{:S(2)}) collective-permute-start(f32[24,128]{1,0:T(8,128)S(1)} %get-tuple-element.33), channel_id=1, source_target_pairs={{0,4},{4,0},{1,5},{5,1},{2,6},{6,2},{3,7},{7,3},{8,12},{12,8},{9,1... | collective-permute-start | bytes 36872 | tf_op jit(solution)/shard_map/ppermute | solution.py:806
  40.4 9.1 %collective-permute-start.10 = (f32[8,128]{1,0:T(8,128)S(1)}, f32[8,128]{1,0:T(8,128)S(1)}, u32[]{:S(2)}, u32[]{:S(2)}) collective-permute-start(f32[8,128]{1,0:T(8,128)S(1)} %get-tuple-element.34), channel_id=1, source_target_pairs={{1,2},{2,1},{5,6},{6,5},{9,10},{10,9},{13,14},{14,13},{17,18},{18,... | collective-permute-start | bytes 12296 | tf_op jit(solution)/shard_map/ppermute | solution.py:831
  48.2 2.5 %collective-permute-start.11 = (f32[8,128]{1,0:T(8,128)S(1)}, f32[8,128]{1,0:T(8,128)S(1)}, u32[]{:S(2)}, u32[]{:S(2)}) collective-permute-start(f32[8,128]{1,0:T(8,128)S(1)} %get-tuple-element.35), channel_id=1, source_target_pairs={{0,4},{4,0},{1,5},{5,1},{2,6},{6,2},{3,7},{7,3},{8,12},{12,8},{9,1... | collective-permute-start | bytes 12296 | tf_op jit(solution)/shard_map/ppermute | solution.py:806
  48.5 2.2 %collective-permute-start.12 = (f32[8,128]{1,0:T(8,128)S(1)}, f32[8,128]{1,0:T(8,128)S(1)}, u32[]{:S(2)}, u32[]{:S(2)}) collective-permute-start(f32[8,128]{1,0:T(8,128)S(1)} %get-tuple-element.36), channel_id=1, source_target_pairs={{0,1},{2,3},{1,0},{3,2},{4,5},{6,7},{5,4},{7,6},{8,9},{10,11},{9,8... | collective-permute-start | bytes 12296 | tf_op jit(solution)/shard_map/ppermute | solution.py:833

commit v9 on v6

--- a/solution.py
+++ b/solution.py
@@ -40,6 +40,7 @@
 far_velocity = (0.02, 0.06, 0.0)
 vmem_bytes = 16 << 20
 group = 8
+fine = jnp.float8_e4m3fn
 
 
 def going(axis, step):
@@ -504,8 +505,11 @@
     ids, mine, _ = wanted_labels(own_ref, slots, owned)
     totals = add_shards((sums_ref[...], area_ref[...], trains_ref[...]), [last_ref], ids, mine)
     forces, own_forces = block_forces(speeds_ref, totals, own_ref, slots, owned)
+    largest = jnp.maximum(jnp.maximum(jnp.abs(forces[0]), jnp.abs(forces[1])), jnp.abs(forces[2]))
+    largest = jnp.maximum(jnp.max(largest, axis=(0, 1), keepdims=True), 1e-20)
+    scale = (224.0 * 16.0) / largest
     for c in range(3):
-        force_ref[c] = forces[c]
+        force_ref[c] = forces[c] * scale
         marker_ref[c] = own_forces[c]
     marker_copy = pltpu.make_async_copy(marker_ref, marker_any, sem)
     marker_copy.start()
@@ -527,8 +531,9 @@
             parts = []
             for c in range(3):
                 value = weight * force[c]
-                high = value.astype(bf).astype(jnp.float32)
-                parts += [high, value - high]
+                for _ in range(3):
+                    parts.append(value.astype(fine).astype(jnp.float32))
+                    value = (value - parts[-1]) * 16.0
             for which, entries in enumerate([lane, row] + parts):
                 lines_ref[k, which] = entries
 
@@ -539,17 +544,14 @@
             left, right = ([], [])
             for i in range(group):
                 lane_i, row_i = (wide(0, i), wide(1, i))
-                right.append(
-                    jnp.concatenate(
-                        [jnp.where(steps[j] == lane_i, one, zero) for j in range(lanes // 16)],
-                        axis=0,
-                    )
-                )
+                match = [jnp.where(steps[j] == lane_i, one, zero) for j in range(lanes // 16)]
+                right.append(jnp.concatenate(match, axis=0).astype(fine))
                 masks = [steps[j] == row_i for j in range(rows // 16)]
                 pieces = []
                 for which in range(len(parts)):
                     part_i = wide(2 + which, i)
-                    pieces += [jnp.where(mask, part_i, zero) for mask in masks]
+                    piece = [jnp.where(mask, part_i, zero) for mask in masks]
+                    pieces.append(jnp.concatenate(piece, axis=0).astype(fine))
                 left.append(jnp.concatenate(pieces, axis=0))
             acc[...] += lax.dot_general(
                 jnp.concatenate(left, axis=1),
@@ -560,10 +562,12 @@
         return carry
 
     lax.fori_loop(0, slots // group, body, 0)
-    cell_force = [
-        acc[2 * c * rows : (2 * c + 1) * rows, :] + acc[(2 * c + 1) * rows : (2 * c + 2) * rows, :]
-        for c in range(3)
-    ]
+    cell_force = []
+    for c in range(3):
+        total = acc[3 * c * rows : (3 * c + 1) * rows, :]
+        total = total + acc[(3 * c + 1) * rows : (3 * c + 2) * rows, :] * (1.0 / 16.0)
+        total = total + acc[(3 * c + 2) * rows : (3 * c + 3) * rows, :] * (1.0 / 256.0)
+        cell_force.append(total * (1.0 / scale))
     relaxed = collide([pop_ref[q] for q in range(19)], cell_force, solid_ref[...])
     for q in range(19):
         relaxed_ref[q] = relaxed[q]
@@ -601,8 +605,8 @@
         scratch_shapes=[
             pltpu.VMEM((3, owned, mark), jnp.float32),
             pltpu.VMEM((3, slots, mark), jnp.float32),
-            pltpu.VMEM((cells.shape[0] // slots, 8, group, mark), jnp.float32),
-            pltpu.VMEM((6 * line_count, lanes), jnp.float32),
+            pltpu.VMEM((cells.shape[0] // slots, 11, group, mark), jnp.float32),
+            pltpu.VMEM((9 * line_count, lanes), jnp.float32),
             pltpu.SemaphoreType.DMA,
         ],
         compiler_params=kernel_params(),

time: 50.8 us -> 49.2 us (0.969)
  Pallas kernels: 18.2 us -> 16.6 us
    pallas_call x1, Pallas kernels: 9.05 us -> 7.45 us  [spread(): pl.pallas_call(functools.partial(spread_kernel, slots, owned), out_shape=...]
where the time goes in v9:
time: 49.2 us; the launch traced here: 49 us
  starting transfers between devices  21.5 us (44%)
  Pallas kernels  16.6 us (34%)
  waiting for transfers between devices  10.2 us (21%)
  between operations  0.7 us (1%)
    ppermute x1, starting transfers between devices, per_device(): lax.ppermute(down_first, 'gz', outer + [(j, i) for i, j in outer])  8.66 us
    pallas_call x1, Pallas kernels, spread(): pl.pallas_call(functools.partial(spread_kernel, slots, owned), out_shape=...  7.45 us
    ppermute x5, starting transfers between devices, across_y(): return lax.ppermute(entries, 'gy', swap)  6.1 us
    pallas_call x1, Pallas kernels, sample(): pl.pallas_call(sample_kernel, out_shape=[full((count, cells.shape[1]))] +...  5.9 us
    ppermute x5, waiting for transfers between devices, across_y(): return lax.ppermute(entries, 'gy', swap)  5.53 us
    ppermute x4, starting transfers between devices, across_x(): lax.ppermute(entries, 'gx', [(i, i ^ distance) for i in range(count_x)])  5.38 us
    ppermute x4, waiting for transfers between devices, across_x(): lax.ppermute(entries, 'gx', [(i, i ^ distance) for i in range(count_x)])  3.89 us
    pallas_call x1, Pallas kernels, stream(): pl.pallas_call(functools.partial(stream_kernel, count_z), out_shape=full(...  1.47 us
  transfers between devices with their start and end apart: 13, of which 10 were waited for; matrix products, arithmetic and copies ran while one was open for 0% of the time, Pallas kernels for 2%

profile of v9, /device:TPU:1, one launch (start us, length us, event | category | flops | bytes accessed | tf_op | source)
XLA Modules:
  0.0 49.0 jit_solution(10477207504810062498)
XLA Ops:
  0.6 0.1 pad_add_fusion.place_ref
  0.7 0.0 copy-start.1
  0.7 5.9 %sample.1 = (f32[232,128]{1,0:T(8,128)S(1)}, f32[19,32,128]{2,1,0:T(8,128)S(1)}, s32[512,128]{1,0:T(8,128)S(1)}, f32[512,128]{1,0:T(8,128)S(1)}) custom-call(s32[4]{0:T(128)S(1)} %pad_add_fusion.place_ref, f32[19,32,128]{2,1,0:T(8,128)} %bitcast.16, s32[512,128]{1,0:T(8,128)} %bitcast.17, f32[512,128]{1,0:T(8,128)} %bitcast.18, f32[32,128]{1,0:T(8,128)} %bitcast.19, ...), custom_call_target="tpu_custom_call" | custom-call | tf_op jit(solution)/shard_map/sample/pallas_call | solution.py:383
  6.6 4.2 %collective-permute-start = (f32[232,128]{1,0:T(8,128)S(1)}, f32[232,128]{1,0:T(8,128)S(1)}, u32[]{:S(2)}, u32[]{:S(2)}) collective-permute-start(f32[232,128]{1,0:T(8,128)S(1)} %get-tuple-element.19.refs_0_.own_ref), channel_id=1, source_target_pairs={{0,24},{8,16},{16,8},{24,0},{1,25},{9,17},{17,9},{25,1},{2,26},{10... | collective-permute-start | bytes 356360 | tf_op jit(solution)/shard_map/ppermute | solution.py:807
  10.8 1.2 %collective-permute-start.1 = (f32[232,128]{1,0:T(8,128)S(1)}, f32[232,128]{1,0:T(8,128)S(1)}, u32[]{:S(2)}, u32[]{:S(2)}) collective-permute-start(f32[232,128]{1,0:T(8,128)S(1)} %get-tuple-element.19.refs_0_.own_ref), channel_id=1, source_target_pairs={{0,4},{4,0},{1,5},{5,1},{2,6},{6,2},{3,7},{7,3},{8,12},{12,8},{9,1... | collective-permute-start | bytes 356360 | tf_op jit(solution)/shard_map/ppermute | solution.py:810
  12.1 0.0 collective-permute-start.4
  12.1 1.8 %collective-permute-done.refs_2_ = f32[232,128]{1,0:T(8,128)S(1)} collective-permute-done((f32[232,128]{1,0:T(8,128)S(1)}, f32[232,128]{1,0:T(8,128)S(1)}, u32[]{:S(2)}, u32[]{:S(2)}) %collective-permute-start) | collective-permute-done | bytes 118816 | tf_op jit(solution)/shard_map/ppermute | solution.py:807
  13.8 1.0 %collective-permute-done.1.refs_4_ = f32[232,128]{1,0:T(8,128)S(1)} collective-permute-done((f32[232,128]{1,0:T(8,128)S(1)}, f32[232,128]{1,0:T(8,128)S(1)}, u32[]{:S(2)}, u32[]{:S(2)}) %collective-permute-start.1) | collective-permute-done | bytes 118816 | tf_op jit(solution)/shard_map/ppermute | solution.py:810
  14.8 1.2 %collective-permute-start.2 = (f32[232,128]{1,0:T(8,128)S(1)}, f32[232,128]{1,0:T(8,128)S(1)}, u32[]{:S(2)}, u32[]{:S(2)}) collective-permute-start(f32[232,128]{1,0:T(8,128)S(1)} %collective-permute-done.refs_2_), channel_id=1, source_target_pairs={{0,4},{4,0},{1,5},{5,1},{2,6},{6,2},{3,7},{7,3},{8,12},{12,8},{9,1... | collective-permute-start | bytes 356360 | tf_op jit(solution)/shard_map/ppermute | solution.py:810
  16.0 0.5 collective-permute-start.5
  16.5 0.0 collective-permute-done.4.refs_1_
  16.5 1.1 %collective-permute-start.6 = (f32[232,128]{1,0:T(8,128)S(1)}, f32[232,128]{1,0:T(8,128)S(1)}, u32[]{:S(2)}, u32[]{:S(2)}) collective-permute-start(f32[232,128]{1,0:T(8,128)S(1)} %collective-permute-done.4.refs_1_), channel_id=1, source_target_pairs={{0,4},{4,0},{1,5},{5,1},{2,6},{6,2},{3,7},{7,3},{8,12},{12,8},{9,1... | collective-permute-start | bytes 356360 | tf_op jit(solution)/shard_map/ppermute | solution.py:810
  17.6 0.9 %collective-permute-done.2.refs_6_ = f32[232,128]{1,0:T(8,128)S(1)} collective-permute-done((f32[232,128]{1,0:T(8,128)S(1)}, f32[232,128]{1,0:T(8,128)S(1)}, u32[]{:S(2)}, u32[]{:S(2)}) %collective-permute-start.2) | collective-permute-done | bytes 118816 | tf_op jit(solution)/shard_map/ppermute | solution.py:810
  18.5 0.7 %collective-permute-start.3 = (f32[232,128]{1,0:T(8,128)S(1)}, f32[232,128]{1,0:T(8,128)S(1)}, u32[]{:S(2)}, u32[]{:S(2)}) collective-permute-start(f32[232,128]{1,0:T(8,128)S(1)} %collective-permute-done.2.refs_6_), channel_id=1, source_target_pairs={{0,8},{8,0},{16,24},{24,16},{1,9},{9,1},{17,25},{25,17},{2,10},{10... | collective-permute-start | bytes 356360 | tf_op jit(solution)/shard_map/ppermute | solution.py:807
  19.2 0.8 %collective-permute-done.5.refs_3_ = f32[232,128]{1,0:T(8,128)S(1)} collective-permute-done((f32[232,128]{1,0:T(8,128)S(1)}, f32[232,128]{1,0:T(8,128)S(1)}, u32[]{:S(2)}, u32[]{:S(2)}) %collective-permute-start.5) | collective-permute-done | bytes 118816 | tf_op jit(solution)/shard_map/ppermute | solution.py:807
  20.0 1.3 %collective-permute-done.6.refs_5_ = f32[232,128]{1,0:T(8,128)S(1)} collective-permute-done((f32[232,128]{1,0:T(8,128)S(1)}, f32[232,128]{1,0:T(8,128)S(1)}, u32[]{:S(2)}, u32[]{:S(2)}) %collective-permute-start.6) | collective-permute-done | bytes 118816 | tf_op jit(solution)/shard_map/ppermute | solution.py:810
  21.3 0.0 copy-done.1
  21.3 0.0 copy-start
  21.3 1.1 %settle.1 = (f32[96,384]{1,0:T(8,128)S(1)}, f32[64,128]{1,0:T(8,128)S(1)}, f32[64,128]{1,0:T(8,128)S(1)}, f32[12,128]{1,0:T(8,128)S(1)}) custom-call(f32[4,3]{1,0:T(4,128)S(1)} %copy-done.1, f32[232,128]{1,0:T(8,128)S(1)} %get-tuple-element.19.refs_0_.own_ref, f32[232,128]{1,0:T(8,128)S(1)} %collective-permute-done.4.refs_1_, ...), custom_call_target="tpu_custom_call" | custom-call | flops 1000000000 | bytes 831488 | tf_op jit(solution)/shard_map/settle/pallas_call | solution.py:457
  22.4 1.3 %collective-permute-done.3.last_ref = f32[232,128]{1,0:T(8,128)S(1)} collective-permute-done((f32[232,128]{1,0:T(8,128)S(1)}, f32[232,128]{1,0:T(8,128)S(1)}, u32[]{:S(2)}, u32[]{:S(2)}) %collective-permute-start.3) | collective-permute-done | bytes 118816 | tf_op jit(solution)/shard_map/ppermute | solution.py:807
  23.7 0.0 copy-done
  23.7 7.5 %spread.1 = (f32[19,32,128]{2,1,0:T(8,128)S(1)}, f32[5,8,128]{2,1,0:T(8,128)S(1)}, f32[5,8,128]{2,1,0:T(8,128)S(1)}, f32[24,128]{1,0:T(8,128)S(1)}, f32[3,32,128]{2,1,0:T(8,128)}) custom-call(s32[4]{0:T(128)S(1)} %pad_add_fusion.place_ref, f32[232,128]{1,0:T(8,128)S(1)} %get-tuple-element.19.refs_0_.own_ref, f32[232,128]{1,0:T(8,128)S(1)} %collective-permute-done.3.last_ref, ...), custom_call_target="tpu_custom_call" | custom-call | tf_op jit(solution)/shard_map/spread/pallas_call | solution.py:594
  31.2 1.3 %collective-permute-start.7 = (f32[5,8,128]{2,1,0:T(8,128)S(1)}, f32[5,8,128]{2,1,0:T(8,128)S(1)}, u32[]{:S(2)}, u32[]{:S(2)}) collective-permute-start(f32[5,8,128]{2,1,0:T(8,128)S(1)} %get-tuple-element.29), channel_id=1, source_target_pairs={{0,24},{16,8},{24,0},{8,16},{1,25},{17,9},{25,1},{9,17},{2,26},{18... | collective-permute-start | bytes 61448 | tf_op jit(solution)/shard_map/ppermute | solution.py:825
  32.5 0.0 collective-permute-start.8
  32.5 1.9 %collective-permute-start.9 = (f32[24,128]{1,0:T(8,128)S(1)}, f32[24,128]{1,0:T(8,128)S(1)}, u32[]{:S(2)}, u32[]{:S(2)}) collective-permute-start(f32[24,128]{1,0:T(8,128)S(1)} %get-tuple-element.31), channel_id=1, source_target_pairs={{0,4},{4,0},{1,5},{5,1},{2,6},{6,2},{3,7},{7,3},{8,12},{12,8},{9,1... | collective-permute-start | bytes 36872 | tf_op jit(solution)/shard_map/ppermute | solution.py:810
  34.4 1.1 %collective-permute-done.9.side_ref = f32[24,128]{1,0:T(8,128)S(1)} collective-permute-done((f32[24,128]{1,0:T(8,128)S(1)}, f32[24,128]{1,0:T(8,128)S(1)}, u32[]{:S(2)}, u32[]{:S(2)}) %collective-permute-start.9) | collective-permute-done | bytes 12320 | tf_op jit(solution)/shard_map/ppermute | solution.py:810
  35.4 0.2 collective-permute-done.7.far_ref
  35.7 0.0 collective-permute-done.8.near_ref
  35.7 0.7 %pack.1 = (f32[8,128]{1,0:T(8,128)S(1)}, f32[8,128]{1,0:T(8,128)S(1)}, f32[8,128]{1,0:T(8,128)S(1)}) custom-call(s32[4]{0:T(128)S(1)} %pad_add_fusion.place_ref, f32[19,32,128]{2,1,0:T(8,128)S(1)} %get-tuple-element.28.relaxed_ref, f32[5,8,128]{2,1,0:T(8,128)S(1)} %collective-permute-done.7.far_ref, f32[5,8,128]{2,1,0:T(8,128)S(1)} %collective-permute-done.8.near_ref, ...), custom_call_target="tpu_custom_call" | custom-call | tf_op jit(solution)/shard_map/pack/pallas_call | solution.py:704
  36.3 8.7 %collective-permute-start.10 = (f32[8,128]{1,0:T(8,128)S(1)}, f32[8,128]{1,0:T(8,128)S(1)}, u32[]{:S(2)}, u32[]{:S(2)}) collective-permute-start(f32[8,128]{1,0:T(8,128)S(1)} %get-tuple-element.32), channel_id=1, source_target_pairs={{1,2},{2,1},{5,6},{6,5},{9,10},{10,9},{13,14},{14,13},{17,18},{18,... | collective-permute-start | bytes 12296 | tf_op jit(solution)/shard_map/ppermute | solution.py:835
  45.0 0.7 %collective-permute-start.11 = (f32[8,128]{1,0:T(8,128)S(1)}, f32[8,128]{1,0:T(8,128)S(1)}, u32[]{:S(2)}, u32[]{:S(2)}) collective-permute-start(f32[8,128]{1,0:T(8,128)S(1)} %get-tuple-element.33), channel_id=1, source_target_pairs={{0,4},{4,0},{1,5},{5,1},{2,6},{6,2},{3,7},{7,3},{8,12},{12,8},{9,1... | collective-permute-start | bytes 12296 | tf_op jit(solution)/shard_map/ppermute | solution.py:810
  45.7 0.0 collective-permute-start.12
  45.7 0.6 %collective-permute-done.10.second_ref = f32[8,128]{1,0:T(8,128)S(1)} collective-permute-done((f32[8,128]{1,0:T(8,128)S(1)}, f32[8,128]{1,0:T(8,128)S(1)}, u32[]{:S(2)}, u32[]{:S(2)}) %collective-permute-start.10) | collective-permute-done | bytes 4128 | tf_op jit(solution)/shard_map/ppermute | solution.py:835
  46.3 1.2 %collective-permute-done.11.corner_ref = f32[8,128]{1,0:T(8,128)S(1)} collective-permute-done((f32[8,128]{1,0:T(8,128)S(1)}, f32[8,128]{1,0:T(8,128)S(1)}, u32[]{:S(2)}, u32[]{:S(2)}) %collective-permute-start.11) | collective-permute-done | bytes 4128 | tf_op jit(solution)/shard_map/ppermute | solution.py:810
  47.5 0.0 collective-permute-done.12.first_ref
  47.5 1.5 %stream.1 = f32[19,4,8,128]{3,2,1,0:T(8,128)} custom-call(s32[4]{0:T(128)S(1)} %pad_add_fusion.place_ref, f32[19,32,128]{2,1,0:T(8,128)S(1)} %get-tuple-element.28.relaxed_ref, f32[5,8,128]{2,1,0:T(8,128)S(1)} %collective-permute-done.7.far_ref, f32[5,8,128]{2,1,0:T(8,128)S(1)} %collective-permute-done.8.near_ref, ...), custom_call_target="tpu_custom_call" | custom-call | tf_op jit(solution)/shard_map/stream/pallas_call | solution.py:761
Async XLA Ops:
  0.7 20.6 %copy-start.1 = (f32[4,3]{1,0:T(4,128)S(1)}, f32[4,3]{1,0:T(4,128)}, u32[]{:S(2)}) copy-start(f32[4,3]{1,0:T(4,128)} %speeds_ref.1) | copy-start | bytes 148
  6.6 7.2 %collective-permute-start = (f32[232,128]{1,0:T(8,128)S(1)}, f32[232,128]{1,0:T(8,128)S(1)}, u32[]{:S(2)}, u32[]{:S(2)}) collective-permute-start(f32[232,128]{1,0:T(8,128)S(1)} %get-tuple-element.19.refs_0_.own_ref), channel_id=1, source_target_pairs={{0,24},{8,16},{16,8},{24,0},{1,25},{9,17},{17,9},{25,1},{2,26},{10... | collective-permute-start | bytes 356360 | tf_op jit(solution)/shard_map/ppermute | solution.py:807
  10.8 4.0 %collective-permute-start.1 = (f32[232,128]{1,0:T(8,128)S(1)}, f32[232,128]{1,0:T(8,128)S(1)}, u32[]{:S(2)}, u32[]{:S(2)}) collective-permute-start(f32[232,128]{1,0:T(8,128)S(1)} %get-tuple-element.19.refs_0_.own_ref), channel_id=1, source_target_pairs={{0,4},{4,0},{1,5},{5,1},{2,6},{6,2},{3,7},{7,3},{8,12},{12,8},{9,1... | collective-permute-start | bytes 356360 | tf_op jit(solution)/shard_map/ppermute | solution.py:810
  12.1 4.5 %collective-permute-start.4 = (f32[232,128]{1,0:T(8,128)S(1)}, f32[232,128]{1,0:T(8,128)S(1)}, u32[]{:S(2)}, u32[]{:S(2)}) collective-permute-start(f32[232,128]{1,0:T(8,128)S(1)} %get-tuple-element.19.refs_0_.own_ref), channel_id=1, source_target_pairs={{0,8},{8,0},{16,24},{24,16},{1,9},{9,1},{17,25},{25,17},{2,10},{10... | collective-permute-start | bytes 356360 | tf_op jit(solution)/shard_map/ppermute | solution.py:807
  14.8 3.7 %collective-permute-start.2 = (f32[232,128]{1,0:T(8,128)S(1)}, f32[232,128]{1,0:T(8,128)S(1)}, u32[]{:S(2)}, u32[]{:S(2)}) collective-permute-start(f32[232,128]{1,0:T(8,128)S(1)} %collective-permute-done.refs_2_), channel_id=1, source_target_pairs={{0,4},{4,0},{1,5},{5,1},{2,6},{6,2},{3,7},{7,3},{8,12},{12,8},{9,1... | collective-permute-start | bytes 356360 | tf_op jit(solution)/shard_map/ppermute | solution.py:810
  16.0 4.0 %collective-permute-start.5 = (f32[232,128]{1,0:T(8,128)S(1)}, f32[232,128]{1,0:T(8,128)S(1)}, u32[]{:S(2)}, u32[]{:S(2)}) collective-permute-start(f32[232,128]{1,0:T(8,128)S(1)} %collective-permute-done.refs_2_), channel_id=1, source_target_pairs={{0,8},{8,0},{16,24},{24,16},{1,9},{9,1},{17,25},{25,17},{2,10},{10... | collective-permute-start | bytes 356360 | tf_op jit(solution)/shard_map/ppermute | solution.py:807
  16.5 4.8 %collective-permute-start.6 = (f32[232,128]{1,0:T(8,128)S(1)}, f32[232,128]{1,0:T(8,128)S(1)}, u32[]{:S(2)}, u32[]{:S(2)}) collective-permute-start(f32[232,128]{1,0:T(8,128)S(1)} %collective-permute-done.4.refs_1_), channel_id=1, source_target_pairs={{0,4},{4,0},{1,5},{5,1},{2,6},{6,2},{3,7},{7,3},{8,12},{12,8},{9,1... | collective-permute-start | bytes 356360 | tf_op jit(solution)/shard_map/ppermute | solution.py:810
  18.5 5.2 %collective-permute-start.3 = (f32[232,128]{1,0:T(8,128)S(1)}, f32[232,128]{1,0:T(8,128)S(1)}, u32[]{:S(2)}, u32[]{:S(2)}) collective-permute-start(f32[232,128]{1,0:T(8,128)S(1)} %collective-permute-done.2.refs_6_), channel_id=1, source_target_pairs={{0,8},{8,0},{16,24},{24,16},{1,9},{9,1},{17,25},{25,17},{2,10},{10... | collective-permute-start | bytes 356360 | tf_op jit(solution)/shard_map/ppermute | solution.py:807
  21.3 2.4 %copy-start = (s32[4,8,128]{2,1,0:T(8,128)S(1)}, s32[4,8,128]{2,1,0:T(8,128)}, u32[]{:S(2)}) copy-start(s32[4,8,128]{2,1,0:T(8,128)} %param.10) | copy-start | bytes 49156
  31.2 4.5 %collective-permute-start.7 = (f32[5,8,128]{2,1,0:T(8,128)S(1)}, f32[5,8,128]{2,1,0:T(8,128)S(1)}, u32[]{:S(2)}, u32[]{:S(2)}) collective-permute-start(f32[5,8,128]{2,1,0:T(8,128)S(1)} %get-tuple-element.29), channel_id=1, source_target_pairs={{0,24},{16,8},{24,0},{8,16},{1,25},{17,9},{25,1},{9,17},{2,26},{18... | collective-permute-start | bytes 61448 | tf_op jit(solution)/shard_map/ppermute | solution.py:825
  32.5 3.2 %collective-permute-start.8 = (f32[5,8,128]{2,1,0:T(8,128)S(1)}, f32[5,8,128]{2,1,0:T(8,128)S(1)}, u32[]{:S(2)}, u32[]{:S(2)}) collective-permute-start(f32[5,8,128]{2,1,0:T(8,128)S(1)} %get-tuple-element.30), channel_id=1, source_target_pairs={{0,8},{16,24},{8,0},{24,16},{1,9},{17,25},{9,1},{25,17},{2,10},{18... | collective-permute-start | bytes 61448 | tf_op jit(solution)/shard_map/ppermute | solution.py:830
  32.5 3.0 %collective-permute-start.9 = (f32[24,128]{1,0:T(8,128)S(1)}, f32[24,128]{1,0:T(8,128)S(1)}, u32[]{:S(2)}, u32[]{:S(2)}) collective-permute-start(f32[24,128]{1,0:T(8,128)S(1)} %get-tuple-element.31), channel_id=1, source_target_pairs={{0,4},{4,0},{1,5},{5,1},{2,6},{6,2},{3,7},{7,3},{8,12},{12,8},{9,1... | collective-permute-start | bytes 36872 | tf_op jit(solution)/shard_map/ppermute | solution.py:810
  36.3 9.9 %collective-permute-start.10 = (f32[8,128]{1,0:T(8,128)S(1)}, f32[8,128]{1,0:T(8,128)S(1)}, u32[]{:S(2)}, u32[]{:S(2)}) collective-permute-start(f32[8,128]{1,0:T(8,128)S(1)} %get-tuple-element.32), channel_id=1, source_target_pairs={{1,2},{2,1},{5,6},{6,5},{9,10},{10,9},{13,14},{14,13},{17,18},{18,... | collective-permute-start | bytes 12296 | tf_op jit(solution)/shard_map/ppermute | solution.py:835
  45.0 2.5 %collective-permute-start.11 = (f32[8,128]{1,0:T(8,128)S(1)}, f32[8,128]{1,0:T(8,128)S(1)}, u32[]{:S(2)}, u32[]{:S(2)}) collective-permute-start(f32[8,128]{1,0:T(8,128)S(1)} %get-tuple-element.33), channel_id=1, source_target_pairs={{0,4},{4,0},{1,5},{5,1},{2,6},{6,2},{3,7},{7,3},{8,12},{12,8},{9,1... | collective-permute-start | bytes 12296 | tf_op jit(solution)/shard_map/ppermute | solution.py:810
  45.7 1.8 %collective-permute-start.12 = (f32[8,128]{1,0:T(8,128)S(1)}, f32[8,128]{1,0:T(8,128)S(1)}, u32[]{:S(2)}, u32[]{:S(2)}) collective-permute-start(f32[8,128]{1,0:T(8,128)S(1)} %get-tuple-element.34), channel_id=1, source_target_pairs={{0,1},{2,3},{1,0},{3,2},{4,5},{6,7},{5,4},{7,6},{8,9},{10,11},{9,8... | collective-permute-start | bytes 12296 | tf_op jit(solution)/shard_map/ppermute | solution.py:837

commit v10 on v9

--- a/solution.py
+++ b/solution.py
@@ -580,8 +580,7 @@
         for x in range(rows // size_y):
             up = relaxed[going(1, 1)[i]][size_y * x + size_y - 1 : size_y * x + size_y, :]
             down = relaxed[going(1, -1)[i]][size_y * x : size_y * x + 1, :]
-            at = rows // size_y * i + x
-            side_ref[at : at + 1, :] = jnp.where(place_ref[0] == 0, up, down)
+            side_ref[i, x : x + 1, :] = jnp.where(place_ref[0] == 0, up, down)
     marker_copy.wait()
 
 
@@ -597,7 +596,7 @@
             full(populations.shape),
             full((5, 8, lanes)),
             full((5, 8, lanes)),
-            full((24, lanes)),
+            full((5, 8, lanes)),
             full((3, owned, mark)),
         ),
         in_specs=[smem] + [vmem] * 10,
@@ -632,16 +631,17 @@
     return cells
 
 
-def sideways(cells, side_ref, edge):
+def sideways(size_x, cells, side_ref, edge):
     def result(q, x, y_at):
         step_x, step_y = (int(step) for step in velocity_table[q][:2])
         size_y = y_at.shape[0]
-        size_x = side_ref.shape[0] // 6
         if step_y == 0:
             return cells(q, x)
         source = x - step_x
-        at = size_x * going(1, step_y).index(q) + source
-        halo = side_ref[at : at + 1, :] if 0 <= source < size_x else edge(q)
+        if 0 <= source < size_x:
+            halo = side_ref[going(1, step_y).index(q), source : source + 1, :]
+        else:
+            halo = edge(q)
         turned = pltpu.roll(cells(q, x), step_y % size_y, 0)
         return jnp.where(y_at == (0 if step_y == 1 else size_y - 1), halo, turned)
 
@@ -654,7 +654,7 @@
 
 
 def pack_kernel(
-    place_ref, relaxed_ref, far_ref, near_ref, side_ref, corner_ref, first_ref, second_ref
+    place_ref, relaxed_ref, far_ref, side_ref, near_ref, corner_ref, first_ref, second_ref
 ):
     size_y, lanes = far_ref.shape[1:]
     size_x = relaxed_ref.shape[1] // size_y
@@ -681,7 +681,7 @@
 
     y_at = lax.broadcasted_iota(jnp.int32, (size_y, lanes), 0)
     lane_at = lax.broadcasted_iota(jnp.int32, (size_y, lanes), 1)
-    level = sideways(cells, side_ref, None)
+    level = sideways(size_x, cells, side_ref, None)
     packs = []
     for step in (1, -1):
         packed = jnp.zeros((size_y, lanes), jnp.float32)
@@ -697,7 +697,7 @@
     second_ref[...] = jnp.where(even, packs[1], packs[0])
 
 
-def pack(place, relaxed, far, near, side):
+def pack(place, relaxed, far, side, near):
     smem = pl.BlockSpec(memory_space=pltpu.SMEM)
     vmem = pl.BlockSpec(memory_space=pltpu.VMEM)
     edge = full(far.shape[1:])
@@ -707,11 +707,11 @@
         in_specs=[smem] + [vmem] * 4,
         compiler_params=kernel_params(),
         name="pack",
-    )(place, relaxed, far, near, side)
+    )(place, relaxed, far, side, near)
 
 
 def stream_kernel(
-    count_z, place_ref, relaxed_ref, far_ref, near_ref, side_ref, second_ref, corner_ref,
+    count_z, place_ref, relaxed_ref, far_ref, side_ref, near_ref, second_ref, corner_ref,
     first_ref, out_any, out_ref, sems,
 ):
     size_x, size_y, lanes = out_ref.shape[1:]
@@ -720,6 +720,7 @@
     z_at = lax.broadcasted_iota(jnp.int32, shape, 1)
     y_index, z_index = (place_ref[0], place_ref[1])
     streamed = sideways(
+        size_x,
         downwind(place_ref, relaxed_ref, far_ref, near_ref),
         side_ref,
         lambda q: corner_ref[corner_index(q) : corner_index(q) + 1, :],
@@ -827,16 +828,16 @@
         "gx",
         [(i, (i - 1) % count_x) for i in evens] + [((i - 1) % count_x, i) for i in evens],
     )
+    side = across_y(side)
     near = lax.ppermute(near, "gx", [(i, i + 1) for i in evens] + [(i + 1, i) for i in evens])
-    side = across_y(side)
-    corner, up_first, down_first = pack(place, relaxed, far, near, side)
+    corner, up_first, down_first = pack(place, relaxed, far, side, near)
     inner = [(i, i + 1) for i in range(0, count_z - 1, 2)]
     outer = [(i, i + 1) for i in range(1, count_z - 1, 2)]
     down_first = lax.ppermute(down_first, "gz", outer + [(j, i) for i, j in outer])
     corner = across_y(corner)
     up_first = lax.ppermute(up_first, "gz", inner + [(j, i) for i, j in inner])
     populations_next = stream(
-        count_z, place, relaxed, far, near, side, down_first, corner, up_first
+        count_z, place, relaxed, far, side, near, down_first, corner, up_first
     )
     marker_force = marker_force.transpose(1, 0, 2).reshape(1, 1, 1, owned, 3, mark)
     return (populations_next, marker_force)

time: 49.2 us -> 50.1 us (1.018)
  waiting for transfers between devices: 10.2 us -> 11.4 us
    ppermute x1, waiting for transfers between devices: 0.01 us -> 1.33 us  [per_device(): lax.ppermute(near, 'gx', [(i, i + 1) for i in evens] + [(i + 1, i) for i...]
    ppermute x1, waiting for transfers between devices: 0.22 us -> 1.3 us  [per_device(): lax.ppermute(far, 'gx', [(i, (i - 1) % count_x) for i in evens] + [((i -...]
    ppermute x5, waiting for transfers between devices: 5.53 us -> 4.45 us  [across_y(): return lax.ppermute(entries, 'gy', swap)]
where the time goes in v10:
time: 50.1 us; the launch traced here: 49.9 us
  starting transfers between devices  21.2 us (42%)
  Pallas kernels  16.6 us (33%)
  waiting for transfers between devices  11.4 us (23%)
  between operations  0.7 us (1%)
    ppermute x1, starting transfers between devices, per_device(): lax.ppermute(down_first, 'gz', outer + [(j, i) for i, j in outer])  8.26 us
    pallas_call x1, Pallas kernels, spread(): pl.pallas_call(functools.partial(spread_kernel, slots, owned), out_shape=...  7.44 us
    ppermute x5, starting transfers between devices, across_y(): return lax.ppermute(entries, 'gy', swap)  6.28 us
    pallas_call x1, Pallas kernels, sample(): pl.pallas_call(sample_kernel, out_shape=[full((count, cells.shape[1]))] +...  5.9 us
    ppermute x4, starting transfers between devices, across_x(): lax.ppermute(entries, 'gx', [(i, i ^ distance) for i in range(count_x)])  5.38 us
    ppermute x5, waiting for transfers between devices, across_y(): return lax.ppermute(entries, 'gy', swap)  4.45 us
    ppermute x4, waiting for transfers between devices, across_x(): lax.ppermute(entries, 'gx', [(i, i ^ distance) for i in range(count_x)])  3.89 us
    pallas_call x1, Pallas kernels, stream(): pl.pallas_call(functools.partial(stream_kernel, count_z), out_shape=full(...  1.47 us
  transfers between devices with their start and end apart: 13, of which 10 were waited for; matrix products, arithmetic and copies ran while one was open for 0% of the time, Pallas kernels for 2%

profile of v10, /device:TPU:1, one launch (start us, length us, event | category | flops | bytes accessed | tf_op | source)
XLA Modules:
  0.0 49.9 jit_solution(4979844064721840674)
XLA Ops:
  0.6 0.1 pad_add_fusion.place_ref
  0.7 0.0 copy-start.1
  0.7 5.9 %sample.1 = (f32[232,128]{1,0:T(8,128)S(1)}, f32[19,32,128]{2,1,0:T(8,128)S(1)}, s32[512,128]{1,0:T(8,128)S(1)}, f32[512,128]{1,0:T(8,128)S(1)}) custom-call(s32[4]{0:T(128)S(1)} %pad_add_fusion.place_ref, f32[19,32,128]{2,1,0:T(8,128)} %bitcast.16, s32[512,128]{1,0:T(8,128)} %bitcast.17, f32[512,128]{1,0:T(8,128)} %bitcast.18, f32[32,128]{1,0:T(8,128)} %bitcast.19, ...), custom_call_target="tpu_custom_call" | custom-call | tf_op jit(solution)/shard_map/sample/pallas_call | solution.py:383
  6.6 4.2 %collective-permute-start = (f32[232,128]{1,0:T(8,128)S(1)}, f32[232,128]{1,0:T(8,128)S(1)}, u32[]{:S(2)}, u32[]{:S(2)}) collective-permute-start(f32[232,128]{1,0:T(8,128)S(1)} %get-tuple-element.19.refs_0_.own_ref), channel_id=1, source_target_pairs={{0,24},{8,16},{16,8},{24,0},{1,25},{9,17},{17,9},{25,1},{2,26},{10... | collective-permute-start | bytes 356360 | tf_op jit(solution)/shard_map/ppermute | solution.py:808
  10.8 1.2 %collective-permute-start.1 = (f32[232,128]{1,0:T(8,128)S(1)}, f32[232,128]{1,0:T(8,128)S(1)}, u32[]{:S(2)}, u32[]{:S(2)}) collective-permute-start(f32[232,128]{1,0:T(8,128)S(1)} %get-tuple-element.19.refs_0_.own_ref), channel_id=1, source_target_pairs={{0,4},{4,0},{1,5},{5,1},{2,6},{6,2},{3,7},{7,3},{8,12},{12,8},{9,1... | collective-permute-start | bytes 356360 | tf_op jit(solution)/shard_map/ppermute | solution.py:811
  12.1 0.0 collective-permute-start.4
  12.1 1.8 %collective-permute-done.refs_2_ = f32[232,128]{1,0:T(8,128)S(1)} collective-permute-done((f32[232,128]{1,0:T(8,128)S(1)}, f32[232,128]{1,0:T(8,128)S(1)}, u32[]{:S(2)}, u32[]{:S(2)}) %collective-permute-start) | collective-permute-done | bytes 118816 | tf_op jit(solution)/shard_map/ppermute | solution.py:808
  13.8 1.0 %collective-permute-done.1.refs_4_ = f32[232,128]{1,0:T(8,128)S(1)} collective-permute-done((f32[232,128]{1,0:T(8,128)S(1)}, f32[232,128]{1,0:T(8,128)S(1)}, u32[]{:S(2)}, u32[]{:S(2)}) %collective-permute-start.1) | collective-permute-done | bytes 118816 | tf_op jit(solution)/shard_map/ppermute | solution.py:811
  14.8 1.2 %collective-permute-start.2 = (f32[232,128]{1,0:T(8,128)S(1)}, f32[232,128]{1,0:T(8,128)S(1)}, u32[]{:S(2)}, u32[]{:S(2)}) collective-permute-start(f32[232,128]{1,0:T(8,128)S(1)} %collective-permute-done.refs_2_), channel_id=1, source_target_pairs={{0,4},{4,0},{1,5},{5,1},{2,6},{6,2},{3,7},{7,3},{8,12},{12,8},{9,1... | collective-permute-start | bytes 356360 | tf_op jit(solution)/shard_map/ppermute | solution.py:811
  16.0 0.5 collective-permute-start.5
  16.5 0.0 collective-permute-done.4.refs_1_
  16.5 1.1 %collective-permute-start.6 = (f32[232,128]{1,0:T(8,128)S(1)}, f32[232,128]{1,0:T(8,128)S(1)}, u32[]{:S(2)}, u32[]{:S(2)}) collective-permute-start(f32[232,128]{1,0:T(8,128)S(1)} %collective-permute-done.4.refs_1_), channel_id=1, source_target_pairs={{0,4},{4,0},{1,5},{5,1},{2,6},{6,2},{3,7},{7,3},{8,12},{12,8},{9,1... | collective-permute-start | bytes 356360 | tf_op jit(solution)/shard_map/ppermute | solution.py:811
  17.6 0.9 %collective-permute-done.2.refs_6_ = f32[232,128]{1,0:T(8,128)S(1)} collective-permute-done((f32[232,128]{1,0:T(8,128)S(1)}, f32[232,128]{1,0:T(8,128)S(1)}, u32[]{:S(2)}, u32[]{:S(2)}) %collective-permute-start.2) | collective-permute-done | bytes 118816 | tf_op jit(solution)/shard_map/ppermute | solution.py:811
  18.5 0.7 %collective-permute-start.3 = (f32[232,128]{1,0:T(8,128)S(1)}, f32[232,128]{1,0:T(8,128)S(1)}, u32[]{:S(2)}, u32[]{:S(2)}) collective-permute-start(f32[232,128]{1,0:T(8,128)S(1)} %collective-permute-done.2.refs_6_), channel_id=1, source_target_pairs={{0,8},{8,0},{16,24},{24,16},{1,9},{9,1},{17,25},{25,17},{2,10},{10... | collective-permute-start | bytes 356360 | tf_op jit(solution)/shard_map/ppermute | solution.py:808
  19.2 0.8 %collective-permute-done.5.refs_3_ = f32[232,128]{1,0:T(8,128)S(1)} collective-permute-done((f32[232,128]{1,0:T(8,128)S(1)}, f32[232,128]{1,0:T(8,128)S(1)}, u32[]{:S(2)}, u32[]{:S(2)}) %collective-permute-start.5) | collective-permute-done | bytes 118816 | tf_op jit(solution)/shard_map/ppermute | solution.py:808
  20.0 1.3 %collective-permute-done.6.refs_5_ = f32[232,128]{1,0:T(8,128)S(1)} collective-permute-done((f32[232,128]{1,0:T(8,128)S(1)}, f32[232,128]{1,0:T(8,128)S(1)}, u32[]{:S(2)}, u32[]{:S(2)}) %collective-permute-start.6) | collective-permute-done | bytes 118816 | tf_op jit(solution)/shard_map/ppermute | solution.py:811
  21.3 0.0 copy-done.1
  21.3 0.0 copy-start
  21.3 1.1 %settle.1 = (f32[96,384]{1,0:T(8,128)S(1)}, f32[64,128]{1,0:T(8,128)S(1)}, f32[64,128]{1,0:T(8,128)S(1)}, f32[12,128]{1,0:T(8,128)S(1)}) custom-call(f32[4,3]{1,0:T(4,128)S(1)} %copy-done.1, f32[232,128]{1,0:T(8,128)S(1)} %get-tuple-element.19.refs_0_.own_ref, f32[232,128]{1,0:T(8,128)S(1)} %collective-permute-done.4.refs_1_, ...), custom_call_target="tpu_custom_call" | custom-call | flops 1000000000 | bytes 831488 | tf_op jit(solution)/shard_map/settle/pallas_call | solution.py:457
  22.4 1.3 %collective-permute-done.3.last_ref = f32[232,128]{1,0:T(8,128)S(1)} collective-permute-done((f32[232,128]{1,0:T(8,128)S(1)}, f32[232,128]{1,0:T(8,128)S(1)}, u32[]{:S(2)}, u32[]{:S(2)}) %collective-permute-start.3) | collective-permute-done | bytes 118816 | tf_op jit(solution)/shard_map/ppermute | solution.py:808
  23.7 0.0 copy-done
  23.7 7.4 %spread.1 = (f32[19,32,128]{2,1,0:T(8,128)S(1)}, f32[5,8,128]{2,1,0:T(8,128)S(1)}, f32[5,8,128]{2,1,0:T(8,128)S(1)}, f32[5,8,128]{2,1,0:T(8,128)S(1)}, f32[3,32,128]{2,1,0:T(8,128)}) custom-call(s32[4]{0:T(128)S(1)} %pad_add_fusion.place_ref, f32[232,128]{1,0:T(8,128)S(1)} %get-tuple-element.19.refs_0_.own_ref, ...), custom_call_target="tpu_custom_call" | custom-call | tf_op jit(solution)/shard_map/spread/pallas_call | solution.py:593
  31.1 1.3 %collective-permute-start.7 = (f32[5,8,128]{2,1,0:T(8,128)S(1)}, f32[5,8,128]{2,1,0:T(8,128)S(1)}, u32[]{:S(2)}, u32[]{:S(2)}) collective-permute-start(f32[5,8,128]{2,1,0:T(8,128)S(1)} %get-tuple-element.29), channel_id=1, source_target_pairs={{0,24},{16,8},{24,0},{8,16},{1,25},{17,9},{25,1},{9,17},{2,26},{18... | collective-permute-start | bytes 61448 | tf_op jit(solution)/shard_map/ppermute | solution.py:826
  32.4 1.9 %collective-permute-start.8 = (f32[5,8,128]{2,1,0:T(8,128)S(1)}, f32[5,8,128]{2,1,0:T(8,128)S(1)}, u32[]{:S(2)}, u32[]{:S(2)}) collective-permute-start(f32[5,8,128]{2,1,0:T(8,128)S(1)} %get-tuple-element.30), channel_id=1, source_target_pairs={{0,4},{4,0},{1,5},{5,1},{2,6},{6,2},{3,7},{7,3},{8,12},{12,8},{9,1... | collective-permute-start | bytes 61448 | tf_op jit(solution)/shard_map/ppermute | solution.py:811
  34.3 0.0 collective-permute-start.9
  34.3 1.3 %collective-permute-done.7.far_ref = f32[5,8,128]{2,1,0:T(8,128)S(1)} collective-permute-done((f32[5,8,128]{2,1,0:T(8,128)S(1)}, f32[5,8,128]{2,1,0:T(8,128)S(1)}, u32[]{:S(2)}, u32[]{:S(2)}) %collective-permute-start.7) | collective-permute-done | bytes 20512 | tf_op jit(solution)/shard_map/ppermute | solution.py:826
  35.6 0.0 collective-permute-done.8.side_ref
  35.6 1.3 %collective-permute-done.9.near_ref = f32[5,8,128]{2,1,0:T(8,128)S(1)} collective-permute-done((f32[5,8,128]{2,1,0:T(8,128)S(1)}, f32[5,8,128]{2,1,0:T(8,128)S(1)}, u32[]{:S(2)}, u32[]{:S(2)}) %collective-permute-start.9) | collective-permute-done | bytes 20512 | tf_op jit(solution)/shard_map/ppermute | solution.py:832
  37.0 0.7 %pack.1 = (f32[8,128]{1,0:T(8,128)S(1)}, f32[8,128]{1,0:T(8,128)S(1)}, f32[8,128]{1,0:T(8,128)S(1)}) custom-call(s32[4]{0:T(128)S(1)} %pad_add_fusion.place_ref, f32[19,32,128]{2,1,0:T(8,128)S(1)} %get-tuple-element.28.relaxed_ref, f32[5,8,128]{2,1,0:T(8,128)S(1)} %collective-permute-done.7.far_ref, f32[5,8,128]{2,1,0:T(8,128)S(1)} %collective-permute-done.8.side_ref, ...), custom_call_target="tpu_custom_call" | custom-call | tf_op jit(solution)/shard_map/pack/pallas_call | solution.py:704
  37.6 8.3 %collective-permute-start.10 = (f32[8,128]{1,0:T(8,128)S(1)}, f32[8,128]{1,0:T(8,128)S(1)}, u32[]{:S(2)}, u32[]{:S(2)}) collective-permute-start(f32[8,128]{1,0:T(8,128)S(1)} %get-tuple-element.32), channel_id=1, source_target_pairs={{1,2},{2,1},{5,6},{6,5},{9,10},{10,9},{13,14},{14,13},{17,18},{18,... | collective-permute-start | bytes 12296 | tf_op jit(solution)/shard_map/ppermute | solution.py:836
  45.9 0.9 %collective-permute-start.11 = (f32[8,128]{1,0:T(8,128)S(1)}, f32[8,128]{1,0:T(8,128)S(1)}, u32[]{:S(2)}, u32[]{:S(2)}) collective-permute-start(f32[8,128]{1,0:T(8,128)S(1)} %get-tuple-element.33), channel_id=1, source_target_pairs={{0,4},{4,0},{1,5},{5,1},{2,6},{6,2},{3,7},{7,3},{8,12},{12,8},{9,1... | collective-permute-start | bytes 12296 | tf_op jit(solution)/shard_map/ppermute | solution.py:811
  46.8 0.0 collective-permute-start.12
  46.8 0.4 collective-permute-done.10.second_ref
  47.2 1.2 %collective-permute-done.11.corner_ref = f32[8,128]{1,0:T(8,128)S(1)} collective-permute-done((f32[8,128]{1,0:T(8,128)S(1)}, f32[8,128]{1,0:T(8,128)S(1)}, u32[]{:S(2)}, u32[]{:S(2)}) %collective-permute-start.11) | collective-permute-done | bytes 4128 | tf_op jit(solution)/shard_map/ppermute | solution.py:811
  48.4 0.0 collective-permute-done.12.first_ref
  48.4 1.5 %stream.1 = f32[19,4,8,128]{3,2,1,0:T(8,128)} custom-call(s32[4]{0:T(128)S(1)} %pad_add_fusion.place_ref, f32[19,32,128]{2,1,0:T(8,128)S(1)} %get-tuple-element.28.relaxed_ref, f32[5,8,128]{2,1,0:T(8,128)S(1)} %collective-permute-done.7.far_ref, f32[5,8,128]{2,1,0:T(8,128)S(1)} %collective-permute-done.8.side_ref, ...), custom_call_target="tpu_custom_call" | custom-call | tf_op jit(solution)/shard_map/stream/pallas_call | solution.py:762
Async XLA Ops:
  0.7 20.6 %copy-start.1 = (f32[4,3]{1,0:T(4,128)S(1)}, f32[4,3]{1,0:T(4,128)}, u32[]{:S(2)}) copy-start(f32[4,3]{1,0:T(4,128)} %speeds_ref.1) | copy-start | bytes 148
  6.6 7.2 %collective-permute-start = (f32[232,128]{1,0:T(8,128)S(1)}, f32[232,128]{1,0:T(8,128)S(1)}, u32[]{:S(2)}, u32[]{:S(2)}) collective-permute-start(f32[232,128]{1,0:T(8,128)S(1)} %get-tuple-element.19.refs_0_.own_ref), channel_id=1, source_target_pairs={{0,24},{8,16},{16,8},{24,0},{1,25},{9,17},{17,9},{25,1},{2,26},{10... | collective-permute-start | bytes 356360 | tf_op jit(solution)/shard_map/ppermute | solution.py:808
  10.8 4.0 %collective-permute-start.1 = (f32[232,128]{1,0:T(8,128)S(1)}, f32[232,128]{1,0:T(8,128)S(1)}, u32[]{:S(2)}, u32[]{:S(2)}) collective-permute-start(f32[232,128]{1,0:T(8,128)S(1)} %get-tuple-element.19.refs_0_.own_ref), channel_id=1, source_target_pairs={{0,4},{4,0},{1,5},{5,1},{2,6},{6,2},{3,7},{7,3},{8,12},{12,8},{9,1... | collective-permute-start | bytes 356360 | tf_op jit(solution)/shard_map/ppermute | solution.py:811
  12.1 4.5 %collective-permute-start.4 = (f32[232,128]{1,0:T(8,128)S(1)}, f32[232,128]{1,0:T(8,128)S(1)}, u32[]{:S(2)}, u32[]{:S(2)}) collective-permute-start(f32[232,128]{1,0:T(8,128)S(1)} %get-tuple-element.19.refs_0_.own_ref), channel_id=1, source_target_pairs={{0,8},{8,0},{16,24},{24,16},{1,9},{9,1},{17,25},{25,17},{2,10},{10... | collective-permute-start | bytes 356360 | tf_op jit(solution)/shard_map/ppermute | solution.py:808
  14.8 3.7 %collective-permute-start.2 = (f32[232,128]{1,0:T(8,128)S(1)}, f32[232,128]{1,0:T(8,128)S(1)}, u32[]{:S(2)}, u32[]{:S(2)}) collective-permute-start(f32[232,128]{1,0:T(8,128)S(1)} %collective-permute-done.refs_2_), channel_id=1, source_target_pairs={{0,4},{4,0},{1,5},{5,1},{2,6},{6,2},{3,7},{7,3},{8,12},{12,8},{9,1... | collective-permute-start | bytes 356360 | tf_op jit(solution)/shard_map/ppermute | solution.py:811
  16.0 4.0 %collective-permute-start.5 = (f32[232,128]{1,0:T(8,128)S(1)}, f32[232,128]{1,0:T(8,128)S(1)}, u32[]{:S(2)}, u32[]{:S(2)}) collective-permute-start(f32[232,128]{1,0:T(8,128)S(1)} %collective-permute-done.refs_2_), channel_id=1, source_target_pairs={{0,8},{8,0},{16,24},{24,16},{1,9},{9,1},{17,25},{25,17},{2,10},{10... | collective-permute-start | bytes 356360 | tf_op jit(solution)/shard_map/ppermute | solution.py:808
  16.5 4.8 %collective-permute-start.6 = (f32[232,128]{1,0:T(8,128)S(1)}, f32[232,128]{1,0:T(8,128)S(1)}, u32[]{:S(2)}, u32[]{:S(2)}) collective-permute-start(f32[232,128]{1,0:T(8,128)S(1)} %collective-permute-done.4.refs_1_), channel_id=1, source_target_pairs={{0,4},{4,0},{1,5},{5,1},{2,6},{6,2},{3,7},{7,3},{8,12},{12,8},{9,1... | collective-permute-start | bytes 356360 | tf_op jit(solution)/shard_map/ppermute | solution.py:811
  18.5 5.2 %collective-permute-start.3 = (f32[232,128]{1,0:T(8,128)S(1)}, f32[232,128]{1,0:T(8,128)S(1)}, u32[]{:S(2)}, u32[]{:S(2)}) collective-permute-start(f32[232,128]{1,0:T(8,128)S(1)} %collective-permute-done.2.refs_6_), channel_id=1, source_target_pairs={{0,8},{8,0},{16,24},{24,16},{1,9},{9,1},{17,25},{25,17},{2,10},{10... | collective-permute-start | bytes 356360 | tf_op jit(solution)/shard_map/ppermute | solution.py:808
  21.3 2.4 %copy-start = (s32[4,8,128]{2,1,0:T(8,128)S(1)}, s32[4,8,128]{2,1,0:T(8,128)}, u32[]{:S(2)}) copy-start(s32[4,8,128]{2,1,0:T(8,128)} %param.10) | copy-start | bytes 49156
  31.1 4.5 %collective-permute-start.7 = (f32[5,8,128]{2,1,0:T(8,128)S(1)}, f32[5,8,128]{2,1,0:T(8,128)S(1)}, u32[]{:S(2)}, u32[]{:S(2)}) collective-permute-start(f32[5,8,128]{2,1,0:T(8,128)S(1)} %get-tuple-element.29), channel_id=1, source_target_pairs={{0,24},{16,8},{24,0},{8,16},{1,25},{17,9},{25,1},{9,17},{2,26},{18... | collective-permute-start | bytes 61448 | tf_op jit(solution)/shard_map/ppermute | solution.py:826
  32.4 3.2 %collective-permute-start.8 = (f32[5,8,128]{2,1,0:T(8,128)S(1)}, f32[5,8,128]{2,1,0:T(8,128)S(1)}, u32[]{:S(2)}, u32[]{:S(2)}) collective-permute-start(f32[5,8,128]{2,1,0:T(8,128)S(1)} %get-tuple-element.30), channel_id=1, source_target_pairs={{0,4},{4,0},{1,5},{5,1},{2,6},{6,2},{3,7},{7,3},{8,12},{12,8},{9,1... | collective-permute-start | bytes 61448 | tf_op jit(solution)/shard_map/ppermute | solution.py:811
  34.3 2.6 %collective-permute-start.9 = (f32[5,8,128]{2,1,0:T(8,128)S(1)}, f32[5,8,128]{2,1,0:T(8,128)S(1)}, u32[]{:S(2)}, u32[]{:S(2)}) collective-permute-start(f32[5,8,128]{2,1,0:T(8,128)S(1)} %get-tuple-element.31), channel_id=1, source_target_pairs={{0,8},{16,24},{8,0},{24,16},{1,9},{17,25},{9,1},{25,17},{2,10},{18... | collective-permute-start | bytes 61448 | tf_op jit(solution)/shard_map/ppermute | solution.py:832
  37.6 9.5 %collective-permute-start.10 = (f32[8,128]{1,0:T(8,128)S(1)}, f32[8,128]{1,0:T(8,128)S(1)}, u32[]{:S(2)}, u32[]{:S(2)}) collective-permute-start(f32[8,128]{1,0:T(8,128)S(1)} %get-tuple-element.32), channel_id=1, source_target_pairs={{1,2},{2,1},{5,6},{6,5},{9,10},{10,9},{13,14},{14,13},{17,18},{18,... | collective-permute-start | bytes 12296 | tf_op jit(solution)/shard_map/ppermute | solution.py:836
  45.9 2.5 %collective-permute-start.11 = (f32[8,128]{1,0:T(8,128)S(1)}, f32[8,128]{1,0:T(8,128)S(1)}, u32[]{:S(2)}, u32[]{:S(2)}) collective-permute-start(f32[8,128]{1,0:T(8,128)S(1)} %get-tuple-element.33), channel_id=1, source_target_pairs={{0,4},{4,0},{1,5},{5,1},{2,6},{6,2},{3,7},{7,3},{8,12},{12,8},{9,1... | collective-permute-start | bytes 12296 | tf_op jit(solution)/shard_map/ppermute | solution.py:811
  46.8 1.6 %collective-permute-start.12 = (f32[8,128]{1,0:T(8,128)S(1)}, f32[8,128]{1,0:T(8,128)S(1)}, u32[]{:S(2)}, u32[]{:S(2)}) collective-permute-start(f32[8,128]{1,0:T(8,128)S(1)} %get-tuple-element.34), channel_id=1, source_target_pairs={{0,1},{2,3},{1,0},{3,2},{4,5},{6,7},{5,4},{7,6},{8,9},{10,11},{9,8... | collective-permute-start | bytes 12296 | tf_op jit(solution)/shard_map/ppermute | solution.py:838

commit v11 on v9

--- a/solution.py
+++ b/solution.py
@@ -440,13 +440,14 @@
 
 
 def settle_kernel(slots, owned, speeds_ref, *refs):
-    *shards, sums_ref, area_ref, trains_ref, rows_ref = refs
+    *shards, sums_ref, area_ref, trains_ref, rows_ref, labels_ref = refs
     mark = rows_ref.shape[1]
     for train in range(speeds_ref.shape[0]):
         for c in range(3):
             at = 3 * train + c
             rows_ref[at : at + 1, :] = jnp.full((1, mark), speeds_ref[train, c], jnp.float32)
-    ids, mine, _ = wanted_labels(shards[0], slots, owned)
+    ids, mine, own_trains = wanted_labels(shards[0], slots, owned)
+    labels_ref[...] = jnp.concatenate([ids, mine, own_trains], axis=0)
     sums_ref[...], area_ref[...], trains_ref[...] = add_shards(None, shards, ids, mine)
 
 
@@ -461,6 +462,7 @@
             full((slots, mark)),
             full((slots, mark)),
             full((3 * speeds.shape[0], mark)),
+            full((slots + 2 * owned, mark)),
         ),
         in_specs=[smem] + [vmem] * len(shards),
         compiler_params=kernel_params(),
@@ -471,10 +473,10 @@
     )(speeds, *shards)
 
 
-def block_forces(rows_ref, totals, own_ref, slots, owned):
+def block_forces(rows_ref, totals, own_ref, own_trains):
     mark = own_ref.shape[1]
-    ids, mine, own_trains = wanted_labels(own_ref, slots, owned)
     sums, area, trains = totals
+    slots, owned = (area.shape[0], own_trains.shape[0])
     trains = jnp.broadcast_to(jnp.sum(trains, axis=1, keepdims=True), area.shape)
     own_area = own_ref[8 : 8 + owned, :]
     forces, own_forces = ([], [])
@@ -493,6 +495,7 @@
 
 def spread_kernel(
     slots, owned, place_ref, own_ref, last_ref, sums_ref, area_ref, trains_ref, speeds_ref,
+    labels_ref,
     cells_ref, weights_ref, pop_ref, solid_ref,
     relaxed_ref, far_ref, near_ref, side_ref, marker_any, marker_ref, force_ref, lines_ref, acc,
     sem,
@@ -502,9 +505,10 @@
     mark = cells_ref.shape[1]
     kernel = cells_ref.shape[0] // slots
     bf = jnp.bfloat16
-    ids, mine, _ = wanted_labels(own_ref, slots, owned)
+    ids = labels_ref[0:slots]
+    mine, own_trains = (labels_ref[at : at + owned] for at in (slots, slots + owned))
     totals = add_shards((sums_ref[...], area_ref[...], trains_ref[...]), [last_ref], ids, mine)
-    forces, own_forces = block_forces(speeds_ref, totals, own_ref, slots, owned)
+    forces, own_forces = block_forces(speeds_ref, totals, own_ref, own_trains)
     largest = jnp.maximum(jnp.maximum(jnp.abs(forces[0]), jnp.abs(forces[1])), jnp.abs(forces[2]))
     largest = jnp.maximum(jnp.max(largest, axis=(0, 1), keepdims=True), 1e-20)
     scale = (224.0 * 16.0) / largest
@@ -600,7 +604,7 @@
             full((24, lanes)),
             full((3, owned, mark)),
         ),
-        in_specs=[smem] + [vmem] * 10,
+        in_specs=[smem] + [vmem] * 11,
         out_specs=[vmem] * 4 + [pl.BlockSpec(memory_space=pltpu.HBM)],
         scratch_shapes=[
             pltpu.VMEM((3, owned, mark), jnp.float32),
@@ -811,8 +815,8 @@
 
     third, first = (across_x(own, distance) for distance in (3, 1))
     beside = across_y(own)
-    third_beside = across_y(lax.optimization_barrier((third, beside))[0])
-    second = across_x(third, 1)
+    third_beside = across_y(third)
+    second = across_x(lax.optimization_barrier((third, beside))[0], 1)
     first_beside = across_y(first)
     last = across_x(third_beside, 1)
     whole = [own, first, third, second, beside, first_beside, third_beside]

time: 49.2 us -> 49.2 us (level)
    ppermute x1, starting transfers between devices: 1.3 us -> 2.29 us  [per_device(): lax.ppermute(far, 'gx', [(i, (i - 1) % count_x) for i in evens] + [((i -...]
    ppermute x5, starting transfers between devices: 6.1 us -> 5.12 us  [across_y(): return lax.ppermute(entries, 'gy', swap)]
  transfers between devices with their start and end apart: 13 -> 13, of which waited for: 10 -> 9; matrix products, arithmetic and copies ran while one was open for 0% -> 0% of each run, Pallas kernels for 2% -> 2%
where the time goes in v11:
time: 49.2 us; the launch traced here: 49 us
  starting transfers between devices  21.8 us (44%)
  Pallas kernels  16.5 us (34%)
  waiting for transfers between devices  9.78 us (20%)
  between operations  0.71 us (1%)
    ppermute x1, starting transfers between devices, per_device(): lax.ppermute(down_first, 'gz', outer + [(j, i) for i, j in outer])  8.54 us
    pallas_call x1, Pallas kernels, spread(): pl.pallas_call(functools.partial(spread_kernel, slots, owned), out_shape=...  7.4 us
    pallas_call x1, Pallas kernels, sample(): pl.pallas_call(sample_kernel, out_shape=[full((count, cells.shape[1]))] +...  5.9 us
    ppermute x4, starting transfers between devices, across_x(): lax.ppermute(entries, 'gx', [(i, i ^ distance) for i in range(count_x)])  5.8 us
    ppermute x5, waiting for transfers between devices, across_y(): return lax.ppermute(entries, 'gy', swap)  5.13 us
    ppermute x5, starting transfers between devices, across_y(): return lax.ppermute(entries, 'gy', swap)  5.12 us
    ppermute x4, waiting for transfers between devices, across_x(): lax.ppermute(entries, 'gx', [(i, i ^ distance) for i in range(count_x)])  3.99 us
    ppermute x1, starting transfers between devices, per_device(): lax.ppermute(far, 'gx', [(i, (i - 1) % count_x) for i in evens] + [((i -...  2.29 us
  transfers between devices with their start and end apart: 13, of which 9 were waited for; matrix products, arithmetic and copies ran while one was open for 0% of the time, Pallas kernels for 2%

profile of v11, /device:TPU:1, one launch (start us, length us, event | category | flops | bytes accessed | tf_op | source)
XLA Modules:
  0.0 49.0 jit_solution(4685234271362794091)
XLA Ops:
  0.6 0.1 pad_add_fusion.place_ref
  0.7 0.0 copy-start.1
  0.7 5.9 %sample.1 = (f32[232,128]{1,0:T(8,128)S(1)}, f32[19,32,128]{2,1,0:T(8,128)S(1)}, s32[512,128]{1,0:T(8,128)S(1)}, f32[512,128]{1,0:T(8,128)S(1)}) custom-call(s32[4]{0:T(128)S(1)} %pad_add_fusion.place_ref, f32[19,32,128]{2,1,0:T(8,128)} %bitcast.16, s32[512,128]{1,0:T(8,128)} %bitcast.17, f32[512,128]{1,0:T(8,128)} %bitcast.18, f32[32,128]{1,0:T(8,128)} %bitcast.19, ...), custom_call_target="tpu_custom_call" | custom-call | tf_op jit(solution)/shard_map/sample/pallas_call | solution.py:383
  6.6 4.2 %collective-permute-start = (f32[232,128]{1,0:T(8,128)S(1)}, f32[232,128]{1,0:T(8,128)S(1)}, u32[]{:S(2)}, u32[]{:S(2)}) collective-permute-start(f32[232,128]{1,0:T(8,128)S(1)} %get-tuple-element.20.refs_0_.own_ref), channel_id=1, source_target_pairs={{0,24},{8,16},{16,8},{24,0},{1,25},{9,17},{17,9},{25,1},{2,26},{10... | collective-permute-start | bytes 356360 | tf_op jit(solution)/shard_map/ppermute | solution.py:811
  10.8 1.2 %collective-permute-start.4 = (f32[232,128]{1,0:T(8,128)S(1)}, f32[232,128]{1,0:T(8,128)S(1)}, u32[]{:S(2)}, u32[]{:S(2)}) collective-permute-start(f32[232,128]{1,0:T(8,128)S(1)} %get-tuple-element.20.refs_0_.own_ref), channel_id=1, source_target_pairs={{0,4},{4,0},{1,5},{5,1},{2,6},{6,2},{3,7},{7,3},{8,12},{12,8},{9,1... | collective-permute-start | bytes 356360 | tf_op jit(solution)/shard_map/ppermute | solution.py:814
  12.1 0.0 collective-permute-start.3
  12.1 1.8 %collective-permute-done.refs_2_ = f32[232,128]{1,0:T(8,128)S(1)} collective-permute-done((f32[232,128]{1,0:T(8,128)S(1)}, f32[232,128]{1,0:T(8,128)S(1)}, u32[]{:S(2)}, u32[]{:S(2)}) %collective-permute-start) | collective-permute-done | bytes 118816 | tf_op jit(solution)/shard_map/ppermute | solution.py:811
  13.8 1.0 %collective-permute-start.1 = (f32[232,128]{1,0:T(8,128)S(1)}, f32[232,128]{1,0:T(8,128)S(1)}, u32[]{:S(2)}, u32[]{:S(2)}) collective-permute-start(f32[232,128]{1,0:T(8,128)S(1)} %collective-permute-done.refs_2_), channel_id=1, source_target_pairs={{0,4},{4,0},{1,5},{5,1},{2,6},{6,2},{3,7},{7,3},{8,12},{12,8},{9,1... | collective-permute-start | bytes 356360 | tf_op jit(solution)/shard_map/ppermute | solution.py:814
  14.9 0.0 collective-permute-done.4.refs_4_
  14.9 1.4 %collective-permute-done.3.refs_1_ = f32[232,128]{1,0:T(8,128)S(1)} collective-permute-done((f32[232,128]{1,0:T(8,128)S(1)}, f32[232,128]{1,0:T(8,128)S(1)}, u32[]{:S(2)}, u32[]{:S(2)}) %collective-permute-start.3) | collective-permute-done | bytes 118816 | tf_op jit(solution)/shard_map/ppermute | solution.py:811
  16.2 1.4 %collective-permute-start.6 = (f32[232,128]{1,0:T(8,128)S(1)}, f32[232,128]{1,0:T(8,128)S(1)}, u32[]{:S(2)}, u32[]{:S(2)}) collective-permute-start(f32[232,128]{1,0:T(8,128)S(1)} %collective-permute-done.3.refs_1_), channel_id=1, source_target_pairs={{0,4},{4,0},{1,5},{5,1},{2,6},{6,2},{3,7},{7,3},{8,12},{12,8},{9,1... | collective-permute-start | bytes 356360 | tf_op jit(solution)/shard_map/ppermute | solution.py:814
  17.6 1.2 %collective-permute-start.5 = (f32[232,128]{1,0:T(8,128)S(1)}, f32[232,128]{1,0:T(8,128)S(1)}, u32[]{:S(2)}, u32[]{:S(2)}) collective-permute-start(f32[232,128]{1,0:T(8,128)S(1)} %collective-permute-done.refs_2_), channel_id=1, source_target_pairs={{0,8},{8,0},{16,24},{24,16},{1,9},{9,1},{17,25},{25,17},{2,10},{10... | collective-permute-start | bytes 356360 | tf_op jit(solution)/shard_map/ppermute | solution.py:811
  18.8 0.0 collective-permute-done.1.refs_6_
  18.8 0.4 collective-permute-start.2
  19.2 2.2 %collective-permute-done.6.refs_5_ = f32[232,128]{1,0:T(8,128)S(1)} collective-permute-done((f32[232,128]{1,0:T(8,128)S(1)}, f32[232,128]{1,0:T(8,128)S(1)}, u32[]{:S(2)}, u32[]{:S(2)}) %collective-permute-start.6) | collective-permute-done | bytes 118816 | tf_op jit(solution)/shard_map/ppermute | solution.py:814
  21.4 0.2 collective-permute-done.5.refs_3_
  21.6 0.0 copy-done.1
  21.6 1.1 %settle.1 = (f32[96,384]{1,0:T(8,128)S(1)}, f32[64,128]{1,0:T(8,128)S(1)}, f32[64,128]{1,0:T(8,128)S(1)}, f32[12,128]{1,0:T(8,128)S(1)}, f32[128,128]{1,0:T(8,128)S(1)}) custom-call(f32[4,3]{1,0:T(4,128)S(1)} %copy-done.1, f32[232,128]{1,0:T(8,128)S(1)} %get-tuple-element.20.refs_0_.own_ref, f32[232,128]{1,0:T(8,128)S(1)} %collective-permute-done.3.refs_1_, ...), custom_call_target="tpu_custom_call" | custom-call | flops 1000000000 | bytes 831488 | tf_op jit(solution)/shard_map/settle/pallas_call | solution.py:458
  22.7 0.0 copy-start
  22.7 0.6 %collective-permute-done.2.last_ref = f32[232,128]{1,0:T(8,128)S(1)} collective-permute-done((f32[232,128]{1,0:T(8,128)S(1)}, f32[232,128]{1,0:T(8,128)S(1)}, u32[]{:S(2)}, u32[]{:S(2)}) %collective-permute-start.2) | collective-permute-done | bytes 118816 | tf_op jit(solution)/shard_map/ppermute | solution.py:811
  23.3 0.1 copy-done
  23.4 7.4 %spread.1 = (f32[19,32,128]{2,1,0:T(8,128)S(1)}, f32[5,8,128]{2,1,0:T(8,128)S(1)}, f32[5,8,128]{2,1,0:T(8,128)S(1)}, f32[24,128]{1,0:T(8,128)S(1)}, f32[3,32,128]{2,1,0:T(8,128)}) custom-call(s32[4]{0:T(128)S(1)} %pad_add_fusion.place_ref, f32[232,128]{1,0:T(8,128)S(1)} %get-tuple-element.20.refs_0_.own_ref, f32[232,128]{1,0:T(8,128)S(1)} %collective-permute-done.2.last_ref, ...), custom_call_target="tpu_custom_call" | custom-call | tf_op jit(solution)/shard_map/spread/pallas_call | solution.py:598
  30.8 2.3 %collective-permute-start.7 = (f32[5,8,128]{2,1,0:T(8,128)S(1)}, f32[5,8,128]{2,1,0:T(8,128)S(1)}, u32[]{:S(2)}, u32[]{:S(2)}) collective-permute-start(f32[5,8,128]{2,1,0:T(8,128)S(1)} %get-tuple-element.31), channel_id=1, source_target_pairs={{0,24},{16,8},{24,0},{8,16},{1,25},{17,9},{25,1},{9,17},{2,26},{18... | collective-permute-start | bytes 61448 | tf_op jit(solution)/shard_map/ppermute | solution.py:829
  33.1 0.0 collective-permute-start.8
  33.1 0.8 %collective-permute-start.9 = (f32[24,128]{1,0:T(8,128)S(1)}, f32[24,128]{1,0:T(8,128)S(1)}, u32[]{:S(2)}, u32[]{:S(2)}) collective-permute-start(f32[24,128]{1,0:T(8,128)S(1)} %get-tuple-element.33), channel_id=1, source_target_pairs={{0,4},{4,0},{1,5},{5,1},{2,6},{6,2},{3,7},{7,3},{8,12},{12,8},{9,1... | collective-permute-start | bytes 36872 | tf_op jit(solution)/shard_map/ppermute | solution.py:814
  33.9 1.7 %collective-permute-done.9.side_ref = f32[24,128]{1,0:T(8,128)S(1)} collective-permute-done((f32[24,128]{1,0:T(8,128)S(1)}, f32[24,128]{1,0:T(8,128)S(1)}, u32[]{:S(2)}, u32[]{:S(2)}) %collective-permute-start.9) | collective-permute-done | bytes 12320 | tf_op jit(solution)/shard_map/ppermute | solution.py:814
  35.6 0.0 collective-permute-done.7.far_ref
  35.6 0.1 collective-permute-done.8.near_ref
  35.7 0.7 %pack.1 = (f32[8,128]{1,0:T(8,128)S(1)}, f32[8,128]{1,0:T(8,128)S(1)}, f32[8,128]{1,0:T(8,128)S(1)}) custom-call(s32[4]{0:T(128)S(1)} %pad_add_fusion.place_ref, f32[19,32,128]{2,1,0:T(8,128)S(1)} %get-tuple-element.30.relaxed_ref, f32[5,8,128]{2,1,0:T(8,128)S(1)} %collective-permute-done.7.far_ref, f32[5,8,128]{2,1,0:T(8,128)S(1)} %collective-permute-done.8.near_ref, ...), custom_call_target="tpu_custom_call" | custom-call | tf_op jit(solution)/shard_map/pack/pallas_call | solution.py:708
  36.4 8.5 %collective-permute-start.10 = (f32[8,128]{1,0:T(8,128)S(1)}, f32[8,128]{1,0:T(8,128)S(1)}, u32[]{:S(2)}, u32[]{:S(2)}) collective-permute-start(f32[8,128]{1,0:T(8,128)S(1)} %get-tuple-element.34), channel_id=1, source_target_pairs={{1,2},{2,1},{5,6},{6,5},{9,10},{10,9},{13,14},{14,13},{17,18},{18,... | collective-permute-start | bytes 12296 | tf_op jit(solution)/shard_map/ppermute | solution.py:839
  44.9 0.7 %collective-permute-start.11 = (f32[8,128]{1,0:T(8,128)S(1)}, f32[8,128]{1,0:T(8,128)S(1)}, u32[]{:S(2)}, u32[]{:S(2)}) collective-permute-start(f32[8,128]{1,0:T(8,128)S(1)} %get-tuple-element.35), channel_id=1, source_target_pairs={{0,4},{4,0},{1,5},{5,1},{2,6},{6,2},{3,7},{7,3},{8,12},{12,8},{9,1... | collective-permute-start | bytes 12296 | tf_op jit(solution)/shard_map/ppermute | solution.py:814
  45.7 0.0 collective-permute-start.12
  45.7 0.6 %collective-permute-done.10.second_ref = f32[8,128]{1,0:T(8,128)S(1)} collective-permute-done((f32[8,128]{1,0:T(8,128)S(1)}, f32[8,128]{1,0:T(8,128)S(1)}, u32[]{:S(2)}, u32[]{:S(2)}) %collective-permute-start.10) | collective-permute-done | bytes 4128 | tf_op jit(solution)/shard_map/ppermute | solution.py:839
  46.2 1.2 %collective-permute-done.11.corner_ref = f32[8,128]{1,0:T(8,128)S(1)} collective-permute-done((f32[8,128]{1,0:T(8,128)S(1)}, f32[8,128]{1,0:T(8,128)S(1)}, u32[]{:S(2)}, u32[]{:S(2)}) %collective-permute-start.11) | collective-permute-done | bytes 4128 | tf_op jit(solution)/shard_map/ppermute | solution.py:814
  47.5 0.0 collective-permute-done.12.first_ref
  47.5 1.5 %stream.1 = f32[19,4,8,128]{3,2,1,0:T(8,128)} custom-call(s32[4]{0:T(128)S(1)} %pad_add_fusion.place_ref, f32[19,32,128]{2,1,0:T(8,128)S(1)} %get-tuple-element.30.relaxed_ref, f32[5,8,128]{2,1,0:T(8,128)S(1)} %collective-permute-done.7.far_ref, f32[5,8,128]{2,1,0:T(8,128)S(1)} %collective-permute-done.8.near_ref, ...), custom_call_target="tpu_custom_call" | custom-call | tf_op jit(solution)/shard_map/stream/pallas_call | solution.py:765
Async XLA Ops:
  0.7 20.9 %copy-start.1 = (f32[4,3]{1,0:T(4,128)S(1)}, f32[4,3]{1,0:T(4,128)}, u32[]{:S(2)}) copy-start(f32[4,3]{1,0:T(4,128)} %speeds_ref.1) | copy-start | bytes 148
  6.6 7.2 %collective-permute-start = (f32[232,128]{1,0:T(8,128)S(1)}, f32[232,128]{1,0:T(8,128)S(1)}, u32[]{:S(2)}, u32[]{:S(2)}) collective-permute-start(f32[232,128]{1,0:T(8,128)S(1)} %get-tuple-element.20.refs_0_.own_ref), channel_id=1, source_target_pairs={{0,24},{8,16},{16,8},{24,0},{1,25},{9,17},{17,9},{25,1},{2,26},{10... | collective-permute-start | bytes 356360 | tf_op jit(solution)/shard_map/ppermute | solution.py:811
  10.8 4.0 %collective-permute-start.4 = (f32[232,128]{1,0:T(8,128)S(1)}, f32[232,128]{1,0:T(8,128)S(1)}, u32[]{:S(2)}, u32[]{:S(2)}) collective-permute-start(f32[232,128]{1,0:T(8,128)S(1)} %get-tuple-element.20.refs_0_.own_ref), channel_id=1, source_target_pairs={{0,4},{4,0},{1,5},{5,1},{2,6},{6,2},{3,7},{7,3},{8,12},{12,8},{9,1... | collective-permute-start | bytes 356360 | tf_op jit(solution)/shard_map/ppermute | solution.py:814
  12.1 4.2 %collective-permute-start.3 = (f32[232,128]{1,0:T(8,128)S(1)}, f32[232,128]{1,0:T(8,128)S(1)}, u32[]{:S(2)}, u32[]{:S(2)}) collective-permute-start(f32[232,128]{1,0:T(8,128)S(1)} %get-tuple-element.20.refs_0_.own_ref), channel_id=1, source_target_pairs={{0,8},{8,0},{16,24},{24,16},{1,9},{9,1},{17,25},{25,17},{2,10},{10... | collective-permute-start | bytes 356360 | tf_op jit(solution)/shard_map/ppermute | solution.py:811
  13.8 4.9 %collective-permute-start.1 = (f32[232,128]{1,0:T(8,128)S(1)}, f32[232,128]{1,0:T(8,128)S(1)}, u32[]{:S(2)}, u32[]{:S(2)}) collective-permute-start(f32[232,128]{1,0:T(8,128)S(1)} %collective-permute-done.refs_2_), channel_id=1, source_target_pairs={{0,4},{4,0},{1,5},{5,1},{2,6},{6,2},{3,7},{7,3},{8,12},{12,8},{9,1... | collective-permute-start | bytes 356360 | tf_op jit(solution)/shard_map/ppermute | solution.py:814
  16.2 5.1 %collective-permute-start.6 = (f32[232,128]{1,0:T(8,128)S(1)}, f32[232,128]{1,0:T(8,128)S(1)}, u32[]{:S(2)}, u32[]{:S(2)}) collective-permute-start(f32[232,128]{1,0:T(8,128)S(1)} %collective-permute-done.3.refs_1_), channel_id=1, source_target_pairs={{0,4},{4,0},{1,5},{5,1},{2,6},{6,2},{3,7},{7,3},{8,12},{12,8},{9,1... | collective-permute-start | bytes 356360 | tf_op jit(solution)/shard_map/ppermute | solution.py:814
  17.6 4.0 %collective-permute-start.5 = (f32[232,128]{1,0:T(8,128)S(1)}, f32[232,128]{1,0:T(8,128)S(1)}, u32[]{:S(2)}, u32[]{:S(2)}) collective-permute-start(f32[232,128]{1,0:T(8,128)S(1)} %collective-permute-done.refs_2_), channel_id=1, source_target_pairs={{0,8},{8,0},{16,24},{24,16},{1,9},{9,1},{17,25},{25,17},{2,10},{10... | collective-permute-start | bytes 356360 | tf_op jit(solution)/shard_map/ppermute | solution.py:811
  18.8 4.5 %collective-permute-start.2 = (f32[232,128]{1,0:T(8,128)S(1)}, f32[232,128]{1,0:T(8,128)S(1)}, u32[]{:S(2)}, u32[]{:S(2)}) collective-permute-start(f32[232,128]{1,0:T(8,128)S(1)} %collective-permute-done.1.refs_6_), channel_id=1, source_target_pairs={{0,8},{8,0},{16,24},{24,16},{1,9},{9,1},{17,25},{25,17},{2,10},{10... | collective-permute-start | bytes 356360 | tf_op jit(solution)/shard_map/ppermute | solution.py:811
  22.7 0.7 %copy-start = (s32[4,8,128]{2,1,0:T(8,128)S(1)}, s32[4,8,128]{2,1,0:T(8,128)}, u32[]{:S(2)}) copy-start(s32[4,8,128]{2,1,0:T(8,128)} %param.10) | copy-start | bytes 49156
  30.8 4.8 %collective-permute-start.7 = (f32[5,8,128]{2,1,0:T(8,128)S(1)}, f32[5,8,128]{2,1,0:T(8,128)S(1)}, u32[]{:S(2)}, u32[]{:S(2)}) collective-permute-start(f32[5,8,128]{2,1,0:T(8,128)S(1)} %get-tuple-element.31), channel_id=1, source_target_pairs={{0,24},{16,8},{24,0},{8,16},{1,25},{17,9},{25,1},{9,17},{2,26},{18... | collective-permute-start | bytes 61448 | tf_op jit(solution)/shard_map/ppermute | solution.py:829
  33.1 2.6 %collective-permute-start.8 = (f32[5,8,128]{2,1,0:T(8,128)S(1)}, f32[5,8,128]{2,1,0:T(8,128)S(1)}, u32[]{:S(2)}, u32[]{:S(2)}) collective-permute-start(f32[5,8,128]{2,1,0:T(8,128)S(1)} %get-tuple-element.32), channel_id=1, source_target_pairs={{0,8},{16,24},{8,0},{24,16},{1,9},{17,25},{9,1},{25,17},{2,10},{18... | collective-permute-start | bytes 61448 | tf_op jit(solution)/shard_map/ppermute | solution.py:834
  33.1 2.5 %collective-permute-start.9 = (f32[24,128]{1,0:T(8,128)S(1)}, f32[24,128]{1,0:T(8,128)S(1)}, u32[]{:S(2)}, u32[]{:S(2)}) collective-permute-start(f32[24,128]{1,0:T(8,128)S(1)} %get-tuple-element.33), channel_id=1, source_target_pairs={{0,4},{4,0},{1,5},{5,1},{2,6},{6,2},{3,7},{7,3},{8,12},{12,8},{9,1... | collective-permute-start | bytes 36872 | tf_op jit(solution)/shard_map/ppermute | solution.py:814
  36.4 9.8 %collective-permute-start.10 = (f32[8,128]{1,0:T(8,128)S(1)}, f32[8,128]{1,0:T(8,128)S(1)}, u32[]{:S(2)}, u32[]{:S(2)}) collective-permute-start(f32[8,128]{1,0:T(8,128)S(1)} %get-tuple-element.34), channel_id=1, source_target_pairs={{1,2},{2,1},{5,6},{6,5},{9,10},{10,9},{13,14},{14,13},{17,18},{18,... | collective-permute-start | bytes 12296 | tf_op jit(solution)/shard_map/ppermute | solution.py:839
  44.9 2.5 %collective-permute-start.11 = (f32[8,128]{1,0:T(8,128)S(1)}, f32[8,128]{1,0:T(8,128)S(1)}, u32[]{:S(2)}, u32[]{:S(2)}) collective-permute-start(f32[8,128]{1,0:T(8,128)S(1)} %get-tuple-element.35), channel_id=1, source_target_pairs={{0,4},{4,0},{1,5},{5,1},{2,6},{6,2},{3,7},{7,3},{8,12},{12,8},{9,1... | collective-permute-start | bytes 12296 | tf_op jit(solution)/shard_map/ppermute | solution.py:814
  45.7 1.8 %collective-permute-start.12 = (f32[8,128]{1,0:T(8,128)S(1)}, f32[8,128]{1,0:T(8,128)S(1)}, u32[]{:S(2)}, u32[]{:S(2)}) collective-permute-start(f32[8,128]{1,0:T(8,128)S(1)} %get-tuple-element.36), channel_id=1, source_target_pairs={{0,1},{2,3},{1,0},{3,2},{4,5},{6,7},{5,4},{7,6},{8,9},{10,11},{9,8... | collective-permute-start | bytes 12296 | tf_op jit(solution)/shard_map/ppermute | solution.py:841

commit v12 on v11

--- a/solution.py
+++ b/solution.py
@@ -813,13 +813,13 @@
     def across_y(entries):
         return lax.ppermute(entries, "gy", swap)
 
-    third, first = (across_x(own, distance) for distance in (3, 1))
+    second, first = (across_x(own, distance) for distance in (2, 1))
     beside = across_y(own)
-    third_beside = across_y(third)
-    second = across_x(lax.optimization_barrier((third, beside))[0], 1)
+    second_beside = across_y(second)
+    third = across_x(lax.optimization_barrier((second, beside))[0], 1)
     first_beside = across_y(first)
-    last = across_x(third_beside, 1)
-    whole = [own, first, third, second, beside, first_beside, third_beside]
+    last = across_x(second_beside, 1)
+    whole = [own, first, second, third, beside, first_beside, second_beside]
     early = settle_early(slots, owned, train_velocity, whole)
     solid = solid_cells.reshape(lines, size_z)
     relaxed, far, near, side, marker_force = spread(

time: 49.2 us -> 50.3 us (1.022)
  starting transfers between devices: 21.8 us -> 23.7 us
  waiting for transfers between devices: 9.78 us -> 9.14 us
    ppermute x4, starting transfers between devices: 5.8 us -> 8.13 us  [across_x(): lax.ppermute(entries, 'gx', [(i, i ^ distance) for i in range(count_x)])]
    ppermute x1, starting transfers between devices: 2.29 us -> 3.86 us  [per_device(): lax.ppermute(far, 'gx', [(i, (i - 1) % count_x) for i in evens] + [((i -...]
    ppermute x5, waiting for transfers between devices: 5.13 us -> 3.89 us  [across_y(): return lax.ppermute(entries, 'gy', swap)]
    ppermute x1, starting transfers between devices: 8.54 us -> 7.37 us  [per_device(): lax.ppermute(down_first, 'gz', outer + [(j, i) for i, j in outer])]
    ppermute x4, waiting for transfers between devices: 3.99 us -> 5.04 us  [across_x(): lax.ppermute(entries, 'gx', [(i, i ^ distance) for i in range(count_x)])]
    ppermute x5, starting transfers between devices: 5.12 us -> 4.32 us  [across_y(): return lax.ppermute(entries, 'gy', swap)]
where the time goes in v12:
time: 50.3 us; the launch traced here: 50.1 us
  starting transfers between devices  23.7 us (47%)
  Pallas kernels  16.5 us (33%)
  waiting for transfers between devices  9.14 us (18%)
  between operations  0.7 us (1%)
    ppermute x4, starting transfers between devices, across_x(): lax.ppermute(entries, 'gx', [(i, i ^ distance) for i in range(count_x)])  8.13 us
    pallas_call x1, Pallas kernels, spread(): pl.pallas_call(functools.partial(spread_kernel, slots, owned), out_shape=...  7.41 us
    ppermute x1, starting transfers between devices, per_device(): lax.ppermute(down_first, 'gz', outer + [(j, i) for i, j in outer])  7.37 us
    pallas_call x1, Pallas kernels, sample(): pl.pallas_call(sample_kernel, out_shape=[full((count, cells.shape[1]))] +...  5.9 us
    ppermute x4, waiting for transfers between devices, across_x(): lax.ppermute(entries, 'gx', [(i, i ^ distance) for i in range(count_x)])  5.04 us
    ppermute x5, starting transfers between devices, across_y(): return lax.ppermute(entries, 'gy', swap)  4.32 us
    ppermute x5, waiting for transfers between devices, across_y(): return lax.ppermute(entries, 'gy', swap)  3.89 us
    ppermute x1, starting transfers between devices, per_device(): lax.ppermute(far, 'gx', [(i, (i - 1) % count_x) for i in evens] + [((i -...  3.86 us
  transfers between devices with their start and end apart: 13, of which 9 were waited for; matrix products, arithmetic and copies ran while one was open for 0% of the time, Pallas kernels for 2%

profile of v12, /device:TPU:1, one launch (start us, length us, event | category | flops | bytes accessed | tf_op | source)
XLA Modules:
  0.0 50.1 jit_solution(6535590566692659768)
XLA Ops:
  0.6 0.1 pad_add_fusion.place_ref
  0.7 0.0 copy-start.1
  0.7 5.9 %sample.1 = (f32[232,128]{1,0:T(8,128)S(1)}, f32[19,32,128]{2,1,0:T(8,128)S(1)}, s32[512,128]{1,0:T(8,128)S(1)}, f32[512,128]{1,0:T(8,128)S(1)}) custom-call(s32[4]{0:T(128)S(1)} %pad_add_fusion.place_ref, f32[19,32,128]{2,1,0:T(8,128)} %bitcast.16, s32[512,128]{1,0:T(8,128)} %bitcast.17, f32[512,128]{1,0:T(8,128)} %bitcast.18, f32[32,128]{1,0:T(8,128)} %bitcast.19, ...), custom_call_target="tpu_custom_call" | custom-call | tf_op jit(solution)/shard_map/sample/pallas_call | solution.py:383
  6.6 3.2 %collective-permute-start = (f32[232,128]{1,0:T(8,128)S(1)}, f32[232,128]{1,0:T(8,128)S(1)}, u32[]{:S(2)}, u32[]{:S(2)}) collective-permute-start(f32[232,128]{1,0:T(8,128)S(1)} %get-tuple-element.20.refs_0_.own_ref), channel_id=1, source_target_pairs={{0,16},{8,24},{16,0},{24,8},{1,17},{9,25},{17,1},{25,9},{2,18},{10... | collective-permute-start | bytes 356360 | tf_op jit(solution)/shard_map/ppermute | solution.py:811
  9.8 1.2 %collective-permute-start.4 = (f32[232,128]{1,0:T(8,128)S(1)}, f32[232,128]{1,0:T(8,128)S(1)}, u32[]{:S(2)}, u32[]{:S(2)}) collective-permute-start(f32[232,128]{1,0:T(8,128)S(1)} %get-tuple-element.20.refs_0_.own_ref), channel_id=1, source_target_pairs={{0,4},{4,0},{1,5},{5,1},{2,6},{6,2},{3,7},{7,3},{8,12},{12,8},{9,1... | collective-permute-start | bytes 356360 | tf_op jit(solution)/shard_map/ppermute | solution.py:814
  11.0 1.3 %collective-permute-start.3 = (f32[232,128]{1,0:T(8,128)S(1)}, f32[232,128]{1,0:T(8,128)S(1)}, u32[]{:S(2)}, u32[]{:S(2)}) collective-permute-start(f32[232,128]{1,0:T(8,128)S(1)} %get-tuple-element.20.refs_0_.own_ref), channel_id=1, source_target_pairs={{0,8},{8,0},{16,24},{24,16},{1,9},{9,1},{17,25},{25,17},{2,10},{10... | collective-permute-start | bytes 356360 | tf_op jit(solution)/shard_map/ppermute | solution.py:811
  12.3 2.5 %collective-permute-done.refs_2_ = f32[232,128]{1,0:T(8,128)S(1)} collective-permute-done((f32[232,128]{1,0:T(8,128)S(1)}, f32[232,128]{1,0:T(8,128)S(1)}, u32[]{:S(2)}, u32[]{:S(2)}) %collective-permute-start) | collective-permute-done | bytes 118816 | tf_op jit(solution)/shard_map/ppermute | solution.py:811
  14.8 0.7 %collective-permute-start.1 = (f32[232,128]{1,0:T(8,128)S(1)}, f32[232,128]{1,0:T(8,128)S(1)}, u32[]{:S(2)}, u32[]{:S(2)}) collective-permute-start(f32[232,128]{1,0:T(8,128)S(1)} %collective-permute-done.refs_2_), channel_id=1, source_target_pairs={{0,4},{4,0},{1,5},{5,1},{2,6},{6,2},{3,7},{7,3},{8,12},{12,8},{9,1... | collective-permute-start | bytes 356360 | tf_op jit(solution)/shard_map/ppermute | solution.py:814
  15.6 0.0 collective-permute-done.4.refs_4_
  15.6 1.2 %collective-permute-done.3.refs_1_ = f32[232,128]{1,0:T(8,128)S(1)} collective-permute-done((f32[232,128]{1,0:T(8,128)S(1)}, f32[232,128]{1,0:T(8,128)S(1)}, u32[]{:S(2)}, u32[]{:S(2)}) %collective-permute-start.3) | collective-permute-done | bytes 118816 | tf_op jit(solution)/shard_map/ppermute | solution.py:811
  16.8 0.0 collective-permute-start.6
  16.8 1.3 %collective-permute-start.5 = (f32[232,128]{1,0:T(8,128)S(1)}, f32[232,128]{1,0:T(8,128)S(1)}, u32[]{:S(2)}, u32[]{:S(2)}) collective-permute-start(f32[232,128]{1,0:T(8,128)S(1)} %collective-permute-done.refs_2_), channel_id=1, source_target_pairs={{0,8},{8,0},{16,24},{24,16},{1,9},{9,1},{17,25},{25,17},{2,10},{10... | collective-permute-start | bytes 356360 | tf_op jit(solution)/shard_map/ppermute | solution.py:811
  18.0 0.5 collective-permute-done.1.refs_6_
  18.5 2.4 %collective-permute-start.2 = (f32[232,128]{1,0:T(8,128)S(1)}, f32[232,128]{1,0:T(8,128)S(1)}, u32[]{:S(2)}, u32[]{:S(2)}) collective-permute-start(f32[232,128]{1,0:T(8,128)S(1)} %collective-permute-done.1.refs_6_), channel_id=1, source_target_pairs={{0,8},{8,0},{16,24},{24,16},{1,9},{9,1},{17,25},{25,17},{2,10},{10... | collective-permute-start | bytes 356360 | tf_op jit(solution)/shard_map/ppermute | solution.py:811
  20.9 0.9 %collective-permute-done.6.refs_5_ = f32[232,128]{1,0:T(8,128)S(1)} collective-permute-done((f32[232,128]{1,0:T(8,128)S(1)}, f32[232,128]{1,0:T(8,128)S(1)}, u32[]{:S(2)}, u32[]{:S(2)}) %collective-permute-start.6) | collective-permute-done | bytes 118816 | tf_op jit(solution)/shard_map/ppermute | solution.py:814
  21.7 0.0 collective-permute-done.5.refs_3_
  21.7 0.0 copy-done.1
  21.7 1.1 %settle.1 = (f32[96,384]{1,0:T(8,128)S(1)}, f32[64,128]{1,0:T(8,128)S(1)}, f32[64,128]{1,0:T(8,128)S(1)}, f32[12,128]{1,0:T(8,128)S(1)}, f32[128,128]{1,0:T(8,128)S(1)}) custom-call(f32[4,3]{1,0:T(4,128)S(1)} %copy-done.1, f32[232,128]{1,0:T(8,128)S(1)} %get-tuple-element.20.refs_0_.own_ref, f32[232,128]{1,0:T(8,128)S(1)} %collective-permute-done.3.refs_1_, ...), custom_call_target="tpu_custom_call" | custom-call | flops 1000000000 | bytes 831488 | tf_op jit(solution)/shard_map/settle/pallas_call | solution.py:458
  22.8 0.0 copy-start
  22.8 1.3 %collective-permute-done.2.last_ref = f32[232,128]{1,0:T(8,128)S(1)} collective-permute-done((f32[232,128]{1,0:T(8,128)S(1)}, f32[232,128]{1,0:T(8,128)S(1)}, u32[]{:S(2)}, u32[]{:S(2)}) %collective-permute-start.2) | collective-permute-done | bytes 118816 | tf_op jit(solution)/shard_map/ppermute | solution.py:811
  24.2 0.0 copy-done
  24.2 7.4 %spread.1 = (f32[19,32,128]{2,1,0:T(8,128)S(1)}, f32[5,8,128]{2,1,0:T(8,128)S(1)}, f32[5,8,128]{2,1,0:T(8,128)S(1)}, f32[24,128]{1,0:T(8,128)S(1)}, f32[3,32,128]{2,1,0:T(8,128)}) custom-call(s32[4]{0:T(128)S(1)} %pad_add_fusion.place_ref, f32[232,128]{1,0:T(8,128)S(1)} %get-tuple-element.20.refs_0_.own_ref, f32[232,128]{1,0:T(8,128)S(1)} %collective-permute-done.2.last_ref, ...), custom_call_target="tpu_custom_call" | custom-call | tf_op jit(solution)/shard_map/spread/pallas_call | solution.py:598
  31.6 3.9 %collective-permute-start.7 = (f32[5,8,128]{2,1,0:T(8,128)S(1)}, f32[5,8,128]{2,1,0:T(8,128)S(1)}, u32[]{:S(2)}, u32[]{:S(2)}) collective-permute-start(f32[5,8,128]{2,1,0:T(8,128)S(1)} %get-tuple-element.31), channel_id=1, source_target_pairs={{0,24},{16,8},{24,0},{8,16},{1,25},{17,9},{25,1},{9,17},{2,26},{18... | collective-permute-start | bytes 61448 | tf_op jit(solution)/shard_map/ppermute | solution.py:829
  35.5 0.0 collective-permute-start.8
  35.5 1.2 %collective-permute-start.9 = (f32[24,128]{1,0:T(8,128)S(1)}, f32[24,128]{1,0:T(8,128)S(1)}, u32[]{:S(2)}, u32[]{:S(2)}) collective-permute-start(f32[24,128]{1,0:T(8,128)S(1)} %get-tuple-element.33), channel_id=1, source_target_pairs={{0,4},{4,0},{1,5},{5,1},{2,6},{6,2},{3,7},{7,3},{8,12},{12,8},{9,1... | collective-permute-start | bytes 36872 | tf_op jit(solution)/shard_map/ppermute | solution.py:814
  36.7 1.3 %collective-permute-done.9.side_ref = f32[24,128]{1,0:T(8,128)S(1)} collective-permute-done((f32[24,128]{1,0:T(8,128)S(1)}, f32[24,128]{1,0:T(8,128)S(1)}, u32[]{:S(2)}, u32[]{:S(2)}) %collective-permute-start.9) | collective-permute-done | bytes 12320 | tf_op jit(solution)/shard_map/ppermute | solution.py:814
  38.0 0.0 collective-permute-done.7.far_ref
  38.0 0.1 collective-permute-done.8.near_ref
  38.1 0.7 %pack.1 = (f32[8,128]{1,0:T(8,128)S(1)}, f32[8,128]{1,0:T(8,128)S(1)}, f32[8,128]{1,0:T(8,128)S(1)}) custom-call(s32[4]{0:T(128)S(1)} %pad_add_fusion.place_ref, f32[19,32,128]{2,1,0:T(8,128)S(1)} %get-tuple-element.30.relaxed_ref, f32[5,8,128]{2,1,0:T(8,128)S(1)} %collective-permute-done.7.far_ref, f32[5,8,128]{2,1,0:T(8,128)S(1)} %collective-permute-done.8.near_ref, ...), custom_call_target="tpu_custom_call" | custom-call | tf_op jit(solution)/shard_map/pack/pallas_call | solution.py:708
  38.8 7.4 %collective-permute-start.10 = (f32[8,128]{1,0:T(8,128)S(1)}, f32[8,128]{1,0:T(8,128)S(1)}, u32[]{:S(2)}, u32[]{:S(2)}) collective-permute-start(f32[8,128]{1,0:T(8,128)S(1)} %get-tuple-element.34), channel_id=1, source_target_pairs={{1,2},{2,1},{5,6},{6,5},{9,10},{10,9},{13,14},{14,13},{17,18},{18,... | collective-permute-start | bytes 12296 | tf_op jit(solution)/shard_map/ppermute | solution.py:839
  46.1 1.2 %collective-permute-start.11 = (f32[8,128]{1,0:T(8,128)S(1)}, f32[8,128]{1,0:T(8,128)S(1)}, u32[]{:S(2)}, u32[]{:S(2)}) collective-permute-start(f32[8,128]{1,0:T(8,128)S(1)} %get-tuple-element.35), channel_id=1, source_target_pairs={{0,4},{4,0},{1,5},{5,1},{2,6},{6,2},{3,7},{7,3},{8,12},{12,8},{9,1... | collective-permute-start | bytes 12296 | tf_op jit(solution)/shard_map/ppermute | solution.py:814
  47.3 0.0 collective-permute-start.12
  47.3 0.1 collective-permute-done.10.second_ref
  47.4 1.2 %collective-permute-done.11.corner_ref = f32[8,128]{1,0:T(8,128)S(1)} collective-permute-done((f32[8,128]{1,0:T(8,128)S(1)}, f32[8,128]{1,0:T(8,128)S(1)}, u32[]{:S(2)}, u32[]{:S(2)}) %collective-permute-start.11) | collective-permute-done | bytes 4128 | tf_op jit(solution)/shard_map/ppermute | solution.py:814
  48.7 0.0 collective-permute-done.12.first_ref
  48.7 1.5 %stream.1 = f32[19,4,8,128]{3,2,1,0:T(8,128)} custom-call(s32[4]{0:T(128)S(1)} %pad_add_fusion.place_ref, f32[19,32,128]{2,1,0:T(8,128)S(1)} %get-tuple-element.30.relaxed_ref, f32[5,8,128]{2,1,0:T(8,128)S(1)} %collective-permute-done.7.far_ref, f32[5,8,128]{2,1,0:T(8,128)S(1)} %collective-permute-done.8.near_ref, ...), custom_call_target="tpu_custom_call" | custom-call | tf_op jit(solution)/shard_map/stream/pallas_call | solution.py:765
Async XLA Ops:
  0.7 21.0 %copy-start.1 = (f32[4,3]{1,0:T(4,128)S(1)}, f32[4,3]{1,0:T(4,128)}, u32[]{:S(2)}) copy-start(f32[4,3]{1,0:T(4,128)} %speeds_ref.1) | copy-start | bytes 148
  6.6 8.2 %collective-permute-start = (f32[232,128]{1,0:T(8,128)S(1)}, f32[232,128]{1,0:T(8,128)S(1)}, u32[]{:S(2)}, u32[]{:S(2)}) collective-permute-start(f32[232,128]{1,0:T(8,128)S(1)} %get-tuple-element.20.refs_0_.own_ref), channel_id=1, source_target_pairs={{0,16},{8,24},{16,0},{24,8},{1,17},{9,25},{17,1},{25,9},{2,18},{10... | collective-permute-start | bytes 356360 | tf_op jit(solution)/shard_map/ppermute | solution.py:811
  9.8 5.7 %collective-permute-start.4 = (f32[232,128]{1,0:T(8,128)S(1)}, f32[232,128]{1,0:T(8,128)S(1)}, u32[]{:S(2)}, u32[]{:S(2)}) collective-permute-start(f32[232,128]{1,0:T(8,128)S(1)} %get-tuple-element.20.refs_0_.own_ref), channel_id=1, source_target_pairs={{0,4},{4,0},{1,5},{5,1},{2,6},{6,2},{3,7},{7,3},{8,12},{12,8},{9,1... | collective-permute-start | bytes 356360 | tf_op jit(solution)/shard_map/ppermute | solution.py:814
  11.0 5.7 %collective-permute-start.3 = (f32[232,128]{1,0:T(8,128)S(1)}, f32[232,128]{1,0:T(8,128)S(1)}, u32[]{:S(2)}, u32[]{:S(2)}) collective-permute-start(f32[232,128]{1,0:T(8,128)S(1)} %get-tuple-element.20.refs_0_.own_ref), channel_id=1, source_target_pairs={{0,8},{8,0},{16,24},{24,16},{1,9},{9,1},{17,25},{25,17},{2,10},{10... | collective-permute-start | bytes 356360 | tf_op jit(solution)/shard_map/ppermute | solution.py:811
  14.8 3.7 %collective-permute-start.1 = (f32[232,128]{1,0:T(8,128)S(1)}, f32[232,128]{1,0:T(8,128)S(1)}, u32[]{:S(2)}, u32[]{:S(2)}) collective-permute-start(f32[232,128]{1,0:T(8,128)S(1)} %collective-permute-done.refs_2_), channel_id=1, source_target_pairs={{0,4},{4,0},{1,5},{5,1},{2,6},{6,2},{3,7},{7,3},{8,12},{12,8},{9,1... | collective-permute-start | bytes 356360 | tf_op jit(solution)/shard_map/ppermute | solution.py:814
  16.8 5.0 %collective-permute-start.6 = (f32[232,128]{1,0:T(8,128)S(1)}, f32[232,128]{1,0:T(8,128)S(1)}, u32[]{:S(2)}, u32[]{:S(2)}) collective-permute-start(f32[232,128]{1,0:T(8,128)S(1)} %collective-permute-done.3.refs_1_), channel_id=1, source_target_pairs={{0,4},{4,0},{1,5},{5,1},{2,6},{6,2},{3,7},{7,3},{8,12},{12,8},{9,1... | collective-permute-start | bytes 356360 | tf_op jit(solution)/shard_map/ppermute | solution.py:814
  16.8 5.0 %collective-permute-start.5 = (f32[232,128]{1,0:T(8,128)S(1)}, f32[232,128]{1,0:T(8,128)S(1)}, u32[]{:S(2)}, u32[]{:S(2)}) collective-permute-start(f32[232,128]{1,0:T(8,128)S(1)} %collective-permute-done.refs_2_), channel_id=1, source_target_pairs={{0,8},{8,0},{16,24},{24,16},{1,9},{9,1},{17,25},{25,17},{2,10},{10... | collective-permute-start | bytes 356360 | tf_op jit(solution)/shard_map/ppermute | solution.py:811
  18.5 5.7 %collective-permute-start.2 = (f32[232,128]{1,0:T(8,128)S(1)}, f32[232,128]{1,0:T(8,128)S(1)}, u32[]{:S(2)}, u32[]{:S(2)}) collective-permute-start(f32[232,128]{1,0:T(8,128)S(1)} %collective-permute-done.1.refs_6_), channel_id=1, source_target_pairs={{0,8},{8,0},{16,24},{24,16},{1,9},{9,1},{17,25},{25,17},{2,10},{10... | collective-permute-start | bytes 356360 | tf_op jit(solution)/shard_map/ppermute | solution.py:811
  22.8 1.4 %copy-start = (s32[4,8,128]{2,1,0:T(8,128)S(1)}, s32[4,8,128]{2,1,0:T(8,128)}, u32[]{:S(2)}) copy-start(s32[4,8,128]{2,1,0:T(8,128)} %param.10) | copy-start | bytes 49156
  31.6 6.4 %collective-permute-start.7 = (f32[5,8,128]{2,1,0:T(8,128)S(1)}, f32[5,8,128]{2,1,0:T(8,128)S(1)}, u32[]{:S(2)}, u32[]{:S(2)}) collective-permute-start(f32[5,8,128]{2,1,0:T(8,128)S(1)} %get-tuple-element.31), channel_id=1, source_target_pairs={{0,24},{16,8},{24,0},{8,16},{1,25},{17,9},{25,1},{9,17},{2,26},{18... | collective-permute-start | bytes 61448 | tf_op jit(solution)/shard_map/ppermute | solution.py:829
  35.5 2.6 %collective-permute-start.8 = (f32[5,8,128]{2,1,0:T(8,128)S(1)}, f32[5,8,128]{2,1,0:T(8,128)S(1)}, u32[]{:S(2)}, u32[]{:S(2)}) collective-permute-start(f32[5,8,128]{2,1,0:T(8,128)S(1)} %get-tuple-element.32), channel_id=1, source_target_pairs={{0,8},{16,24},{8,0},{24,16},{1,9},{17,25},{9,1},{25,17},{2,10},{18... | collective-permute-start | bytes 61448 | tf_op jit(solution)/shard_map/ppermute | solution.py:834
  35.5 2.5 %collective-permute-start.9 = (f32[24,128]{1,0:T(8,128)S(1)}, f32[24,128]{1,0:T(8,128)S(1)}, u32[]{:S(2)}, u32[]{:S(2)}) collective-permute-start(f32[24,128]{1,0:T(8,128)S(1)} %get-tuple-element.33), channel_id=1, source_target_pairs={{0,4},{4,0},{1,5},{5,1},{2,6},{6,2},{3,7},{7,3},{8,12},{12,8},{9,1... | collective-permute-start | bytes 36872 | tf_op jit(solution)/shard_map/ppermute | solution.py:814
  38.8 8.7 %collective-permute-start.10 = (f32[8,128]{1,0:T(8,128)S(1)}, f32[8,128]{1,0:T(8,128)S(1)}, u32[]{:S(2)}, u32[]{:S(2)}) collective-permute-start(f32[8,128]{1,0:T(8,128)S(1)} %get-tuple-element.34), channel_id=1, source_target_pairs={{1,2},{2,1},{5,6},{6,5},{9,10},{10,9},{13,14},{14,13},{17,18},{18,... | collective-permute-start | bytes 12296 | tf_op jit(solution)/shard_map/ppermute | solution.py:839
  46.1 2.5 %collective-permute-start.11 = (f32[8,128]{1,0:T(8,128)S(1)}, f32[8,128]{1,0:T(8,128)S(1)}, u32[]{:S(2)}, u32[]{:S(2)}) collective-permute-start(f32[8,128]{1,0:T(8,128)S(1)} %get-tuple-element.35), channel_id=1, source_target_pairs={{0,4},{4,0},{1,5},{5,1},{2,6},{6,2},{3,7},{7,3},{8,12},{12,8},{9,1... | collective-permute-start | bytes 12296 | tf_op jit(solution)/shard_map/ppermute | solution.py:814
  47.3 1.4 %collective-permute-start.12 = (f32[8,128]{1,0:T(8,128)S(1)}, f32[8,128]{1,0:T(8,128)S(1)}, u32[]{:S(2)}, u32[]{:S(2)}) collective-permute-start(f32[8,128]{1,0:T(8,128)S(1)} %get-tuple-element.36), channel_id=1, source_target_pairs={{0,1},{2,3},{1,0},{3,2},{4,5},{6,7},{5,4},{7,6},{8,9},{10,11},{9,8... | collective-permute-start | bytes 12296 | tf_op jit(solution)/shard_map/ppermute | solution.py:841

commit v13 on v11

--- a/solution.py
+++ b/solution.py
@@ -41,6 +41,7 @@
 vmem_bytes = 16 << 20
 group = 8
 fine = jnp.float8_e4m3fn
+matrix_points = 2
 
 
 def going(axis, step):
@@ -294,7 +295,7 @@
 def sample_kernel(
     place_ref, pop_any, cells_any, weights_any, areas_any, owner_any, block_any, trains_any,
     out_ref, pop_ref, cells_ref, weights_ref, areas_ref, owner_ref, block_ref, trains_ref,
-    table, sems,
+    table, parts_ref, lines_ref, spread_ref, sems,
 ):
     rows, lanes = (pop_ref.shape[1], pop_ref.shape[2])
     mark = cells_ref.shape[1]
@@ -330,6 +331,12 @@
     )
     for r in range(table.shape[0]):
         table[r] = jnp.broadcast_to(words[r : r + 1], (group, lanes))
+    for c in range(3):
+        value = speed[c] * (224.0 / largest)
+        for part in range(4):
+            piece = value.astype(fine)
+            parts_ref[c * rows : (c + 1) * rows, part * lanes : (part + 1) * lanes] = piece
+            value = value - piece.astype(jnp.float32)
     for copy in copies[1:]:
         copy.wait()
     out_ref[8 : 8 + owned, :] = areas_ref[...]
@@ -340,10 +347,53 @@
     mine = lax.broadcasted_iota(jnp.int32, (1, mark), 1) % owned + place_ref[2] * owned
     out_ref[2:3, :] = mine.astype(jnp.float32)
 
+    bf = jnp.bfloat16
+    iota = lax.broadcasted_iota(jnp.int32, (16, mark), 0).astype(jnp.float32)
+    steps = [(iota + 16.0 * j).astype(bf) for j in range(lanes // 16)]
+    line_at = [iota[0:8] + 8.0 * j for j in range(rows // 8)]
+    one, zero = (jnp.ones((16, mark), bf), jnp.zeros((16, mark), bf))
+
+    def by_matrix(first):
+        for which, k in enumerate(range(kernel - matrix_points, kernel)):
+            at = pl.ds(first * kernel + k, group, stride=kernel)
+            cells = cells_ref[at, :]
+            lines_ref[which, 0] = (cells & (lanes - 1)).astype(jnp.float32)
+            lines_ref[which, 1] = (cells >> (lanes.bit_length() - 1)).astype(jnp.float32)
+            lines_ref[which, 2] = weights_ref[at, :]
+        for i in range(group):
+            sums = [jnp.zeros((8, mark), jnp.float32) for c in range(3)]
+            for which in range(matrix_points):
+                lane, row, weight = (
+                    lines_ref[which, entry, pl.ds(i, 8, stride=0), :] for entry in range(3)
+                )
+                lane = jnp.concatenate([lane, lane], axis=0).astype(bf)
+                match = [jnp.where(step == lane, one, zero) for step in steps]
+                match = jnp.concatenate(match, axis=0).astype(fine)
+                got = jnp.dot(
+                    parts_ref[...],
+                    jnp.concatenate([match] * 4, axis=0),
+                    preferred_element_type=jnp.float32,
+                )
+                for j in range(rows // 8):
+                    share = jnp.where(line_at[j] == row, weight, 0.0)
+                    for c in range(3):
+                        here = c * rows + 8 * j
+                        sums[c] = sums[c] + share * got[here : here + 8]
+            for c in range(3):
+                spread_ref[c, 8 * i : 8 * i + 8, :] = sums[c]
+        result = []
+        for c in range(3):
+            total = spread_ref[c, pl.ds(0, group, stride=8), :]
+            for j in range(1, 8):
+                total = total + spread_ref[c, pl.ds(j, group, stride=8), :]
+            result.append(total)
+        return result
+
     def body(step, carry):
         first = pl.multiple_of(step * group, group)
         total = [jnp.zeros((group, mark), jnp.float32) for c in range(3)]
-        for k in range(kernel):
+        other = by_matrix(first)
+        for k in range(kernel - matrix_points):
             at = pl.ds(first * kernel + k, group, stride=kernel)
             cells = cells_ref[at, :]
             lane = cells & (lanes - 1)
@@ -368,7 +418,7 @@
                 total[c] = total[c] + weight * (picked[c].astype(jnp.float32) - 32768.0)
         for c in range(3):
             here = pl.ds(pl.multiple_of(8 + owned + c * slots + first, group), group)
-            out_ref[here, :] = total[c] * scale
+            out_ref[here, :] = total[c] * scale + other[c] * (largest * (1.0 / 224.0))
         return carry
 
     lax.fori_loop(0, slots // group, body, 0)
@@ -391,6 +441,9 @@
         ]
         + [
             pltpu.VMEM((populations.shape[1] * 3 // 2, group, populations.shape[2]), jnp.int32),
+            pltpu.VMEM((3 * populations.shape[1], 4 * populations.shape[2]), fine),
+            pltpu.VMEM((matrix_points, 3, group, cells.shape[1]), jnp.float32),
+            pltpu.VMEM((3, 8 * group, cells.shape[1]), jnp.float32),
             pltpu.SemaphoreType.DMA((7,)),
         ],
         compiler_params=kernel_params(),

time: 49.2 us -> 48.7 us (0.990)
  no operation moved by 1% of the time
where the time goes in v13:
time: 48.7 us; the launch traced here: 48.6 us
  starting transfers between devices  21.8 us (45%)
  Pallas kernels  16.1 us (33%)
  waiting for transfers between devices  9.77 us (20%)
  between operations  0.7 us (1%)
    ppermute x1, starting transfers between devices, per_device(): lax.ppermute(down_first, 'gz', outer + [(j, i) for i, j in outer])  8.54 us
    pallas_call x1, Pallas kernels, spread(): pl.pallas_call(functools.partial(spread_kernel, slots, owned), out_shape=...  7.4 us
    ppermute x4, starting transfers between devices, across_x(): lax.ppermute(entries, 'gx', [(i, i ^ distance) for i in range(count_x)])  5.8 us
    pallas_call x1, Pallas kernels, sample(): pl.pallas_call(sample_kernel, out_shape=[full((count, cells.shape[1]))] +...  5.5 us
    ppermute x5, waiting for transfers between devices, across_y(): return lax.ppermute(entries, 'gy', swap)  5.13 us
    ppermute x5, starting transfers between devices, across_y(): return lax.ppermute(entries, 'gy', swap)  5.13 us
    ppermute x4, waiting for transfers between devices, across_x(): lax.ppermute(entries, 'gx', [(i, i ^ distance) for i in range(count_x)])  3.99 us
    ppermute x1, starting transfers between devices, per_device(): lax.ppermute(far, 'gx', [(i, (i - 1) % count_x) for i in evens] + [((i -...  2.29 us
  transfers between devices with their start and end apart: 13, of which 9 were waited for; matrix products, arithmetic and copies ran while one was open for 0% of the time, Pallas kernels for 2%

profile of v13, /device:TPU:1, one launch (start us, length us, event | category | flops | bytes accessed | tf_op | source)
XLA Modules:
  0.0 48.6 jit_solution(7842879251011405872)
XLA Ops:
  0.6 0.1 pad_add_fusion.place_ref
  0.7 0.0 copy-start.1
  0.7 5.5 %sample.1 = (f32[232,128]{1,0:T(8,128)S(1)}, f32[19,32,128]{2,1,0:T(8,128)S(1)}, s32[512,128]{1,0:T(8,128)S(1)}, f32[512,128]{1,0:T(8,128)S(1)}) custom-call(s32[4]{0:T(128)S(1)} %pad_add_fusion.place_ref, f32[19,32,128]{2,1,0:T(8,128)} %bitcast.16, s32[512,128]{1,0:T(8,128)} %bitcast.17, f32[512,128]{1,0:T(8,128)} %bitcast.18, f32[32,128]{1,0:T(8,128)} %bitcast.19, ...), custom_call_target="tpu_custom_call" | custom-call | tf_op jit(solution)/shard_map/sample/pallas_call | solution.py:433
  6.2 4.2 %collective-permute-start = (f32[232,128]{1,0:T(8,128)S(1)}, f32[232,128]{1,0:T(8,128)S(1)}, u32[]{:S(2)}, u32[]{:S(2)}) collective-permute-start(f32[232,128]{1,0:T(8,128)S(1)} %get-tuple-element.20.refs_0_.own_ref), channel_id=1, source_target_pairs={{0,24},{8,16},{16,8},{24,0},{1,25},{9,17},{17,9},{25,1},{2,26},{10... | collective-permute-start | bytes 356360 | tf_op jit(solution)/shard_map/ppermute | solution.py:864
  10.5 1.2 %collective-permute-start.4 = (f32[232,128]{1,0:T(8,128)S(1)}, f32[232,128]{1,0:T(8,128)S(1)}, u32[]{:S(2)}, u32[]{:S(2)}) collective-permute-start(f32[232,128]{1,0:T(8,128)S(1)} %get-tuple-element.20.refs_0_.own_ref), channel_id=1, source_target_pairs={{0,4},{4,0},{1,5},{5,1},{2,6},{6,2},{3,7},{7,3},{8,12},{12,8},{9,1... | collective-permute-start | bytes 356360 | tf_op jit(solution)/shard_map/ppermute | solution.py:867
  11.7 0.0 collective-permute-start.3
  11.7 1.8 %collective-permute-done.refs_2_ = f32[232,128]{1,0:T(8,128)S(1)} collective-permute-done((f32[232,128]{1,0:T(8,128)S(1)}, f32[232,128]{1,0:T(8,128)S(1)}, u32[]{:S(2)}, u32[]{:S(2)}) %collective-permute-start) | collective-permute-done | bytes 118816 | tf_op jit(solution)/shard_map/ppermute | solution.py:864
  13.5 1.0 %collective-permute-start.1 = (f32[232,128]{1,0:T(8,128)S(1)}, f32[232,128]{1,0:T(8,128)S(1)}, u32[]{:S(2)}, u32[]{:S(2)}) collective-permute-start(f32[232,128]{1,0:T(8,128)S(1)} %collective-permute-done.refs_2_), channel_id=1, source_target_pairs={{0,4},{4,0},{1,5},{5,1},{2,6},{6,2},{3,7},{7,3},{8,12},{12,8},{9,1... | collective-permute-start | bytes 356360 | tf_op jit(solution)/shard_map/ppermute | solution.py:867
  14.5 0.0 collective-permute-done.4.refs_4_
  14.5 1.4 %collective-permute-done.3.refs_1_ = f32[232,128]{1,0:T(8,128)S(1)} collective-permute-done((f32[232,128]{1,0:T(8,128)S(1)}, f32[232,128]{1,0:T(8,128)S(1)}, u32[]{:S(2)}, u32[]{:S(2)}) %collective-permute-start.3) | collective-permute-done | bytes 118816 | tf_op jit(solution)/shard_map/ppermute | solution.py:864
  15.8 1.4 %collective-permute-start.6 = (f32[232,128]{1,0:T(8,128)S(1)}, f32[232,128]{1,0:T(8,128)S(1)}, u32[]{:S(2)}, u32[]{:S(2)}) collective-permute-start(f32[232,128]{1,0:T(8,128)S(1)} %collective-permute-done.3.refs_1_), channel_id=1, source_target_pairs={{0,4},{4,0},{1,5},{5,1},{2,6},{6,2},{3,7},{7,3},{8,12},{12,8},{9,1... | collective-permute-start | bytes 356360 | tf_op jit(solution)/shard_map/ppermute | solution.py:867
  17.2 1.2 %collective-permute-start.5 = (f32[232,128]{1,0:T(8,128)S(1)}, f32[232,128]{1,0:T(8,128)S(1)}, u32[]{:S(2)}, u32[]{:S(2)}) collective-permute-start(f32[232,128]{1,0:T(8,128)S(1)} %collective-permute-done.refs_2_), channel_id=1, source_target_pairs={{0,8},{8,0},{16,24},{24,16},{1,9},{9,1},{17,25},{25,17},{2,10},{10... | collective-permute-start | bytes 356360 | tf_op jit(solution)/shard_map/ppermute | solution.py:864
  18.4 0.0 collective-permute-done.1.refs_6_
  18.4 0.4 collective-permute-start.2
  18.8 2.2 %collective-permute-done.6.refs_5_ = f32[232,128]{1,0:T(8,128)S(1)} collective-permute-done((f32[232,128]{1,0:T(8,128)S(1)}, f32[232,128]{1,0:T(8,128)S(1)}, u32[]{:S(2)}, u32[]{:S(2)}) %collective-permute-start.6) | collective-permute-done | bytes 118816 | tf_op jit(solution)/shard_map/ppermute | solution.py:867
  21.0 0.2 collective-permute-done.5.refs_3_
  21.2 0.0 copy-done.1
  21.2 1.1 %settle.1 = (f32[96,384]{1,0:T(8,128)S(1)}, f32[64,128]{1,0:T(8,128)S(1)}, f32[64,128]{1,0:T(8,128)S(1)}, f32[12,128]{1,0:T(8,128)S(1)}, f32[128,128]{1,0:T(8,128)S(1)}) custom-call(f32[4,3]{1,0:T(4,128)S(1)} %copy-done.1, f32[232,128]{1,0:T(8,128)S(1)} %get-tuple-element.20.refs_0_.own_ref, f32[232,128]{1,0:T(8,128)S(1)} %collective-permute-done.3.refs_1_, ...), custom_call_target="tpu_custom_call" | custom-call | flops 1000000000 | bytes 831488 | tf_op jit(solution)/shard_map/settle/pallas_call | solution.py:511
  22.3 0.0 copy-start
  22.3 0.6 %collective-permute-done.2.last_ref = f32[232,128]{1,0:T(8,128)S(1)} collective-permute-done((f32[232,128]{1,0:T(8,128)S(1)}, f32[232,128]{1,0:T(8,128)S(1)}, u32[]{:S(2)}, u32[]{:S(2)}) %collective-permute-start.2) | collective-permute-done | bytes 118816 | tf_op jit(solution)/shard_map/ppermute | solution.py:864
  22.9 0.1 copy-done
  23.0 7.4 %spread.1 = (f32[19,32,128]{2,1,0:T(8,128)S(1)}, f32[5,8,128]{2,1,0:T(8,128)S(1)}, f32[5,8,128]{2,1,0:T(8,128)S(1)}, f32[24,128]{1,0:T(8,128)S(1)}, f32[3,32,128]{2,1,0:T(8,128)}) custom-call(s32[4]{0:T(128)S(1)} %pad_add_fusion.place_ref, f32[232,128]{1,0:T(8,128)S(1)} %get-tuple-element.20.refs_0_.own_ref, f32[232,128]{1,0:T(8,128)S(1)} %collective-permute-done.2.last_ref, ...), custom_call_target="tpu_custom_call" | custom-call | tf_op jit(solution)/shard_map/spread/pallas_call | solution.py:651
  30.4 2.3 %collective-permute-start.7 = (f32[5,8,128]{2,1,0:T(8,128)S(1)}, f32[5,8,128]{2,1,0:T(8,128)S(1)}, u32[]{:S(2)}, u32[]{:S(2)}) collective-permute-start(f32[5,8,128]{2,1,0:T(8,128)S(1)} %get-tuple-element.31), channel_id=1, source_target_pairs={{0,24},{16,8},{24,0},{8,16},{1,25},{17,9},{25,1},{9,17},{2,26},{18... | collective-permute-start | bytes 61448 | tf_op jit(solution)/shard_map/ppermute | solution.py:882
  32.7 0.0 collective-permute-start.8
  32.7 0.8 %collective-permute-start.9 = (f32[24,128]{1,0:T(8,128)S(1)}, f32[24,128]{1,0:T(8,128)S(1)}, u32[]{:S(2)}, u32[]{:S(2)}) collective-permute-start(f32[24,128]{1,0:T(8,128)S(1)} %get-tuple-element.33), channel_id=1, source_target_pairs={{0,4},{4,0},{1,5},{5,1},{2,6},{6,2},{3,7},{7,3},{8,12},{12,8},{9,1... | collective-permute-start | bytes 36872 | tf_op jit(solution)/shard_map/ppermute | solution.py:867
  33.5 1.7 %collective-permute-done.9.side_ref = f32[24,128]{1,0:T(8,128)S(1)} collective-permute-done((f32[24,128]{1,0:T(8,128)S(1)}, f32[24,128]{1,0:T(8,128)S(1)}, u32[]{:S(2)}, u32[]{:S(2)}) %collective-permute-start.9) | collective-permute-done | bytes 12320 | tf_op jit(solution)/shard_map/ppermute | solution.py:867
  35.2 0.0 collective-permute-done.7.far_ref
  35.3 0.1 collective-permute-done.8.near_ref
  35.3 0.7 %pack.1 = (f32[8,128]{1,0:T(8,128)S(1)}, f32[8,128]{1,0:T(8,128)S(1)}, f32[8,128]{1,0:T(8,128)S(1)}) custom-call(s32[4]{0:T(128)S(1)} %pad_add_fusion.place_ref, f32[19,32,128]{2,1,0:T(8,128)S(1)} %get-tuple-element.30.relaxed_ref, f32[5,8,128]{2,1,0:T(8,128)S(1)} %collective-permute-done.7.far_ref, f32[5,8,128]{2,1,0:T(8,128)S(1)} %collective-permute-done.8.near_ref, ...), custom_call_target="tpu_custom_call" | custom-call | tf_op jit(solution)/shard_map/pack/pallas_call | solution.py:761
  36.0 8.5 %collective-permute-start.10 = (f32[8,128]{1,0:T(8,128)S(1)}, f32[8,128]{1,0:T(8,128)S(1)}, u32[]{:S(2)}, u32[]{:S(2)}) collective-permute-start(f32[8,128]{1,0:T(8,128)S(1)} %get-tuple-element.34), channel_id=1, source_target_pairs={{1,2},{2,1},{5,6},{6,5},{9,10},{10,9},{13,14},{14,13},{17,18},{18,... | collective-permute-start | bytes 12296 | tf_op jit(solution)/shard_map/ppermute | solution.py:892
  44.6 0.7 %collective-permute-start.11 = (f32[8,128]{1,0:T(8,128)S(1)}, f32[8,128]{1,0:T(8,128)S(1)}, u32[]{:S(2)}, u32[]{:S(2)}) collective-permute-start(f32[8,128]{1,0:T(8,128)S(1)} %get-tuple-element.35), channel_id=1, source_target_pairs={{0,4},{4,0},{1,5},{5,1},{2,6},{6,2},{3,7},{7,3},{8,12},{12,8},{9,1... | collective-permute-start | bytes 12296 | tf_op jit(solution)/shard_map/ppermute | solution.py:867
  45.3 0.0 collective-permute-start.12
  45.3 0.6 %collective-permute-done.10.second_ref = f32[8,128]{1,0:T(8,128)S(1)} collective-permute-done((f32[8,128]{1,0:T(8,128)S(1)}, f32[8,128]{1,0:T(8,128)S(1)}, u32[]{:S(2)}, u32[]{:S(2)}) %collective-permute-start.10) | collective-permute-done | bytes 4128 | tf_op jit(solution)/shard_map/ppermute | solution.py:892
  45.8 1.2 %collective-permute-done.11.corner_ref = f32[8,128]{1,0:T(8,128)S(1)} collective-permute-done((f32[8,128]{1,0:T(8,128)S(1)}, f32[8,128]{1,0:T(8,128)S(1)}, u32[]{:S(2)}, u32[]{:S(2)}) %collective-permute-start.11) | collective-permute-done | bytes 4128 | tf_op jit(solution)/shard_map/ppermute | solution.py:867
  47.1 0.0 collective-permute-done.12.first_ref
  47.1 1.5 %stream.1 = f32[19,4,8,128]{3,2,1,0:T(8,128)} custom-call(s32[4]{0:T(128)S(1)} %pad_add_fusion.place_ref, f32[19,32,128]{2,1,0:T(8,128)S(1)} %get-tuple-element.30.relaxed_ref, f32[5,8,128]{2,1,0:T(8,128)S(1)} %collective-permute-done.7.far_ref, f32[5,8,128]{2,1,0:T(8,128)S(1)} %collective-permute-done.8.near_ref, ...), custom_call_target="tpu_custom_call" | custom-call | tf_op jit(solution)/shard_map/stream/pallas_call | solution.py:818
Async XLA Ops:
  0.7 20.5 %copy-start.1 = (f32[4,3]{1,0:T(4,128)S(1)}, f32[4,3]{1,0:T(4,128)}, u32[]{:S(2)}) copy-start(f32[4,3]{1,0:T(4,128)} %speeds_ref.1) | copy-start | bytes 148
  6.2 7.2 %collective-permute-start = (f32[232,128]{1,0:T(8,128)S(1)}, f32[232,128]{1,0:T(8,128)S(1)}, u32[]{:S(2)}, u32[]{:S(2)}) collective-permute-start(f32[232,128]{1,0:T(8,128)S(1)} %get-tuple-element.20.refs_0_.own_ref), channel_id=1, source_target_pairs={{0,24},{8,16},{16,8},{24,0},{1,25},{9,17},{17,9},{25,1},{2,26},{10... | collective-permute-start | bytes 356360 | tf_op jit(solution)/shard_map/ppermute | solution.py:864
  10.5 4.0 %collective-permute-start.4 = (f32[232,128]{1,0:T(8,128)S(1)}, f32[232,128]{1,0:T(8,128)S(1)}, u32[]{:S(2)}, u32[]{:S(2)}) collective-permute-start(f32[232,128]{1,0:T(8,128)S(1)} %get-tuple-element.20.refs_0_.own_ref), channel_id=1, source_target_pairs={{0,4},{4,0},{1,5},{5,1},{2,6},{6,2},{3,7},{7,3},{8,12},{12,8},{9,1... | collective-permute-start | bytes 356360 | tf_op jit(solution)/shard_map/ppermute | solution.py:867
  11.7 4.2 %collective-permute-start.3 = (f32[232,128]{1,0:T(8,128)S(1)}, f32[232,128]{1,0:T(8,128)S(1)}, u32[]{:S(2)}, u32[]{:S(2)}) collective-permute-start(f32[232,128]{1,0:T(8,128)S(1)} %get-tuple-element.20.refs_0_.own_ref), channel_id=1, source_target_pairs={{0,8},{8,0},{16,24},{24,16},{1,9},{9,1},{17,25},{25,17},{2,10},{10... | collective-permute-start | bytes 356360 | tf_op jit(solution)/shard_map/ppermute | solution.py:864
  13.5 4.9 %collective-permute-start.1 = (f32[232,128]{1,0:T(8,128)S(1)}, f32[232,128]{1,0:T(8,128)S(1)}, u32[]{:S(2)}, u32[]{:S(2)}) collective-permute-start(f32[232,128]{1,0:T(8,128)S(1)} %collective-permute-done.refs_2_), channel_id=1, source_target_pairs={{0,4},{4,0},{1,5},{5,1},{2,6},{6,2},{3,7},{7,3},{8,12},{12,8},{9,1... | collective-permute-start | bytes 356360 | tf_op jit(solution)/shard_map/ppermute | solution.py:867
  15.8 5.1 %collective-permute-start.6 = (f32[232,128]{1,0:T(8,128)S(1)}, f32[232,128]{1,0:T(8,128)S(1)}, u32[]{:S(2)}, u32[]{:S(2)}) collective-permute-start(f32[232,128]{1,0:T(8,128)S(1)} %collective-permute-done.3.refs_1_), channel_id=1, source_target_pairs={{0,4},{4,0},{1,5},{5,1},{2,6},{6,2},{3,7},{7,3},{8,12},{12,8},{9,1... | collective-permute-start | bytes 356360 | tf_op jit(solution)/shard_map/ppermute | solution.py:867
  17.2 4.0 %collective-permute-start.5 = (f32[232,128]{1,0:T(8,128)S(1)}, f32[232,128]{1,0:T(8,128)S(1)}, u32[]{:S(2)}, u32[]{:S(2)}) collective-permute-start(f32[232,128]{1,0:T(8,128)S(1)} %collective-permute-done.refs_2_), channel_id=1, source_target_pairs={{0,8},{8,0},{16,24},{24,16},{1,9},{9,1},{17,25},{25,17},{2,10},{10... | collective-permute-start | bytes 356360 | tf_op jit(solution)/shard_map/ppermute | solution.py:864
  18.4 4.5 %collective-permute-start.2 = (f32[232,128]{1,0:T(8,128)S(1)}, f32[232,128]{1,0:T(8,128)S(1)}, u32[]{:S(2)}, u32[]{:S(2)}) collective-permute-start(f32[232,128]{1,0:T(8,128)S(1)} %collective-permute-done.1.refs_6_), channel_id=1, source_target_pairs={{0,8},{8,0},{16,24},{24,16},{1,9},{9,1},{17,25},{25,17},{2,10},{10... | collective-permute-start | bytes 356360 | tf_op jit(solution)/shard_map/ppermute | solution.py:864
  22.3 0.7 %copy-start = (s32[4,8,128]{2,1,0:T(8,128)S(1)}, s32[4,8,128]{2,1,0:T(8,128)}, u32[]{:S(2)}) copy-start(s32[4,8,128]{2,1,0:T(8,128)} %param.10) | copy-start | bytes 49156
  30.4 4.8 %collective-permute-start.7 = (f32[5,8,128]{2,1,0:T(8,128)S(1)}, f32[5,8,128]{2,1,0:T(8,128)S(1)}, u32[]{:S(2)}, u32[]{:S(2)}) collective-permute-start(f32[5,8,128]{2,1,0:T(8,128)S(1)} %get-tuple-element.31), channel_id=1, source_target_pairs={{0,24},{16,8},{24,0},{8,16},{1,25},{17,9},{25,1},{9,17},{2,26},{18... | collective-permute-start | bytes 61448 | tf_op jit(solution)/shard_map/ppermute | solution.py:882
  32.7 2.6 %collective-permute-start.8 = (f32[5,8,128]{2,1,0:T(8,128)S(1)}, f32[5,8,128]{2,1,0:T(8,128)S(1)}, u32[]{:S(2)}, u32[]{:S(2)}) collective-permute-start(f32[5,8,128]{2,1,0:T(8,128)S(1)} %get-tuple-element.32), channel_id=1, source_target_pairs={{0,8},{16,24},{8,0},{24,16},{1,9},{17,25},{9,1},{25,17},{2,10},{18... | collective-permute-start | bytes 61448 | tf_op jit(solution)/shard_map/ppermute | solution.py:887
  32.7 2.5 %collective-permute-start.9 = (f32[24,128]{1,0:T(8,128)S(1)}, f32[24,128]{1,0:T(8,128)S(1)}, u32[]{:S(2)}, u32[]{:S(2)}) collective-permute-start(f32[24,128]{1,0:T(8,128)S(1)} %get-tuple-element.33), channel_id=1, source_target_pairs={{0,4},{4,0},{1,5},{5,1},{2,6},{6,2},{3,7},{7,3},{8,12},{12,8},{9,1... | collective-permute-start | bytes 36872 | tf_op jit(solution)/shard_map/ppermute | solution.py:867
  36.0 9.8 %collective-permute-start.10 = (f32[8,128]{1,0:T(8,128)S(1)}, f32[8,128]{1,0:T(8,128)S(1)}, u32[]{:S(2)}, u32[]{:S(2)}) collective-permute-start(f32[8,128]{1,0:T(8,128)S(1)} %get-tuple-element.34), channel_id=1, source_target_pairs={{1,2},{2,1},{5,6},{6,5},{9,10},{10,9},{13,14},{14,13},{17,18},{18,... | collective-permute-start | bytes 12296 | tf_op jit(solution)/shard_map/ppermute | solution.py:892
  44.6 2.5 %collective-permute-start.11 = (f32[8,128]{1,0:T(8,128)S(1)}, f32[8,128]{1,0:T(8,128)S(1)}, u32[]{:S(2)}, u32[]{:S(2)}) collective-permute-start(f32[8,128]{1,0:T(8,128)S(1)} %get-tuple-element.35), channel_id=1, source_target_pairs={{0,4},{4,0},{1,5},{5,1},{2,6},{6,2},{3,7},{7,3},{8,12},{12,8},{9,1... | collective-permute-start | bytes 12296 | tf_op jit(solution)/shard_map/ppermute | solution.py:867
  45.3 1.8 %collective-permute-start.12 = (f32[8,128]{1,0:T(8,128)S(1)}, f32[8,128]{1,0:T(8,128)S(1)}, u32[]{:S(2)}, u32[]{:S(2)}) collective-permute-start(f32[8,128]{1,0:T(8,128)S(1)} %get-tuple-element.36), channel_id=1, source_target_pairs={{0,1},{2,3},{1,0},{3,2},{4,5},{6,7},{5,4},{7,6},{8,9},{10,11},{9,8... | collective-permute-start | bytes 12296 | tf_op jit(solution)/shard_map/ppermute | solution.py:894

commit v14 on v13

--- a/solution.py
+++ b/solution.py
@@ -41,7 +41,7 @@
 vmem_bytes = 16 << 20
 group = 8
 fine = jnp.float8_e4m3fn
-matrix_points = 2
+matrix_points = 3
 
 
 def going(axis, step):

time: 48.7 us -> 49.2 us (1.010)
  Pallas kernels: 16.1 us -> 16.6 us
where the time goes in v14:
time: 49.2 us; the launch traced here: 49 us
  starting transfers between devices  21.8 us (44%)
  Pallas kernels  16.6 us (34%)
  waiting for transfers between devices  9.78 us (20%)
  between operations  0.7 us (1%)
    ppermute x1, starting transfers between devices, per_device(): lax.ppermute(down_first, 'gz', outer + [(j, i) for i, j in outer])  8.54 us
    pallas_call x1, Pallas kernels, spread(): pl.pallas_call(functools.partial(spread_kernel, slots, owned), out_shape=...  7.4 us
    pallas_call x1, Pallas kernels, sample(): pl.pallas_call(sample_kernel, out_shape=[full((count, cells.shape[1]))] +...  5.95 us
    ppermute x4, starting transfers between devices, across_x(): lax.ppermute(entries, 'gx', [(i, i ^ distance) for i in range(count_x)])  5.8 us
    ppermute x5, waiting for transfers between devices, across_y(): return lax.ppermute(entries, 'gy', swap)  5.13 us
    ppermute x5, starting transfers between devices, across_y(): return lax.ppermute(entries, 'gy', swap)  5.12 us
    ppermute x4, waiting for transfers between devices, across_x(): lax.ppermute(entries, 'gx', [(i, i ^ distance) for i in range(count_x)])  3.99 us
    ppermute x1, starting transfers between devices, per_device(): lax.ppermute(far, 'gx', [(i, (i - 1) % count_x) for i in evens] + [((i -...  2.29 us
  transfers between devices with their start and end apart: 13, of which 9 were waited for; matrix products, arithmetic and copies ran while one was open for 0% of the time, Pallas kernels for 2%

profile of v14, /device:TPU:1, one launch (start us, length us, event | category | flops | bytes accessed | tf_op | source)
XLA Modules:
  0.0 49.0 jit_solution(4279598726597069524)
XLA Ops:
  0.6 0.1 pad_add_fusion.place_ref
  0.7 0.0 copy-start.1
  0.7 6.0 %sample.1 = (f32[232,128]{1,0:T(8,128)S(1)}, f32[19,32,128]{2,1,0:T(8,128)S(1)}, s32[512,128]{1,0:T(8,128)S(1)}, f32[512,128]{1,0:T(8,128)S(1)}) custom-call(s32[4]{0:T(128)S(1)} %pad_add_fusion.place_ref, f32[19,32,128]{2,1,0:T(8,128)} %bitcast.16, s32[512,128]{1,0:T(8,128)} %bitcast.17, f32[512,128]{1,0:T(8,128)} %bitcast.18, f32[32,128]{1,0:T(8,128)} %bitcast.19, ...), custom_call_target="tpu_custom_call" | custom-call | tf_op jit(solution)/shard_map/sample/pallas_call | solution.py:433
  6.7 4.2 %collective-permute-start = (f32[232,128]{1,0:T(8,128)S(1)}, f32[232,128]{1,0:T(8,128)S(1)}, u32[]{:S(2)}, u32[]{:S(2)}) collective-permute-start(f32[232,128]{1,0:T(8,128)S(1)} %get-tuple-element.20.refs_0_.own_ref), channel_id=1, source_target_pairs={{0,24},{8,16},{16,8},{24,0},{1,25},{9,17},{17,9},{25,1},{2,26},{10... | collective-permute-start | bytes 356360 | tf_op jit(solution)/shard_map/ppermute | solution.py:864
  10.9 1.2 %collective-permute-start.4 = (f32[232,128]{1,0:T(8,128)S(1)}, f32[232,128]{1,0:T(8,128)S(1)}, u32[]{:S(2)}, u32[]{:S(2)}) collective-permute-start(f32[232,128]{1,0:T(8,128)S(1)} %get-tuple-element.20.refs_0_.own_ref), channel_id=1, source_target_pairs={{0,4},{4,0},{1,5},{5,1},{2,6},{6,2},{3,7},{7,3},{8,12},{12,8},{9,1... | collective-permute-start | bytes 356360 | tf_op jit(solution)/shard_map/ppermute | solution.py:867
  12.1 0.0 collective-permute-start.3
  12.1 1.8 %collective-permute-done.refs_2_ = f32[232,128]{1,0:T(8,128)S(1)} collective-permute-done((f32[232,128]{1,0:T(8,128)S(1)}, f32[232,128]{1,0:T(8,128)S(1)}, u32[]{:S(2)}, u32[]{:S(2)}) %collective-permute-start) | collective-permute-done | bytes 118816 | tf_op jit(solution)/shard_map/ppermute | solution.py:864
  13.9 1.0 %collective-permute-start.1 = (f32[232,128]{1,0:T(8,128)S(1)}, f32[232,128]{1,0:T(8,128)S(1)}, u32[]{:S(2)}, u32[]{:S(2)}) collective-permute-start(f32[232,128]{1,0:T(8,128)S(1)} %collective-permute-done.refs_2_), channel_id=1, source_target_pairs={{0,4},{4,0},{1,5},{5,1},{2,6},{6,2},{3,7},{7,3},{8,12},{12,8},{9,1... | collective-permute-start | bytes 356360 | tf_op jit(solution)/shard_map/ppermute | solution.py:867
  14.9 0.0 collective-permute-done.4.refs_4_
  14.9 1.4 %collective-permute-done.3.refs_1_ = f32[232,128]{1,0:T(8,128)S(1)} collective-permute-done((f32[232,128]{1,0:T(8,128)S(1)}, f32[232,128]{1,0:T(8,128)S(1)}, u32[]{:S(2)}, u32[]{:S(2)}) %collective-permute-start.3) | collective-permute-done | bytes 118816 | tf_op jit(solution)/shard_map/ppermute | solution.py:864
  16.3 1.4 %collective-permute-start.6 = (f32[232,128]{1,0:T(8,128)S(1)}, f32[232,128]{1,0:T(8,128)S(1)}, u32[]{:S(2)}, u32[]{:S(2)}) collective-permute-start(f32[232,128]{1,0:T(8,128)S(1)} %collective-permute-done.3.refs_1_), channel_id=1, source_target_pairs={{0,4},{4,0},{1,5},{5,1},{2,6},{6,2},{3,7},{7,3},{8,12},{12,8},{9,1... | collective-permute-start | bytes 356360 | tf_op jit(solution)/shard_map/ppermute | solution.py:867
  17.7 1.2 %collective-permute-start.5 = (f32[232,128]{1,0:T(8,128)S(1)}, f32[232,128]{1,0:T(8,128)S(1)}, u32[]{:S(2)}, u32[]{:S(2)}) collective-permute-start(f32[232,128]{1,0:T(8,128)S(1)} %collective-permute-done.refs_2_), channel_id=1, source_target_pairs={{0,8},{8,0},{16,24},{24,16},{1,9},{9,1},{17,25},{25,17},{2,10},{10... | collective-permute-start | bytes 356360 | tf_op jit(solution)/shard_map/ppermute | solution.py:864
  18.9 0.0 collective-permute-done.1.refs_6_
  18.9 0.4 collective-permute-start.2
  19.3 2.2 %collective-permute-done.6.refs_5_ = f32[232,128]{1,0:T(8,128)S(1)} collective-permute-done((f32[232,128]{1,0:T(8,128)S(1)}, f32[232,128]{1,0:T(8,128)S(1)}, u32[]{:S(2)}, u32[]{:S(2)}) %collective-permute-start.6) | collective-permute-done | bytes 118816 | tf_op jit(solution)/shard_map/ppermute | solution.py:867
  21.4 0.2 collective-permute-done.5.refs_3_
  21.6 0.0 copy-done.1
  21.6 1.1 %settle.1 = (f32[96,384]{1,0:T(8,128)S(1)}, f32[64,128]{1,0:T(8,128)S(1)}, f32[64,128]{1,0:T(8,128)S(1)}, f32[12,128]{1,0:T(8,128)S(1)}, f32[128,128]{1,0:T(8,128)S(1)}) custom-call(f32[4,3]{1,0:T(4,128)S(1)} %copy-done.1, f32[232,128]{1,0:T(8,128)S(1)} %get-tuple-element.20.refs_0_.own_ref, f32[232,128]{1,0:T(8,128)S(1)} %collective-permute-done.3.refs_1_, ...), custom_call_target="tpu_custom_call" | custom-call | flops 1000000000 | bytes 831488 | tf_op jit(solution)/shard_map/settle/pallas_call | solution.py:511
  22.7 0.0 copy-start
  22.7 0.6 %collective-permute-done.2.last_ref = f32[232,128]{1,0:T(8,128)S(1)} collective-permute-done((f32[232,128]{1,0:T(8,128)S(1)}, f32[232,128]{1,0:T(8,128)S(1)}, u32[]{:S(2)}, u32[]{:S(2)}) %collective-permute-start.2) | collective-permute-done | bytes 118816 | tf_op jit(solution)/shard_map/ppermute | solution.py:864
  23.3 0.1 copy-done
  23.4 7.4 %spread.1 = (f32[19,32,128]{2,1,0:T(8,128)S(1)}, f32[5,8,128]{2,1,0:T(8,128)S(1)}, f32[5,8,128]{2,1,0:T(8,128)S(1)}, f32[24,128]{1,0:T(8,128)S(1)}, f32[3,32,128]{2,1,0:T(8,128)}) custom-call(s32[4]{0:T(128)S(1)} %pad_add_fusion.place_ref, f32[232,128]{1,0:T(8,128)S(1)} %get-tuple-element.20.refs_0_.own_ref, f32[232,128]{1,0:T(8,128)S(1)} %collective-permute-done.2.last_ref, ...), custom_call_target="tpu_custom_call" | custom-call | tf_op jit(solution)/shard_map/spread/pallas_call | solution.py:651
  30.9 2.3 %collective-permute-start.7 = (f32[5,8,128]{2,1,0:T(8,128)S(1)}, f32[5,8,128]{2,1,0:T(8,128)S(1)}, u32[]{:S(2)}, u32[]{:S(2)}) collective-permute-start(f32[5,8,128]{2,1,0:T(8,128)S(1)} %get-tuple-element.31), channel_id=1, source_target_pairs={{0,24},{16,8},{24,0},{8,16},{1,25},{17,9},{25,1},{9,17},{2,26},{18... | collective-permute-start | bytes 61448 | tf_op jit(solution)/shard_map/ppermute | solution.py:882
  33.2 0.0 collective-permute-start.8
  33.2 0.8 %collective-permute-start.9 = (f32[24,128]{1,0:T(8,128)S(1)}, f32[24,128]{1,0:T(8,128)S(1)}, u32[]{:S(2)}, u32[]{:S(2)}) collective-permute-start(f32[24,128]{1,0:T(8,128)S(1)} %get-tuple-element.33), channel_id=1, source_target_pairs={{0,4},{4,0},{1,5},{5,1},{2,6},{6,2},{3,7},{7,3},{8,12},{12,8},{9,1... | collective-permute-start | bytes 36872 | tf_op jit(solution)/shard_map/ppermute | solution.py:867
  34.0 1.7 %collective-permute-done.9.side_ref = f32[24,128]{1,0:T(8,128)S(1)} collective-permute-done((f32[24,128]{1,0:T(8,128)S(1)}, f32[24,128]{1,0:T(8,128)S(1)}, u32[]{:S(2)}, u32[]{:S(2)}) %collective-permute-start.9) | collective-permute-done | bytes 12320 | tf_op jit(solution)/shard_map/ppermute | solution.py:867
  35.7 0.0 collective-permute-done.7.far_ref
  35.7 0.1 collective-permute-done.8.near_ref
  35.8 0.7 %pack.1 = (f32[8,128]{1,0:T(8,128)S(1)}, f32[8,128]{1,0:T(8,128)S(1)}, f32[8,128]{1,0:T(8,128)S(1)}) custom-call(s32[4]{0:T(128)S(1)} %pad_add_fusion.place_ref, f32[19,32,128]{2,1,0:T(8,128)S(1)} %get-tuple-element.30.relaxed_ref, f32[5,8,128]{2,1,0:T(8,128)S(1)} %collective-permute-done.7.far_ref, f32[5,8,128]{2,1,0:T(8,128)S(1)} %collective-permute-done.8.near_ref, ...), custom_call_target="tpu_custom_call" | custom-call | tf_op jit(solution)/shard_map/pack/pallas_call | solution.py:761
  36.5 8.5 %collective-permute-start.10 = (f32[8,128]{1,0:T(8,128)S(1)}, f32[8,128]{1,0:T(8,128)S(1)}, u32[]{:S(2)}, u32[]{:S(2)}) collective-permute-start(f32[8,128]{1,0:T(8,128)S(1)} %get-tuple-element.34), channel_id=1, source_target_pairs={{1,2},{2,1},{5,6},{6,5},{9,10},{10,9},{13,14},{14,13},{17,18},{18,... | collective-permute-start | bytes 12296 | tf_op jit(solution)/shard_map/ppermute | solution.py:892
  45.0 0.7 %collective-permute-start.11 = (f32[8,128]{1,0:T(8,128)S(1)}, f32[8,128]{1,0:T(8,128)S(1)}, u32[]{:S(2)}, u32[]{:S(2)}) collective-permute-start(f32[8,128]{1,0:T(8,128)S(1)} %get-tuple-element.35), channel_id=1, source_target_pairs={{0,4},{4,0},{1,5},{5,1},{2,6},{6,2},{3,7},{7,3},{8,12},{12,8},{9,1... | collective-permute-start | bytes 12296 | tf_op jit(solution)/shard_map/ppermute | solution.py:867
  45.7 0.0 collective-permute-start.12
  45.7 0.6 %collective-permute-done.10.second_ref = f32[8,128]{1,0:T(8,128)S(1)} collective-permute-done((f32[8,128]{1,0:T(8,128)S(1)}, f32[8,128]{1,0:T(8,128)S(1)}, u32[]{:S(2)}, u32[]{:S(2)}) %collective-permute-start.10) | collective-permute-done | bytes 4128 | tf_op jit(solution)/shard_map/ppermute | solution.py:892
  46.3 1.2 %collective-permute-done.11.corner_ref = f32[8,128]{1,0:T(8,128)S(1)} collective-permute-done((f32[8,128]{1,0:T(8,128)S(1)}, f32[8,128]{1,0:T(8,128)S(1)}, u32[]{:S(2)}, u32[]{:S(2)}) %collective-permute-start.11) | collective-permute-done | bytes 4128 | tf_op jit(solution)/shard_map/ppermute | solution.py:867
  47.5 0.0 collective-permute-done.12.first_ref
  47.5 1.5 %stream.1 = f32[19,4,8,128]{3,2,1,0:T(8,128)} custom-call(s32[4]{0:T(128)S(1)} %pad_add_fusion.place_ref, f32[19,32,128]{2,1,0:T(8,128)S(1)} %get-tuple-element.30.relaxed_ref, f32[5,8,128]{2,1,0:T(8,128)S(1)} %collective-permute-done.7.far_ref, f32[5,8,128]{2,1,0:T(8,128)S(1)} %collective-permute-done.8.near_ref, ...), custom_call_target="tpu_custom_call" | custom-call | tf_op jit(solution)/shard_map/stream/pallas_call | solution.py:818
Async XLA Ops:
  0.7 20.9 %copy-start.1 = (f32[4,3]{1,0:T(4,128)S(1)}, f32[4,3]{1,0:T(4,128)}, u32[]{:S(2)}) copy-start(f32[4,3]{1,0:T(4,128)} %speeds_ref.1) | copy-start | bytes 148
  6.7 7.2 %collective-permute-start = (f32[232,128]{1,0:T(8,128)S(1)}, f32[232,128]{1,0:T(8,128)S(1)}, u32[]{:S(2)}, u32[]{:S(2)}) collective-permute-start(f32[232,128]{1,0:T(8,128)S(1)} %get-tuple-element.20.refs_0_.own_ref), channel_id=1, source_target_pairs={{0,24},{8,16},{16,8},{24,0},{1,25},{9,17},{17,9},{25,1},{2,26},{10... | collective-permute-start | bytes 356360 | tf_op jit(solution)/shard_map/ppermute | solution.py:864
  10.9 4.0 %collective-permute-start.4 = (f32[232,128]{1,0:T(8,128)S(1)}, f32[232,128]{1,0:T(8,128)S(1)}, u32[]{:S(2)}, u32[]{:S(2)}) collective-permute-start(f32[232,128]{1,0:T(8,128)S(1)} %get-tuple-element.20.refs_0_.own_ref), channel_id=1, source_target_pairs={{0,4},{4,0},{1,5},{5,1},{2,6},{6,2},{3,7},{7,3},{8,12},{12,8},{9,1... | collective-permute-start | bytes 356360 | tf_op jit(solution)/shard_map/ppermute | solution.py:867
  12.1 4.2 %collective-permute-start.3 = (f32[232,128]{1,0:T(8,128)S(1)}, f32[232,128]{1,0:T(8,128)S(1)}, u32[]{:S(2)}, u32[]{:S(2)}) collective-permute-start(f32[232,128]{1,0:T(8,128)S(1)} %get-tuple-element.20.refs_0_.own_ref), channel_id=1, source_target_pairs={{0,8},{8,0},{16,24},{24,16},{1,9},{9,1},{17,25},{25,17},{2,10},{10... | collective-permute-start | bytes 356360 | tf_op jit(solution)/shard_map/ppermute | solution.py:864
  13.9 4.9 %collective-permute-start.1 = (f32[232,128]{1,0:T(8,128)S(1)}, f32[232,128]{1,0:T(8,128)S(1)}, u32[]{:S(2)}, u32[]{:S(2)}) collective-permute-start(f32[232,128]{1,0:T(8,128)S(1)} %collective-permute-done.refs_2_), channel_id=1, source_target_pairs={{0,4},{4,0},{1,5},{5,1},{2,6},{6,2},{3,7},{7,3},{8,12},{12,8},{9,1... | collective-permute-start | bytes 356360 | tf_op jit(solution)/shard_map/ppermute | solution.py:867
  16.3 5.1 %collective-permute-start.6 = (f32[232,128]{1,0:T(8,128)S(1)}, f32[232,128]{1,0:T(8,128)S(1)}, u32[]{:S(2)}, u32[]{:S(2)}) collective-permute-start(f32[232,128]{1,0:T(8,128)S(1)} %collective-permute-done.3.refs_1_), channel_id=1, source_target_pairs={{0,4},{4,0},{1,5},{5,1},{2,6},{6,2},{3,7},{7,3},{8,12},{12,8},{9,1... | collective-permute-start | bytes 356360 | tf_op jit(solution)/shard_map/ppermute | solution.py:867
  17.7 4.0 %collective-permute-start.5 = (f32[232,128]{1,0:T(8,128)S(1)}, f32[232,128]{1,0:T(8,128)S(1)}, u32[]{:S(2)}, u32[]{:S(2)}) collective-permute-start(f32[232,128]{1,0:T(8,128)S(1)} %collective-permute-done.refs_2_), channel_id=1, source_target_pairs={{0,8},{8,0},{16,24},{24,16},{1,9},{9,1},{17,25},{25,17},{2,10},{10... | collective-permute-start | bytes 356360 | tf_op jit(solution)/shard_map/ppermute | solution.py:864
  18.9 4.5 %collective-permute-start.2 = (f32[232,128]{1,0:T(8,128)S(1)}, f32[232,128]{1,0:T(8,128)S(1)}, u32[]{:S(2)}, u32[]{:S(2)}) collective-permute-start(f32[232,128]{1,0:T(8,128)S(1)} %collective-permute-done.1.refs_6_), channel_id=1, source_target_pairs={{0,8},{8,0},{16,24},{24,16},{1,9},{9,1},{17,25},{25,17},{2,10},{10... | collective-permute-start | bytes 356360 | tf_op jit(solution)/shard_map/ppermute | solution.py:864
  22.7 0.7 %copy-start = (s32[4,8,128]{2,1,0:T(8,128)S(1)}, s32[4,8,128]{2,1,0:T(8,128)}, u32[]{:S(2)}) copy-start(s32[4,8,128]{2,1,0:T(8,128)} %param.10) | copy-start | bytes 49156
  30.9 4.8 %collective-permute-start.7 = (f32[5,8,128]{2,1,0:T(8,128)S(1)}, f32[5,8,128]{2,1,0:T(8,128)S(1)}, u32[]{:S(2)}, u32[]{:S(2)}) collective-permute-start(f32[5,8,128]{2,1,0:T(8,128)S(1)} %get-tuple-element.31), channel_id=1, source_target_pairs={{0,24},{16,8},{24,0},{8,16},{1,25},{17,9},{25,1},{9,17},{2,26},{18... | collective-permute-start | bytes 61448 | tf_op jit(solution)/shard_map/ppermute | solution.py:882
  33.2 2.6 %collective-permute-start.8 = (f32[5,8,128]{2,1,0:T(8,128)S(1)}, f32[5,8,128]{2,1,0:T(8,128)S(1)}, u32[]{:S(2)}, u32[]{:S(2)}) collective-permute-start(f32[5,8,128]{2,1,0:T(8,128)S(1)} %get-tuple-element.32), channel_id=1, source_target_pairs={{0,8},{16,24},{8,0},{24,16},{1,9},{17,25},{9,1},{25,17},{2,10},{18... | collective-permute-start | bytes 61448 | tf_op jit(solution)/shard_map/ppermute | solution.py:887
  33.2 2.5 %collective-permute-start.9 = (f32[24,128]{1,0:T(8,128)S(1)}, f32[24,128]{1,0:T(8,128)S(1)}, u32[]{:S(2)}, u32[]{:S(2)}) collective-permute-start(f32[24,128]{1,0:T(8,128)S(1)} %get-tuple-element.33), channel_id=1, source_target_pairs={{0,4},{4,0},{1,5},{5,1},{2,6},{6,2},{3,7},{7,3},{8,12},{12,8},{9,1... | collective-permute-start | bytes 36872 | tf_op jit(solution)/shard_map/ppermute | solution.py:867
  36.5 9.8 %collective-permute-start.10 = (f32[8,128]{1,0:T(8,128)S(1)}, f32[8,128]{1,0:T(8,128)S(1)}, u32[]{:S(2)}, u32[]{:S(2)}) collective-permute-start(f32[8,128]{1,0:T(8,128)S(1)} %get-tuple-element.34), channel_id=1, source_target_pairs={{1,2},{2,1},{5,6},{6,5},{9,10},{10,9},{13,14},{14,13},{17,18},{18,... | collective-permute-start | bytes 12296 | tf_op jit(solution)/shard_map/ppermute | solution.py:892
  45.0 2.5 %collective-permute-start.11 = (f32[8,128]{1,0:T(8,128)S(1)}, f32[8,128]{1,0:T(8,128)S(1)}, u32[]{:S(2)}, u32[]{:S(2)}) collective-permute-start(f32[8,128]{1,0:T(8,128)S(1)} %get-tuple-element.35), channel_id=1, source_target_pairs={{0,4},{4,0},{1,5},{5,1},{2,6},{6,2},{3,7},{7,3},{8,12},{12,8},{9,1... | collective-permute-start | bytes 12296 | tf_op jit(solution)/shard_map/ppermute | solution.py:867
  45.7 1.8 %collective-permute-start.12 = (f32[8,128]{1,0:T(8,128)S(1)}, f32[8,128]{1,0:T(8,128)S(1)}, u32[]{:S(2)}, u32[]{:S(2)}) collective-permute-start(f32[8,128]{1,0:T(8,128)S(1)} %get-tuple-element.36), channel_id=1, source_target_pairs={{0,1},{2,3},{1,0},{3,2},{4,5},{6,7},{5,4},{7,6},{8,9},{10,11},{9,8... | collective-permute-start | bytes 12296 | tf_op jit(solution)/shard_map/ppermute | solution.py:894

commit v15 on v13

--- a/solution.py
+++ b/solution.py
@@ -870,7 +870,7 @@
     beside = across_y(own)
     third_beside = across_y(third)
     second = across_x(lax.optimization_barrier((third, beside))[0], 1)
-    first_beside = across_y(first)
+    first_beside = across_y(lax.optimization_barrier((first, second))[0])
     last = across_x(third_beside, 1)
     whole = [own, first, third, second, beside, first_beside, third_beside]
     early = settle_early(slots, owned, train_velocity, whole)

time: 48.7 us -> 52.4 us (1.076)
  waiting for transfers between devices: 9.77 us -> 12.8 us
  local copies, waits for them, and re-layouts: 0.11 us -> 0.71 us
    ppermute x5, starting transfers between devices: 5.13 us -> 3.13 us  [across_y(): return lax.ppermute(entries, 'gy', swap)]
    ppermute x5, waiting for transfers between devices: 5.13 us -> 6.4 us  [across_y(): return lax.ppermute(entries, 'gy', swap)]
    ppermute x4, waiting for transfers between devices: 3.99 us -> 5.24 us  [across_x(): lax.ppermute(entries, 'gx', [(i, i ^ distance) for i in range(count_x)])]
    ppermute x1, starting transfers between devices: 8.54 us -> 9.51 us  [per_device(): lax.ppermute(down_first, 'gz', outer + [(j, i) for i, j in outer])]
    unnamed x4, local copies, waits for them, and re-layouts: 0.11 us -> 0.71 us
    ppermute x4, starting transfers between devices: 5.8 us -> 6.39 us  [across_x(): lax.ppermute(entries, 'gx', [(i, i ^ distance) for i in range(count_x)])]
    ppermute x1, waiting for transfers between devices: 0.57 us -> 1.12 us  [per_device(): lax.ppermute(down_first, 'gz', outer + [(j, i) for i, j in outer])]
where the time goes in v15:
time: 52.4 us; the launch traced here: 52.1 us
  starting transfers between devices  21.7 us (41%)
  Pallas kernels  16.1 us (31%)
  waiting for transfers between devices  12.8 us (24%)
  between operations  0.73 us (1%)
  local copies, waits for them, and re-layouts  0.71 us (1%)
    ppermute x1, starting transfers between devices, per_device(): lax.ppermute(down_first, 'gz', outer + [(j, i) for i, j in outer])  9.51 us
    pallas_call x1, Pallas kernels, spread(): pl.pallas_call(functools.partial(spread_kernel, slots, owned), out_shape=...  7.4 us
    ppermute x5, waiting for transfers between devices, across_y(): return lax.ppermute(entries, 'gy', swap)  6.4 us
    ppermute x4, starting transfers between devices, across_x(): lax.ppermute(entries, 'gx', [(i, i ^ distance) for i in range(count_x)])  6.39 us
    pallas_call x1, Pallas kernels, sample(): pl.pallas_call(sample_kernel, out_shape=[full((count, cells.shape[1]))] +...  5.5 us
    ppermute x4, waiting for transfers between devices, across_x(): lax.ppermute(entries, 'gx', [(i, i ^ distance) for i in range(count_x)])  5.24 us
    ppermute x5, starting transfers between devices, across_y(): return lax.ppermute(entries, 'gy', swap)  3.13 us
    ppermute x1, starting transfers between devices, per_device(): lax.ppermute(far, 'gx', [(i, (i - 1) % count_x) for i in evens] + [((i -...  2.56 us
  transfers between devices with their start and end apart: 13, of which 9 were waited for; matrix products, arithmetic and copies ran while one was open for 0% of the time, Pallas kernels for 2%

profile of v15, /device:TPU:1, one launch (start us, length us, event | category | flops | bytes accessed | tf_op | source)
XLA Modules:
  0.0 52.1 jit_solution(4126477132137230326)
XLA Ops:
  0.6 0.1 pad_add_fusion.place_ref
  0.7 0.0 copy-start.1
  0.7 5.5 %sample.1 = (f32[232,128]{1,0:T(8,128)S(1)}, f32[19,32,128]{2,1,0:T(8,128)S(1)}, s32[512,128]{1,0:T(8,128)S(1)}, f32[512,128]{1,0:T(8,128)S(1)}) custom-call(s32[4]{0:T(128)S(1)} %pad_add_fusion.place_ref, f32[19,32,128]{2,1,0:T(8,128)} %bitcast.16, s32[512,128]{1,0:T(8,128)} %bitcast.17, f32[512,128]{1,0:T(8,128)} %bitcast.18, f32[32,128]{1,0:T(8,128)} %bitcast.19, ...), custom_call_target="tpu_custom_call" | custom-call | tf_op jit(solution)/shard_map/sample/pallas_call | solution.py:433
  6.2 2.1 %collective-permute-start.4 = (f32[232,128]{1,0:T(8,128)S(1)}, f32[232,128]{1,0:T(8,128)S(1)}, u32[]{:S(2)}, u32[]{:S(2)}) collective-permute-start(f32[232,128]{1,0:T(8,128)S(1)} %get-tuple-element.21.refs_0_.own_ref), channel_id=1, source_target_pairs={{0,4},{4,0},{1,5},{5,1},{2,6},{6,2},{3,7},{7,3},{8,12},{12,8},{9,1... | collective-permute-start | bytes 356360 | tf_op jit(solution)/shard_map/ppermute | solution.py:867
  8.3 3.3 %collective-permute-start = (f32[232,128]{1,0:T(8,128)S(1)}, f32[232,128]{1,0:T(8,128)S(1)}, u32[]{:S(2)}, u32[]{:S(2)}) collective-permute-start(f32[232,128]{1,0:T(8,128)S(1)} %get-tuple-element.21.refs_0_.own_ref), channel_id=1, source_target_pairs={{0,24},{8,16},{16,8},{24,0},{1,25},{9,17},{17,9},{25,1},{2,26},{10... | collective-permute-start | bytes 356360 | tf_op jit(solution)/shard_map/ppermute | solution.py:864
  11.7 0.0 collective-permute-start.3
  11.7 0.0 collective-permute-done.4.refs_4_
  11.7 2.3 %collective-permute-done.refs_2_ = f32[232,128]{1,0:T(8,128)S(1)} collective-permute-done((f32[232,128]{1,0:T(8,128)S(1)}, f32[232,128]{1,0:T(8,128)S(1)}, u32[]{:S(2)}, u32[]{:S(2)}) %collective-permute-start) | collective-permute-done | bytes 118816 | tf_op jit(solution)/shard_map/ppermute | solution.py:864
  14.0 1.7 %collective-permute-start.5 = (f32[232,128]{1,0:T(8,128)S(1)}, f32[232,128]{1,0:T(8,128)S(1)}, u32[]{:S(2)}, u32[]{:S(2)}) collective-permute-start(f32[232,128]{1,0:T(8,128)S(1)} %collective-permute-done.refs_2_), channel_id=1, source_target_pairs={{0,8},{8,0},{16,24},{24,16},{1,9},{9,1},{17,25},{25,17},{2,10},{10... | collective-permute-start | bytes 356360 | tf_op jit(solution)/shard_map/ppermute | solution.py:864
  15.7 0.5 collective-permute-start.1
  16.2 1.0 %collective-permute-done.3.refs_1_ = f32[232,128]{1,0:T(8,128)S(1)} collective-permute-done((f32[232,128]{1,0:T(8,128)S(1)}, f32[232,128]{1,0:T(8,128)S(1)}, u32[]{:S(2)}, u32[]{:S(2)}) %collective-permute-start.3) | collective-permute-done | bytes 118816 | tf_op jit(solution)/shard_map/ppermute | solution.py:864
  17.2 1.9 %collective-permute-done.5.refs_3_ = f32[232,128]{1,0:T(8,128)S(1)} collective-permute-done((f32[232,128]{1,0:T(8,128)S(1)}, f32[232,128]{1,0:T(8,128)S(1)}, u32[]{:S(2)}, u32[]{:S(2)}) %collective-permute-start.5) | collective-permute-done | bytes 118816 | tf_op jit(solution)/shard_map/ppermute | solution.py:864
  19.1 0.2 collective-permute-start.6
  19.3 0.1 collective-permute-done.1.refs_6_
  19.4 1.3 %collective-permute-start.2 = (f32[232,128]{1,0:T(8,128)S(1)}, f32[232,128]{1,0:T(8,128)S(1)}, u32[]{:S(2)}, u32[]{:S(2)}) collective-permute-start(f32[232,128]{1,0:T(8,128)S(1)} %collective-permute-done.1.refs_6_), channel_id=1, source_target_pairs={{0,8},{8,0},{16,24},{24,16},{1,9},{9,1},{17,25},{25,17},{2,10},{10... | collective-permute-start | bytes 356360 | tf_op jit(solution)/shard_map/ppermute | solution.py:864
  20.7 2.8 %collective-permute-done.6.refs_5_ = f32[232,128]{1,0:T(8,128)S(1)} collective-permute-done((f32[232,128]{1,0:T(8,128)S(1)}, f32[232,128]{1,0:T(8,128)S(1)}, u32[]{:S(2)}, u32[]{:S(2)}) %collective-permute-start.6) | collective-permute-done | bytes 118816 | tf_op jit(solution)/shard_map/ppermute | solution.py:867
  23.5 0.0 copy-done.1
  23.5 1.1 %settle.1 = (f32[96,384]{1,0:T(8,128)S(1)}, f32[64,128]{1,0:T(8,128)S(1)}, f32[64,128]{1,0:T(8,128)S(1)}, f32[12,128]{1,0:T(8,128)S(1)}, f32[128,128]{1,0:T(8,128)S(1)}) custom-call(f32[4,3]{1,0:T(4,128)S(1)} %copy-done.1, f32[232,128]{1,0:T(8,128)S(1)} %get-tuple-element.21.refs_0_.own_ref, f32[232,128]{1,0:T(8,128)S(1)} %collective-permute-done.3.refs_1_, ...), custom_call_target="tpu_custom_call" | custom-call | flops 1000000000 | bytes 831488 | tf_op jit(solution)/shard_map/settle/pallas_call | solution.py:511
  24.6 0.0 copy-start
  24.6 0.0 collective-permute-done.2.last_ref
  24.6 0.7 %copy-done = s32[4,8,128]{2,1,0:T(8,128)S(1)} copy-done((s32[4,8,128]{2,1,0:T(8,128)S(1)}, s32[4,8,128]{2,1,0:T(8,128)}, u32[]{:S(2)}) %copy-start) | copy-done | bytes 16408
  25.3 7.4 %spread.1 = (f32[19,32,128]{2,1,0:T(8,128)S(1)}, f32[5,8,128]{2,1,0:T(8,128)S(1)}, f32[5,8,128]{2,1,0:T(8,128)S(1)}, f32[24,128]{1,0:T(8,128)S(1)}, f32[3,32,128]{2,1,0:T(8,128)}) custom-call(s32[4]{0:T(128)S(1)} %pad_add_fusion.place_ref, f32[232,128]{1,0:T(8,128)S(1)} %get-tuple-element.21.refs_0_.own_ref, f32[232,128]{1,0:T(8,128)S(1)} %collective-permute-done.2.last_ref, ...), custom_call_target="tpu_custom_call" | custom-call | tf_op jit(solution)/shard_map/spread/pallas_call | solution.py:651
  32.8 2.6 %collective-permute-start.7 = (f32[5,8,128]{2,1,0:T(8,128)S(1)}, f32[5,8,128]{2,1,0:T(8,128)S(1)}, u32[]{:S(2)}, u32[]{:S(2)}) collective-permute-start(f32[5,8,128]{2,1,0:T(8,128)S(1)} %get-tuple-element.33), channel_id=1, source_target_pairs={{0,24},{16,8},{24,0},{8,16},{1,25},{17,9},{25,1},{9,17},{2,26},{18... | collective-permute-start | bytes 61448 | tf_op jit(solution)/shard_map/ppermute | solution.py:882
  35.3 0.0 collective-permute-start.8
  35.3 0.3 collective-permute-start.9
  35.6 2.3 %collective-permute-done.9.side_ref = f32[24,128]{1,0:T(8,128)S(1)} collective-permute-done((f32[24,128]{1,0:T(8,128)S(1)}, f32[24,128]{1,0:T(8,128)S(1)}, u32[]{:S(2)}, u32[]{:S(2)}) %collective-permute-start.9) | collective-permute-done | bytes 12320 | tf_op jit(solution)/shard_map/ppermute | solution.py:867
  37.9 0.0 collective-permute-done.7.far_ref
  37.9 0.1 collective-permute-done.8.near_ref
  37.9 0.7 %pack.1 = (f32[8,128]{1,0:T(8,128)S(1)}, f32[8,128]{1,0:T(8,128)S(1)}, f32[8,128]{1,0:T(8,128)S(1)}) custom-call(s32[4]{0:T(128)S(1)} %pad_add_fusion.place_ref, f32[19,32,128]{2,1,0:T(8,128)S(1)} %get-tuple-element.32.relaxed_ref, f32[5,8,128]{2,1,0:T(8,128)S(1)} %collective-permute-done.7.far_ref, f32[5,8,128]{2,1,0:T(8,128)S(1)} %collective-permute-done.8.near_ref, ...), custom_call_target="tpu_custom_call" | custom-call | tf_op jit(solution)/shard_map/pack/pallas_call | solution.py:761
  38.6 9.5 %collective-permute-start.10 = (f32[8,128]{1,0:T(8,128)S(1)}, f32[8,128]{1,0:T(8,128)S(1)}, u32[]{:S(2)}, u32[]{:S(2)}) collective-permute-start(f32[8,128]{1,0:T(8,128)S(1)} %get-tuple-element.36), channel_id=1, source_target_pairs={{1,2},{2,1},{5,6},{6,5},{9,10},{10,9},{13,14},{14,13},{17,18},{18,... | collective-permute-start | bytes 12296 | tf_op jit(solution)/shard_map/ppermute | solution.py:892
  48.1 0.1 collective-permute-start.11
  48.2 0.1 collective-permute-start.12
  48.3 1.1 %collective-permute-done.10.second_ref = f32[8,128]{1,0:T(8,128)S(1)} collective-permute-done((f32[8,128]{1,0:T(8,128)S(1)}, f32[8,128]{1,0:T(8,128)S(1)}, u32[]{:S(2)}, u32[]{:S(2)}) %collective-permute-start.10) | collective-permute-done | bytes 4128 | tf_op jit(solution)/shard_map/ppermute | solution.py:892
  49.4 1.2 %collective-permute-done.11.corner_ref = f32[8,128]{1,0:T(8,128)S(1)} collective-permute-done((f32[8,128]{1,0:T(8,128)S(1)}, f32[8,128]{1,0:T(8,128)S(1)}, u32[]{:S(2)}, u32[]{:S(2)}) %collective-permute-start.11) | collective-permute-done | bytes 4128 | tf_op jit(solution)/shard_map/ppermute | solution.py:867
  50.7 0.0 collective-permute-done.12.first_ref
  50.7 1.5 %stream.1 = f32[19,4,8,128]{3,2,1,0:T(8,128)} custom-call(s32[4]{0:T(128)S(1)} %pad_add_fusion.place_ref, f32[19,32,128]{2,1,0:T(8,128)S(1)} %get-tuple-element.32.relaxed_ref, f32[5,8,128]{2,1,0:T(8,128)S(1)} %collective-permute-done.7.far_ref, f32[5,8,128]{2,1,0:T(8,128)S(1)} %collective-permute-done.8.near_ref, ...), custom_call_target="tpu_custom_call" | custom-call | tf_op jit(solution)/shard_map/stream/pallas_call | solution.py:818
Async XLA Ops:
  0.7 22.8 %copy-start.1 = (f32[4,3]{1,0:T(4,128)S(1)}, f32[4,3]{1,0:T(4,128)}, u32[]{:S(2)}) copy-start(f32[4,3]{1,0:T(4,128)} %speeds_ref.1) | copy-start | bytes 148
  6.2 5.4 %collective-permute-start.4 = (f32[232,128]{1,0:T(8,128)S(1)}, f32[232,128]{1,0:T(8,128)S(1)}, u32[]{:S(2)}, u32[]{:S(2)}) collective-permute-start(f32[232,128]{1,0:T(8,128)S(1)} %get-tuple-element.21.refs_0_.own_ref), channel_id=1, source_target_pairs={{0,4},{4,0},{1,5},{5,1},{2,6},{6,2},{3,7},{7,3},{8,12},{12,8},{9,1... | collective-permute-start | bytes 356360 | tf_op jit(solution)/shard_map/ppermute | solution.py:867
  8.3 5.7 %collective-permute-start = (f32[232,128]{1,0:T(8,128)S(1)}, f32[232,128]{1,0:T(8,128)S(1)}, u32[]{:S(2)}, u32[]{:S(2)}) collective-permute-start(f32[232,128]{1,0:T(8,128)S(1)} %get-tuple-element.21.refs_0_.own_ref), channel_id=1, source_target_pairs={{0,24},{8,16},{16,8},{24,0},{1,25},{9,17},{17,9},{25,1},{2,26},{10... | collective-permute-start | bytes 356360 | tf_op jit(solution)/shard_map/ppermute | solution.py:864
  11.7 5.6 %collective-permute-start.3 = (f32[232,128]{1,0:T(8,128)S(1)}, f32[232,128]{1,0:T(8,128)S(1)}, u32[]{:S(2)}, u32[]{:S(2)}) collective-permute-start(f32[232,128]{1,0:T(8,128)S(1)} %get-tuple-element.21.refs_0_.own_ref), channel_id=1, source_target_pairs={{0,8},{8,0},{16,24},{24,16},{1,9},{9,1},{17,25},{25,17},{2,10},{10... | collective-permute-start | bytes 356360 | tf_op jit(solution)/shard_map/ppermute | solution.py:864
  14.0 5.1 %collective-permute-start.5 = (f32[232,128]{1,0:T(8,128)S(1)}, f32[232,128]{1,0:T(8,128)S(1)}, u32[]{:S(2)}, u32[]{:S(2)}) collective-permute-start(f32[232,128]{1,0:T(8,128)S(1)} %collective-permute-done.refs_2_), channel_id=1, source_target_pairs={{0,8},{8,0},{16,24},{24,16},{1,9},{9,1},{17,25},{25,17},{2,10},{10... | collective-permute-start | bytes 356360 | tf_op jit(solution)/shard_map/ppermute | solution.py:864
  15.7 3.7 %collective-permute-start.1 = (f32[232,128]{1,0:T(8,128)S(1)}, f32[232,128]{1,0:T(8,128)S(1)}, u32[]{:S(2)}, u32[]{:S(2)}) collective-permute-start(f32[232,128]{1,0:T(8,128)S(1)} %collective-permute-done.refs_2_), channel_id=1, source_target_pairs={{0,4},{4,0},{1,5},{5,1},{2,6},{6,2},{3,7},{7,3},{8,12},{12,8},{9,1... | collective-permute-start | bytes 356360 | tf_op jit(solution)/shard_map/ppermute | solution.py:867
  19.1 4.4 %collective-permute-start.6 = (f32[232,128]{1,0:T(8,128)S(1)}, f32[232,128]{1,0:T(8,128)S(1)}, u32[]{:S(2)}, u32[]{:S(2)}) collective-permute-start(f32[232,128]{1,0:T(8,128)S(1)} %collective-permute-done.3.refs_1_), channel_id=1, source_target_pairs={{0,4},{4,0},{1,5},{5,1},{2,6},{6,2},{3,7},{7,3},{8,12},{12,8},{9,1... | collective-permute-start | bytes 356360 | tf_op jit(solution)/shard_map/ppermute | solution.py:867
  19.4 5.2 %collective-permute-start.2 = (f32[232,128]{1,0:T(8,128)S(1)}, f32[232,128]{1,0:T(8,128)S(1)}, u32[]{:S(2)}, u32[]{:S(2)}) collective-permute-start(f32[232,128]{1,0:T(8,128)S(1)} %collective-permute-done.1.refs_6_), channel_id=1, source_target_pairs={{0,8},{8,0},{16,24},{24,16},{1,9},{9,1},{17,25},{25,17},{2,10},{10... | collective-permute-start | bytes 356360 | tf_op jit(solution)/shard_map/ppermute | solution.py:864
  24.6 0.7 %copy-start = (s32[4,8,128]{2,1,0:T(8,128)S(1)}, s32[4,8,128]{2,1,0:T(8,128)}, u32[]{:S(2)}) copy-start(s32[4,8,128]{2,1,0:T(8,128)} %param.10) | copy-start | bytes 49156
  32.8 5.1 %collective-permute-start.7 = (f32[5,8,128]{2,1,0:T(8,128)S(1)}, f32[5,8,128]{2,1,0:T(8,128)S(1)}, u32[]{:S(2)}, u32[]{:S(2)}) collective-permute-start(f32[5,8,128]{2,1,0:T(8,128)S(1)} %get-tuple-element.33), channel_id=1, source_target_pairs={{0,24},{16,8},{24,0},{8,16},{1,25},{17,9},{25,1},{9,17},{2,26},{18... | collective-permute-start | bytes 61448 | tf_op jit(solution)/shard_map/ppermute | solution.py:882
  35.3 2.6 %collective-permute-start.8 = (f32[5,8,128]{2,1,0:T(8,128)S(1)}, f32[5,8,128]{2,1,0:T(8,128)S(1)}, u32[]{:S(2)}, u32[]{:S(2)}) collective-permute-start(f32[5,8,128]{2,1,0:T(8,128)S(1)} %get-tuple-element.34), channel_id=1, source_target_pairs={{0,8},{16,24},{8,0},{24,16},{1,9},{17,25},{9,1},{25,17},{2,10},{18... | collective-permute-start | bytes 61448 | tf_op jit(solution)/shard_map/ppermute | solution.py:887
  35.3 2.5 %collective-permute-start.9 = (f32[24,128]{1,0:T(8,128)S(1)}, f32[24,128]{1,0:T(8,128)S(1)}, u32[]{:S(2)}, u32[]{:S(2)}) collective-permute-start(f32[24,128]{1,0:T(8,128)S(1)} %get-tuple-element.35), channel_id=1, source_target_pairs={{0,4},{4,0},{1,5},{5,1},{2,6},{6,2},{3,7},{7,3},{8,12},{12,8},{9,1... | collective-permute-start | bytes 36872 | tf_op jit(solution)/shard_map/ppermute | solution.py:867
  38.6 10.8 %collective-permute-start.10 = (f32[8,128]{1,0:T(8,128)S(1)}, f32[8,128]{1,0:T(8,128)S(1)}, u32[]{:S(2)}, u32[]{:S(2)}) collective-permute-start(f32[8,128]{1,0:T(8,128)S(1)} %get-tuple-element.36), channel_id=1, source_target_pairs={{1,2},{2,1},{5,6},{6,5},{9,10},{10,9},{13,14},{14,13},{17,18},{18,... | collective-permute-start | bytes 12296 | tf_op jit(solution)/shard_map/ppermute | solution.py:892
  48.1 2.5 %collective-permute-start.11 = (f32[8,128]{1,0:T(8,128)S(1)}, f32[8,128]{1,0:T(8,128)S(1)}, u32[]{:S(2)}, u32[]{:S(2)}) collective-permute-start(f32[8,128]{1,0:T(8,128)S(1)} %get-tuple-element.37), channel_id=1, source_target_pairs={{0,4},{4,0},{1,5},{5,1},{2,6},{6,2},{3,7},{7,3},{8,12},{12,8},{9,1... | collective-permute-start | bytes 12296 | tf_op jit(solution)/shard_map/ppermute | solution.py:867
  48.2 2.4 %collective-permute-start.12 = (f32[8,128]{1,0:T(8,128)S(1)}, f32[8,128]{1,0:T(8,128)S(1)}, u32[]{:S(2)}, u32[]{:S(2)}) collective-permute-start(f32[8,128]{1,0:T(8,128)S(1)} %get-tuple-element.38), channel_id=1, source_target_pairs={{0,1},{2,3},{1,0},{3,2},{4,5},{6,7},{5,4},{7,6},{8,9},{10,11},{9,8... | collective-permute-start | bytes 12296 | tf_op jit(solution)/shard_map/ppermute | solution.py:894
